TPU v7x, 256 devices: a whole 4x4x8 slice. The times are simulated.
256 devices in a mesh: gz: 4 (over y), gy: 4 (over z_lo, core), gx: 16 (over x, z_hi).
Axes of the slice: x: 4, y: 4, z: 8 (z_hi: 4, z_lo: 2; z = z_hi * 2 + z_lo), core: 2. Of those that a mesh axis runs over, the one named last changes fastest.
Arguments:
- filtered: float32 [64, 512, 2048], P('gz', 'gy', 'gx'), may hold values from 0.3 to 1
- printed: float32 [64, 512, 2048], P('gz', 'gy', 'gx'), may hold values from 0.3 to 0.7
- sensitivity: float32 [64, 512, 2048], P('gz', 'gy', 'gx'), may hold values from -6 to 6
- passive: int32 [64, 512, 2048], P('gz', 'gy', 'gx'), may hold values 0 or 1
Outputs:
- design_grad: float32 [64, 512, 2048], P('gz', 'gy', 'gx')
All inputs are finite; a program needn't handle non-finite values. No bound on the sum of `passive` on one device may be relied on, other than what follows from the above.
Results may differ from a plain program's by a relative error of at most 0.000064.
Values sent between devices are 32-bit elements; how exact they have to be, the bound alone decides.
No kernel may reach another device: no remote copies, remote signals or barrier semaphores. Data moves between devices by JAX's collectives and lax.ppermute only.
A program may use at most 128 MiB of HBM per device.

v0:
```python
import math

import jax
import jax.numpy as jnp
from jax import lax
from jax.sharding import PartitionSpec as P

RADIUS = 4


PENALTY = 40.0
EXPONENT = PENALTY + math.log(5.0) / math.log(0.5)
SMOOTH = 0.001


def passed_along(value, axis, steps):
    count = lax.axis_size(axis)
    initial, last = (max(0, -steps), min(count, count - steps))
    return lax.ppermute(value, axis, [(source, source + steps) for source in range(initial, last)])


def extended(value, sides, width):
    for axis, dim in sides:
        size, length = (lax.axis_size(axis), value.shape[dim])
        up = [(i, (i + 1) % size) for i in range(size - 1)]
        down = [(j, i) for i, j in up]
        last = lax.slice_in_dim(value, length - width, length, axis=dim)
        initial = lax.slice_in_dim(value, 0, width, axis=dim)
        before = lax.ppermute(last, axis, up)
        after = lax.ppermute(initial, axis, down)
        value = jnp.concatenate([before, value, after], axis=dim)
    return value


def support_terms(lower_plane, density, valid):
    members = (
        lower_plane[..., 1:-1, 1:-1],
        lower_plane[..., :-2, 1:-1],
        lower_plane[..., 2:, 1:-1],
        lower_plane[..., 1:-1, :-2],
        lower_plane[..., 1:-1, 2:],
    )
    largest = members[0]
    for member in members[1:]:
        largest = jnp.maximum(largest, member)
    largest = jnp.where(valid, largest, 1.0)
    powers = [jnp.power(member / largest, PENALTY - 1.0) for member in members]
    total = powers[0] * (members[0] / largest)
    for power_term, member in zip(powers[1:], members[1:]):
        total = total + power_term * (member / largest)
    smooth_max = jnp.power(largest, PENALTY / EXPONENT) * jnp.power(total, 1.0 / EXPONENT)
    gap = density - smooth_max
    radical = jnp.sqrt(gap * gap + SMOOTH)
    weight_low = 0.5 * (1.0 - gap / radical)
    weight_high = 0.5 * (1.0 + gap / radical)
    factor = jnp.where(
        valid, weight_high * (PENALTY / EXPONENT) * smooth_max / (largest * total), 0.0
    )
    ratios = tuple((jnp.where(valid, power_term, 0.0) for power_term in powers))
    return (factor, ratios, weight_low)


def tent_pass(padded, dim, count):
    total = None
    for offset in range(-RADIUS, RADIUS + 1):
        sliced = lax.slice_in_dim(
            padded, RADIUS + offset, RADIUS + offset + count, axis=dim
        ) * float(RADIUS + 1 - abs(offset))
        total = sliced if total is None else total + sliced
    return total


def axis_norm(start, count, extent):
    position = start + jnp.arange(count, dtype=jnp.int32)
    total = jnp.zeros((count,), jnp.float32)
    for offset in range(-RADIUS, RADIUS + 1):
        inside = ((position + offset >= 0) & (position + offset < extent)).astype(jnp.float32)
        total = total + inside * float(RADIUS + 1 - abs(offset))
    return total


def per_device(filtered, printed, sensitivity, passive):
    layers, rows, cols = printed.shape
    depth_no = lax.axis_index("gz")
    row_no = lax.axis_index("gy")
    col_no = lax.axis_index("gx")
    total_rows = rows * lax.axis_size("gy")
    total_cols = cols * lax.axis_size("gx")
    below_top = passed_along(printed[layers - 1], "gz", 1)
    above_base = passed_along(filtered[0], "gz", -1)
    lower_stack = jnp.concatenate([below_top[None], printed], axis=0)
    density_stack = jnp.concatenate([filtered, above_base[None]], axis=0)
    layer_ok = depth_no * layers + jnp.arange(layers + 1, dtype=jnp.int32) >= 1
    margin = 1
    lower_ext = extended(lower_stack, (("gy", 1), ("gx", 2)), 2)
    density_ext = jnp.pad(density_stack, ((0, 0), (1, 1), (1, 1)))
    row_pos = row_no * rows - margin + jnp.arange(rows + 2 * margin, dtype=jnp.int32)
    col_pos = col_no * cols - margin + jnp.arange(cols + 2 * margin, dtype=jnp.int32)
    rows_in = (row_pos >= 0) & (row_pos < total_rows)
    cols_in = (col_pos >= 0) & (col_pos < total_cols)
    factor, ratios, weight_low = support_terms(
        lower_ext,
        density_ext,
        layer_ok[:, None, None] & rows_in[None, :, None] & cols_in[None, None, :],
    )
    ratio_stack = jnp.stack(ratios, axis=1)
    own_low = weight_low[:layers, margin : margin + rows, margin : margin + cols]
    own_low = jnp.where(layer_ok[:layers, None, None], own_low, 1.0)
    factor_own = factor[:, margin : margin + rows, margin : margin + cols]

    def layer_step(sens_above, planes):
        factor_plane, ratio_plane, extra_plane = planes
        scaled = sens_above * factor_plane
        border = extended(scaled, (("gy", 0), ("gx", 1)), 1)
        sens_below = (
            extra_plane
            + scaled * ratio_plane[0][1:-1, 1:-1]
            + (border * ratio_plane[1])[2:, 1:-1]
            + (border * ratio_plane[2])[:-2, 1:-1]
            + (border * ratio_plane[3])[1:-1, 2:]
            + (border * ratio_plane[4])[1:-1, :-2]
        )
        return (sens_below, sens_below)

    sens_planes = None
    carry_in = jnp.zeros((rows, cols), jnp.float32)
    for section_no in range(lax.axis_size("gz")):
        if section_no > 0:
            carry_in = passed_along(sens_planes[0], "gz", -1)
        final_plane, sens_planes = lax.scan(
            layer_step, carry_in, (factor_own[1:], ratio_stack[1:], sensitivity), reverse=True
        )
    raw_terms = sens_planes * own_low
    norm_z = axis_norm(depth_no * layers, layers, layers * lax.axis_size("gz"))
    norm_y = axis_norm(row_no * rows, rows, total_rows)
    norm_x = axis_norm(col_no * cols, cols, total_cols)
    weighted = raw_terms / (norm_z[:, None, None] * norm_y[None, :, None] * norm_x[None, None, :])
    padded = extended(weighted, (("gz", 0), ("gy", 1), ("gx", 2)), RADIUS)
    along_z = tent_pass(padded, 0, layers)
    along_y = tent_pass(along_z, 1, rows)
    smoothed = tent_pass(along_y, 2, cols)
    return jnp.where(passive > 0, 0.0, smoothed)


def solution(mesh):
    in_specs = (P("gz", "gy", "gx"), P("gz", "gy", "gx"), P("gz", "gy", "gx"), P("gz", "gy", "gx"))
    out_specs = P("gz", "gy", "gx")
    return jax.shard_map(
        per_device, mesh=mesh, in_specs=in_specs, out_specs=out_specs, check_vma=False
    )
```

profile of v0, /device:TPU:1, one launch (start us, length us, event | category | flops | bytes accessed | tf_op | source)
XLA Modules:
  0.0 1388.2 jit_solution(8124415985458377542)
XLA Ops:
  51.8 9.4 slice.814
  61.2 9.1 copy.38
  70.3 11.9 rsqrt_multiply_fusion
  85.4 298.4 %while.68 = (s32[]{:T(128)}, f32[128,128]{1,0:T(8,128)S(1)}, f32[16,128,128]{2,1,0:T(8,128)S(1)}, f32[16,128,128]{2,1,0:T(8,128)}, f32[16,128,128]{2,1,0:T(8,128...) while((s32[]{:T(128)}, f32[128,128]{1,0:T(8,128)S(1)}, ...), condition=%wide.region_1.2_spmd.clone, body=%wide.region_0.1_spmd.clone.sunk | while | flops 297496 | bytes 2005663 | solution.py:130
  258.2 7.6 collective-permute-start.15
  277.5 7.6 collective-permute-start.15
  296.7 7.6 collective-permute-start.15
  316.0 7.6 collective-permute-start.15
  335.2 7.6 collective-permute-start.15
  354.5 7.6 collective-permute-start.15
  373.7 7.6 collective-permute-start.15
  389.9 308.8 %while.65 = (s32[]{:T(128)}, f32[128,128]{1,0:T(8,128)S(1)}, f32[16,128,128]{2,1,0:T(8,128)S(1)}, f32[16,128,128]{2,1,0:T(8,128)}, f32[16,128,128]{2,1,0:T(8,128...) while((s32[]{:T(128)}, f32[128,128]{1,0:T(8,128)S(1)}, ...), condition=%wide.region_3.4_spmd, body=%wide.region_2.3_spmd.sunk | while | flops 281111 | bytes 2005653 | solution.py:130
  399.9 7.6 collective-permute-start.3
  419.1 7.6 collective-permute-start.3
  438.4 7.6 collective-permute-start.3
  457.6 7.6 collective-permute-start.3
  476.9 7.6 collective-permute-start.3
  496.1 7.6 collective-permute-start.3
  515.4 7.6 collective-permute-start.3
  534.6 7.6 collective-permute-start.3
  553.9 7.6 collective-permute-start.3
  704.2 308.8 %while.66 = (s32[]{:T(128)}, f32[128,128]{1,0:T(8,128)S(1)}, f32[16,128,128]{2,1,0:T(8,128)S(1)}, f32[16,128,128]{2,1,0:T(8,128)}, f32[16,128,128]{2,1,0:T(8,128...) while((s32[]{:T(128)}, f32[128,128]{1,0:T(8,128)S(1)}, ...), condition=%wide.region_5.6_spmd, body=%wide.region_4.5_spmd.sunk | while | flops 281111 | bytes 2005653 | solution.py:130
  1018.4 308.8 %while.67 = (s32[]{:T(128)}, f32[128,128]{1,0:T(8,128)S(1)}, f32[16,128,128]{2,1,0:T(8,128)S(1)}, f32[16,128,128]{2,1,0:T(8,128)}, f32[16,128,128]{2,1,0:T(8,128...) while((s32[]{:T(128)}, f32[128,128]{1,0:T(8,128)S(1)}, ...), condition=%wide.region_7.8_spmd, body=%wide.region_6.7_spmd.sunk | while | flops 281111 | bytes 2005653 | solution.py:130
  1367.4 8.0 collective-permute-done.30
  (1047 shorter events, 1220.8 us)
Async XLA Ops:
  6.4 63.9 %collective-permute-start.16 = (f32[128,128]{1,0:T(8,128)}, f32[128,128]{1,0:T(8,128)}, u32[]{:S(2)}, u32[]{:S(2)}) collective-permute-start(f32[128,128]{1,0:T(8,128)} %slice_bitcast_fusion.4), channel_id=1, source_target_pairs={{64,0},{128,64},{192,128},{65,1},{129,65},{193,129},{66,2},{130,66... | collective-permute-start | bytes 196616 | tf_op jit(solution)/shard_map/ppermute | solution.py:19
  256.9 10.2 collective-permute-start.14
  295.4 10.2 collective-permute-start.14
  314.7 10.2 collective-permute-start.14
  353.2 10.2 collective-permute-start.14
  372.4 10.2 collective-permute-start.14
  398.6 10.2 collective-permute-start.2
  417.8 10.2 collective-permute-start.2
  437.1 10.2 collective-permute-start.2
  456.3 10.2 collective-permute-start.2
  475.6 10.2 collective-permute-start.2
  514.1 10.2 collective-permute-start.2
  533.3 10.2 collective-permute-start.2
  552.6 10.2 collective-permute-start.2
  571.8 10.2 collective-permute-start.2
  591.0 10.2 collective-permute-start.2
  610.3 10.2 collective-permute-start.2
  629.5 10.2 collective-permute-start.2
  648.8 10.2 collective-permute-start.2
  668.0 10.2 collective-permute-start.2
  712.8 10.2 collective-permute-start.6
  732.1 10.2 collective-permute-start.6
  751.3 10.2 collective-permute-start.6
  1356.5 10.3 collective-permute-start.29
  (259 other events, 2551.2 us)
where the time goes:
time: 1410 us; the launch traced here: 1390 us
  starting transfers between devices  1050 us (74%)
  other arithmetic  124 us (9%)
  local copies, waits for them, and re-layouts  120 us (9%)
  waiting for transfers between devices  88.2 us (6%)
    ppermute x133, starting transfers between devices, extended(): before = lax.ppermute(last, axis, up)  827 us
    ppermute x133, starting transfers between devices, extended(): after = lax.ppermute(initial, axis, down)  213 us
    squeeze x64, local copies, waits for them, and re-layouts, layer_step(): ratio_plane[0][1:-1, 1:-1]  79.5 us
    dynamic_update_slice x64, other arithmetic, per_device(): lax.scan(layer_step, carry_in, (factor_own[1:], ratio_stack[1:], sensitiv...  66.7 us
    ppermute x133, waiting for transfers between devices, extended(): before = lax.ppermute(last, axis, up)  53.7 us
  transfers between devices with their start and end apart: 271, of which 137 were waited for; matrix products, arithmetic and copies ran while one was open for 9% of the time, Pallas kernels for 0%

commit v1 on v0

v1 whole, which is shorter than its diff:
```python
import functools
import math

import jax
import jax.numpy as jnp
from jax import lax
from jax.experimental import pallas as pl
from jax.experimental.pallas import tpu as pltpu
from jax.sharding import PartitionSpec as P

RADIUS = 4
PENALTY = 40.0
EXPONENT = PENALTY + math.log(5.0) / math.log(0.5)
SMOOTH = 0.001
AXES = ("gz", "gy", "gx")
F32 = jnp.float32

GROUPS = ((13, 16, 24), (9, 13, 16), (3, 9, 16), (0, 3, 8))
PAD = 24
RING = 8


def strips_of(group):
    first, end, _ = GROUPS[group]
    strips, at = [], 0
    for layer in range(end - 1, first - 1, -1):
        for name in ("u", "v"):
            strips.append((name, layer, at, RADIUS + layer))
            at += RADIUS + layer
    if first == 0:
        for layer in range(16):
            strips.append(("w", layer, at, RADIUS))
            at += RADIUS
    assert at <= 128
    return strips


def send(value, dz, dy, dx):
    sizes = tuple(lax.axis_size(axis) for axis in AXES)
    pairs = []
    for z in range(sizes[0]):
        for y in range(sizes[1]):
            for x in range(sizes[2]):
                tz, ty, tx = z + dz, y + dy, x + dx
                if 0 <= tz < sizes[0] and 0 <= ty < sizes[1] and 0 <= tx < sizes[2]:
                    pairs.append(
                        ((z * sizes[1] + y) * sizes[2] + x, (tz * sizes[1] + ty) * sizes[2] + tx)
                    )
    return lax.ppermute(value, AXES, pairs)


def shape(*dims):
    return jax.ShapeDtypeStruct(dims, F32)


def call(kernel, outs, *args, scratch=(), cost=None):
    return pl.pallas_call(
        kernel,
        out_shape=outs,
        scratch_shapes=list(scratch),
        compiler_params=pltpu.CompilerParams(vmem_limit_bytes=56 * 1024 * 1024),
        name=kernel.func.__name__ if isinstance(kernel, functools.partial) else kernel.__name__,
    )(*args)


def lanes(rows):
    return lax.broadcasted_iota(jnp.int32, (rows, 128), 1)


def power40(p):
    x = p + p
    x2 = x * x
    x4 = x2 * x2
    x8 = x4 * x4
    x32 = x8 * x8
    x32 = x32 * x32
    return x32 * x8


def power39(p):
    x = p + p
    x2 = x * x
    x4 = x2 * x2
    x8 = x4 * x4
    x32 = x8 * x8
    x32 = x32 * x32
    return x32 * (x4 * (x2 * x))


def edges(p_ref, top_ref, bottom_ref, left_ref, right_ref, turned):
    lane = lanes(128)
    packed = jnp.zeros((128, 128), F32)
    for layer in range(16):
        top_ref[pl.ds(layer, 1), :] = p_ref[layer, pl.ds(0, 1), :]
        bottom_ref[pl.ds(layer, 1), :] = p_ref[layer, pl.ds(127, 1), :]
        moved = pltpu.roll(p_ref[layer], 2 * layer + 1, 1)
        packed = jnp.where((lane >> 1) == layer, moved, packed)
    turned[...] = packed.T
    right_ref[...] = turned[pl.ds(0, 16, stride=2), :]
    left_ref[...] = turned[pl.ds(1, 16, stride=2), :]


def norm_of(position, extent):
    def missing(k):
        k = jnp.maximum(k, 0)
        return (k * (k + 1)) >> 1

    return ((RADIUS + 1) ** 2 - missing(RADIUS - position) - missing(RADIUS - (extent - 1 - position))).astype(F32)


def terms(total, density, sens, p39):
    total = jnp.maximum(total, 1e-30)
    offset = PENALTY * math.log(2.0) / EXPONENT
    smax = jnp.exp(jnp.log(total) * (1.0 / EXPONENT) - offset)
    gap = density - smax
    half = 0.5 * gap * lax.rsqrt(gap * gap + SMOOTH)
    low = 0.5 - half
    top = (0.5 + half) * (2.0 * PENALTY / EXPONENT) * smax
    h = top / total
    return h * sens, h * p39, low, total / top


def plane_norms(sizes):
    row0 = lax.axis_index("gy") * 128
    col0 = lax.axis_index("gx") * 128
    rows = lax.broadcasted_iota(jnp.int32, (128, 128), 0) + row0
    cols = lax.broadcasted_iota(jnp.int32, (128, 128), 1) + col0
    return norm_of(rows, sizes[1] * 128) * norm_of(cols, sizes[2] * 128)


def terms_upper(
    sizes, p_ref, f_ref, s_ref, up_ref, down_ref, left_ref, right_ref, u_ref, v_ref, w_ref, above_ref, powers, turned
):
    lane = lanes(128)
    turned[...] = jnp.zeros((128, 128), F32)
    turned[pl.ds(0, 16, stride=2), :] = right_ref[...]
    turned[pl.ds(1, 16, stride=2), :] = left_ref[...]
    beside = power40(turned[...].T)
    norms = 1.0 / plane_norms(sizes)
    layer0 = lax.axis_index("gz") * 16
    for layer in range(16):
        own = power40(p_ref[layer])
        powers[pl.ds(8, 128), :] = own
        powers[pl.ds(7, 1), :] = power40(up_ref[pl.ds(layer, 1), :])
        powers[pl.ds(136, 1), :] = power40(down_ref[pl.ds(layer, 1), :])
        side = pltpu.roll(beside, (128 - (2 * layer + 1)) % 128, 1)
        right = jnp.where(lane == 127, side, pltpu.roll(own, 127, 1))
        left = jnp.where(lane == 0, side, pltpu.roll(own, 1, 1))
        total = (own + right) + left + (powers[pl.ds(7, 128), :] + powers[pl.ds(9, 128), :])
        if layer == 15:
            above_ref[...] = total
        else:
            k = layer + 1
            u, v, low, inverse = terms(total, f_ref[k], s_ref[k], power39(p_ref[k]))
            u_ref[k] = u
            v_ref[k] = v
            norm_z = norm_of(layer0 + k, sizes[0] * 16)
            w_ref[k] = low * inverse * (norms * (1.0 / norm_z))


def terms_lowest(sizes, p_ref, f_ref, s_ref, total_ref, u_ref, v_ref, w_ref):
    norms = 1.0 / plane_norms(sizes)
    layer0 = lax.axis_index("gz") * 16
    p39 = power39(p_ref[...])
    s = s_ref[...]
    u, v, low, inverse = terms(total_ref[...], f_ref[...], s, p39)
    ground = layer0 == 0
    norm_z = norm_of(layer0, sizes[0] * 16)
    u_ref[...] = jnp.where(ground, s, u)
    v_ref[...] = jnp.where(ground, p39, v)
    w_ref[...] = jnp.where(ground, 1.0, low * inverse) * (norms * (1.0 / norm_z))


def pack(group, u_ref, v_ref, w_ref, left_ref, right_ref, top_ref, bottom_ref):
    first, end, rows = GROUPS[group]
    lane = lanes(128)
    left = jnp.zeros((128, 128), F32)
    right = jnp.zeros((128, 128), F32)
    refs = {"u": u_ref, "v": v_ref, "w": w_ref}
    for place, (name, layer, at, width) in enumerate(strips_of(group)):
        ref = refs[name]
        if name != "w":
            index = layer - first
        else:
            index = layer
        moved = pltpu.roll(ref[index], at, 1) if at else ref[index]
        left = jnp.where((lane >= at) & (lane < at + width), moved, left)
        back = (at - width) % 128
        right = jnp.where((lane >= back) & (lane < back + width), moved, right)
        top_ref[place] = ref[index, pl.ds(0, rows), :]
        bottom_ref[place] = ref[index, pl.ds(128 - rows, rows), :]
    left_ref[...] = left
    right_ref[...] = right


def unpack(
    group, u_ref, v_ref, w_ref,
    left, right, top, bottom, top_left, top_right, bottom_left, bottom_right,
    *outs,
):
    first, end, rows = GROUPS[group]
    refs = {"u": u_ref, "v": v_ref, "w": w_ref}
    targets = dict(zip(("u", "v", "w"), outs))
    for name, target in targets.items():
        if name != "w":
            target[...] = jnp.zeros(target.shape, F32)
    for place, (name, layer, at, width) in enumerate(strips_of(group)):
        index = layer if name == "w" else layer - first
        pad = RING if name == "w" else PAD
        target = targets[name]
        target[index, pl.ds(pad, 128), pl.ds(0, 128)] = refs[name][index]
        target[index, pl.ds(pad - rows, rows), pl.ds(0, 128)] = top[place]
        target[index, pl.ds(pad + 128, rows), pl.ds(0, 128)] = bottom[place]
        for left_one, right_one, start, count in (
            (top_left, top_right, pad - rows, rows),
            (left, right, pad, 128),
            (bottom_left, bottom_right, pad + 128, rows),
        ):
            lane = lanes(count)
            both = jnp.where((lane >= at) & (lane < at + width), right_one[...], left_one[...])
            both = pltpu.roll(both, 128 - at, 1) if at else both
            both = jnp.where((lane < width) | (lane >= 128 - width), both, 0.0)
            target[index, pl.ds(start, count), pl.ds(128, 128)] = both


def five(value):
    rows = value.shape[0]
    return (value + pltpu.roll(value, 1, 1)) + pltpu.roll(value, 255, 1) + (
        pltpu.roll(value, 1, 0) + pltpu.roll(value, rows - 1, 0)
    )


def set_carry(carry, center, top, bottom, left, right, top_left, top_right, bottom_left, bottom_right, turned):
    lane = lanes(24)
    carry[pl.ds(24, 128), pl.ds(0, 128)] = center[...]
    carry[pl.ds(0, 24), pl.ds(0, 128)] = top[...]
    carry[pl.ds(152, 24), pl.ds(0, 128)] = bottom[...]
    carry[pl.ds(0, 24), pl.ds(128, 128)] = jnp.where(lane < 64, top_right[...], top_left[...])
    carry[pl.ds(152, 24), pl.ds(128, 128)] = jnp.where(lane < 64, bottom_right[...], bottom_left[...])
    turned[...] = jnp.zeros((128, 128), F32)
    turned[pl.ds(0, 24), :] = right[...]
    turned[pl.ds(104, 24), :] = left[...]
    carry[pl.ds(24, 128), pl.ds(128, 128)] = turned[...].T


def section(first, *refs):
    us, vs = refs[0:4], refs[4:8]
    refs = refs[8:]
    pieces = () if first else refs[:9]
    refs = refs[len(pieces):]
    center, top, bottom, left, right, carry, turned = refs
    if first:
        carry[...] = jnp.zeros((176, 256), F32)
    else:
        set_carry(carry, *pieces, turned)
    value = carry[...]
    for (begin, end, _), u_ref, v_ref in zip(GROUPS, us, vs):
        def step(i, value):
            at = end - 1 - begin - i
            return u_ref[at] + v_ref[at] * five(value)
        value = lax.fori_loop(0, end - begin, step, value)
    carry[...] = value
    center[...] = carry[pl.ds(24, 128), pl.ds(0, 128)]
    top[...] = carry[pl.ds(24, 24), pl.ds(0, 128)]
    bottom[...] = carry[pl.ds(128, 24), pl.ds(0, 128)]
    turned[...] = carry[pl.ds(24, 128), pl.ds(0, 128)].T
    left[...] = turned[pl.ds(0, 24), :]
    right[...] = turned[pl.ds(104, 24), :]


def tent_rows(ref, start):
    total = ref[pl.ds(start, 128), :] * 5.0
    for offset in range(1, RADIUS + 1):
        total = total + (ref[pl.ds(start - offset, 128), :] + ref[pl.ds(start + offset, 128), :]) * (5.0 - offset)
    return total


def tent_cols(value):
    total = value * 5.0
    for offset in range(1, RADIUS + 1):
        total = total + (pltpu.roll(value, offset, 1) + pltpu.roll(value, 256 - offset, 1)) * (5.0 - offset)
    return total


def last_section(*refs):
    us, vs = refs[0:4], refs[4:8]
    w_ref = refs[8]
    pieces = refs[9:18]
    out_ref, carry, turned, weighted = refs[18:]
    set_carry(carry, *pieces, turned)
    value = carry[...]
    for (begin, end, _), u_ref, v_ref in zip(GROUPS, us, vs):
        def step(i, value):
            at = end - 1 - begin - i
            value = u_ref[at] + v_ref[at] * five(value)
            weighted[...] = value[PAD - RING:PAD + 128 + RING] * w_ref[begin + at]
            out_ref[begin + at] = tent_cols(tent_rows(weighted, RING))[:, :128]
            return value
        value = lax.fori_loop(0, end - begin, step, value)


def finish(own_ref, below_ref, above_ref, passive_ref, out_ref):
    def layer(k):
        if k < 0:
            return below_ref[k + RADIUS]
        if k >= 16:
            return above_ref[k - 16]
        return own_ref[k]

    for k in range(16):
        total = layer(k) * 5.0
        for offset in range(1, RADIUS + 1):
            total = total + (layer(k - offset) + layer(k + offset)) * (5.0 - offset)
        out_ref[k] = jnp.where(passive_ref[k] > 0, 0.0, total)


def per_device(filtered, printed, sensitivity, passive):
    sizes = tuple(lax.axis_size(axis) for axis in AXES)
    plane = shape(128, 128)
    edge = shape(16, 128)
    top, bottom, left, right = call(edges, [edge] * 4, printed, scratch=[pltpu.VMEM((128, 128), F32)])
    up = send(bottom, 0, 1, 0)
    down = send(top, 0, -1, 0)
    from_left = send(right, 0, 0, 1)
    from_right = send(left, 0, 0, -1)
    block = shape(16, 128, 128)
    u, v, w, above = call(
        functools.partial(terms_upper, sizes),
        [block, block, block, plane],
        printed, filtered, sensitivity, up, down, from_left, from_right,
        scratch=[pltpu.VMEM((144, 128), F32), pltpu.VMEM((128, 128), F32)],
    )
    total0 = send(above, 1, 0, 0)
    u0, v0, w0 = call(
        functools.partial(terms_lowest, sizes), [plane] * 3, printed[0], filtered[0], sensitivity[0], total0
    )
    u = u.at[0].set(u0)
    v = v.at[0].set(v0)
    w = w.at[0].set(w0)
    us, vs, w_ext = [], [], None
    for group, (first, end, rows) in enumerate(GROUPS):
        count = len(strips_of(group))
        strip = shape(count, rows, 128)
        args = (u[first:end], v[first:end], w)
        left, right, top, bottom = call(functools.partial(pack, group), [plane, plane, strip, strip], *args)
        outs = [shape(end - first, 176, 256)] * 2
        if first == 0:
            outs = outs + [shape(16, 144, 256)]
        got = call(
            functools.partial(unpack, group),
            outs,
            *args,
            send(right, 0, 0, 1),
            send(left, 0, 0, -1),
            send(bottom, 0, 1, 0),
            send(top, 0, -1, 0),
            send(right[128 - rows:], 0, 1, 1),
            send(left[128 - rows:], 0, 1, -1),
            send(right[:rows], 0, -1, 1),
            send(left[:rows], 0, -1, -1),
        )
        us.append(got[0])
        vs.append(got[1])
        if first == 0:
            w_ext = got[2]
    strip = shape(24, 128)
    scratch = [pltpu.VMEM((176, 256), F32), pltpu.VMEM((128, 128), F32)]
    pieces = ()
    for step in range(sizes[0]):
        if step < sizes[0] - 1:
            center, top, bottom, left, right = call(
                functools.partial(section, step == 0),
                [plane, strip, strip, strip, strip],
                *us, *vs, *pieces,
                scratch=scratch,
            )
            pieces = (
                send(center, -1, 0, 0),
                send(bottom, -1, 1, 0),
                send(top, -1, -1, 0),
                send(right, -1, 0, 1),
                send(left, -1, 0, -1),
                send(bottom, -1, 1, 1),
                send(bottom, -1, 1, -1),
                send(top, -1, -1, 1),
                send(top, -1, -1, -1),
            )
    smoothed = call(
        last_section, block, *us, *vs, w_ext, *pieces,
        scratch=scratch + [pltpu.VMEM((144, 256), F32)],
    )
    below = send(smoothed[16 - RADIUS:], 1, 0, 0)
    over = send(smoothed[:RADIUS], -1, 0, 0)
    return call(finish, block, smoothed, below, over, passive)


def solution(mesh):
    spec = P(*AXES)
    return jax.shard_map(
        per_device, mesh=mesh, in_specs=(spec,) * 4, out_specs=spec, check_vma=False
    )
```

time: 1410 us -> 322 us (0.23)
  the two profiles are of different devices: /device:TPU:1 before, /device:TPU:31 now
where the time goes in v1:
time: 322 us; the launch traced here: 319 us
  starting transfers between devices  208 us (65%)
  Pallas kernels  66.5 us (21%)
  local copies, waits for them, and re-layouts  23.6 us (7%)
  waiting for transfers between devices  19.8 us (6%)
    ppermute x66, starting transfers between devices, send(): return lax.ppermute(value, AXES, pairs)  208 us
    pallas_call x15, Pallas kernels, call(): pl.pallas_call(kernel, out_shape=outs, scratch_shapes=list(scratch), comp...  66.5 us
    ppermute x66, waiting for transfers between devices, send(): return lax.ppermute(value, AXES, pairs)  19.8 us
    slice x6, local copies, waits for them, and re-layouts, per_device(): args = (u[first:end], v[first:end], w)  7.63 us
  transfers between devices with their start and end apart: 66, of which 8 were waited for; matrix products, arithmetic and copies ran while one was open for 2% of the time, Pallas kernels for 5%

profile of v1, /device:TPU:31, one launch (start us, length us, event | category | flops | bytes accessed | tf_op | source)
XLA Modules:
  0.0 319.5 jit_solution(346955426565227954)
XLA Ops:
  8.2 4.9 %collective-permute-start.2 = (f32[16,128]{1,0:T(8,128)}, f32[16,128]{1,0:T(8,128)S(1)}, u32[]{:S(2)}, u32[]{:S(2)}) collective-permute-start(f32[16,128]{1,0:T(8,128)} %get-tuple-element.94), channel_id=1, source_target_pairs={{0,1},{1,2},{2,3},{3,4},{4,5},{5,6},{6,7},{7,8},{8,9},{9,10},{10,1... | collective-permute-start | bytes 24584 | tf_op jit(solution)/shard_map/ppermute | solution.py:49
  20.4 5.5 %terms_upper.1 = (f32[16,128,128]{2,1,0:T(8,128)}, f32[16,128,128]{2,1,0:T(8,128)}, f32[16,128,128]{2,1,0:T(8,128)}, f32[128,128]{1,0:T(8,128)}) custom-call(f32[16,128,128]{2,1,0:T(8,128)} %p_ref.3, f32[16,128,128]{2,1,0:T(8,128)} %f_ref.1, f32[16,128,128]{2,1,0:T(8,128)} %s_ref.1, f32[16,128]{1,0:T(8,128)} %copy-done.60, f32[16,128]{1,0:T(8,128)} %copy-done.61, ...), custom_call_target="tpu_custom_call" | custom-call | tf_op jit(solution)/shard_map/terms_upper/pallas_call | solution.py:57
  44.8 5.6 %collective-permute-start.20 = (f32[16,128]{1,0:T(8,128)S(1)}, f32[16,128]{1,0:T(8,128)S(1)}, u32[]{:S(2)}, u32[]{:S(2)}) collective-permute-start(f32[16,128]{1,0:T(8,128)S(1)} %get-tuple-element.163), channel_id=1, source_target_pairs={{17,0},{18,1},{19,2},{20,3},{21,4},{22,5},{23,6},{24,7},{25,8},{26... | collective-permute-start | bytes 24584 | tf_op jit(solution)/shard_map/ppermute | solution.py:49
  61.0 4.4 %collective-permute-start.36 = (f32[8,128]{1,0:T(8,128)S(1)}, f32[8,128]{1,0:T(8,128)S(1)}, u32[]{:S(2)}, u32[]{:S(2)}) collective-permute-start(f32[8,128]{1,0:T(8,128)S(1)} %get-tuple-element.155), channel_id=1, source_target_pairs={{17,0},{18,1},{19,2},{20,3},{21,4},{22,5},{23,6},{24,7},{25,8},{26... | collective-permute-start | bytes 12296 | tf_op jit(solution)/shard_map/ppermute | solution.py:49
  77.1 4.7 %collective-permute-start.17 = (f32[16,128]{1,0:T(8,128)S(1)}, f32[16,128]{1,0:T(8,128)S(1)}, u32[]{:S(2)}, u32[]{:S(2)}) collective-permute-start(f32[16,128]{1,0:T(8,128)S(1)} %get-tuple-element.166), channel_id=1, source_target_pairs={{0,17},{1,18},{2,19},{3,20},{4,21},{5,22},{6,23},{7,24},{8,25},{9,... | collective-permute-start | bytes 24584 | tf_op jit(solution)/shard_map/ppermute | solution.py:49
  97.2 5.8 %collective-permute-start.26 = (f32[16,128]{1,0:T(8,128)S(1)}, f32[16,128]{1,0:T(8,128)S(1)}, u32[]{:S(2)}, u32[]{:S(2)}) collective-permute-start(f32[16,128]{1,0:T(8,128)S(1)} %get-tuple-element.160), channel_id=1, source_target_pairs={{1,16},{2,17},{3,18},{4,19},{5,20},{6,21},{7,22},{8,23},{9,24},{10... | collective-permute-start | bytes 24584 | tf_op jit(solution)/shard_map/ppermute | solution.py:49
  104.9 5.4 %collective-permute-start.9 = (f32[24,128]{1,0:T(8,128)S(1)}, f32[24,128]{1,0:T(8,128)S(1)}, u32[]{:S(2)}, u32[]{:S(2)}) collective-permute-start(f32[24,128]{1,0:T(8,128)S(1)} %get-tuple-element.170), channel_id=1, source_target_pairs={{0,17},{1,18},{2,19},{3,20},{4,21},{5,22},{6,23},{7,24},{8,25},{9,... | collective-permute-start | bytes 36872 | tf_op jit(solution)/shard_map/ppermute | solution.py:49
  115.5 4.5 %collective-permute-start.10 = (f32[24,128]{1,0:T(8,128)S(1)}, f32[24,128]{1,0:T(8,128)S(1)}, u32[]{:S(2)}, u32[]{:S(2)}) collective-permute-start(f32[24,128]{1,0:T(8,128)S(1)} %get-tuple-element.168), channel_id=1, source_target_pairs={{1,16},{2,17},{3,18},{4,19},{5,20},{6,21},{7,22},{8,23},{9,24},{10... | collective-permute-start | bytes 36872 | tf_op jit(solution)/shard_map/ppermute | solution.py:49
  124.0 4.4 %collective-permute-start.14 = (f32[128,128]{1,0:T(8,128)S(1)}, f32[128,128]{1,0:T(8,128)S(1)}, u32[]{:S(2)}, u32[]{:S(2)}) collective-permute-start(f32[128,128]{1,0:T(8,128)S(1)} %copy-done.68), channel_id=1, source_target_pairs={{1,0},{2,1},{3,2},{4,3},{5,4},{6,5},{7,6},{8,7},{9,8},{10,9},{11,1... | collective-permute-start | bytes 196616 | tf_op jit(solution)/shard_map/ppermute | solution.py:49
  130.4 6.4 %collective-permute-start.6 = (f32[128,128]{1,0:T(8,128)S(1)}, f32[128,128]{1,0:T(8,128)S(1)}, u32[]{:S(2)}, u32[]{:S(2)}) collective-permute-start(f32[128,128]{1,0:T(8,128)S(1)} %copy-done.50), channel_id=1, source_target_pairs={{1,0},{2,1},{3,2},{4,3},{5,4},{6,5},{7,6},{8,7},{9,8},{10,9},{11,1... | collective-permute-start | bytes 196616 | tf_op jit(solution)/shard_map/ppermute | solution.py:49
  136.8 4.6 %collective-permute-start.7 = (f32[6,24,128]{2,1,0:T(8,128)S(1)}, f32[6,24,128]{2,1,0:T(8,128)S(1)}, u32[]{:S(2)}, u32[]{:S(2)}) collective-permute-start(f32[6,24,128]{2,1,0:T(8,128)S(1)} %copy-done.75), channel_id=1, source_target_pairs={{0,16},{1,17},{2,18},{3,19},{4,20},{5,21},{6,22},{7,23},{8,24},{9,... | collective-permute-start | bytes 221192 | tf_op jit(solution)/shard_map/ppermute | solution.py:49
  143.4 6.4 %collective-permute-start.30 = (f32[128,128]{1,0:T(8,128)S(1)}, f32[128,128]{1,0:T(8,128)S(1)}, u32[]{:S(2)}, u32[]{:S(2)}) collective-permute-start(f32[128,128]{1,0:T(8,128)S(1)} %copy-done.70), channel_id=1, source_target_pairs={{1,0},{2,1},{3,2},{4,3},{5,4},{6,5},{7,6},{8,7},{9,8},{10,9},{11,1... | collective-permute-start | bytes 196616 | tf_op jit(solution)/shard_map/ppermute | solution.py:49
  163.8 6.4 %collective-permute-start.22 = (f32[128,128]{1,0:T(8,128)}, f32[128,128]{1,0:T(8,128)S(1)}, u32[]{:S(2)}, u32[]{:S(2)}) collective-permute-start(f32[128,128]{1,0:T(8,128)} %get-tuple-element.114), channel_id=1, source_target_pairs={{1,0},{2,1},{3,2},{4,3},{5,4},{6,5},{7,6},{8,7},{9,8},{10,9},{11,1... | collective-permute-start | bytes 196616 | tf_op jit(solution)/shard_map/ppermute | solution.py:49
  186.3 6.2 %section.3 = (f32[128,128]{1,0:T(8,128)}, f32[24,128]{1,0:T(8,128)}, f32[24,128]{1,0:T(8,128)}, f32[24,128]{1,0:T(8,128)}, f32[24,128]{1,0:T(8,128)}) custom-call(f32[3,176,256]{2,1,0:T(8,128)} %get-tuple-element.107.refs_0_, f32[4,176,256]{2,1,0:T(8,128)} %get-tuple-element.112.refs_1_, f32[6,176,256]{2,1,0:T(8,128)} %get-tuple-element.117.refs_2_, ...), custom_call_target="tpu_custom_call" | custom-call | tf_op jit(solution)/shard_map/section/pallas_call | solution.py:57
  197.5 7.6 %collective-permute-start.41 = (f32[24,128]{1,0:T(8,128)}, f32[24,128]{1,0:T(8,128)S(1)}, u32[]{:S(2)}, u32[]{:S(2)}) collective-permute-start(f32[24,128]{1,0:T(8,128)} %get-tuple-element.132), channel_id=1, source_target_pairs={{65,0},{66,1},{67,2},{68,3},{69,4},{70,5},{71,6},{72,7},{73,8},{74... | collective-permute-start | bytes 36872 | tf_op jit(solution)/shard_map/ppermute | solution.py:49
  210.1 4.6 %collective-permute-start.45 = (f32[24,128]{1,0:T(8,128)}, f32[24,128]{1,0:T(8,128)S(1)}, u32[]{:S(2)}, u32[]{:S(2)}) collective-permute-start(f32[24,128]{1,0:T(8,128)} %get-tuple-element.130), channel_id=1, source_target_pairs={{81,0},{82,1},{83,2},{84,3},{85,4},{86,5},{87,6},{88,7},{89,8},{90... | collective-permute-start | bytes 36872 | tf_op jit(solution)/shard_map/ppermute | solution.py:49
  219.5 6.4 %section.4 = (f32[128,128]{1,0:T(8,128)}, f32[24,128]{1,0:T(8,128)}, f32[24,128]{1,0:T(8,128)}, f32[24,128]{1,0:T(8,128)}, f32[24,128]{1,0:T(8,128)}) custom-call(f32[3,176,256]{2,1,0:T(8,128)} %get-tuple-element.107.refs_0_, f32[4,176,256]{2,1,0:T(8,128)} %get-tuple-element.112.refs_1_, f32[6,176,256]{2,1,0:T(8,128)} %get-tuple-element.117.refs_2_, ...), custom_call_target="tpu_custom_call" | custom-call | tf_op jit(solution)/shard_map/section/pallas_call | solution.py:57
  225.9 5.9 %collective-permute-start.46 = (f32[128,128]{1,0:T(8,128)}, f32[128,128]{1,0:T(8,128)S(1)}, u32[]{:S(2)}, u32[]{:S(2)}) collective-permute-start(f32[128,128]{1,0:T(8,128)} %get-tuple-element.133), channel_id=1, source_target_pairs={{64,0},{65,1},{66,2},{67,3},{68,4},{69,5},{70,6},{71,7},{72,8},{73... | collective-permute-start | bytes 196616 | tf_op jit(solution)/shard_map/ppermute | solution.py:49
  233.1 5.9 %collective-permute-start.50 = (f32[24,128]{1,0:T(8,128)}, f32[24,128]{1,0:T(8,128)S(1)}, u32[]{:S(2)}, u32[]{:S(2)}) collective-permute-start(f32[24,128]{1,0:T(8,128)} %get-tuple-element.137), channel_id=1, source_target_pairs={{65,0},{66,1},{67,2},{68,3},{69,4},{70,5},{71,6},{72,7},{73,8},{74... | collective-permute-start | bytes 36872 | tf_op jit(solution)/shard_map/ppermute | solution.py:49
  253.5 6.4 %section.5 = (f32[128,128]{1,0:T(8,128)}, f32[24,128]{1,0:T(8,128)}, f32[24,128]{1,0:T(8,128)}, f32[24,128]{1,0:T(8,128)}, f32[24,128]{1,0:T(8,128)}) custom-call(f32[3,176,256]{2,1,0:T(8,128)} %get-tuple-element.107.refs_0_, f32[4,176,256]{2,1,0:T(8,128)} %get-tuple-element.112.refs_1_, f32[6,176,256]{2,1,0:T(8,128)} %get-tuple-element.117.refs_2_, ...), custom_call_target="tpu_custom_call" | custom-call | tf_op jit(solution)/shard_map/section/pallas_call | solution.py:57
  265.6 6.1 %collective-permute-start.59 = (f32[24,128]{1,0:T(8,128)}, f32[24,128]{1,0:T(8,128)S(1)}, u32[]{:S(2)}, u32[]{:S(2)}) collective-permute-start(f32[24,128]{1,0:T(8,128)} %get-tuple-element.142), channel_id=1, source_target_pairs={{65,0},{66,1},{67,2},{68,3},{69,4},{70,5},{71,6},{72,7},{73,8},{74... | collective-permute-start | bytes 36872 | tf_op jit(solution)/shard_map/ppermute | solution.py:49
  285.2 14.6 %last_section.1.own_ref = f32[16,128,128]{2,1,0:T(8,128)} custom-call(f32[3,176,256]{2,1,0:T(8,128)} %get-tuple-element.107.refs_0_, f32[4,176,256]{2,1,0:T(8,128)} %get-tuple-element.112.refs_1_, f32[6,176,256]{2,1,0:T(8,128)} %get-tuple-element.117.refs_2_, f32[3,176,256]{2,1,0:T(8,128)} %get-tuple-element.122.refs_3_, ...), custom_call_target="tpu_custom_call" | custom-call | tf_op jit(solution)/shard_map/last_section/pallas_call | solution.py:57
  300.8 4.8 %collective-permute-start.65 = (f32[4,128,128]{2,1,0:T(8,128)S(1)}, f32[4,128,128]{2,1,0:T(8,128)S(1)}, u32[]{:S(2)}, u32[]{:S(2)}) collective-permute-start(f32[4,128,128]{2,1,0:T(8,128)S(1)} %get-tuple-element.149), channel_id=1, source_target_pairs={{64,0},{65,1},{66,2},{67,3},{68,4},{69,5},{70,6},{71,7},{72,8},{73... | collective-permute-start | bytes 786440 | tf_op jit(solution)/shard_map/ppermute | solution.py:49
  306.9 4.8 %collective-permute-done.65.above_ref = f32[4,128,128]{2,1,0:T(8,128)S(1)} collective-permute-done((f32[4,128,128]{2,1,0:T(8,128)S(1)}, f32[4,128,128]{2,1,0:T(8,128)S(1)}, u32[]{:S(2)}, u32[]{:S(2)}) %collective-permute-start.65) | collective-permute-done | bytes 262176 | tf_op jit(solution)/shard_map/ppermute | solution.py:49
  (299 shorter events, 175.4 us)
Async XLA Ops:
  2.2 17.0 %collective-permute-start = (f32[16,128]{1,0:T(8,128)}, f32[16,128]{1,0:T(8,128)S(1)}, u32[]{:S(2)}, u32[]{:S(2)}) collective-permute-start(f32[16,128]{1,0:T(8,128)} %get-tuple-element.92), channel_id=1, source_target_pairs={{0,16},{1,17},{2,18},{3,19},{4,20},{5,21},{6,22},{7,23},{8,24},{9,... | collective-permute-start | bytes 24584 | tf_op jit(solution)/shard_map/ppermute | solution.py:49
  44.8 48.5 %collective-permute-start.20 = (f32[16,128]{1,0:T(8,128)S(1)}, f32[16,128]{1,0:T(8,128)S(1)}, u32[]{:S(2)}, u32[]{:S(2)}) collective-permute-start(f32[16,128]{1,0:T(8,128)S(1)} %get-tuple-element.163), channel_id=1, source_target_pairs={{17,0},{18,1},{19,2},{20,3},{21,4},{22,5},{23,6},{24,7},{25,8},{26... | collective-permute-start | bytes 24584 | tf_op jit(solution)/shard_map/ppermute | solution.py:49
  50.4 44.9 %collective-permute-start.18 = (f32[16,128]{1,0:T(8,128)S(1)}, f32[16,128]{1,0:T(8,128)S(1)}, u32[]{:S(2)}, u32[]{:S(2)}) collective-permute-start(f32[16,128]{1,0:T(8,128)S(1)} %get-tuple-element.164), channel_id=1, source_target_pairs={{1,16},{2,17},{3,18},{4,19},{5,20},{6,21},{7,22},{8,23},{9,24},{10... | collective-permute-start | bytes 24584 | tf_op jit(solution)/shard_map/ppermute | solution.py:49
  61.0 14.1 %collective-permute-start.36 = (f32[8,128]{1,0:T(8,128)S(1)}, f32[8,128]{1,0:T(8,128)S(1)}, u32[]{:S(2)}, u32[]{:S(2)}) collective-permute-start(f32[8,128]{1,0:T(8,128)S(1)} %get-tuple-element.155), channel_id=1, source_target_pairs={{17,0},{18,1},{19,2},{20,3},{21,4},{22,5},{23,6},{24,7},{25,8},{26... | collective-permute-start | bytes 12296 | tf_op jit(solution)/shard_map/ppermute | solution.py:49
  75.1 22.0 %collective-permute-start.19 = (f32[16,128]{1,0:T(8,128)S(1)}, f32[16,128]{1,0:T(8,128)S(1)}, u32[]{:S(2)}, u32[]{:S(2)}) collective-permute-start(f32[16,128]{1,0:T(8,128)S(1)} %get-tuple-element.165), channel_id=1, source_target_pairs={{16,1},{17,2},{18,3},{19,4},{20,5},{21,6},{22,7},{23,8},{24,9},{25... | collective-permute-start | bytes 24584 | tf_op jit(solution)/shard_map/ppermute | solution.py:49
  77.1 25.9 %collective-permute-start.17 = (f32[16,128]{1,0:T(8,128)S(1)}, f32[16,128]{1,0:T(8,128)S(1)}, u32[]{:S(2)}, u32[]{:S(2)}) collective-permute-start(f32[16,128]{1,0:T(8,128)S(1)} %get-tuple-element.166), channel_id=1, source_target_pairs={{0,17},{1,18},{2,19},{3,20},{4,21},{5,22},{6,23},{7,24},{8,25},{9,... | collective-permute-start | bytes 24584 | tf_op jit(solution)/shard_map/ppermute | solution.py:49
  89.7 40.7 %collective-permute-start.15 = (f32[8,16,128]{2,1,0:T(8,128)S(1)}, f32[8,16,128]{2,1,0:T(8,128)S(1)}, u32[]{:S(2)}, u32[]{:S(2)}) collective-permute-start(f32[8,16,128]{2,1,0:T(8,128)S(1)} %copy-done.77), channel_id=1, source_target_pairs={{0,16},{1,17},{2,18},{3,19},{4,20},{5,21},{6,22},{7,23},{8,24},{9,... | collective-permute-start | bytes 196616 | tf_op jit(solution)/shard_map/ppermute | solution.py:49
  93.3 22.2 %collective-permute-start.11 = (f32[24,128]{1,0:T(8,128)S(1)}, f32[24,128]{1,0:T(8,128)S(1)}, u32[]{:S(2)}, u32[]{:S(2)}) collective-permute-start(f32[24,128]{1,0:T(8,128)S(1)} %get-tuple-element.169), channel_id=1, source_target_pairs={{16,1},{17,2},{18,3},{19,4},{20,5},{21,6},{22,7},{23,8},{24,9},{25... | collective-permute-start | bytes 36872 | tf_op jit(solution)/shard_map/ppermute | solution.py:49
  104.9 15.1 %collective-permute-start.9 = (f32[24,128]{1,0:T(8,128)S(1)}, f32[24,128]{1,0:T(8,128)S(1)}, u32[]{:S(2)}, u32[]{:S(2)}) collective-permute-start(f32[24,128]{1,0:T(8,128)S(1)} %get-tuple-element.170), channel_id=1, source_target_pairs={{0,17},{1,18},{2,19},{3,20},{4,21},{5,22},{6,23},{7,24},{8,25},{9,... | collective-permute-start | bytes 36872 | tf_op jit(solution)/shard_map/ppermute | solution.py:49
  113.6 23.2 %collective-permute-start.16 = (f32[8,16,128]{2,1,0:T(8,128)S(1)}, f32[8,16,128]{2,1,0:T(8,128)S(1)}, u32[]{:S(2)}, u32[]{:S(2)}) collective-permute-start(f32[8,16,128]{2,1,0:T(8,128)S(1)} %copy-done.76), channel_id=1, source_target_pairs={{16,0},{17,1},{18,2},{19,3},{20,4},{21,5},{22,6},{23,7},{24,8},{25... | collective-permute-start | bytes 196616 | tf_op jit(solution)/shard_map/ppermute | solution.py:49
  120.1 21.3 %collective-permute-start.13 = (f32[128,128]{1,0:T(8,128)S(1)}, f32[128,128]{1,0:T(8,128)S(1)}, u32[]{:S(2)}, u32[]{:S(2)}) collective-permute-start(f32[128,128]{1,0:T(8,128)S(1)} %copy-done.69), channel_id=1, source_target_pairs={{0,1},{1,2},{2,3},{3,4},{4,5},{5,6},{6,7},{7,8},{8,9},{9,10},{10,1... | collective-permute-start | bytes 196616 | tf_op jit(solution)/shard_map/ppermute | solution.py:49
  124.0 19.4 %collective-permute-start.14 = (f32[128,128]{1,0:T(8,128)S(1)}, f32[128,128]{1,0:T(8,128)S(1)}, u32[]{:S(2)}, u32[]{:S(2)}) collective-permute-start(f32[128,128]{1,0:T(8,128)S(1)} %copy-done.68), channel_id=1, source_target_pairs={{1,0},{2,1},{3,2},{4,3},{5,4},{6,5},{7,6},{8,7},{9,8},{10,9},{11,1... | collective-permute-start | bytes 196616 | tf_op jit(solution)/shard_map/ppermute | solution.py:49
  128.5 21.3 %collective-permute-start.5 = (f32[128,128]{1,0:T(8,128)S(1)}, f32[128,128]{1,0:T(8,128)S(1)}, u32[]{:S(2)}, u32[]{:S(2)}) collective-permute-start(f32[128,128]{1,0:T(8,128)S(1)} %copy-done.51), channel_id=1, source_target_pairs={{0,1},{1,2},{2,3},{3,4},{4,5},{5,6},{6,7},{7,8},{8,9},{9,10},{10,1... | collective-permute-start | bytes 196616 | tf_op jit(solution)/shard_map/ppermute | solution.py:49
  130.4 21.9 %collective-permute-start.6 = (f32[128,128]{1,0:T(8,128)S(1)}, f32[128,128]{1,0:T(8,128)S(1)}, u32[]{:S(2)}, u32[]{:S(2)}) collective-permute-start(f32[128,128]{1,0:T(8,128)S(1)} %copy-done.50), channel_id=1, source_target_pairs={{1,0},{2,1},{3,2},{4,3},{5,4},{6,5},{7,6},{8,7},{9,8},{10,9},{11,1... | collective-permute-start | bytes 196616 | tf_op jit(solution)/shard_map/ppermute | solution.py:49
  136.8 23.1 %collective-permute-start.7 = (f32[6,24,128]{2,1,0:T(8,128)S(1)}, f32[6,24,128]{2,1,0:T(8,128)S(1)}, u32[]{:S(2)}, u32[]{:S(2)}) collective-permute-start(f32[6,24,128]{2,1,0:T(8,128)S(1)} %copy-done.75), channel_id=1, source_target_pairs={{0,16},{1,17},{2,18},{3,19},{4,20},{5,21},{6,22},{7,23},{8,24},{9,... | collective-permute-start | bytes 221192 | tf_op jit(solution)/shard_map/ppermute | solution.py:49
  149.8 14.0 %collective-permute-start.31 = (f32[22,8,128]{2,1,0:T(8,128)S(1)}, f32[22,8,128]{2,1,0:T(8,128)S(1)}, u32[]{:S(2)}, u32[]{:S(2)}) collective-permute-start(f32[22,8,128]{2,1,0:T(8,128)S(1)} %copy-done.73), channel_id=1, source_target_pairs={{0,16},{1,17},{2,18},{3,19},{4,20},{5,21},{6,22},{7,23},{8,24},{9,... | collective-permute-start | bytes 270344 | tf_op jit(solution)/shard_map/ppermute | solution.py:49
  154.3 15.9 %collective-permute-start.32 = (f32[22,8,128]{2,1,0:T(8,128)S(1)}, f32[22,8,128]{2,1,0:T(8,128)S(1)}, u32[]{:S(2)}, u32[]{:S(2)}) collective-permute-start(f32[22,8,128]{2,1,0:T(8,128)S(1)} %copy-done.72), channel_id=1, source_target_pairs={{16,0},{17,1},{18,2},{19,3},{20,4},{21,5},{22,6},{23,7},{24,8},{25... | collective-permute-start | bytes 270344 | tf_op jit(solution)/shard_map/ppermute | solution.py:49
  156.3 25.5 %collective-permute-start.23 = (f32[12,16,128]{2,1,0:T(8,128)}, f32[12,16,128]{2,1,0:T(8,128)S(1)}, u32[]{:S(2)}, u32[]{:S(2)}) collective-permute-start(f32[12,16,128]{2,1,0:T(8,128)} %get-tuple-element.115), channel_id=1, source_target_pairs={{0,16},{1,17},{2,18},{3,19},{4,20},{5,21},{6,22},{7,23},{8,24},{9,... | collective-permute-start | bytes 294920 | tf_op jit(solution)/shard_map/ppermute | solution.py:49
  159.9 21.9 %collective-permute-start.24 = (f32[12,16,128]{2,1,0:T(8,128)}, f32[12,16,128]{2,1,0:T(8,128)S(1)}, u32[]{:S(2)}, u32[]{:S(2)}) collective-permute-start(f32[12,16,128]{2,1,0:T(8,128)} %get-tuple-element.116), channel_id=1, source_target_pairs={{16,0},{17,1},{18,2},{19,3},{20,4},{21,5},{22,6},{23,7},{24,8},{25... | collective-permute-start | bytes 294920 | tf_op jit(solution)/shard_map/ppermute | solution.py:49
  161.9 19.8 %collective-permute-start.21 = (f32[128,128]{1,0:T(8,128)}, f32[128,128]{1,0:T(8,128)S(1)}, u32[]{:S(2)}, u32[]{:S(2)}) collective-permute-start(f32[128,128]{1,0:T(8,128)} %get-tuple-element.113), channel_id=1, source_target_pairs={{0,1},{1,2},{2,3},{3,4},{4,5},{5,6},{6,7},{7,8},{8,9},{9,10},{10,1... | collective-permute-start | bytes 196616 | tf_op jit(solution)/shard_map/ppermute | solution.py:49
  163.8 17.9 %collective-permute-start.22 = (f32[128,128]{1,0:T(8,128)}, f32[128,128]{1,0:T(8,128)S(1)}, u32[]{:S(2)}, u32[]{:S(2)}) collective-permute-start(f32[128,128]{1,0:T(8,128)} %get-tuple-element.114), channel_id=1, source_target_pairs={{1,0},{2,1},{3,2},{4,3},{5,4},{6,5},{7,6},{8,7},{9,8},{10,9},{11,1... | collective-permute-start | bytes 196616 | tf_op jit(solution)/shard_map/ppermute | solution.py:49
  192.5 25.8 %collective-permute-start.37 = (f32[128,128]{1,0:T(8,128)}, f32[128,128]{1,0:T(8,128)S(1)}, u32[]{:S(2)}, u32[]{:S(2)}) collective-permute-start(f32[128,128]{1,0:T(8,128)} %get-tuple-element.128), channel_id=1, source_target_pairs={{64,0},{65,1},{66,2},{67,3},{68,4},{69,5},{70,6},{71,7},{72,8},{73... | collective-permute-start | bytes 196616 | tf_op jit(solution)/shard_map/ppermute | solution.py:49
  225.9 26.4 %collective-permute-start.46 = (f32[128,128]{1,0:T(8,128)}, f32[128,128]{1,0:T(8,128)S(1)}, u32[]{:S(2)}, u32[]{:S(2)}) collective-permute-start(f32[128,128]{1,0:T(8,128)} %get-tuple-element.133), channel_id=1, source_target_pairs={{64,0},{65,1},{66,2},{67,3},{68,4},{69,5},{70,6},{71,7},{72,8},{73... | collective-permute-start | bytes 196616 | tf_op jit(solution)/shard_map/ppermute | solution.py:49
  259.9 24.6 %collective-permute-start.55 = (f32[128,128]{1,0:T(8,128)}, f32[128,128]{1,0:T(8,128)S(1)}, u32[]{:S(2)}, u32[]{:S(2)}) collective-permute-start(f32[128,128]{1,0:T(8,128)} %get-tuple-element.138), channel_id=1, source_target_pairs={{64,0},{65,1},{66,2},{67,3},{68,4},{69,5},{70,6},{71,7},{72,8},{73... | collective-permute-start | bytes 196616 | tf_op jit(solution)/shard_map/ppermute | solution.py:49
  (120 other events, 2723.0 us)

commit v2 on v1

v2 whole, which is shorter than its diff:
```python
import functools
import math

import jax
import jax.numpy as jnp
from jax import lax
from jax.experimental import pallas as pl
from jax.experimental.pallas import tpu as pltpu
from jax.sharding import PartitionSpec as P

RADIUS = 4
PENALTY = 40.0
EXPONENT = PENALTY + math.log(5.0) / math.log(0.5)
SMOOTH = 0.001
AXES = ("gz", "gy", "gx")
F32 = jnp.float32

GROUPS = ((13, 16, 24), (9, 13, 16), (3, 9, 16), (0, 3, 8))
PLANE = 288
LAYERS = 16


def strips_of(group):
    first, end, _ = GROUPS[group]
    strips, at = [], 0
    for layer in range(end - 1, first - 1, -1):
        for _ in range(2):
            strips.append((at, RADIUS + layer))
            at += RADIUS + layer
    if first == 0:
        for layer in range(LAYERS):
            strips.append((at, RADIUS))
            at += RADIUS
    assert at <= 128
    return strips


def moved(value, where):
    sizes = tuple(lax.axis_size(axis) for axis in AXES)
    pairs = []
    for z in range(sizes[0]):
        for y in range(sizes[1]):
            for x in range(sizes[2]):
                to = where(z, y, x)
                if to is not None and all(0 <= t < n for t, n in zip(to, sizes)):
                    pairs.append(((z * sizes[1] + y) * sizes[2] + x, (to[0] * sizes[1] + to[1]) * sizes[2] + to[2]))
    return lax.ppermute(value, AXES, pairs)


def shape(*dims):
    return jax.ShapeDtypeStruct(dims, F32)


def call(kernel, outs, *args, scratch=(), in_specs=None, **params):
    name = kernel.func.__name__ if isinstance(kernel, functools.partial) else kernel.__name__
    more = {} if in_specs is None else {"in_specs": in_specs}
    return pl.pallas_call(
        kernel,
        out_shape=outs,
        scratch_shapes=list(scratch),
        compiler_params=pltpu.CompilerParams(vmem_limit_bytes=40 * 1024 * 1024),
        name=name,
        **more,
    )(*args)


def lanes(rows):
    return lax.broadcasted_iota(jnp.int32, (rows, 128), 1)


def core():
    return lax.axis_index("gy") & 1


def seam():
    return lax.axis_index("gy") >> 1


def aligned(value, to):
    return pl.multiple_of(value, to)


def power40(p):
    x = p + p
    x2 = x * x
    x4 = x2 * x2
    x8 = x4 * x4
    x32 = x8 * x8
    x32 = x32 * x32
    return x32 * x8


def power39(p):
    x = p + p
    x2 = x * x
    x4 = x2 * x2
    x8 = x4 * x4
    x32 = x8 * x8
    x32 = x32 * x32
    return x32 * (x4 * (x2 * x))


def edges(p_ref, inner_ref, outer_ref, left_ref, right_ref, turned):
    lane = lanes(128)
    c = core()
    packed = jnp.zeros((128, 128), F32)
    for layer in range(LAYERS):
        inner_ref[pl.ds(layer, 1), :] = p_ref[layer, pl.ds(127 * (1 - c), 1), :]
        outer_ref[pl.ds(layer, 1), :] = p_ref[layer, pl.ds(127 * c, 1), :]
        rolled = pltpu.roll(p_ref[layer], 2 * layer + 1, 1)
        packed = jnp.where((lane >> 1) == layer, rolled, packed)
    turned[...] = packed.T
    right_ref[...] = turned[pl.ds(0, 16, stride=2), :]
    left_ref[...] = turned[pl.ds(1, 16, stride=2), :]


def norm_of(position, extent):
    def missing(k):
        k = jnp.maximum(k, 0)
        return (k * (k + 1)) >> 1

    return ((RADIUS + 1) ** 2 - missing(RADIUS - position) - missing(RADIUS - (extent - 1 - position))).astype(F32)


def terms(total, density, sens, p39):
    total = jnp.maximum(total, 1e-30)
    offset = PENALTY * math.log(2.0) / EXPONENT
    smax = jnp.exp(jnp.log(total) * (1.0 / EXPONENT) - offset)
    gap = density - smax
    half = 0.5 * gap * lax.rsqrt(gap * gap + SMOOTH)
    low = 0.5 - half
    top = (0.5 + half) * (2.0 * PENALTY / EXPONENT) * smax
    h = top / total
    return h * sens, h * p39, low, total / top


def plane_norms(sizes):
    row0 = lax.axis_index("gy") * 128
    col0 = lax.axis_index("gx") * 128
    rows = lax.broadcasted_iota(jnp.int32, (128, 128), 0) + row0
    cols = lax.broadcasted_iota(jnp.int32, (128, 128), 1) + col0
    return norm_of(rows, sizes[1] * 128) * norm_of(cols, sizes[2] * 128)


def terms_upper(
    sizes, p_ref, f_ref, s_ref, inner_ref, outer_ref, left_ref, right_ref,
    uv0_ref, uv1_ref, uv2_ref, uv3_ref, y0_ref, y1_ref, y2_ref, above_ref, powers, turned,
):
    c = core()
    lane = lanes(128)
    turned[...] = jnp.zeros((128, 128), F32)
    turned[pl.ds(0, 16, stride=2), :] = right_ref[...]
    turned[pl.ds(1, 16, stride=2), :] = left_ref[...]
    beside = power40(turned[...].T)
    norms = 1.0 / plane_norms(sizes)
    layer0 = lax.axis_index("gz") * LAYERS
    uvs = (uv0_ref, uv1_ref, uv2_ref, uv3_ref)
    ys = (y0_ref, y1_ref, y2_ref)
    for layer in range(LAYERS):
        own = power40(p_ref[layer])
        powers[pl.ds(8, 128), :] = own
        powers[pl.ds(7 + 129 * (1 - c), 1), :] = power40(inner_ref[pl.ds(layer, 1), :])
        powers[pl.ds(7 + 129 * c, 1), :] = power40(outer_ref[pl.ds(layer, 1), :])
        side = pltpu.roll(beside, (128 - (2 * layer + 1)) % 128, 1)
        right = jnp.where(lane == 127, side, pltpu.roll(own, 127, 1))
        left = jnp.where(lane == 0, side, pltpu.roll(own, 1, 1))
        total = (own + right) + left + (powers[pl.ds(7, 128), :] + powers[pl.ds(9, 128), :])
        if layer == LAYERS - 1:
            above_ref[...] = total
            continue
        k = layer + 1
        u, v, low, inverse = terms(total, f_ref[k], s_ref[k], power39(p_ref[k]))
        norm_z = norm_of(layer0 + k, sizes[0] * LAYERS)
        uv3_ref[6 + k] = low * inverse * (norms * (1.0 / norm_z))
        for group, (first, end, rows) in enumerate(GROUPS):
            if first <= k < end:
                place = 2 * (end - 1 - k)
                uvs[group][place] = u
                uvs[group][place + 1] = v
                if group < 3:
                    start = aligned(c * (128 - rows), 8)
                    for i in range(2):
                        ys[group][place + i] = uvs[group][place + i, pl.ds(start, rows), :]
    uv3_ref[4] = jnp.zeros((128, 128), F32)
    uv3_ref[5] = jnp.zeros((128, 128), F32)
    uv3_ref[6] = jnp.zeros((128, 128), F32)


def terms_lowest(sizes, p_ref, f_ref, s_ref, total_ref, uvw_ref, out_ref, y_ref):
    norms = 1.0 / plane_norms(sizes)
    layer0 = lax.axis_index("gz") * LAYERS
    p39 = power39(p_ref[...])
    s = s_ref[...]
    u, v, low, inverse = terms(total_ref[...], f_ref[...], s, p39)
    ground = layer0 == 0
    norm_z = norm_of(layer0, sizes[0] * LAYERS)
    out_ref[...] = uvw_ref[...]
    out_ref[4] = jnp.where(ground, s, u)
    out_ref[5] = jnp.where(ground, p39, v)
    out_ref[6] = jnp.where(ground, 1.0, low * inverse) * (norms * (1.0 / norm_z))
    rows = GROUPS[3][2]
    y_ref[...] = out_ref[:, pl.ds(aligned(core() * (128 - rows), 8), rows), :]


def regions(rows):
    c = core()
    return ((aligned(c * 128, 128), 128), (aligned((1 - c) * 128, 128), 128), (256, rows))


def pack(group, own_ref, other_ref, halo_ref, slab_ref):
    rows = GROUPS[group][2]
    c = core()
    for ref, (start, count) in zip((own_ref, other_ref, halo_ref), regions(rows)):
        lane = lanes(count)
        slab = jnp.zeros((count, 128), F32)
        for place, (at, width) in enumerate(strips_of(group)):
            rolled = pltpu.roll(ref[place], at, 1) if at else ref[place]
            begin = (at + 128 - c * width) & 127
            slab = jnp.where(((lane - begin) & 127) < width, rolled, slab)
        slab_ref[pl.ds(start, count), :] = slab


def assemble(group, own_ref, other_ref, halo_ref, slab_ref, uv_ref, *w_refs):
    first, end, rows = GROUPS[group]
    c = core()
    here = regions(rows)
    to = aligned(256 + seam() * (32 - rows), 8)
    for place, (at, width) in enumerate(strips_of(group)):
        target = uv_ref if place < 2 * (end - first) else w_refs[0]
        index = place if place < 2 * (end - first) else place - 2 * (end - first)
        target[index, pl.ds(256, 32), :] = jnp.zeros((32, 128), F32)
        for ref, (start, count), into in zip(
            (own_ref, other_ref, halo_ref), here, (here[0][0], here[1][0], to)
        ):
            lane = lanes(count)
            got = slab_ref[pl.ds(start, count), :]
            got = pltpu.roll(got, 128 - at, 1) if at else got
            begin = (1 - c) * (128 - width)
            outer = (lane >= begin) & (lane < begin + width)
            target[index, pl.ds(into, count), :] = jnp.where(outer, got, ref[place])


def five(value):
    return (value + pltpu.roll(value, 1, 1)) + pltpu.roll(value, 127, 1) + (
        pltpu.roll(value, 1, 0) + pltpu.roll(value, PLANE - 1, 0)
    )


def set_carry(carry, main_ref, other_ref, outer_ref, halo_ref, halo_other_ref, halo_outer_ref):
    c = core()
    lane = lanes(64)
    mine = (lane >> 6) == c
    for i in range(4):
        rows = pl.ds(64 * (i % 2), 64)
        own, other = main_ref[rows, :], other_ref[rows, :]
        if i < 2:
            value = jnp.where(mine, own, other)
        else:
            value = pltpu.roll(jnp.where(mine, other, own), 64, 1)
        outer = pltpu.roll(outer_ref[...], (128 - 32 * i) % 128, 1) if i else outer_ref[...]
        begin = (1 - c) * 108
        value = jnp.where((lane >= begin) & (lane < begin + 20), outer, value)
        carry[pl.ds(64 * i, 64), :] = value
    lane = lanes(24)
    value = jnp.where((lane >> 6) == c, halo_ref[...], halo_other_ref[...])
    begin = (1 - c) * 108
    value = jnp.where((lane >= begin) & (lane < begin + 20), halo_outer_ref[...], value)
    carry[pl.ds(256, 32), :] = jnp.zeros((32, 128), F32)
    carry[pl.ds(aligned(256 + 8 * seam(), 8), 24), :] = value


def section(active, *refs):
    uv_refs, refs = refs[:4], refs[4:]
    pieces = refs[:6] if len(refs) > 6 else ()
    refs = refs[len(pieces):]
    if len(refs) == 5:
        layers_ref, main_ref, outer_ref, halo_ref, carry = refs
    else:
        layers_ref, carry = refs
        main_ref = None

    @pl.when(lax.axis_index("gz") == active)
    def _():
        if pieces:
            set_carry(carry, *pieces)
            value = carry[...]
        else:
            value = jnp.zeros((PLANE, 128), F32)
        for (first, end, _), uv_ref in zip(GROUPS, uv_refs):
            def step(i, value):
                value = uv_ref[2 * i] + uv_ref[2 * i + 1] * five(value)
                layers_ref[end - 1 - i] = value
                return value
            value = lax.fori_loop(0, end - first, step, value)
        if main_ref is None:
            return
        c = core()
        lane = lanes(128)
        bottom = layers_ref.at[0]
        mine = (lane >> 6) == c
        main_ref[...] = jnp.where(mine, bottom[pl.ds(0, 128), :], pltpu.roll(bottom[pl.ds(128, 128), :], 64, 1))
        lane = lanes(64)
        slab = jnp.zeros((64, 128), F32)
        for i in range(4):
            rolled = bottom[pl.ds(64 * i, 64), :]
            rolled = pltpu.roll(rolled, 32 * i, 1) if i else rolled
            begin = (32 * i + 128 - c * 32) & 127
            slab = jnp.where(((lane - begin) & 127) < 32, rolled, slab)
        outer_ref[...] = slab
        halo_ref[...] = bottom[pl.ds(aligned((1 - seam()) * 232, 8), 24), :]


def smooth(active, layers_ref, w_ref, out_ref, give_ref, top_ref, bottom_ref, weighted):
    @pl.when(lax.axis_index("gz") == active)
    def _():
        c = core()
        lane = lanes(128)
        mine = (lane >> 6) == c

        def layer(k, _):
            weighted[pl.ds(8, PLANE), :] = layers_ref[k] * w_ref[k]
            weighted[pl.ds(0, 8), :] = weighted[pl.ds(PLANE, 8), :]
            halves = []
            for half in range(2):
                start = 8 + 128 * half
                total = weighted[pl.ds(start, 128), :] * 5.0
                for offset in range(1, RADIUS + 1):
                    total = total + (
                        weighted[pl.ds(start - offset, 128), :] + weighted[pl.ds(start + offset, 128), :]
                    ) * (5.0 - offset)
                value = total * 5.0
                for offset in range(1, RADIUS + 1):
                    value = value + (pltpu.roll(total, offset, 1) + pltpu.roll(total, 128 - offset, 1)) * (5.0 - offset)
                halves.append(value)
            out_ref[k] = jnp.where(mine, halves[0], pltpu.roll(halves[1], 64, 1))
            return 0

        lax.fori_loop(0, LAYERS, layer, 0)
        top_ref[...] = out_ref[pl.ds(LAYERS - RADIUS, RADIUS)]
        bottom_ref[...] = out_ref[pl.ds(0, RADIUS)]
        give(out_ref, give_ref)


def give(from_ref, to_ref):
    count = to_ref.shape[0]
    low = (lanes(128) >> 6) == 0
    for k in range(count):
        to_ref[k] = jnp.where(low, pltpu.roll(from_ref[k + count], 64, 1), from_ref[k])


def finish(depth, *refs):
    (q_refs, got_refs, below_refs, below_got_refs, above_refs, above_got_refs) = (
        refs[0:depth], refs[depth:2 * depth],
        refs[2 * depth:3 * depth - 1], refs[3 * depth - 1:4 * depth - 2],
        refs[4 * depth - 2:5 * depth - 3], refs[5 * depth - 3:6 * depth - 4],
    )
    passive_ref, out_ref, packed, got, sem = refs[6 * depth - 4:]
    gz = lax.axis_index("gz")
    c = core()
    low = (lanes(128) >> 6) == 0

    def load(active, pairs):
        @pl.when(gz == active)
        def _():
            copies = [pltpu.make_async_copy(src, dst, sem.at[i]) for i, (src, dst) in enumerate(pairs)]
            for copy in copies:
                copy.start()
            for copy in copies:
                copy.wait()

    zeros = jnp.zeros((RADIUS, 128, 128), F32)

    @pl.when(gz == 0)
    def _():
        packed[pl.ds(0, RADIUS)] = zeros
        got[pl.ds(0, RADIUS // 2)] = zeros[:RADIUS // 2]

    @pl.when(gz == depth - 1)
    def _():
        packed[pl.ds(LAYERS + RADIUS, RADIUS)] = zeros
        got[pl.ds(LAYERS // 2 + RADIUS // 2, RADIUS // 2)] = zeros[:RADIUS // 2]

    for z in range(depth):
        pairs = [
            (q_refs[z], packed.at[pl.ds(RADIUS, LAYERS)]),
            (got_refs[z], got.at[pl.ds(RADIUS // 2, LAYERS // 2)]),
        ]
        if z > 0:
            pairs += [
                (below_refs[z - 1], packed.at[pl.ds(0, RADIUS)]),
                (below_got_refs[z - 1], got.at[pl.ds(0, RADIUS // 2)]),
            ]
        if z < depth - 1:
            pairs += [
                (above_refs[z], packed.at[pl.ds(LAYERS + RADIUS, RADIUS)]),
                (above_got_refs[z], got.at[pl.ds(LAYERS // 2 + RADIUS // 2, RADIUS // 2)]),
            ]
        load(z, pairs)

    mine = low == (c == 0)

    def layer(k):
        if k < RADIUS:
            base, count, i = 0, RADIUS // 2, k
        elif k < RADIUS + LAYERS:
            base, count, i = RADIUS // 2, LAYERS // 2, k - RADIUS
        else:
            base, count, i = RADIUS // 2 + LAYERS // 2, RADIUS // 2, k - RADIUS - LAYERS
        own = packed[k]
        other = got[base + i % count]
        own = jnp.where(c == 0, own, pltpu.roll(own, 64, 1))
        first = i < count
        upper = other if first else pltpu.roll(other, 64, 1)
        value = jnp.where(c == 0, upper, pltpu.roll(upper, 64, 1))
        return jnp.where(mine, own, value)

    for k in range(LAYERS + 2 * RADIUS):
        packed[k] = layer(k)
    for k in range(LAYERS):
        total = packed[k + RADIUS] * 5.0
        for offset in range(1, RADIUS + 1):
            total = total + (packed[k + RADIUS - offset] + packed[k + RADIUS + offset]) * (5.0 - offset)
        out_ref[k] = jnp.where(passive_ref[k] > 0, 0.0, total)


def to_other(value):
    return moved(value, lambda z, y, x: (z, y ^ 1, x))


def per_device(filtered, printed, sensitivity, passive):
    sizes = tuple(lax.axis_size(axis) for axis in AXES)
    depth = sizes[0]
    plane = shape(128, 128)
    edge = shape(16, 128)
    inner, outer, left, right = call(edges, [edge] * 4, printed, scratch=[pltpu.VMEM((128, 128), F32)])

    def across(z, y, x):
        return (z, y ^ 3, x) if y in (1, 2) else None

    def beside(z, y, x):
        return (z, y ^ 1, x + (1 if y & 1 else -1))

    inner = to_other(inner)
    outer = moved(outer, across)
    from_left = moved(right, lambda z, y, x: (z, y, x + 1))
    from_right = moved(left, lambda z, y, x: (z, y, x - 1))
    counts = [len(strips_of(group)) for group in range(4)]
    blocks = [shape(count, 128, 128) for count in counts]
    halos = [shape(count, rows, 128) for count, (_, _, rows) in zip(counts, GROUPS)]
    *owns, y0, y1, y2, above = call(
        functools.partial(terms_upper, sizes),
        blocks + halos[:3] + [plane],
        printed, filtered, sensitivity, inner, outer, from_left, from_right,
        scratch=[pltpu.VMEM((144, 128), F32), pltpu.VMEM((128, 128), F32)],
    )
    total0 = moved(above, lambda z, y, x: (z + 1, y, x))
    owns[3], y3 = call(
        functools.partial(terms_lowest, sizes), [blocks[3], halos[3]],
        printed[0], filtered[0], sensitivity[0], total0, owns[3],
    )
    uvs, ws = [], None
    for group, (y, own) in enumerate(zip((y0, y1, y2, y3), owns)):
        first, end, rows = GROUPS[group]
        other = to_other(own)
        got = moved(y, across)
        shared = moved(got, lambda z, y, x: (z, y ^ 1, x) if y in (1, 2) else None)
        halo = jnp.where((lax.axis_index("gy") == 1) | (lax.axis_index("gy") == 2), got, shared)
        slab = call(functools.partial(pack, group), shape(256 + rows, 128), own, other, halo)
        slab = moved(slab, beside)
        outs = [shape(2 * (end - first), PLANE, 128)]
        if first == 0:
            outs = outs + [shape(LAYERS, PLANE, 128)]
        outs = call(functools.partial(assemble, group), outs, own, other, halo, slab)
        uvs.append(outs[0])
        if first == 0:
            ws = outs[1]
    pieces = ()
    stack = shape(LAYERS, PLANE, 128)
    quarter = shape(RADIUS, 128, 128)
    tiles, gots, belows, below_gots, aboves, above_gots = [], [], [], [], [], []
    for active in range(depth - 1, -1, -1):
        outs = [stack]
        if active > 0:
            outs = outs + [plane, shape(64, 128), shape(24, 128)]
        layers, *ends = call(
            functools.partial(section, active), outs, *uvs, *pieces, scratch=[pltpu.VMEM((PLANE, 128), F32)]
        )
        if active > 0:
            main, side, strip = ends

            def down(where):
                def to(z, y, x):
                    _, ty, tx = where(z, y, x)
                    return (z - 1, ty, tx) if z == active else None
                return to

            def over(z, y, x):
                return (z, y ^ 2, x)

            def corner(z, y, x):
                _, ty, tx = beside(z, y, x)
                return (z, ty ^ 2, tx)

            def sibling(z, y, x):
                return (z, y ^ 1, x) if z == active - 1 else None

            main = moved(main, down(lambda z, y, x: (z, y, x)))
            halo = moved(strip, down(over))
            pieces = (
                main,
                moved(main, sibling),
                moved(side, down(beside)),
                halo,
                moved(halo, sibling),
                moved(strip, down(corner)),
            )
        tile, given, top, bottom = call(
            functools.partial(smooth, active),
            [shape(LAYERS, 128, 128), shape(LAYERS // 2, 128, 128), quarter, quarter],
            layers, ws,
            scratch=[pltpu.VMEM((PLANE + 8, 128), F32)],
        )
        tiles.insert(0, tile)
        gots.insert(0, moved(given, lambda z, y, x: (z, y ^ 1, x) if z == active else None))
        if active < depth - 1:
            below = moved(top, lambda z, y, x: (z + 1, y, x) if z == active else None)
            belows.insert(0, below)
            half = call(give_part, shape(RADIUS // 2, 128, 128), below)
            below_gots.insert(0, moved(half, lambda z, y, x: (z, y ^ 1, x) if z == active + 1 else None))
        if active > 0:
            above = moved(bottom, lambda z, y, x: (z - 1, y, x) if z == active else None)
            aboves.insert(0, above)
            half = call(give_part, shape(RADIUS // 2, 128, 128), above)
            above_gots.insert(0, moved(half, lambda z, y, x: (z, y ^ 1, x) if z == active - 1 else None))
    hbm = pl.BlockSpec(memory_space=pl.ANY)
    operands = tiles + gots + belows + below_gots + aboves + above_gots
    return call(
        functools.partial(finish, depth),
        shape(LAYERS, 128, 128),
        *operands,
        passive,
        in_specs=[hbm] * len(operands) + [pl.BlockSpec(memory_space=pltpu.VMEM)],
        scratch=[
            pltpu.VMEM((LAYERS + 2 * RADIUS, 128, 128), F32),
            pltpu.VMEM((LAYERS // 2 + RADIUS, 128, 128), F32),
            pltpu.SemaphoreType.DMA((6,)),
        ],
    )


def give_part(from_ref, to_ref):
    give(from_ref, to_ref)


def solution(mesh):
    spec = P(*AXES)
    return jax.shard_map(
        per_device, mesh=mesh, in_specs=(spec,) * 4, out_specs=spec, check_vma=False
    )
```

time: 322 us -> 232 us (0.72)
  the two profiles are of different devices: /device:TPU:31 before, /device:TPU:47 now
where the time goes in v2:
time: 232 us; the launch traced here: 231 us
  starting transfers between devices  135 us (58%)
  waiting for transfers between devices  63.4 us (27%)
  Pallas kernels  24.8 us (11%)
  local copies, waits for them, and re-layouts  5.57 us (2%)
    ppermute x55, starting transfers between devices, moved(): return lax.ppermute(value, AXES, pairs)  135 us
    ppermute x55, waiting for transfers between devices, moved(): return lax.ppermute(value, AXES, pairs)  63.4 us
    pallas_call x26, Pallas kernels, call(): pl.pallas_call(kernel, out_shape=outs, scratch_shapes=list(scratch), comp...  24.8 us
    unnamed x16, local copies, waits for them, and re-layouts  4.68 us
  transfers between devices with their start and end apart: 55, of which 11 were waited for; matrix products, arithmetic and copies ran while one was open for 1% of the time, Pallas kernels for 7%

profile of v2, /device:TPU:47, one launch (start us, length us, event | category | flops | bytes accessed | tf_op | source)
XLA Modules:
  0.0 230.7 jit_solution(8471228539479395968)
XLA Ops:
  3.0 4.9 %collective-permute-start.2 = (f32[16,128]{1,0:T(8,128)S(1)}, f32[16,128]{1,0:T(8,128)S(1)}, u32[]{:S(2)}, u32[]{:S(2)}) collective-permute-start(f32[16,128]{1,0:T(8,128)S(1)} %get-tuple-element.49), channel_id=1, source_target_pairs={{0,1},{1,2},{2,3},{3,4},{4,5},{5,6},{6,7},{7,8},{8,9},{9,10},{10,1... | collective-permute-start | bytes 24584 | tf_op jit(solution)/shard_map/ppermute | solution.py:47
  7.9 4.3 %collective-permute-start.3 = (f32[16,128]{1,0:T(8,128)S(1)}, f32[16,128]{1,0:T(8,128)S(1)}, u32[]{:S(2)}, u32[]{:S(2)}) collective-permute-start(f32[16,128]{1,0:T(8,128)S(1)} %get-tuple-element.50), channel_id=1, source_target_pairs={{1,0},{2,1},{3,2},{4,3},{5,4},{6,5},{7,6},{8,7},{9,8},{10,9},{11,1... | collective-permute-start | bytes 24584 | tf_op jit(solution)/shard_map/ppermute | solution.py:47
  16.7 2.7 %terms_upper.1 = (f32[6,128,128]{2,1,0:T(8,128)S(1)}, f32[8,128,128]{2,1,0:T(8,128)S(1)}, f32[12,128,128]{2,1,0:T(8,128)}, f32[22,128,128]{2,1,0:T(8,128)S(1)}, ...) custom-call(f32[16,128,128]{2,1,0:T(8,128)S(1)} %copy-done, ...), custom_call_target="tpu_custom_call" | custom-call | tf_op jit(solution)/shard_map/terms_upper/pallas_call | solution.py:57
  19.3 3.2 %collective-permute-start.16 = (f32[128,128]{1,0:T(8,128)S(1)}, f32[128,128]{1,0:T(8,128)S(1)}, u32[]{:S(2)}, u32[]{:S(2)}) collective-permute-start(f32[128,128]{1,0:T(8,128)S(1)} %get-tuple-element.57), channel_id=1, source_target_pairs={{0,64},{1,65},{2,66},{3,67},{4,68},{5,69},{6,70},{7,71},{8,72},{9,... | collective-permute-start | bytes 196616 | tf_op jit(solution)/shard_map/ppermute | solution.py:47
  24.6 15.1 %collective-permute-start.17 = (f32[22,128,128]{2,1,0:T(8,128)S(1)}, f32[22,128,128]{2,1,0:T(8,128)S(1)}, u32[]{:S(2)}, u32[]{:S(2)}) collective-permute-start(f32[22,128,128]{2,1,0:T(8,128)S(1)} %get-tuple-element.59.own_ref), channel_id=1, source_target_pairs={{0,16},{1,17},{2,18},{3,19},{4,20},{5,21},{6,22},{7,23},{8,24},{9,... | collective-permute-start | bytes 4325384 | tf_op jit(solution)/shard_map/ppermute | solution.py:47
  42.2 14.7 %collective-permute-start.12 = (f32[12,128,128]{2,1,0:T(8,128)}, f32[12,128,128]{2,1,0:T(8,128)}, u32[]{:S(2)}, u32[]{:S(2)}) collective-permute-start(f32[12,128,128]{2,1,0:T(8,128)} %get-tuple-element.55.own_ref), channel_id=1, source_target_pairs={{0,16},{1,17},{2,18},{3,19},{4,20},{5,21},{6,22},{7,23},{8,24},{9,... | collective-permute-start | bytes 2359304 | tf_op jit(solution)/shard_map/ppermute | solution.py:47
  59.5 3.7 %collective-permute-start.8 = (f32[8,128,128]{2,1,0:T(8,128)S(1)}, f32[8,128,128]{2,1,0:T(8,128)S(1)}, u32[]{:S(2)}, u32[]{:S(2)}) collective-permute-start(f32[8,128,128]{2,1,0:T(8,128)S(1)} %get-tuple-element.53.own_ref), channel_id=1, source_target_pairs={{0,16},{1,17},{2,18},{3,19},{4,20},{5,21},{6,22},{7,23},{8,24},{9,... | collective-permute-start | bytes 1572872 | tf_op jit(solution)/shard_map/ppermute | solution.py:47
  69.0 2.6 %collective-permute-done.14 = f32[12,16,128]{2,1,0:T(8,128)S(1)} collective-permute-done((f32[12,16,128]{2,1,0:T(8,128)}, f32[12,16,128]{2,1,0:T(8,128)S(1)}, u32[]{:S(2)}, u32[]{:S(2)}) %collective-permute-start.14) | collective-permute-done | bytes 98336 | tf_op jit(solution)/shard_map/ppermute | solution.py:47
  74.2 6.4 %collective-permute-start.7 = (f32[280,128]{1,0:T(8,128)S(1)}, f32[280,128]{1,0:T(8,128)S(1)}, u32[]{:S(2)}, u32[]{:S(2)}) collective-permute-start(f32[280,128]{1,0:T(8,128)S(1)} %pack.4), channel_id=1, source_target_pairs={{1,16},{2,17},{3,18},{4,19},{5,20},{6,21},{7,22},{8,23},{9,24},{10... | collective-permute-start | bytes 430088 | tf_op jit(solution)/shard_map/ppermute | solution.py:47
  84.9 4.5 %collective-permute-start.15 = (f32[272,128]{1,0:T(8,128)S(1)}, f32[272,128]{1,0:T(8,128)S(1)}, u32[]{:S(2)}, u32[]{:S(2)}) collective-permute-start(f32[272,128]{1,0:T(8,128)S(1)} %pack.6), channel_id=1, source_target_pairs={{1,16},{2,17},{3,18},{4,19},{5,20},{6,21},{7,22},{8,23},{9,24},{10... | collective-permute-start | bytes 417800 | tf_op jit(solution)/shard_map/ppermute | solution.py:47
  94.7 4.0 %collective-permute-done.20.slab_ref = f32[264,128]{1,0:T(8,128)S(1)} collective-permute-done((f32[264,128]{1,0:T(8,128)S(1)}, f32[264,128]{1,0:T(8,128)S(1)}, u32[]{:S(2)}, u32[]{:S(2)}) %collective-permute-start.20) | collective-permute-done | bytes 135200 | tf_op jit(solution)/shard_map/ppermute | solution.py:47
  107.1 42.9 %collective-permute-done.27.refs_4_ = f32[128,128]{1,0:T(8,128)S(1)} collective-permute-done((f32[128,128]{1,0:T(8,128)S(1)}, f32[128,128]{1,0:T(8,128)S(1)}, u32[]{:S(2)}, u32[]{:S(2)}) %collective-permute-start.27) | collective-permute-done | bytes 65568 | tf_op jit(solution)/shard_map/ppermute | solution.py:47
  150.0 2.7 %collective-permute-start.28 = (f32[128,128]{1,0:T(8,128)S(1)}, f32[128,128]{1,0:T(8,128)S(1)}, u32[]{:S(2)}, u32[]{:S(2)}) collective-permute-start(f32[128,128]{1,0:T(8,128)S(1)} %collective-permute-done.27.refs_4_), channel_id=1, source_target_pairs={{64,80},{65,81},{66,82},{67,83},{68,84},{69,85},{70,86},{71,87},{7... | collective-permute-start | bytes 196616 | tf_op jit(solution)/shard_map/ppermute | solution.py:47
  155.3 4.0 %collective-permute-done.30.refs_7_ = f32[24,128]{1,0:T(8,128)S(1)} collective-permute-done((f32[24,128]{1,0:T(8,128)S(1)}, f32[24,128]{1,0:T(8,128)S(1)}, u32[]{:S(2)}, u32[]{:S(2)}) %collective-permute-start.30) | collective-permute-done | bytes 12320 | tf_op jit(solution)/shard_map/ppermute | solution.py:47
  160.7 5.2 %collective-permute-start.31 = (f32[24,128]{1,0:T(8,128)S(1)}, f32[24,128]{1,0:T(8,128)S(1)}, u32[]{:S(2)}, u32[]{:S(2)}) collective-permute-start(f32[24,128]{1,0:T(8,128)S(1)} %collective-permute-done.30.refs_7_), channel_id=1, source_target_pairs={{64,80},{65,81},{66,82},{67,83},{68,84},{69,85},{70,86},{71,87},{7... | collective-permute-start | bytes 36872 | tf_op jit(solution)/shard_map/ppermute | solution.py:47
  166.9 2.6 %section.6 = (f32[16,288,128]{2,1,0:T(8,128)S(1)}, f32[128,128]{1,0:T(8,128)S(1)}, f32[64,128]{1,0:T(8,128)S(1)}, f32[24,128]{1,0:T(8,128)S(1)}) custom-call(f32[6,288,128]{2,1,0:T(8,128)S(1)} %assemble.4.refs_0_, f32[8,288,128]{2,1,0:T(8,128)S(1)} %assemble.5.refs_1_, f32[12,288,128]{2,1,0:T(8,128)S(1)} %assemble.6.refs_2_, ...), custom_call_target="tpu_custom_call" | custom-call | tf_op jit(solution)/shard_map/section/pallas_call | solution.py:57
  173.5 8.0 %collective-permute-start.36 = (f32[24,128]{1,0:T(8,128)S(1)}, f32[24,128]{1,0:T(8,128)S(1)}, u32[]{:S(2)}, u32[]{:S(2)}) collective-permute-start(f32[24,128]{1,0:T(8,128)S(1)} %get-tuple-element.70), channel_id=1, source_target_pairs={{64,32},{65,33},{66,34},{67,35},{68,36},{69,37},{70,38},{71,39},{7... | collective-permute-start | bytes 36872 | tf_op jit(solution)/shard_map/ppermute | solution.py:47
  185.0 7.2 %smooth.5 = (f32[16,128,128]{2,1,0:T(8,128)S(1)}, f32[8,128,128]{2,1,0:T(8,128)S(1)}, f32[4,128,128]{2,1,0:T(8,128)S(1)}, f32[4,128,128]{2,1,0:T(8,128)S(1)}) custom-call(f32[16,288,128]{2,1,0:T(8,128)S(1)} %get-tuple-element.73.layers_ref, f32[16,288,128]{2,1,0:T(8,128)S(1)} %get-tuple-element.71.w_ref), custom_call_target="tpu_custom_call" | custom-call | tf_op jit(solution)/shard_map/smooth/pallas_call | solution.py:57
  195.6 14.2 %collective-permute-start.49 = (f32[4,128,128]{2,1,0:T(8,128)S(1)}, f32[4,128,128]{2,1,0:T(8,128)S(1)}, u32[]{:S(2)}, u32[]{:S(2)}) collective-permute-start(f32[4,128,128]{2,1,0:T(8,128)S(1)} %get-tuple-element.86), channel_id=1, source_target_pairs={{64,0},{65,1},{66,2},{67,3},{68,4},{69,5},{70,6},{71,7},{72,8},{73... | collective-permute-start | bytes 786440 | tf_op jit(solution)/shard_map/ppermute | solution.py:47
  211.2 2.5 %collective-permute-start.40 = (f32[8,128,128]{2,1,0:T(8,128)S(1)}, f32[8,128,128]{2,1,0:T(8,128)S(1)}, u32[]{:S(2)}, u32[]{:S(2)}) collective-permute-start(f32[8,128,128]{2,1,0:T(8,128)S(1)} %get-tuple-element.80), channel_id=1, source_target_pairs={{64,80},{65,81},{66,82},{67,83},{68,84},{69,85},{70,86},{71,87},{7... | collective-permute-start | bytes 1572872 | tf_op jit(solution)/shard_map/ppermute | solution.py:47
  215.9 3.2 %collective-permute-done.43.from_ref.refs_8_ = f32[4,128,128]{2,1,0:T(8,128)S(1)} collective-permute-done((f32[4,128,128]{2,1,0:T(8,128)S(1)}, f32[4,128,128]{2,1,0:T(8,128)S(1)}, u32[]{:S(2)}, u32[]{:S(2)}) %collective-permute-start.43) | collective-permute-done | bytes 262176 | tf_op jit(solution)/shard_map/ppermute | solution.py:47
  219.0 3.4 %collective-permute-start.53 = (f32[2,128,128]{2,1,0:T(8,128)S(1)}, f32[2,128,128]{2,1,0:T(8,128)S(1)}, u32[]{:S(2)}, u32[]{:S(2)}) collective-permute-start(f32[2,128,128]{2,1,0:T(8,128)S(1)} %give_part.10), channel_id=1, source_target_pairs={{64,80},{65,81},{66,82},{67,83},{68,84},{69,85},{70,86},{71,87},{7... | collective-permute-start | bytes 393224 | tf_op jit(solution)/shard_map/ppermute | solution.py:47
  224.1 2.2 collective-permute-start.46
  227.4 3.2 %finish.1 = f32[16,128,128]{2,1,0:T(8,128)} custom-call(f32[16,128,128]{2,1,0:T(8,128)S(1)} %get-tuple-element.72.refs_0_, f32[16,128,128]{2,1,0:T(8,128)S(1)} %get-tuple-element.74.refs_1_, f32[16,128,128]{2,1,0:T(8,128)S(1)} %get-tuple-element.76.refs_2_, f32[16,128,128]{2,1,0:T(8,128)S(1)} %get-tuple-element.78.refs_3_, ...), custom_call_target="tpu_custom_call" | custom-call | tf_op jit(solution)/shard_map/finish/pallas_call | solution.py:57
  (134 shorter events, 62.0 us)
Async XLA Ops:
  1.6 11.5 %collective-permute-start = (f32[16,128]{1,0:T(8,128)S(1)}, f32[16,128]{1,0:T(8,128)S(1)}, u32[]{:S(2)}, u32[]{:S(2)}) collective-permute-start(f32[16,128]{1,0:T(8,128)S(1)} %get-tuple-element.47), channel_id=1, source_target_pairs={{0,16},{1,17},{2,18},{3,19},{4,20},{5,21},{6,22},{7,23},{8,24},{9,... | collective-permute-start | bytes 24584 | tf_op jit(solution)/shard_map/ppermute | solution.py:47
  24.6 64.8 %collective-permute-start.17 = (f32[22,128,128]{2,1,0:T(8,128)S(1)}, f32[22,128,128]{2,1,0:T(8,128)S(1)}, u32[]{:S(2)}, u32[]{:S(2)}) collective-permute-start(f32[22,128,128]{2,1,0:T(8,128)S(1)} %get-tuple-element.59.own_ref), channel_id=1, source_target_pairs={{0,16},{1,17},{2,18},{3,19},{4,20},{5,21},{6,22},{7,23},{8,24},{9,... | collective-permute-start | bytes 4325384 | tf_op jit(solution)/shard_map/ppermute | solution.py:47
  39.7 18.5 %collective-permute-start.9 = (f32[8,16,128]{2,1,0:T(8,128)S(1)}, f32[8,16,128]{2,1,0:T(8,128)}, u32[]{:S(2)}, u32[]{:S(2)}) collective-permute-start(f32[8,16,128]{2,1,0:T(8,128)S(1)} %get-tuple-element.54), channel_id=1, source_target_pairs={{16,32},{17,33},{18,34},{19,35},{20,36},{21,37},{22,38},{23,39},{2... | collective-permute-start | bytes 196616 | tf_op jit(solution)/shard_map/ppermute | solution.py:47
  40.9 22.3 %collective-permute-start.13 = (f32[12,16,128]{2,1,0:T(8,128)S(1)}, f32[12,16,128]{2,1,0:T(8,128)}, u32[]{:S(2)}, u32[]{:S(2)}) collective-permute-start(f32[12,16,128]{2,1,0:T(8,128)S(1)} %get-tuple-element.56), channel_id=1, source_target_pairs={{16,32},{17,33},{18,34},{19,35},{20,36},{21,37},{22,38},{23,39},{2... | collective-permute-start | bytes 294920 | tf_op jit(solution)/shard_map/ppermute | solution.py:47
  42.2 40.8 %collective-permute-start.12 = (f32[12,128,128]{2,1,0:T(8,128)}, f32[12,128,128]{2,1,0:T(8,128)}, u32[]{:S(2)}, u32[]{:S(2)}) collective-permute-start(f32[12,128,128]{2,1,0:T(8,128)} %get-tuple-element.55.own_ref), channel_id=1, source_target_pairs={{0,16},{1,17},{2,18},{3,19},{4,20},{5,21},{6,22},{7,23},{8,24},{9,... | collective-permute-start | bytes 2359304 | tf_op jit(solution)/shard_map/ppermute | solution.py:47
  59.5 21.1 %collective-permute-start.8 = (f32[8,128,128]{2,1,0:T(8,128)S(1)}, f32[8,128,128]{2,1,0:T(8,128)S(1)}, u32[]{:S(2)}, u32[]{:S(2)}) collective-permute-start(f32[8,128,128]{2,1,0:T(8,128)S(1)} %get-tuple-element.53.own_ref), channel_id=1, source_target_pairs={{0,16},{1,17},{2,18},{3,19},{4,20},{5,21},{6,22},{7,23},{8,24},{9,... | collective-permute-start | bytes 1572872 | tf_op jit(solution)/shard_map/ppermute | solution.py:47
  71.6 17.8 %collective-permute-start.19 = (f32[22,8,128]{2,1,0:T(8,128)S(1)}, f32[22,8,128]{2,1,0:T(8,128)S(1)}, u32[]{:S(2)}, u32[]{:S(2)}) collective-permute-start(f32[22,8,128]{2,1,0:T(8,128)S(1)} %collective-permute-done.18), channel_id=1, source_target_pairs={{16,0},{17,1},{18,2},{19,3},{20,4},{21,5},{22,6},{23,7},{24,8},{25... | collective-permute-start | bytes 270344 | tf_op jit(solution)/shard_map/ppermute | solution.py:47
  74.2 18.0 %collective-permute-start.7 = (f32[280,128]{1,0:T(8,128)S(1)}, f32[280,128]{1,0:T(8,128)S(1)}, u32[]{:S(2)}, u32[]{:S(2)}) collective-permute-start(f32[280,128]{1,0:T(8,128)S(1)} %pack.4), channel_id=1, source_target_pairs={{1,16},{2,17},{3,18},{4,19},{5,20},{6,21},{7,22},{8,23},{9,24},{10... | collective-permute-start | bytes 430088 | tf_op jit(solution)/shard_map/ppermute | solution.py:47
  80.9 11.5 %collective-permute-start.11 = (f32[272,128]{1,0:T(8,128)S(1)}, f32[272,128]{1,0:T(8,128)S(1)}, u32[]{:S(2)}, u32[]{:S(2)}) collective-permute-start(f32[272,128]{1,0:T(8,128)S(1)} %pack.5), channel_id=1, source_target_pairs={{1,16},{2,17},{3,18},{4,19},{5,20},{6,21},{7,22},{8,23},{9,24},{10... | collective-permute-start | bytes 417800 | tf_op jit(solution)/shard_map/ppermute | solution.py:47
  100.3 60.4 %collective-permute-start.51 = (f32[4,128,128]{2,1,0:T(8,128)S(1)}, f32[4,128,128]{2,1,0:T(8,128)S(1)}, u32[]{:S(2)}, u32[]{:S(2)}) collective-permute-start(f32[4,128,128]{2,1,0:T(8,128)S(1)} %get-tuple-element.88), channel_id=1, source_target_pairs={{192,128},{193,129},{194,130},{195,131},{196,132},{197,133},{198,1... | collective-permute-start | bytes 786440 | tf_op jit(solution)/shard_map/ppermute | solution.py:47
  102.3 108.9 %collective-permute-start.42 = (f32[8,128,128]{2,1,0:T(8,128)S(1)}, f32[8,128,128]{2,1,0:T(8,128)S(1)}, u32[]{:S(2)}, u32[]{:S(2)}) collective-permute-start(f32[8,128,128]{2,1,0:T(8,128)S(1)} %get-tuple-element.82), channel_id=1, source_target_pairs={{192,208},{193,209},{194,210},{195,211},{196,212},{197,213},{198,2... | collective-permute-start | bytes 1572872 | tf_op jit(solution)/shard_map/ppermute | solution.py:47
  105.8 44.2 %collective-permute-start.27 = (f32[128,128]{1,0:T(8,128)S(1)}, f32[128,128]{1,0:T(8,128)S(1)}, u32[]{:S(2)}, u32[]{:S(2)}) collective-permute-start(f32[128,128]{1,0:T(8,128)S(1)} %get-tuple-element.65), channel_id=1, source_target_pairs={{128,64},{129,65},{130,66},{131,67},{132,68},{133,69},{134,70},{13... | collective-permute-start | bytes 196616 | tf_op jit(solution)/shard_map/ppermute | solution.py:47
  150.0 16.9 %collective-permute-start.28 = (f32[128,128]{1,0:T(8,128)S(1)}, f32[128,128]{1,0:T(8,128)S(1)}, u32[]{:S(2)}, u32[]{:S(2)}) collective-permute-start(f32[128,128]{1,0:T(8,128)S(1)} %collective-permute-done.27.refs_4_), channel_id=1, source_target_pairs={{64,80},{65,81},{66,82},{67,83},{68,84},{69,85},{70,86},{71,87},{7... | collective-permute-start | bytes 196616 | tf_op jit(solution)/shard_map/ppermute | solution.py:47
  152.7 14.2 %collective-permute-start.29 = (f32[64,128]{1,0:T(8,128)S(1)}, f32[64,128]{1,0:T(8,128)S(1)}, u32[]{:S(2)}, u32[]{:S(2)}) collective-permute-start(f32[64,128]{1,0:T(8,128)S(1)} %get-tuple-element.66), channel_id=1, source_target_pairs={{129,80},{130,81},{131,82},{132,83},{133,84},{134,85},{135,86},{13... | collective-permute-start | bytes 98312 | tf_op jit(solution)/shard_map/ppermute | solution.py:47
  166.0 27.4 %collective-permute-start.54 = (f32[2,128,128]{2,1,0:T(8,128)S(1)}, f32[2,128,128]{2,1,0:T(8,128)S(1)}, u32[]{:S(2)}, u32[]{:S(2)}) collective-permute-start(f32[2,128,128]{2,1,0:T(8,128)S(1)} %give_part.11), channel_id=1, source_target_pairs={{128,144},{129,145},{130,146},{131,147},{132,148},{133,149},{134,1... | collective-permute-start | bytes 393224 | tf_op jit(solution)/shard_map/ppermute | solution.py:47
  169.6 22.6 %collective-permute-start.33 = (f32[128,128]{1,0:T(8,128)S(1)}, f32[128,128]{1,0:T(8,128)S(1)}, u32[]{:S(2)}, u32[]{:S(2)}) collective-permute-start(f32[128,128]{1,0:T(8,128)S(1)} %get-tuple-element.68), channel_id=1, source_target_pairs={{64,0},{65,1},{66,2},{67,3},{68,4},{69,5},{70,6},{71,7},{72,8},{73... | collective-permute-start | bytes 196616 | tf_op jit(solution)/shard_map/ppermute | solution.py:47
  172.2 11.5 %collective-permute-start.35 = (f32[64,128]{1,0:T(8,128)S(1)}, f32[64,128]{1,0:T(8,128)S(1)}, u32[]{:S(2)}, u32[]{:S(2)}) collective-permute-start(f32[64,128]{1,0:T(8,128)S(1)} %get-tuple-element.69), channel_id=1, source_target_pairs={{65,16},{66,17},{67,18},{68,19},{69,20},{70,21},{71,22},{72,23},{7... | collective-permute-start | bytes 98312 | tf_op jit(solution)/shard_map/ppermute | solution.py:47
  183.0 12.6 %collective-permute-start.45 = (f32[4,128,128]{2,1,0:T(8,128)S(1)}, f32[4,128,128]{2,1,0:T(8,128)S(1)}, u32[]{:S(2)}, u32[]{:S(2)}) collective-permute-start(f32[4,128,128]{2,1,0:T(8,128)S(1)} %get-tuple-element.85), channel_id=1, source_target_pairs={{128,192},{129,193},{130,194},{131,195},{132,196},{133,197},{134,1... | collective-permute-start | bytes 786440 | tf_op jit(solution)/shard_map/ppermute | solution.py:47
  183.7 26.2 %collective-permute-start.50 = (f32[4,128,128]{2,1,0:T(8,128)S(1)}, f32[4,128,128]{2,1,0:T(8,128)S(1)}, u32[]{:S(2)}, u32[]{:S(2)}) collective-permute-start(f32[4,128,128]{2,1,0:T(8,128)S(1)} %get-tuple-element.87), channel_id=1, source_target_pairs={{128,64},{129,65},{130,66},{131,67},{132,68},{133,69},{134,70},{13... | collective-permute-start | bytes 786440 | tf_op jit(solution)/shard_map/ppermute | solution.py:47
  192.1 21.6 %collective-permute-start.44 = (f32[4,128,128]{2,1,0:T(8,128)S(1)}, f32[4,128,128]{2,1,0:T(8,128)S(1)}, u32[]{:S(2)}, u32[]{:S(2)}) collective-permute-start(f32[4,128,128]{2,1,0:T(8,128)S(1)} %get-tuple-element.84), channel_id=1, source_target_pairs={{64,128},{65,129},{66,130},{67,131},{68,132},{69,133},{70,134},{71... | collective-permute-start | bytes 786440 | tf_op jit(solution)/shard_map/ppermute | solution.py:47
  194.2 29.9 %collective-permute-start.41 = (f32[8,128,128]{2,1,0:T(8,128)S(1)}, f32[8,128,128]{2,1,0:T(8,128)S(1)}, u32[]{:S(2)}, u32[]{:S(2)}) collective-permute-start(f32[8,128,128]{2,1,0:T(8,128)S(1)} %get-tuple-element.81), channel_id=1, source_target_pairs={{128,144},{129,145},{130,146},{131,147},{132,148},{133,149},{134,1... | collective-permute-start | bytes 1572872 | tf_op jit(solution)/shard_map/ppermute | solution.py:47
  195.6 19.6 %collective-permute-start.49 = (f32[4,128,128]{2,1,0:T(8,128)S(1)}, f32[4,128,128]{2,1,0:T(8,128)S(1)}, u32[]{:S(2)}, u32[]{:S(2)}) collective-permute-start(f32[4,128,128]{2,1,0:T(8,128)S(1)} %get-tuple-element.86), channel_id=1, source_target_pairs={{64,0},{65,1},{66,2},{67,3},{68,4},{69,5},{70,6},{71,7},{72,8},{73... | collective-permute-start | bytes 786440 | tf_op jit(solution)/shard_map/ppermute | solution.py:47
  211.2 16.1 %collective-permute-start.40 = (f32[8,128,128]{2,1,0:T(8,128)S(1)}, f32[8,128,128]{2,1,0:T(8,128)S(1)}, u32[]{:S(2)}, u32[]{:S(2)}) collective-permute-start(f32[8,128,128]{2,1,0:T(8,128)S(1)} %get-tuple-element.80), channel_id=1, source_target_pairs={{64,80},{65,81},{66,82},{67,83},{68,84},{69,85},{70,86},{71,87},{7... | collective-permute-start | bytes 1572872 | tf_op jit(solution)/shard_map/ppermute | solution.py:47
  213.7 13.6 %collective-permute-start.39 = (f32[8,128,128]{2,1,0:T(8,128)S(1)}, f32[8,128,128]{2,1,0:T(8,128)S(1)}, u32[]{:S(2)}, u32[]{:S(2)}) collective-permute-start(f32[8,128,128]{2,1,0:T(8,128)S(1)} %get-tuple-element.79), channel_id=1, source_target_pairs={{0,16},{1,17},{2,18},{3,19},{4,20},{5,21},{6,22},{7,23},{8,24},{9,... | collective-permute-start | bytes 1572872 | tf_op jit(solution)/shard_map/ppermute | solution.py:47
  (39 other events, 216.8 us)

commit v3 on v2

v3 whole, which is shorter than its diff:
```python
import functools
import math

import jax
import jax.numpy as jnp
from jax import lax
from jax.experimental import pallas as pl
from jax.experimental.pallas import tpu as pltpu
from jax.sharding import PartitionSpec as P

RADIUS = 4
PENALTY = 40.0
EXPONENT = PENALTY + math.log(5.0) / math.log(0.5)
SMOOTH = 0.001
AXES = ("gz", "gy", "gx")
F32 = jnp.float32

LAYERS = 16
PLANE = 288
SLABS = ((15, 14, 13, 6), (12, 11, 10, 9, 2), (8, 7, 5, 4, 3, 1, 0))
SLAB_ROWS = 3 * 128 + 64
CORNER_ROWS = 3 * 24 + 8


def width_of(layer):
    return RADIUS + layer


def rows_of(layer):
    return -(-width_of(layer) // 8) * 8


MICROSECONDS = {"terms_upper": 2.7, "assemble": 2.5, "section": 2.6, "smooth": 4.0, "finish": 3.0, "ends": 1.0}


def strips():
    out = []
    for slab, layers in enumerate(SLABS):
        at = 0
        for layer in layers:
            for name in ("u", "v"):
                out.append((name, layer, slab, at))
                at += width_of(layer)
        assert at <= 128
    return out


def row_places():
    places, at = {}, 0
    for layer in range(LAYERS):
        for name in ("u", "v"):
            places[name, layer] = (at, rows_of(layer))
            at += rows_of(layer)
    for layer in range(LAYERS):
        places["w", layer] = (at, 8)
        at += 8
    return places, at


ROW_PLACES, ROW_TOTAL = row_places()


def moved(value, where):
    sizes = tuple(lax.axis_size(axis) for axis in AXES)
    pairs = []
    for z in range(sizes[0]):
        for y in range(sizes[1]):
            for x in range(sizes[2]):
                to = where(z, y, x)
                if to is not None and all(0 <= t < n for t, n in zip(to, sizes)):
                    pairs.append(((z * sizes[1] + y) * sizes[2] + x, (to[0] * sizes[1] + to[1]) * sizes[2] + to[2]))
    return lax.ppermute(value, AXES, pairs)


def shape(*dims):
    return jax.ShapeDtypeStruct(dims, F32)


def call(kernel, outs, *args, scratch=(), in_specs=None, **params):
    name = kernel.func.__name__ if isinstance(kernel, functools.partial) else kernel.__name__
    more = {} if in_specs is None else {"in_specs": in_specs}
    return pl.pallas_call(
        kernel,
        out_shape=outs,
        scratch_shapes=list(scratch),
        compiler_params=pltpu.CompilerParams(vmem_limit_bytes=40 * 1024 * 1024),
        cost_estimate=pl.CostEstimate(flops=0, bytes_accessed=int(MICROSECONDS.get(name, 0.5) * 3e6), transcendentals=0),
        name=name,
        **more,
    )(*args)


def lanes(rows):
    return lax.broadcasted_iota(jnp.int32, (rows, 128), 1)


def core():
    return lax.axis_index("gy") & 1


def seam():
    return lax.axis_index("gy") >> 1


def aligned(value, to):
    return pl.multiple_of(value, to)


def power40(p):
    x = p + p
    x2 = x * x
    x4 = x2 * x2
    x8 = x4 * x4
    x32 = x8 * x8
    x32 = x32 * x32
    return x32 * x8


def power39(p):
    x = p + p
    x2 = x * x
    x4 = x2 * x2
    x8 = x4 * x4
    x32 = x8 * x8
    x32 = x32 * x32
    return x32 * (x4 * (x2 * x))


def edges(p_ref, inner_ref, outer_ref, left_ref, right_ref, turned):
    lane = lanes(128)
    c = core()
    packed = jnp.zeros((128, 128), F32)
    for layer in range(LAYERS):
        inner_ref[pl.ds(layer, 1), :] = p_ref[layer, pl.ds(127 * (1 - c), 1), :]
        outer_ref[pl.ds(layer, 1), :] = p_ref[layer, pl.ds(127 * c, 1), :]
        rolled = pltpu.roll(p_ref[layer], 2 * layer + 1, 1)
        packed = jnp.where((lane >> 1) == layer, rolled, packed)
    turned[...] = packed.T
    right_ref[...] = turned[pl.ds(0, 16, stride=2), :]
    left_ref[...] = turned[pl.ds(1, 16, stride=2), :]


def norm_of(position, extent):
    def missing(k):
        k = jnp.maximum(k, 0)
        return (k * (k + 1)) >> 1

    return ((RADIUS + 1) ** 2 - missing(RADIUS - position) - missing(RADIUS - (extent - 1 - position))).astype(F32)


def terms(total, density, sens, p39):
    total = jnp.maximum(total, 1e-30)
    offset = PENALTY * math.log(2.0) / EXPONENT
    smax = jnp.exp(jnp.log(total) * (1.0 / EXPONENT) - offset)
    gap = density - smax
    half = 0.5 * gap * lax.rsqrt(gap * gap + SMOOTH)
    low = 0.5 - half
    top = (0.5 + half) * (2.0 * PENALTY / EXPONENT) * smax
    h = top / total
    return h * sens, h * p39, low, total / top


def plane_norms(sizes):
    row0 = lax.axis_index("gy") * 128
    col0 = lax.axis_index("gx") * 128
    rows = lax.broadcasted_iota(jnp.int32, (128, 128), 0) + row0
    cols = lax.broadcasted_iota(jnp.int32, (128, 128), 1) + col0
    return norm_of(rows, sizes[1] * 128) * norm_of(cols, sizes[2] * 128)


def neighbours(p, layer, inner_ref, outer_ref, beside, powers):
    c = core()
    lane = lanes(128)
    own = power40(p)
    powers[pl.ds(8, 128), :] = own
    powers[pl.ds(7 + 129 * (1 - c), 1), :] = power40(inner_ref[pl.ds(layer, 1), :])
    powers[pl.ds(7 + 129 * c, 1), :] = power40(outer_ref[pl.ds(layer, 1), :])
    side = pltpu.roll(beside, (128 - (2 * layer + 1)) % 128, 1)
    right = jnp.where(lane == 127, side, pltpu.roll(own, 127, 1))
    left = jnp.where(lane == 0, side, pltpu.roll(own, 1, 1))
    return (own + right) + left + (powers[pl.ds(7, 128), :] + powers[pl.ds(9, 128), :])


def columns_beside(left_ref, right_ref, turned):
    turned[...] = jnp.zeros((128, 128), F32)
    turned[pl.ds(0, 16, stride=2), :] = right_ref[...]
    turned[pl.ds(1, 16, stride=2), :] = left_ref[...]
    return power40(turned[...].T)


def reach(p_ref, inner_ref, outer_ref, left_ref, right_ref, total_ref, powers, turned):
    beside = columns_beside(left_ref, right_ref, turned)
    total_ref[...] = neighbours(p_ref[LAYERS - 1], LAYERS - 1, inner_ref, outer_ref, beside, powers)


def terms_upper(sizes, p_ref, f_ref, s_ref, inner_ref, outer_ref, left_ref, right_ref, uvw_ref, powers, turned):
    beside = columns_beside(left_ref, right_ref, turned)
    norms = 1.0 / plane_norms(sizes)
    layer0 = lax.axis_index("gz") * LAYERS
    for layer in range(1, LAYERS):
        total = neighbours(p_ref[layer - 1], layer - 1, inner_ref, outer_ref, beside, powers)
        u, v, low, inverse = terms(total, f_ref[layer], s_ref[layer], power39(p_ref[layer]))
        norm_z = norm_of(layer0 + layer, sizes[0] * LAYERS)
        uvw_ref[layer - 1] = u
        uvw_ref[14 + layer] = v
        uvw_ref[29 + layer] = low * inverse * (norms * (1.0 / norm_z))


def terms_lowest(sizes, p_ref, f_ref, s_ref, total_ref, uvw_ref):
    norms = 1.0 / plane_norms(sizes)
    layer0 = lax.axis_index("gz") * LAYERS
    p39 = power39(p_ref[0])
    s = s_ref[0]
    u, v, low, inverse = terms(total_ref[...], f_ref[0], s, p39)
    ground = layer0 == 0
    norm_z = norm_of(layer0, sizes[0] * LAYERS)
    uvw_ref[0] = jnp.where(ground, s, u)
    uvw_ref[1] = jnp.where(ground, p39, v)
    uvw_ref[2] = jnp.where(ground, 1.0, low * inverse) * (norms * (1.0 / norm_z))


def plane_of(upper_ref, low_ref, name, layer):
    kind = "uvw".index(name)
    if layer == 0:
        return low_ref.at[kind]
    return upper_ref.at[15 * kind + layer - 1]


def pack(upper_ref, low_ref, same_ref, cross_ref, corner_left_ref, corner_right_ref):
    c = core()
    lane = lanes(128)
    zero = jnp.zeros((128, 128), F32)

    def put(at, count, corner_at, corner_rows, left, right):
        same_ref[pl.ds(at, count), :] = jnp.where(c == 0, right, left)
        cross_ref[pl.ds(at, count), :] = jnp.where(c == 0, left, right)
        here = pl.ds(corner_at, corner_rows)
        first, last = slice(0, corner_rows), slice(count - corner_rows, count)
        corner_left_ref[here, :] = jnp.where(c == 0, left[first], left[last])
        corner_right_ref[here, :] = jnp.where(c == 0, right[first], right[last])

    for slab in range(3):
        left, right = zero, zero
        for name, layer, where, at in strips():
            if where != slab:
                continue
            width = width_of(layer)
            plane = plane_of(upper_ref, low_ref, name, layer)[...]
            inside = (lane >= at) & (lane < at + width)
            left = jnp.where(inside, pltpu.roll(plane, at, 1) if at else plane, left)
            right = jnp.where(inside, pltpu.roll(plane, (at + width) % 128, 1), right)
        put(128 * slab, 128, 24 * slab, 24, left, right)
    lane = lanes(64)
    left, right = zero[:64], zero[:64]
    for layer in range(LAYERS):
        ref = plane_of(upper_ref, low_ref, "w", layer)
        for half in range(2):
            plane = ref[pl.ds(64 * half, 64), :]
            at = 64 * half + RADIUS * layer
            inside = (lane >= at) & (lane < at + RADIUS)
            left = jnp.where(inside, pltpu.roll(plane, at, 1) if at else plane, left)
            right = jnp.where(inside, pltpu.roll(plane, (at + RADIUS) % 128, 1), right)
    put(384, 64, 72, 8, left, right)


def pack_rows(upper_ref, low_ref, rows_ref):
    c = core()
    for (name, layer), (at, rows) in ROW_PLACES.items():
        start = aligned(c * (128 - rows), 8)
        rows_ref[pl.ds(at, rows), :] = plane_of(upper_ref, low_ref, name, layer)[pl.ds(start, rows), :]


def row_halo(got_ref, shared_ref, at, rows):
    across = (core() ^ seam()) == 1
    return jnp.where(across, got_ref[pl.ds(at, rows), :], shared_ref[pl.ds(at, rows), :])


def place(target, index, at, count, value, halo, lane_at, width):
    c = core()
    lane = lanes(count)
    halo = pltpu.roll(halo, (128 - lane_at - (1 - c) * width) & 127, 1)
    begin = (1 - c) * (128 - width)
    outer = (lane >= begin) & (lane < begin + width)
    target[index, pl.ds(at, count), :] = jnp.where(outer, halo, value)


def place_rows(target, index, key, got_ref, shared_ref, corner, lane_at, width):
    start, rows = ROW_PLACES[key]
    to = aligned(256 + seam() * (32 - rows), 8)
    target[index, pl.ds(256, 32), :] = jnp.zeros((32, 128), F32)
    place(target, index, to, rows, row_halo(got_ref, shared_ref, start, rows), corner(rows), lane_at, width)


def assemble(
    upper_ref, low_ref, upper_other_ref, low_other_ref, got_ref, shared_ref, same_ref, cross_ref,
    corner_left_ref, corner_right_ref, uv_ref,
):
    c = core()
    own_at = aligned(c * 128, 128)
    other_at = aligned((1 - c) * 128, 128)
    for name, layer, slab, at in strips():
        width = width_of(layer)
        index = 2 * (LAYERS - 1 - layer) + (name == "v")
        here = pl.ds(128 * slab, 128)
        own = plane_of(upper_ref, low_ref, name, layer)[...]
        other = plane_of(upper_other_ref, low_other_ref, name, layer)[...]
        place(uv_ref, index, own_at, 128, own, same_ref[here, :], at, width)
        place(uv_ref, index, other_at, 128, other, cross_ref[here, :], at, width)

        def corner(rows):
            here = pl.ds(aligned(24 * slab + seam() * (24 - rows), 8), rows)
            return jnp.where(c == 0, corner_right_ref[here, :], corner_left_ref[here, :])

        place_rows(uv_ref, index, (name, layer), got_ref, shared_ref, corner, at, width)


def assemble_w(
    upper_ref, low_ref, upper_other_ref, low_other_ref, got_ref, shared_ref, same_ref, cross_ref,
    corner_left_ref, corner_right_ref, w_ref,
):
    c = core()
    own_at = aligned(c * 128, 128)
    other_at = aligned((1 - c) * 128, 128)
    slab = pl.ds(384, 64)

    def corner(rows):
        here = pl.ds(72, rows)
        return jnp.where(c == 0, corner_right_ref[here, :], corner_left_ref[here, :])

    for layer in range(LAYERS):
        own = plane_of(upper_ref, low_ref, "w", layer)
        other = plane_of(upper_other_ref, low_other_ref, "w", layer)
        for half in range(2):
            rows = pl.ds(64 * half, 64)
            at = 64 * half + RADIUS * layer
            place(w_ref, layer, aligned(own_at + 64 * half, 64), 64, own[rows, :], same_ref[slab, :], at, RADIUS)
            place(w_ref, layer, aligned(other_at + 64 * half, 64), 64, other[rows, :], cross_ref[slab, :], at, RADIUS)
        place_rows(
            w_ref, layer, ("w", layer), got_ref, shared_ref, corner, RADIUS * layer + 64 * seam(), RADIUS
        )


def five(value):
    return (value + pltpu.roll(value, 1, 1)) + pltpu.roll(value, 127, 1) + (
        pltpu.roll(value, 1, 0) + pltpu.roll(value, PLANE - 1, 0)
    )


def set_carry(carry, main_ref, other_ref, outer_ref, halo_ref, halo_other_ref, halo_outer_ref):
    c = core()
    lane = lanes(64)
    mine = (lane >> 6) == c
    for i in range(4):
        rows = pl.ds(64 * (i % 2), 64)
        own, other = main_ref[rows, :], other_ref[rows, :]
        if i < 2:
            value = jnp.where(mine, own, other)
        else:
            value = pltpu.roll(jnp.where(mine, other, own), 64, 1)
        outer = pltpu.roll(outer_ref[...], (128 - 32 * i) % 128, 1) if i else outer_ref[...]
        begin = (1 - c) * 108
        value = jnp.where((lane >= begin) & (lane < begin + 20), outer, value)
        carry[pl.ds(64 * i, 64), :] = value
    lane = lanes(24)
    value = jnp.where((lane >> 6) == c, halo_ref[...], halo_other_ref[...])
    begin = (1 - c) * 108
    value = jnp.where((lane >= begin) & (lane < begin + 20), halo_outer_ref[...], value)
    carry[pl.ds(256, 32), :] = jnp.zeros((32, 128), F32)
    carry[pl.ds(aligned(256 + 8 * seam(), 8), 24), :] = value


def section(active, *refs):
    uv_ref, refs = refs[0], refs[1:]
    pieces, before_ref = (), None
    if active is not None and len(refs) > 5:
        pieces, before_ref, refs = refs[:6], refs[6], refs[7:]
    if len(refs) == 5:
        layers_ref, main_ref, outer_ref, halo_ref, carry = refs
    else:
        layers_ref, carry = refs
        main_ref = None

    @pl.when(lax.axis_index("gz") == active)
    def _():
        if pieces:
            set_carry(carry, *pieces)
            value = carry[...]
        else:
            value = jnp.zeros((PLANE, 128), F32)

        def step(i, value):
            value = uv_ref[2 * i] + uv_ref[2 * i + 1] * five(value)
            layers_ref[LAYERS - 1 - i] = value
            return value

        lax.fori_loop(0, LAYERS, step, value)
        if main_ref is None:
            return
        c = core()
        lane = lanes(128)
        bottom = layers_ref.at[0]
        mine = (lane >> 6) == c
        main_ref[...] = jnp.where(mine, bottom[pl.ds(0, 128), :], pltpu.roll(bottom[pl.ds(128, 128), :], 64, 1))
        lane = lanes(64)
        slab = jnp.zeros((64, 128), F32)
        for i in range(4):
            rolled = bottom[pl.ds(64 * i, 64), :]
            rolled = pltpu.roll(rolled, 32 * i, 1) if i else rolled
            begin = (32 * i + 128 - c * 32) & 127
            slab = jnp.where(((lane - begin) & 127) < 32, rolled, slab)
        outer_ref[...] = slab
        halo_ref[...] = bottom[pl.ds(aligned((1 - seam()) * 232, 8), 24), :]

    if before_ref is not None:
        @pl.when(lax.axis_index("gz") != active)
        def _():
            layers_ref[...] = before_ref[...]


def tent(value, turn):
    for _ in range(2):
        two = value + turn(value, 1)
        value = (two + turn(two, 2)) + turn(value, 4)
    return value


def smooth(layers_ref, w_ref, out_ref, give_ref, weighted):
    mine = (lanes(128) >> 6) == core()

    def layer(k, _):
        weighted[pl.ds(8, PLANE), :] = layers_ref[k] * w_ref[k]
        weighted[pl.ds(0, 8), :] = weighted[pl.ds(PLANE, 8), :]
        halves = []
        for half in range(2):
            start = 8 + 128 * half
            total = weighted[pl.ds(start, 128), :] * 5.0
            for offset in range(1, RADIUS + 1):
                total = total + (
                    weighted[pl.ds(start - offset, 128), :] + weighted[pl.ds(start + offset, 128), :]
                ) * (5.0 - offset)
            value = tent(total, lambda x, i: pltpu.roll(x, i, 1))
            halves.append(pltpu.roll(value, 124, 1))
        out_ref[k] = jnp.where(mine, halves[0], pltpu.roll(halves[1], 64, 1))
        return 0

    lax.fori_loop(0, LAYERS, layer, 0)
    give(out_ref, give_ref)


def give(from_ref, to_ref):
    count = to_ref.shape[0]
    low = (lanes(128) >> 6) == 0
    for k in range(count):
        to_ref[k] = jnp.where(low, pltpu.roll(from_ref[k + count], 64, 1), from_ref[k])


def merge(keep_ref, got_ref, out_ref):
    c = core()
    count = keep_ref.shape[0] // 2
    mine = (lanes(128) >> 6) == c
    for k in range(2 * count):
        own, other = keep_ref[k], got_ref[k % count]
        own = pltpu.roll(own, 64 * c, 1)
        other = pltpu.roll(other, 64 * c if k < count else 64 * (1 - c), 1)
        out_ref[k] = jnp.where(mine, own, other)


def ends(keep_ref, got_ref, out_ref, top_ref, bottom_ref):
    merge(keep_ref, got_ref, out_ref)
    top_ref[...] = out_ref[pl.ds(LAYERS - RADIUS, RADIUS)]
    bottom_ref[...] = out_ref[pl.ds(0, RADIUS)]


def finish(tile_ref, below_ref, above_ref, passive_ref, out_ref):
    def layer(k):
        if k < 0:
            return below_ref[k + RADIUS]
        if k >= LAYERS:
            return above_ref[k - LAYERS]
        return tile_ref[k]

    for k in range(LAYERS):
        total = layer(k) * 5.0
        for offset in range(1, RADIUS + 1):
            total = total + (layer(k - offset) + layer(k + offset)) * (5.0 - offset)
        out_ref[k] = jnp.where(passive_ref[k] > 0, 0.0, total)


def to_other(value):
    return moved(value, lambda z, y, x: (z, y ^ 1, x))


def after(value, *others):
    return lax.optimization_barrier((value,) + others)[0]


def per_device(filtered, printed, sensitivity, passive):
    sizes = tuple(lax.axis_size(axis) for axis in AXES)
    depth = sizes[0]
    plane = shape(128, 128)
    edge = shape(16, 128)
    inner, outer, left, right = call(edges, [edge] * 4, printed, scratch=[pltpu.VMEM((128, 128), F32)])

    def across(z, y, x):
        return (z, y ^ 3, x) if y in (1, 2) else None

    def beside(z, y, x):
        return (z, y ^ 1, x + (1 if y & 1 else -1))

    def same(z, y, x):
        return (z, y, x + (-1 if y & 1 else 1))

    outer = moved(outer, across)
    from_left = moved(right, lambda z, y, x: (z, y, x + 1))
    from_right = moved(left, lambda z, y, x: (z, y, x - 1))
    inner = to_other(inner)
    near = (inner, outer, from_left, from_right)
    work = [pltpu.VMEM((144, 128), F32), pltpu.VMEM((128, 128), F32)]
    above = call(reach, plane, printed, *near, scratch=work)
    total0 = moved(above, lambda z, y, x: (z + 1, y, x))
    upper = call(
        functools.partial(terms_upper, sizes), shape(45, 128, 128),
        after(printed, above), filtered, sensitivity, *near, scratch=work,
    )
    low = call(functools.partial(terms_lowest, sizes), shape(3, 128, 128), printed, filtered, sensitivity, total0)
    slab = shape(SLAB_ROWS, 128)
    corner = shape(CORNER_ROWS, 128)
    rows = call(pack_rows, shape(ROW_TOTAL, 128), upper, low)
    got = moved(rows, across)
    to_same, to_cross, corner_left, corner_right = call(pack, [slab, slab, corner, corner], after(upper, rows), low)
    from_same = moved(to_same, same)
    from_cross = moved(to_cross, beside)
    corner_right = moved(corner_right, lambda z, y, x: (z, 2 * (2 - y), x + 1) if y in (1, 2) else None)
    corner_left = moved(corner_left, lambda z, y, x: (z, 5 - 2 * y, x - 1) if y in (1, 2) else None)
    got = after(got, from_same, from_cross, corner_left, corner_right)
    shared = moved(got, lambda z, y, x: (z, y ^ 1, x) if y in (1, 2) else None)
    upper_other, low_other = to_other(upper), to_other(low)
    parts = (upper, low, upper_other, low_other, got, shared, from_same, from_cross, corner_left, corner_right)
    uvs = call(assemble, shape(2 * LAYERS, PLANE, 128), *parts)
    ws = None
    pieces, before = (), ()
    stack = shape(LAYERS, PLANE, 128)
    for active in range(depth - 1, -1, -1):
        outs = [stack]
        if active > 0:
            outs = outs + [plane, shape(64, 128), shape(24, 128)]
        layers, *sent = call(
            functools.partial(section, active), outs, uvs, *pieces, *before, scratch=[pltpu.VMEM((PLANE, 128), F32)]
        )
        before = (layers,)
        if active > 0:
            main, side, strip = sent

            def down(where):
                def to(z, y, x):
                    _, ty, tx = where(z, y, x)
                    return (z - 1, ty, tx) if z == active else None
                return to

            def over(z, y, x):
                return (z, y ^ 2, x)

            def corner_of(z, y, x):
                _, ty, tx = beside(z, y, x)
                return (z, ty ^ 2, tx)

            def sibling(z, y, x):
                return (z, y ^ 1, x) if z == active - 1 else None

            main = moved(main, down(lambda z, y, x: (z, y, x)))
            halo = moved(strip, down(over))
            side = moved(side, down(beside))
            edge_piece = moved(strip, down(corner_of))
            main, halo, side, edge_piece = lax.optimization_barrier((main, halo, side, edge_piece))
            pieces = (main, moved(main, sibling), side, halo, moved(halo, sibling), edge_piece)
            if ws is None:
                ws = call(assemble_w, stack, after(upper, side), *parts[1:])
    kept, given = call(
        smooth,
        [shape(LAYERS, 128, 128), shape(LAYERS // 2, 128, 128)],
        layers, ws,
        scratch=[pltpu.VMEM((PLANE + 8, 128), F32)],
    )
    given = to_other(given)
    quarter = shape(RADIUS, 128, 128)
    tile, top, bottom = call(ends, [shape(LAYERS, 128, 128), quarter, quarter], kept, given)
    below = moved(top, lambda z, y, x: (z + 1, y, x))
    over = moved(bottom, lambda z, y, x: (z - 1, y, x))
    return call(finish, shape(LAYERS, 128, 128), tile, below, over, passive)


def solution(mesh):
    spec = P(*AXES)
    return jax.shard_map(
        per_device, mesh=mesh, in_specs=(spec,) * 4, out_specs=spec, check_vma=False
    )
```

time: 232 us -> 139 us (0.60)
  the two profiles are of different devices: /device:TPU:47 before, /device:TPU:38 now
where the time goes in v3:
time: 139 us; the launch traced here: 138 us
  waiting for transfers between devices  61.2 us (44%)
  starting transfers between devices  54.4 us (39%)
  Pallas kernels  19.5 us (14%)
  local copies, waits for them, and re-layouts  2.67 us (2%)
    ppermute x34, waiting for transfers between devices, moved(): return lax.ppermute(value, AXES, pairs)  61.2 us
    ppermute x34, starting transfers between devices, moved(): return lax.ppermute(value, AXES, pairs)  54.4 us
    pallas_call x15, Pallas kernels, call(): pl.pallas_call(kernel, out_shape=outs, scratch_shapes=list(scratch), comp...  19.5 us
  transfers between devices with their start and end apart: 34, of which 10 were waited for; matrix products, arithmetic and copies ran while one was open for 0% of the time, Pallas kernels for 2%

profile of v3, /device:TPU:38, one launch (start us, length us, event | category | flops | bytes accessed | tf_op | source)
XLA Modules:
  0.0 138.3 jit_solution(1697472927878657011)
XLA Ops:
  1.7 2.1 %collective-permute-start.1 = (f32[16,128]{1,0:T(8,128)S(1)}, f32[16,128]{1,0:T(8,128)S(1)}, u32[]{:S(2)}, u32[]{:S(2)}) collective-permute-start(f32[16,128]{1,0:T(8,128)S(1)} %get-tuple-element.47), channel_id=1, source_target_pairs={{16,32},{17,33},{18,34},{19,35},{20,36},{21,37},{22,38},{23,39},{2... | collective-permute-start | bytes 24584 | tf_op jit(solution)/shard_map/ppermute | solution.py:72
  3.8 5.2 %collective-permute-start.2 = (f32[16,128]{1,0:T(8,128)S(1)}, f32[16,128]{1,0:T(8,128)S(1)}, u32[]{:S(2)}, u32[]{:S(2)}) collective-permute-start(f32[16,128]{1,0:T(8,128)S(1)} %get-tuple-element.48), channel_id=1, source_target_pairs={{0,1},{1,2},{2,3},{3,4},{4,5},{5,6},{6,7},{7,8},{8,9},{9,10},{10,1... | collective-permute-start | bytes 24584 | tf_op jit(solution)/shard_map/ppermute | solution.py:72
  9.0 5.2 %collective-permute-start.3 = (f32[16,128]{1,0:T(8,128)S(1)}, f32[16,128]{1,0:T(8,128)S(1)}, u32[]{:S(2)}, u32[]{:S(2)}) collective-permute-start(f32[16,128]{1,0:T(8,128)S(1)} %get-tuple-element.49), channel_id=1, source_target_pairs={{1,0},{2,1},{3,2},{4,3},{5,4},{6,5},{7,6},{8,7},{9,8},{10,9},{11,1... | collective-permute-start | bytes 24584 | tf_op jit(solution)/shard_map/ppermute | solution.py:72
  14.3 2.8 %collective-permute-done.3.right_ref = f32[16,128]{1,0:T(8,128)S(1)} collective-permute-done((f32[16,128]{1,0:T(8,128)S(1)}, f32[16,128]{1,0:T(8,128)S(1)}, u32[]{:S(2)}, u32[]{:S(2)}) %collective-permute-start.3) | collective-permute-done | bytes 8224 | tf_op jit(solution)/shard_map/ppermute | solution.py:72
  17.2 1.8 %terms_upper.1.upper_ref = f32[45,128,128]{2,1,0:T(8,128)S(1)} custom-call(f32[16,128,128]{2,1,0:T(8,128)S(1)} %copy-done, f32[16,128,128]{2,1,0:T(8,128)S(1)} %copy-done.1, f32[16,128,128]{2,1,0:T(8,128)S(1)} %copy-done.2, f32[16,128]{1,0:T(8,128)S(1)} %collective-permute-done.inner_ref, f32[16,128]{1,0:T(8,128)S(1)} %collective-permute-done.1.outer_ref, ...), custom_call_target="tpu_custom_call" | custom-call | bytes 8100000 | tf_op jit(solution)/shard_map/terms_upper/pallas_call | solution.py:82
  19.2 3.5 %collective-permute-start.4 = (f32[128,128]{1,0:T(8,128)S(1)}, f32[128,128]{1,0:T(8,128)S(1)}, u32[]{:S(2)}, u32[]{:S(2)}) collective-permute-start(f32[128,128]{1,0:T(8,128)S(1)} %reach.1), channel_id=1, source_target_pairs={{0,64},{1,65},{2,66},{3,67},{4,68},{5,69},{6,70},{7,71},{8,72},{9,... | collective-permute-start | bytes 196616 | tf_op jit(solution)/shard_map/ppermute | solution.py:72
  22.7 2.0 %collective-permute-done.4.total_ref = f32[128,128]{1,0:T(8,128)S(1)} collective-permute-done((f32[128,128]{1,0:T(8,128)S(1)}, f32[128,128]{1,0:T(8,128)S(1)}, u32[]{:S(2)}, u32[]{:S(2)}) %collective-permute-start.4) | collective-permute-done | bytes 65568 | tf_op jit(solution)/shard_map/ppermute | solution.py:72
  24.9 1.9 %collective-permute-start.7 = (f32[608,128]{1,0:T(8,128)S(1)}, f32[608,128]{1,0:T(8,128)S(1)}, u32[]{:S(2)}, u32[]{:S(2)}) collective-permute-start(f32[608,128]{1,0:T(8,128)S(1)} %pack_rows.1), channel_id=1, source_target_pairs={{16,32},{17,33},{18,34},{19,35},{20,36},{21,37},{22,38},{23,39},{2... | collective-permute-start | bytes 933896 | tf_op jit(solution)/shard_map/ppermute | solution.py:72
  26.8 1.6 %pack.1 = (f32[448,128]{1,0:T(8,128)S(1)}, f32[448,128]{1,0:T(8,128)S(1)}, f32[80,128]{1,0:T(8,128)S(1)}, f32[80,128]{1,0:T(8,128)S(1)}) custom-call(f32[45,128,128]{2,1,0:T(8,128)S(1)} %terms_upper.1.upper_ref, f32[3,128,128]{2,1,0:T(8,128)S(1)} %terms_lowest.1.low_ref), custom_call_target="tpu_custom_call" | custom-call | bytes 1500000 | tf_op jit(solution)/shard_map/pack/pallas_call | solution.py:82
  28.4 6.0 %collective-permute-start.8 = (f32[448,128]{1,0:T(8,128)S(1)}, f32[448,128]{1,0:T(8,128)S(1)}, u32[]{:S(2)}, u32[]{:S(2)}) collective-permute-start(f32[448,128]{1,0:T(8,128)S(1)} %get-tuple-element.52), channel_id=1, source_target_pairs={{0,1},{1,2},{2,3},{3,4},{4,5},{5,6},{6,7},{7,8},{8,9},{9,10},{10,1... | collective-permute-start | bytes 688136 | tf_op jit(solution)/shard_map/ppermute | solution.py:72
  34.4 1.9 %collective-permute-start.9 = (f32[448,128]{1,0:T(8,128)S(1)}, f32[448,128]{1,0:T(8,128)S(1)}, u32[]{:S(2)}, u32[]{:S(2)}) collective-permute-start(f32[448,128]{1,0:T(8,128)S(1)} %get-tuple-element.53), channel_id=1, source_target_pairs={{1,16},{2,17},{3,18},{4,19},{5,20},{6,21},{7,22},{8,23},{9,24},{10... | collective-permute-start | bytes 688136 | tf_op jit(solution)/shard_map/ppermute | solution.py:72
  36.4 4.5 %collective-permute-start.10 = (f32[80,128]{1,0:T(8,128)S(1)}, f32[80,128]{1,0:T(8,128)S(1)}, u32[]{:S(2)}, u32[]{:S(2)}) collective-permute-start(f32[80,128]{1,0:T(8,128)S(1)} %get-tuple-element.54), channel_id=1, source_target_pairs={{17,48},{18,49},{19,50},{20,51},{21,52},{22,53},{23,54},{24,55},{2... | collective-permute-start | bytes 122888 | tf_op jit(solution)/shard_map/ppermute | solution.py:72
  40.8 4.0 %collective-permute-done.10.corner_left_ref = f32[80,128]{1,0:T(8,128)S(1)} collective-permute-done((f32[80,128]{1,0:T(8,128)S(1)}, f32[80,128]{1,0:T(8,128)S(1)}, u32[]{:S(2)}, u32[]{:S(2)}) %collective-permute-start.10) | collective-permute-done | bytes 40992 | tf_op jit(solution)/shard_map/ppermute | solution.py:72
  44.8 1.9 %collective-permute-start.11 = (f32[80,128]{1,0:T(8,128)S(1)}, f32[80,128]{1,0:T(8,128)S(1)}, u32[]{:S(2)}, u32[]{:S(2)}) collective-permute-start(f32[80,128]{1,0:T(8,128)S(1)} %get-tuple-element.55), channel_id=1, source_target_pairs={{16,33},{17,34},{18,35},{19,36},{20,37},{21,38},{22,39},{23,40},{2... | collective-permute-start | bytes 122888 | tf_op jit(solution)/shard_map/ppermute | solution.py:72
  46.7 7.3 %collective-permute-done.11.corner_right_ref = f32[80,128]{1,0:T(8,128)S(1)} collective-permute-done((f32[80,128]{1,0:T(8,128)S(1)}, f32[80,128]{1,0:T(8,128)S(1)}, u32[]{:S(2)}, u32[]{:S(2)}) %collective-permute-start.11) | collective-permute-done | bytes 40992 | tf_op jit(solution)/shard_map/ppermute | solution.py:72
  73.5 32.8 %collective-permute-done.28.refs_6_ = f32[24,128]{1,0:T(8,128)S(1)} collective-permute-done((f32[24,128]{1,0:T(8,128)S(1)}, f32[24,128]{1,0:T(8,128)S(1)}, u32[]{:S(2)}, u32[]{:S(2)}) %collective-permute-start.28) | collective-permute-done | bytes 12320 | tf_op jit(solution)/shard_map/ppermute | solution.py:72
  106.3 1.9 %collective-permute-start.29 = (f32[128,128]{1,0:T(8,128)S(1)}, f32[128,128]{1,0:T(8,128)S(1)}, u32[]{:S(2)}, u32[]{:S(2)}) collective-permute-start(f32[128,128]{1,0:T(8,128)S(1)} %collective-permute-done.25.refs_1_), channel_id=1, source_target_pairs={{0,16},{1,17},{2,18},{3,19},{4,20},{5,21},{6,22},{7,23},{8,24},{9,... | collective-permute-start | bytes 196616 | tf_op jit(solution)/shard_map/ppermute | solution.py:72
  108.2 2.4 %collective-permute-start.30 = (f32[24,128]{1,0:T(8,128)S(1)}, f32[24,128]{1,0:T(8,128)S(1)}, u32[]{:S(2)}, u32[]{:S(2)}) collective-permute-start(f32[24,128]{1,0:T(8,128)S(1)} %collective-permute-done.26.refs_4_), channel_id=1, source_target_pairs={{0,16},{1,17},{2,18},{3,19},{4,20},{5,21},{6,22},{7,23},{8,24},{9,... | collective-permute-start | bytes 36872 | tf_op jit(solution)/shard_map/ppermute | solution.py:72
  111.4 2.5 %section.7.layers_ref = f32[16,288,128]{2,1,0:T(8,128)S(1)} custom-call(f32[32,288,128]{2,1,0:T(8,128)S(1)} %assemble.1.refs_0_, f32[128,128]{1,0:T(8,128)S(1)} %collective-permute-done.25.refs_1_, f32[128,128]{1,0:T(8,128)S(1)} %collective-permute-done.29.refs_2_, f32[64,128]{1,0:T(8,128)S(1)} %collective-permute-done.27.refs_3_, ...), custom_call_target="tpu_custom_call" | custom-call | bytes 7800000 | tf_op jit(solution)/shard_map/section/pallas_call | solution.py:82
  113.9 8.6 %smooth.1 = (f32[16,128,128]{2,1,0:T(8,128)S(1)}, f32[8,128,128]{2,1,0:T(8,128)S(1)}) custom-call(f32[16,288,128]{2,1,0:T(8,128)S(1)} %section.7.layers_ref, f32[16,288,128]{2,1,0:T(8,128)S(1)} %assemble_w.1.w_ref), custom_call_target="tpu_custom_call" | custom-call | bytes 12000000 | tf_op jit(solution)/shard_map/smooth/pallas_call | solution.py:82
  122.9 1.6 %collective-permute-done.31.got_ref = f32[8,128,128]{2,1,0:T(8,128)S(1)} collective-permute-done((f32[8,128,128]{2,1,0:T(8,128)S(1)}, f32[8,128,128]{2,1,0:T(8,128)S(1)}, u32[]{:S(2)}, u32[]{:S(2)}) %collective-permute-start.31) | collective-permute-done | bytes 524320 | tf_op jit(solution)/shard_map/ppermute | solution.py:72
  127.7 5.0 %collective-permute-done.32.below_ref = f32[4,128,128]{2,1,0:T(8,128)S(1)} collective-permute-done((f32[4,128,128]{2,1,0:T(8,128)S(1)}, f32[4,128,128]{2,1,0:T(8,128)S(1)}, u32[]{:S(2)}, u32[]{:S(2)}) %collective-permute-start.32) | collective-permute-done | bytes 262176 | tf_op jit(solution)/shard_map/ppermute | solution.py:72
  132.7 4.1 %collective-permute-done.33.above_ref = f32[4,128,128]{2,1,0:T(8,128)S(1)} collective-permute-done((f32[4,128,128]{2,1,0:T(8,128)S(1)}, f32[4,128,128]{2,1,0:T(8,128)S(1)}, u32[]{:S(2)}, u32[]{:S(2)}) %collective-permute-start.33) | collective-permute-done | bytes 262176 | tf_op jit(solution)/shard_map/ppermute | solution.py:72
  136.9 1.5 %finish.1 = f32[16,128,128]{2,1,0:T(8,128)} custom-call(f32[16,128,128]{2,1,0:T(8,128)S(1)} %get-tuple-element.84.tile_ref, f32[4,128,128]{2,1,0:T(8,128)S(1)} %collective-permute-done.32.below_ref, f32[4,128,128]{2,1,0:T(8,128)S(1)} %collective-permute-done.33.above_ref, s32[16,128,128]{2,1,0:T(8,128)S(1)} %copy-done.5), custom_call_target="tpu_custom_call" | custom-call | bytes 9000000 | tf_op jit(solution)/shard_map/finish/pallas_call | solution.py:82
  (71 shorter events, 25.8 us)
Async XLA Ops:
  1.6 12.6 %collective-permute-start = (f32[16,128]{1,0:T(8,128)S(1)}, f32[16,128]{1,0:T(8,128)S(1)}, u32[]{:S(2)}, u32[]{:S(2)}) collective-permute-start(f32[16,128]{1,0:T(8,128)S(1)} %get-tuple-element.46), channel_id=1, source_target_pairs={{0,16},{1,17},{2,18},{3,19},{4,20},{5,21},{6,22},{7,23},{8,24},{9,... | collective-permute-start | bytes 24584 | tf_op jit(solution)/shard_map/ppermute | solution.py:72
  1.7 12.5 %collective-permute-start.1 = (f32[16,128]{1,0:T(8,128)S(1)}, f32[16,128]{1,0:T(8,128)S(1)}, u32[]{:S(2)}, u32[]{:S(2)}) collective-permute-start(f32[16,128]{1,0:T(8,128)S(1)} %get-tuple-element.47), channel_id=1, source_target_pairs={{16,32},{17,33},{18,34},{19,35},{20,36},{21,37},{22,38},{23,39},{2... | collective-permute-start | bytes 24584 | tf_op jit(solution)/shard_map/ppermute | solution.py:72
  3.8 10.4 %collective-permute-start.2 = (f32[16,128]{1,0:T(8,128)S(1)}, f32[16,128]{1,0:T(8,128)S(1)}, u32[]{:S(2)}, u32[]{:S(2)}) collective-permute-start(f32[16,128]{1,0:T(8,128)S(1)} %get-tuple-element.48), channel_id=1, source_target_pairs={{0,1},{1,2},{2,3},{3,4},{4,5},{5,6},{6,7},{7,8},{8,9},{9,10},{10,1... | collective-permute-start | bytes 24584 | tf_op jit(solution)/shard_map/ppermute | solution.py:72
  9.0 8.0 %collective-permute-start.3 = (f32[16,128]{1,0:T(8,128)S(1)}, f32[16,128]{1,0:T(8,128)S(1)}, u32[]{:S(2)}, u32[]{:S(2)}) collective-permute-start(f32[16,128]{1,0:T(8,128)S(1)} %get-tuple-element.49), channel_id=1, source_target_pairs={{1,0},{2,1},{3,2},{4,3},{5,4},{6,5},{7,6},{8,7},{9,8},{10,9},{11,1... | collective-permute-start | bytes 24584 | tf_op jit(solution)/shard_map/ppermute | solution.py:72
  19.1 37.8 %collective-permute-start.5 = (f32[45,128,128]{2,1,0:T(8,128)S(1)}, f32[45,128,128]{2,1,0:T(8,128)S(1)}, u32[]{:S(2)}, u32[]{:S(2)}) collective-permute-start(f32[45,128,128]{2,1,0:T(8,128)S(1)} %terms_upper.1.upper_ref), channel_id=1, source_target_pairs={{0,16},{1,17},{2,18},{3,19},{4,20},{5,21},{6,22},{7,23},{8,24},{9,... | collective-permute-start | bytes 8847368 | tf_op jit(solution)/shard_map/ppermute | solution.py:72
  19.2 5.5 %collective-permute-start.4 = (f32[128,128]{1,0:T(8,128)S(1)}, f32[128,128]{1,0:T(8,128)S(1)}, u32[]{:S(2)}, u32[]{:S(2)}) collective-permute-start(f32[128,128]{1,0:T(8,128)S(1)} %reach.1), channel_id=1, source_target_pairs={{0,64},{1,65},{2,66},{3,67},{4,68},{5,69},{6,70},{7,71},{8,72},{9,... | collective-permute-start | bytes 196616 | tf_op jit(solution)/shard_map/ppermute | solution.py:72
  24.9 29.2 %collective-permute-start.7 = (f32[608,128]{1,0:T(8,128)S(1)}, f32[608,128]{1,0:T(8,128)S(1)}, u32[]{:S(2)}, u32[]{:S(2)}) collective-permute-start(f32[608,128]{1,0:T(8,128)S(1)} %pack_rows.1), channel_id=1, source_target_pairs={{16,32},{17,33},{18,34},{19,35},{20,36},{21,37},{22,38},{23,39},{2... | collective-permute-start | bytes 933896 | tf_op jit(solution)/shard_map/ppermute | solution.py:72
  28.4 25.6 %collective-permute-start.8 = (f32[448,128]{1,0:T(8,128)S(1)}, f32[448,128]{1,0:T(8,128)S(1)}, u32[]{:S(2)}, u32[]{:S(2)}) collective-permute-start(f32[448,128]{1,0:T(8,128)S(1)} %get-tuple-element.52), channel_id=1, source_target_pairs={{0,1},{1,2},{2,3},{3,4},{4,5},{5,6},{6,7},{7,8},{8,9},{9,10},{10,1... | collective-permute-start | bytes 688136 | tf_op jit(solution)/shard_map/ppermute | solution.py:72
  34.4 19.6 %collective-permute-start.9 = (f32[448,128]{1,0:T(8,128)S(1)}, f32[448,128]{1,0:T(8,128)S(1)}, u32[]{:S(2)}, u32[]{:S(2)}) collective-permute-start(f32[448,128]{1,0:T(8,128)S(1)} %get-tuple-element.53), channel_id=1, source_target_pairs={{1,16},{2,17},{3,18},{4,19},{5,20},{6,21},{7,22},{8,23},{9,24},{10... | collective-permute-start | bytes 688136 | tf_op jit(solution)/shard_map/ppermute | solution.py:72
  36.4 8.5 %collective-permute-start.10 = (f32[80,128]{1,0:T(8,128)S(1)}, f32[80,128]{1,0:T(8,128)S(1)}, u32[]{:S(2)}, u32[]{:S(2)}) collective-permute-start(f32[80,128]{1,0:T(8,128)S(1)} %get-tuple-element.54), channel_id=1, source_target_pairs={{17,48},{18,49},{19,50},{20,51},{21,52},{22,53},{23,54},{24,55},{2... | collective-permute-start | bytes 122888 | tf_op jit(solution)/shard_map/ppermute | solution.py:72
  44.8 9.2 %collective-permute-start.11 = (f32[80,128]{1,0:T(8,128)S(1)}, f32[80,128]{1,0:T(8,128)S(1)}, u32[]{:S(2)}, u32[]{:S(2)}) collective-permute-start(f32[80,128]{1,0:T(8,128)S(1)} %get-tuple-element.55), channel_id=1, source_target_pairs={{16,33},{17,34},{18,35},{19,36},{20,37},{21,38},{22,39},{23,40},{2... | collective-permute-start | bytes 122888 | tf_op jit(solution)/shard_map/ppermute | solution.py:72
  54.1 2.8 %collective-permute-start.12 = (f32[608,128]{1,0:T(8,128)S(1)}, f32[608,128]{1,0:T(8,128)S(1)}, u32[]{:S(2)}, u32[]{:S(2)}) collective-permute-start(f32[608,128]{1,0:T(8,128)S(1)} %collective-permute-done.7.got_ref), channel_id=1, source_target_pairs={{16,0},{17,1},{18,2},{19,3},{20,4},{21,5},{22,6},{23,7},{24,8},{25... | collective-permute-start | bytes 933896 | tf_op jit(solution)/shard_map/ppermute | solution.py:72
  58.2 2.7 %collective-permute-start.13 = (f32[128,128]{1,0:T(8,128)S(1)}, f32[128,128]{1,0:T(8,128)S(1)}, u32[]{:S(2)}, u32[]{:S(2)}) collective-permute-start(f32[128,128]{1,0:T(8,128)S(1)} %get-tuple-element.57), channel_id=1, source_target_pairs={{192,128},{193,129},{194,130},{195,131},{196,132},{197,133},{198,1... | collective-permute-start | bytes 196616 | tf_op jit(solution)/shard_map/ppermute | solution.py:72
  58.8 2.0 %collective-permute-start.15 = (f32[64,128]{1,0:T(8,128)S(1)}, f32[64,128]{1,0:T(8,128)S(1)}, u32[]{:S(2)}, u32[]{:S(2)}) collective-permute-start(f32[64,128]{1,0:T(8,128)S(1)} %get-tuple-element.59), channel_id=1, source_target_pairs={{193,144},{194,145},{195,146},{196,147},{197,148},{198,149},{199,1... | collective-permute-start | bytes 98312 | tf_op jit(solution)/shard_map/ppermute | solution.py:72
  62.4 2.7 %collective-permute-start.19 = (f32[128,128]{1,0:T(8,128)S(1)}, f32[128,128]{1,0:T(8,128)S(1)}, u32[]{:S(2)}, u32[]{:S(2)}) collective-permute-start(f32[128,128]{1,0:T(8,128)S(1)} %get-tuple-element.65), channel_id=1, source_target_pairs={{128,64},{129,65},{130,66},{131,67},{132,68},{133,69},{134,70},{13... | collective-permute-start | bytes 196616 | tf_op jit(solution)/shard_map/ppermute | solution.py:72
  63.1 2.0 %collective-permute-start.21 = (f32[64,128]{1,0:T(8,128)S(1)}, f32[64,128]{1,0:T(8,128)S(1)}, u32[]{:S(2)}, u32[]{:S(2)}) collective-permute-start(f32[64,128]{1,0:T(8,128)S(1)} %get-tuple-element.67), channel_id=1, source_target_pairs={{129,80},{130,81},{131,82},{132,83},{133,84},{134,85},{135,86},{13... | collective-permute-start | bytes 98312 | tf_op jit(solution)/shard_map/ppermute | solution.py:72
  68.1 38.1 %collective-permute-start.25 = (f32[128,128]{1,0:T(8,128)S(1)}, f32[128,128]{1,0:T(8,128)S(1)}, u32[]{:S(2)}, u32[]{:S(2)}) collective-permute-start(f32[128,128]{1,0:T(8,128)S(1)} %get-tuple-element.73), channel_id=1, source_target_pairs={{64,0},{65,1},{66,2},{67,3},{68,4},{69,5},{70,6},{71,7},{72,8},{73... | collective-permute-start | bytes 196616 | tf_op jit(solution)/shard_map/ppermute | solution.py:72
  69.4 36.8 %collective-permute-start.27 = (f32[64,128]{1,0:T(8,128)S(1)}, f32[64,128]{1,0:T(8,128)S(1)}, u32[]{:S(2)}, u32[]{:S(2)}) collective-permute-start(f32[64,128]{1,0:T(8,128)S(1)} %get-tuple-element.75), channel_id=1, source_target_pairs={{65,16},{66,17},{67,18},{68,19},{69,20},{70,21},{71,22},{72,23},{7... | collective-permute-start | bytes 98312 | tf_op jit(solution)/shard_map/ppermute | solution.py:72
  70.7 35.5 %collective-permute-start.28 = (f32[24,128]{1,0:T(8,128)S(1)}, f32[24,128]{1,0:T(8,128)S(1)}, u32[]{:S(2)}, u32[]{:S(2)}) collective-permute-start(f32[24,128]{1,0:T(8,128)S(1)} %get-tuple-element.74), channel_id=1, source_target_pairs={{65,48},{66,49},{67,50},{68,51},{69,52},{70,53},{71,54},{72,55},{7... | collective-permute-start | bytes 36872 | tf_op jit(solution)/shard_map/ppermute | solution.py:72
  72.2 34.1 %collective-permute-start.26 = (f32[24,128]{1,0:T(8,128)S(1)}, f32[24,128]{1,0:T(8,128)S(1)}, u32[]{:S(2)}, u32[]{:S(2)}) collective-permute-start(f32[24,128]{1,0:T(8,128)S(1)} %get-tuple-element.74), channel_id=1, source_target_pairs={{64,32},{65,33},{66,34},{67,35},{68,36},{69,37},{70,38},{71,39},{7... | collective-permute-start | bytes 36872 | tf_op jit(solution)/shard_map/ppermute | solution.py:72
  106.3 5.2 %collective-permute-start.29 = (f32[128,128]{1,0:T(8,128)S(1)}, f32[128,128]{1,0:T(8,128)S(1)}, u32[]{:S(2)}, u32[]{:S(2)}) collective-permute-start(f32[128,128]{1,0:T(8,128)S(1)} %collective-permute-done.25.refs_1_), channel_id=1, source_target_pairs={{0,16},{1,17},{2,18},{3,19},{4,20},{5,21},{6,22},{7,23},{8,24},{9,... | collective-permute-start | bytes 196616 | tf_op jit(solution)/shard_map/ppermute | solution.py:72
  108.2 3.2 %collective-permute-start.30 = (f32[24,128]{1,0:T(8,128)S(1)}, f32[24,128]{1,0:T(8,128)S(1)}, u32[]{:S(2)}, u32[]{:S(2)}) collective-permute-start(f32[24,128]{1,0:T(8,128)S(1)} %collective-permute-done.26.refs_4_), channel_id=1, source_target_pairs={{0,16},{1,17},{2,18},{3,19},{4,20},{5,21},{6,22},{7,23},{8,24},{9,... | collective-permute-start | bytes 36872 | tf_op jit(solution)/shard_map/ppermute | solution.py:72
  125.1 7.6 %collective-permute-start.32 = (f32[4,128,128]{2,1,0:T(8,128)S(1)}, f32[4,128,128]{2,1,0:T(8,128)S(1)}, u32[]{:S(2)}, u32[]{:S(2)}) collective-permute-start(f32[4,128,128]{2,1,0:T(8,128)S(1)} %get-tuple-element.85), channel_id=1, source_target_pairs={{0,64},{1,65},{2,66},{3,67},{4,68},{5,69},{6,70},{7,71},{8,72},{9,... | collective-permute-start | bytes 786440 | tf_op jit(solution)/shard_map/ppermute | solution.py:72
  126.4 10.4 %collective-permute-start.33 = (f32[4,128,128]{2,1,0:T(8,128)S(1)}, f32[4,128,128]{2,1,0:T(8,128)S(1)}, u32[]{:S(2)}, u32[]{:S(2)}) collective-permute-start(f32[4,128,128]{2,1,0:T(8,128)S(1)} %get-tuple-element.86), channel_id=1, source_target_pairs={{64,0},{65,1},{66,2},{67,3},{68,4},{69,5},{70,6},{71,7},{72,8},{73... | collective-permute-start | bytes 786440 | tf_op jit(solution)/shard_map/ppermute | solution.py:72
  (16 other events, 110.0 us)

commit v4 on v3

v4 whole, which is shorter than its diff:
```python
import functools
import math

import jax
import jax.numpy as jnp
from jax import lax
from jax.experimental import pallas as pl
from jax.experimental.pallas import tpu as pltpu
from jax.sharding import PartitionSpec as P

RADIUS = 4
PENALTY = 40.0
EXPONENT = PENALTY + math.log(5.0) / math.log(0.5)
SMOOTH = 0.001
AXES = ("gz", "gy", "gx")
F32 = jnp.float32

LAYERS = 16
STEPS = LAYERS + 1
PLANE = 288
VECTORS = PLANE // 8
REACH = RADIUS + STEPS
SLABS = ((16, 15, 14, 3), (13, 12, 11, 8, 0), (10, 9, 7, 6, 5, 2), (4, 1))
FOLDED = 32
SLAB_ROWS = 3 * 128 + FOLDED + 64
CORNER_ROWS = 3 * 24 + 16 + 8


def width_of(layer):
    return RADIUS + layer


def rows_of(layer):
    return -(-width_of(layer) // 8) * 8


MICROSECONDS = {"all_terms": 2.5, "assemble": 2.5, "section": 2.6, "smooth": 4.0, "finish": 3.0, "ends": 1.0}


def strips():
    out = []
    for slab, layers in enumerate(SLABS):
        at = 0
        for layer in layers:
            for name in ("u", "v"):
                out.append((name, layer, slab, at))
                at += width_of(layer)
        assert at <= (128 if slab < 3 else FOLDED)
    return out


def row_places():
    places, at = {}, 0
    for layer in range(STEPS):
        for name in ("u", "v", "w"):
            if (name, layer) == ("w", 0):
                continue
            rows = 8 if name == "w" else rows_of(layer)
            places[name, layer] = (at, rows)
            at += rows
    return places, at


ROW_PLACES, ROW_TOTAL = row_places()


def moved(value, where):
    sizes = tuple(lax.axis_size(axis) for axis in AXES)
    pairs = []
    for z in range(sizes[0]):
        for y in range(sizes[1]):
            for x in range(sizes[2]):
                to = where(z, y, x)
                if to is not None:
                    tz, ty, tx = to[0] % sizes[0], to[1], to[2] % sizes[2]
                    pairs.append(((z * sizes[1] + y) * sizes[2] + x, (tz * sizes[1] + ty) * sizes[2] + tx))
    return lax.ppermute(value, AXES, pairs)


def shape(*dims):
    return jax.ShapeDtypeStruct(dims, F32)


def call(kernel, outs, *args, scratch=(), in_specs=None, **more):
    name = kernel.func.__name__ if isinstance(kernel, functools.partial) else kernel.__name__
    if in_specs is not None:
        more["in_specs"] = in_specs
    return pl.pallas_call(
        kernel,
        out_shape=outs,
        scratch_shapes=list(scratch),
        compiler_params=pltpu.CompilerParams(vmem_limit_bytes=40 * 1024 * 1024),
        cost_estimate=pl.CostEstimate(flops=0, bytes_accessed=int(MICROSECONDS.get(name, 0.5) * 3e6), transcendentals=0),
        name=name,
        **more,
    )(*args)


def lanes(rows):
    return lax.broadcasted_iota(jnp.int32, (rows, 128), 1)


def core():
    return lax.axis_index("gy") & 1


def seam():
    return lax.axis_index("gy") >> 1


def one_if(condition):
    return jnp.where(condition, 1.0, 0.0)


def outside():
    x, c = lax.axis_index("gx"), core()
    return ((c == 0) & (x == 0)) | ((c == 1) & (x == lax.axis_size("gx") - 1))


def plain_to_plane(ref):
    return jnp.concatenate([ref[pl.ds(t, 8, stride=VECTORS), :] for t in range(VECTORS)], axis=0)


def plane_to_plain(value, ref):
    for t in range(VECTORS):
        ref[pl.ds(t, 8, stride=VECTORS), :] = value[8 * t:8 * t + 8]


def aligned(value, to):
    return pl.multiple_of(value, to)


def power40(p):
    x = p + p
    x2 = x * x
    x4 = x2 * x2
    x8 = x4 * x4
    x32 = x8 * x8
    x32 = x32 * x32
    return x32 * x8


def power39(p):
    x = p + p
    x2 = x * x
    x4 = x2 * x2
    x8 = x4 * x4
    x32 = x8 * x8
    x32 = x32 * x32
    return x32 * (x4 * (x2 * x))


def edges(p_ref, inner_ref, outer_ref, left_ref, right_ref, turned):
    lane = lanes(128)
    c = core()
    packed = jnp.zeros((128, 128), F32)
    for layer in range(LAYERS):
        inner_ref[pl.ds(layer, 1), :] = p_ref[layer, pl.ds(127 * (1 - c), 1), :]
        outer_ref[pl.ds(layer, 1), :] = p_ref[layer, pl.ds(127 * c, 1), :]
        rolled = pltpu.roll(p_ref[layer], 2 * layer + 1, 1)
        packed = jnp.where((lane >> 1) == layer, rolled, packed)
    turned[...] = packed.T
    right_ref[...] = turned[pl.ds(0, 16, stride=2), :]
    left_ref[...] = turned[pl.ds(1, 16, stride=2), :]


def norm_of(position, extent):
    def missing(k):
        k = jnp.maximum(k, 0)
        return (k * (k + 1)) >> 1

    return ((RADIUS + 1) ** 2 - missing(RADIUS - position) - missing(RADIUS - (extent - 1 - position))).astype(F32)


def terms(total, density, sens, p39):
    total = jnp.maximum(total, 1e-30)
    offset = PENALTY * math.log(2.0) / EXPONENT
    smax = jnp.exp(jnp.log(total) * (1.0 / EXPONENT) - offset)
    gap = density - smax
    half = 0.5 * gap * lax.rsqrt(gap * gap + SMOOTH)
    low = 0.5 - half
    top = (0.5 + half) * (2.0 * PENALTY / EXPONENT) * smax
    h = top / total
    return h * sens, h * p39, low, total / top


def plane_norms(sizes):
    row0 = lax.axis_index("gy") * 128
    col0 = lax.axis_index("gx") * 128
    rows = lax.broadcasted_iota(jnp.int32, (128, 128), 0) + row0
    cols = lax.broadcasted_iota(jnp.int32, (128, 128), 1) + col0
    return norm_of(rows, sizes[1] * 128) * norm_of(cols, sizes[2] * 128)


def neighbours(p, layer, inner_ref, outer_ref, beside, powers):
    c = core()
    lane = lanes(128)
    own = power40(p)
    powers[pl.ds(8, 128), :] = own
    y = lax.axis_index("gy")
    there = one_if((y == 1) | (y == 2))
    powers[pl.ds(7 + 129 * (1 - c), 1), :] = power40(inner_ref[pl.ds(layer, 1), :])
    powers[pl.ds(7 + 129 * c, 1), :] = power40(outer_ref[pl.ds(layer, 1), :]) * there
    side = pltpu.roll(beside, (128 - (2 * layer + 1)) % 128, 1)
    right = jnp.where(lane == 127, side, pltpu.roll(own, 127, 1))
    left = jnp.where(lane == 0, side, pltpu.roll(own, 1, 1))
    return (own + right) + left + (powers[pl.ds(7, 128), :] + powers[pl.ds(9, 128), :])


def columns_beside(left_ref, right_ref, turned):
    x = lax.axis_index("gx")
    turned[...] = jnp.zeros((128, 128), F32)
    turned[pl.ds(0, 16, stride=2), :] = right_ref[...] * one_if(x < lax.axis_size("gx") - 1)
    turned[pl.ds(1, 16, stride=2), :] = left_ref[...] * one_if(x > 0)
    return power40(turned[...].T)


def lowest(p_ref, f_ref, s_ref, out_ref):
    out_ref[0] = p_ref[0]
    out_ref[1] = f_ref[0]
    out_ref[2] = s_ref[0]


def all_terms(sizes, p_ref, f_ref, s_ref, above_ref, inner_ref, outer_ref, left_ref, right_ref, uvw_ref, powers, turned):
    beside = columns_beside(left_ref, right_ref, turned)
    norms = 1.0 / plane_norms(sizes)
    gz = lax.axis_index("gz")
    layer0 = gz * LAYERS
    uvw_ref[0] = s_ref[0]
    uvw_ref[STEPS] = power39(p_ref[0])
    uvw_ref[2 * STEPS] = norms * (1.0 / norm_of(0 * layer0, sizes[0] * LAYERS))
    for layer in range(1, STEPS):
        total = neighbours(p_ref[layer - 1], layer - 1, inner_ref, outer_ref, beside, powers)
        if layer < LAYERS:
            p, f, s = p_ref[layer], f_ref[layer], s_ref[layer]
        else:
            p, f, s = above_ref[0], above_ref[1], above_ref[2]
        u, v, low, inverse = terms(total, f, s, power39(p))
        if layer == LAYERS:
            there = one_if(gz < sizes[0] - 1)
            u, v = u * there, v * there
        norm_z = norm_of(layer0 + layer, sizes[0] * LAYERS)
        uvw_ref[layer] = u
        uvw_ref[STEPS + layer] = v
        uvw_ref[2 * STEPS + layer] = low * inverse * (norms * (1.0 / norm_z))


def plane_of(uvw_ref, name, layer):
    return uvw_ref.at[STEPS * "uvw".index(name) + layer]


def pack_rows(uvw_ref, rows_ref):
    c = core()
    for (name, layer), (at, rows) in ROW_PLACES.items():
        start = aligned(c * (128 - rows), 8)
        rows_ref[pl.ds(at, rows), :] = plane_of(uvw_ref, name, layer)[pl.ds(start, rows), :]


def pack(uvw_ref, same_ref, cross_ref, corner_left_ref, corner_right_ref):
    c = core()

    def put(at, left, right):
        count = left.shape[0]
        same_ref[pl.ds(at, count), :] = jnp.where(c == 0, right, left)
        cross_ref[pl.ds(at, count), :] = jnp.where(c == 0, left, right)

    def put_corner(at, rows, left, right):
        first, last = slice(0, rows), slice(left.shape[0] - rows, left.shape[0])
        corner_left_ref[pl.ds(at, rows), :] = jnp.where(c == 0, left[first], left[last])
        corner_right_ref[pl.ds(at, rows), :] = jnp.where(c == 0, right[first], right[last])

    lane = lanes(128)
    for slab in range(4):
        left = right = jnp.zeros((128, 128), F32)
        for name, layer, where, at in strips():
            if where == slab:
                width = width_of(layer)
                plane = plane_of(uvw_ref, name, layer)[...]
                inside = (lane >= at) & (lane < at + width)
                left = jnp.where(inside, pltpu.roll(plane, at, 1) if at else plane, left)
                right = jnp.where(inside, pltpu.roll(plane, (at + width) % 128, 1), right)
        if slab < 3:
            put(128 * slab, left, right)
            put_corner(24 * slab, 24, left, right)
            continue
        put_corner(72, 16, left, right)
        folded = []
        for value in (left, right):
            total = value[:FOLDED]
            for i in range(1, 4):
                total = total + pltpu.roll(value[FOLDED * i:FOLDED * (i + 1)], FOLDED * i, 1)
            folded.append(total)
        put(384, *folded)
    lane = lanes(64)
    left = right = jnp.zeros((64, 128), F32)
    for layer in range(1, STEPS):
        ref = plane_of(uvw_ref, "w", layer)
        for half in range(2):
            plane = ref[pl.ds(64 * half, 64), :]
            at = 64 * half + RADIUS * (layer - 1)
            inside = (lane >= at) & (lane < at + RADIUS)
            left = jnp.where(inside, pltpu.roll(plane, at, 1) if at else plane, left)
            right = jnp.where(inside, pltpu.roll(plane, (at + RADIUS) % 128, 1), right)
    put(384 + FOLDED, left, right)
    put_corner(88, 8, left, right)


def slab_plane(plain, same, cross, corner):
    c = core()
    inside = one_if(jnp.logical_not(outside()))
    plain[pl.ds(256, 32), :] = jnp.zeros((32, 128), F32)
    plain[pl.ds(aligned(c * 128, 128), 128), :] = same * inside
    plain[pl.ds(aligned((1 - c) * 128, 128), 128), :] = cross * inside
    rows = corner.shape[0]
    plain[pl.ds(aligned(256 + seam() * (32 - rows), 8), rows), :] = corner * inside


def full_plane(plain, name, layer, uvw_ref, other_ref, got_ref, shared_ref):
    c = core()
    plain[pl.ds(aligned(c * 128, 128), 128), :] = plane_of(uvw_ref, name, layer)[...]
    plain[pl.ds(aligned((1 - c) * 128, 128), 128), :] = plane_of(other_ref, name, layer)[...]
    plain[pl.ds(256, 32), :] = jnp.zeros((32, 128), F32)
    start, rows = ROW_PLACES[name, layer]
    here = pl.ds(start, rows)
    to = aligned(256 + seam() * (32 - rows), 8)
    plain[pl.ds(to, rows), :] = jnp.where((c ^ seam()) == 1, got_ref[here, :], shared_ref[here, :])
    return plain_to_plane(plain)


def with_columns(base, columns, at, width):
    c = core()
    lane = lanes(PLANE)
    columns = pltpu.roll(columns, (128 - at - (1 - c) * width) & 127, 1)
    begin = (1 - c) * (128 - width)
    return jnp.where((lane >= begin) & (lane < begin + width), columns, base)


def assemble(
    uvw_ref, other_ref, got_ref, shared_ref, same_ref, cross_ref, corner_left_ref, corner_right_ref, uv_ref, plain, slabs
):
    c = core()
    for slab in range(4):
        if slab < 3:
            here = pl.ds(128 * slab, 128)
            same, cross = same_ref[here, :], cross_ref[here, :]
            here = pl.ds(24 * slab, 24)
        else:
            here = pl.ds(384, FOLDED)
            same, cross = (
                jnp.concatenate([value] + [pltpu.roll(value, 128 - FOLDED * i, 1) for i in range(1, 4)], axis=0)
                for value in (same_ref[here, :], cross_ref[here, :])
            )
            here = pl.ds(72, 16)
        corner = jnp.where(c == 0, corner_right_ref[here, :], corner_left_ref[here, :])
        slot = plain.at[slab % 2]
        slab_plane(slot, same, cross, corner)
        slabs[slab] = plain_to_plane(slot)
    for place, (name, layer, slab, at) in enumerate(strips()):
        base = full_plane(plain.at[place % 2], name, layer, uvw_ref, other_ref, got_ref, shared_ref)
        uv_ref[2 * (LAYERS - layer) + (name == "v")] = with_columns(base, slabs[slab], at, width_of(layer))


def assemble_w(
    uvw_ref, other_ref, got_ref, shared_ref, same_ref, cross_ref, corner_left_ref, corner_right_ref, w_ref, plain, slabs
):
    c = core()

    def unfolded(ref):
        value = ref[pl.ds(384 + FOLDED, 64), :]
        return jnp.concatenate([value, pltpu.roll(value, 64, 1)], axis=0)

    here = pl.ds(88, 8)
    corner = jnp.where(c == 0, corner_right_ref[here, :], corner_left_ref[here, :])
    corner = pltpu.roll(corner, 64 * seam(), 1)
    slab_plane(plain.at[0], unfolded(same_ref), unfolded(cross_ref), corner)
    slabs[0] = plain_to_plane(plain.at[0])
    for layer in range(1, STEPS):
        base = full_plane(plain.at[layer % 2], "w", layer, uvw_ref, other_ref, got_ref, shared_ref)
        w_ref[layer] = with_columns(base, slabs[0], RADIUS * (layer - 1), RADIUS)
    row = lax.broadcasted_iota(jnp.int32, (PLANE, 128), 0)
    col = lax.broadcasted_iota(jnp.int32, (PLANE, 128), 1)
    a = seam()
    row = jnp.where((a == 1) & (row >= 256), row - PLANE, row) + 256 * a
    width = jnp.where(c == 0, 108, 20)
    col = jnp.where((c == 0) & (col >= width), col - 128, jnp.where((c == 1) & (col < width), col + 128, col))
    col = col + 128 * lax.axis_index("gx")
    rows, cols = 128 * lax.axis_size("gy"), 128 * lax.axis_size("gx")
    norm = norm_of(row, rows) * norm_of(col, cols) * norm_of(0 * a, LAYERS * lax.axis_size("gz"))
    inside = (row >= 0) & (row < rows) & (col >= 0) & (col < cols)
    plain[0] = jnp.where(inside, 1.0 / jnp.where(inside, norm, 1.0), 0.0)
    w_ref[0] = plain_to_plane(plain.at[0])


def five(value):
    before = jnp.concatenate([pltpu.roll(value[PLANE - 8:], 1, 0), value[:PLANE - 8]], axis=0)
    behind = jnp.concatenate([value[8:], pltpu.roll(value[:8], 7, 0)], axis=0)
    return (value + before + behind) + (pltpu.roll(value, 1, 1) + pltpu.roll(value, 127, 1))


def set_carry(carry, main_ref, other_ref, outer_ref, halo_ref, halo_other_ref, halo_outer_ref):
    c = core()
    lane = lanes(64)
    mine = (lane >> 6) == c
    inside = one_if(jnp.logical_not(outside()))
    for i in range(4):
        rows = pl.ds(64 * (i % 2), 64)
        own, other = main_ref[rows, :], other_ref[rows, :]
        if i < 2:
            value = jnp.where(mine, own, other)
        else:
            value = pltpu.roll(jnp.where(mine, other, own), 64, 1)
        outer = pltpu.roll(outer_ref[...], (128 - 32 * i) % 128, 1) if i else outer_ref[...]
        outer = outer * inside
        begin = (1 - c) * (128 - REACH)
        value = jnp.where((lane >= begin) & (lane < begin + REACH), outer, value)
        carry[pl.ds(64 * i, 64), :] = value
    lane = lanes(24)
    value = jnp.where((lane >> 6) == c, halo_ref[...], halo_other_ref[...])
    begin = (1 - c) * (128 - REACH)
    value = jnp.where((lane >= begin) & (lane < begin + REACH), halo_outer_ref[...] * inside, value)
    carry[pl.ds(256, 32), :] = jnp.zeros((32, 128), F32)
    carry[pl.ds(aligned(256 + 8 * seam(), 8), 24), :] = value


def section(active, *refs):
    uv_ref, refs = refs[0], refs[1:]
    pieces, before_ref = (), None
    if active is not None and len(refs) > 5:
        pieces, before_ref, refs = refs[:6], refs[6], refs[7:]
    if len(refs) == 5:
        layers_ref, main_ref, outer_ref, halo_ref, carry = refs
    else:
        layers_ref, carry = refs
        main_ref = None

    @pl.when(lax.axis_index("gz") == active)
    def _():
        if pieces:
            set_carry(carry, *pieces)
            value = plain_to_plane(carry)
        else:
            value = jnp.zeros((PLANE, 128), F32)

        def step(i, value):
            value = uv_ref[2 * i] + uv_ref[2 * i + 1] * five(value)
            layers_ref[LAYERS - i] = value
            return value

        value = lax.fori_loop(0, LAYERS, step, value)
        layers_ref[0] = uv_ref[2 * LAYERS] + uv_ref[2 * LAYERS + 1] * five(value)
        if main_ref is None:
            return
        c = core()
        lane = lanes(128)
        plane_to_plain(value, carry)
        bottom = carry
        mine = (lane >> 6) == c
        main_ref[...] = jnp.where(mine, bottom[pl.ds(0, 128), :], pltpu.roll(bottom[pl.ds(128, 128), :], 64, 1))
        lane = lanes(64)
        slab = jnp.zeros((64, 128), F32)
        for i in range(4):
            rolled = bottom[pl.ds(64 * i, 64), :]
            rolled = pltpu.roll(rolled, 32 * i, 1) if i else rolled
            begin = (32 * i + 128 - c * 32) & 127
            slab = jnp.where(((lane - begin) & 127) < 32, rolled, slab)
        outer_ref[...] = slab
        halo_ref[...] = bottom[pl.ds(aligned((1 - seam()) * 232, 8), 24), :]

    if before_ref is not None:
        @pl.when(lax.axis_index("gz") != active)
        def _():
            layers_ref[...] = before_ref[...]


def box(values):
    two = [values[i] + values[i + 1] for i in range(len(values) - 1)]
    four = [two[i] + two[i + 2] for i in range(len(two) - 2)]
    return [four[i] + values[i + 4] for i in range(len(values) - 4)]


def smooth(layers_ref, w_ref, kept_ref, give_ref, plain, others, tent):
    c = core()
    mine = (lanes(128) >> 6) == c
    row = lax.broadcasted_iota(jnp.int32, (256, 128), 0)
    col = lax.broadcasted_iota(jnp.int32, (256, 128), 1)
    distance = (row - col + RADIUS) & 127
    weight = jnp.where(distance <= 2 * RADIUS, RADIUS + 1 - jnp.abs(distance - RADIUS), 0)
    tent[...] = weight.astype(F32).astype(jnp.bfloat16)

    def layer(k, _):
        values = [layers_ref[k, pl.ds(8 * t, 8), :] * w_ref[k, pl.ds(8 * t, 8), :] for t in range(VECTORS)]
        first = [pltpu.roll(value, 1, 0) for value in values[VECTORS - RADIUS:]]
        last = [pltpu.roll(value, 7, 0) for value in values[:RADIUS]]
        total = jnp.concatenate(box(box(first + values + last)), axis=0)
        high = total.astype(jnp.bfloat16)
        rest = total - high.astype(F32)
        middle = rest.astype(jnp.bfloat16)
        small = (rest - middle.astype(F32)).astype(jnp.bfloat16)
        value = jnp.dot(jnp.concatenate([high, middle], axis=1), tent[...], preferred_element_type=F32)
        value = value + jnp.dot(small, tent[pl.ds(0, 128), :], preferred_element_type=F32)
        plane_to_plain(value, plain)
        kept_ref[k] = plain[pl.ds(aligned(c * 128, 128), 128), :]
        others[k] = plain[pl.ds(aligned((1 - c) * 128, 128), 128), :]
        return 0

    lax.fori_loop(0, STEPS, layer, 0)
    count = give_ref.shape[0]
    for k in range(count):
        second = others[k + count] if k + count < STEPS else jnp.zeros((128, 128), F32)
        give_ref[k] = jnp.where(mine, others[k], pltpu.roll(second, 64, 1))


def ends(kept_ref, got_ref, out_ref, top_ref, bottom_ref):
    mine = (lanes(128) >> 6) == core()
    count = got_ref.shape[0]
    for k in range(STEPS):
        other = got_ref[k] if k < count else pltpu.roll(got_ref[k - count], 64, 1)
        out_ref[k] = jnp.where(mine, kept_ref[k], other)
    top_ref[...] = out_ref[pl.ds(STEPS - RADIUS - 1, RADIUS + 1)]
    bottom_ref[...] = out_ref[pl.ds(1, RADIUS - 1)]


def finish(tile_ref, below_ref, above_ref, passive_ref, out_ref):
    gz = lax.axis_index("gz")
    has_below, has_above = one_if(gz > 0), one_if(gz < lax.axis_size("gz") - 1)

    def layer(k):
        if k < 0:
            return below_ref[k + RADIUS] * has_below
        if k == 0:
            return jnp.where(gz == 0, tile_ref[0], below_ref[RADIUS])
        if k > LAYERS:
            return above_ref[k - STEPS] * has_above
        return tile_ref[k]

    for k in range(LAYERS):
        total = layer(k) * 5.0
        for offset in range(1, RADIUS + 1):
            total = total + (layer(k - offset) + layer(k + offset)) * (5.0 - offset)
        out_ref[k] = jnp.where(passive_ref[k] > 0, 0.0, total)


def to_other(value):
    return moved(value, lambda z, y, x: (z, y ^ 1, x))


def after(value, *others):
    return lax.optimization_barrier((value,) + others)[0]


def per_device(filtered, printed, sensitivity, passive):
    sizes = tuple(lax.axis_size(axis) for axis in AXES)
    depth = sizes[0]
    plane = shape(128, 128)
    edge = shape(16, 128)

    def across(z, y, x):
        return (z, y ^ 3, x) if y in (1, 2) else None

    def beside(z, y, x):
        return (z, y ^ 1, x + (1 if y & 1 else -1))

    def same(z, y, x):
        return (z, y, x + (-1 if y & 1 else 1))

    one = pl.BlockSpec((1, 128, 128), lambda i: (0, 0, 0))
    lowest_planes = call(lowest, shape(3, 128, 128), printed, filtered, sensitivity, in_specs=[one] * 3, grid=(1,))
    above = moved(lowest_planes, lambda z, y, x: (z - 1, y, x))
    inner, outer, left, right = call(edges, [edge] * 4, printed, scratch=[pltpu.VMEM((128, 128), F32)])
    from_left = moved(right, lambda z, y, x: (z, y, x + 1))
    from_right = moved(left, lambda z, y, x: (z, y, x - 1))
    outer = moved(outer, lambda z, y, x: (z, y ^ 3, x))
    inner = to_other(inner)
    uvw = call(
        functools.partial(all_terms, sizes), shape(3 * STEPS, 128, 128),
        printed, filtered, sensitivity, above, inner, outer, from_left, from_right,
        scratch=[pltpu.VMEM((144, 128), F32), pltpu.VMEM((128, 128), F32)],
    )
    slab, corner = shape(SLAB_ROWS, 128), shape(CORNER_ROWS, 128)
    rows = call(pack_rows, shape(ROW_TOTAL, 128), uvw)
    got = moved(rows, across)
    to_same, to_cross, corner_left, corner_right = call(pack, [slab, slab, corner, corner], after(uvw, rows))
    from_same = moved(to_same, same)
    from_cross = moved(to_cross, beside)
    corner_right = moved(corner_right, lambda z, y, x: (z, 2 * (2 - y), x + 1) if y in (1, 2) else None)
    corner_left = moved(corner_left, lambda z, y, x: (z, 5 - 2 * y, x - 1) if y in (1, 2) else None)
    other = to_other(uvw)
    shared = to_other(after(got, from_same, from_cross, corner_left, corner_right))
    parts = (uvw, other, got, shared, from_same, from_cross, corner_left, corner_right)
    stack = shape(STEPS, PLANE, 128)
    work = [pltpu.VMEM((2, PLANE, 128), F32), pltpu.VMEM((4, PLANE, 128), F32)]
    uvs = call(assemble, shape(2 * STEPS, PLANE, 128), *parts, scratch=work)
    ws = None
    pieces, before = (), ()
    for active in range(depth - 1, -1, -1):
        outs = [stack]
        if active > 0:
            outs = outs + [plane, shape(64, 128), shape(24, 128)]
        layers, *sent = call(
            functools.partial(section, active), outs, uvs, *pieces, *before, scratch=[pltpu.VMEM((PLANE, 128), F32)]
        )
        before = (layers,)
        if active > 0:
            main, side, strip = sent

            def down(where):
                def to(z, y, x):
                    _, ty, tx = where(z, y, x)
                    return (z - 1, ty, tx)
                return to

            def over(z, y, x):
                return (z, y ^ 2, x)

            def corner_of(z, y, x):
                _, ty, tx = beside(z, y, x)
                return (z, ty ^ 2, tx)

            main = moved(main, down(lambda z, y, x: (z, y, x)))
            halo = moved(strip, down(over))
            side = moved(side, down(beside))
            edge_piece = moved(strip, down(corner_of))
            main, halo, side, edge_piece = lax.optimization_barrier((main, halo, side, edge_piece))
            pieces = (main, to_other(main), side, halo, to_other(halo), edge_piece)
            if ws is None:
                ws = call(assemble_w, stack, after(uvw, side), *parts[1:], scratch=work)
    count = STEPS // 2 + 1
    kept, given = call(
        smooth,
        [shape(STEPS, 128, 128), shape(count, 128, 128)],
        layers, ws,
        scratch=[
            pltpu.VMEM((PLANE, 128), F32), pltpu.VMEM((STEPS, 128, 128), F32), pltpu.VMEM((256, 128), jnp.bfloat16)
        ],
    )
    given = to_other(given)
    tile, top, bottom = call(
        ends, [shape(STEPS, 128, 128), shape(RADIUS + 1, 128, 128), shape(RADIUS - 1, 128, 128)], kept, given
    )
    below = moved(top, lambda z, y, x: (z + 1, y, x))
    over = moved(bottom, lambda z, y, x: (z - 1, y, x))
    return call(finish, shape(LAYERS, 128, 128), tile, below, over, passive)


def solution(mesh):
    spec = P(*AXES)
    return jax.shard_map(
        per_device, mesh=mesh, in_specs=(spec,) * 4, out_specs=spec, check_vma=False
    )
```

time: 139 us -> 127 us (0.914)
  the two profiles are of different devices: /device:TPU:38 before, /device:TPU:1 now
where the time goes in v4:
time: 127 us
  starting transfers between devices  73.4 us (58%)
  waiting for transfers between devices  33.7 us (27%)
  Pallas kernels  16.3 us (13%)
  local copies, waits for them, and re-layouts  3.68 us (3%)
    ppermute x33, starting transfers between devices, moved(): return lax.ppermute(value, AXES, pairs)  73.4 us
    ppermute x33, waiting for transfers between devices, moved(): return lax.ppermute(value, AXES, pairs)  33.7 us
    pallas_call x14, Pallas kernels, call(): pl.pallas_call(kernel, out_shape=outs, scratch_shapes=list(scratch), comp...  16.3 us
    unnamed x10, local copies, waits for them, and re-layouts  3.68 us
  transfers between devices with their start and end apart: 33, of which 14 were waited for; matrix products, arithmetic and copies ran while one was open for 0% of the time, Pallas kernels for 3%

profile of v4, /device:TPU:1, one launch (start us, length us, event | category | flops | bytes accessed | tf_op | source)
XLA Modules:
  0.0 127.2 jit_solution(3035934065463746448)
XLA Ops:
  3.7 3.6 %collective-permute-start = (f32[3,128,128]{2,1,0:T(8,128)S(1)}, f32[3,128,128]{2,1,0:T(8,128)S(1)}, u32[]{:S(2)}, u32[]{:S(2)}) collective-permute-start(f32[3,128,128]{2,1,0:T(8,128)S(1)} %lowest.1), channel_id=1, source_target_pairs={{0,192},{1,193},{2,194},{3,195},{4,196},{5,197},{6,198},{7,199},{8... | collective-permute-start | bytes 589832 | tf_op jit(solution)/shard_map/ppermute | solution.py:77
  10.4 3.0 %collective-permute-start.3 = (f32[16,128]{1,0:T(8,128)S(1)}, f32[16,128]{1,0:T(8,128)S(1)}, u32[]{:S(2)}, u32[]{:S(2)}) collective-permute-start(f32[16,128]{1,0:T(8,128)S(1)} %get-tuple-element.47), channel_id=1, source_target_pairs={{0,1},{1,2},{2,3},{3,4},{4,5},{5,6},{6,7},{7,8},{8,9},{9,10},{10,1... | collective-permute-start | bytes 24584 | tf_op jit(solution)/shard_map/ppermute | solution.py:77
  13.4 4.3 %collective-permute-start.4 = (f32[16,128]{1,0:T(8,128)S(1)}, f32[16,128]{1,0:T(8,128)S(1)}, u32[]{:S(2)}, u32[]{:S(2)}) collective-permute-start(f32[16,128]{1,0:T(8,128)S(1)} %get-tuple-element.48), channel_id=1, source_target_pairs={{0,15},{1,0},{2,1},{3,2},{4,3},{5,4},{6,5},{7,6},{8,7},{9,8},{10,9... | collective-permute-start | bytes 24584 | tf_op jit(solution)/shard_map/ppermute | solution.py:77
  22.2 2.5 %collective-permute-start.6 = (f32[656,128]{1,0:T(8,128)S(1)}, f32[656,128]{1,0:T(8,128)S(1)}, u32[]{:S(2)}, u32[]{:S(2)}) collective-permute-start(f32[656,128]{1,0:T(8,128)S(1)} %pack_rows.1), channel_id=1, source_target_pairs={{16,32},{17,33},{18,34},{19,35},{20,36},{21,37},{22,38},{23,39},{2... | collective-permute-start | bytes 1007624 | tf_op jit(solution)/shard_map/ppermute | solution.py:77
  26.5 6.0 %collective-permute-start.7 = (f32[480,128]{1,0:T(8,128)S(1)}, f32[480,128]{1,0:T(8,128)S(1)}, u32[]{:S(2)}, u32[]{:S(2)}) collective-permute-start(f32[480,128]{1,0:T(8,128)S(1)} %get-tuple-element.50), channel_id=1, source_target_pairs={{0,1},{1,2},{2,3},{3,4},{4,5},{5,6},{6,7},{7,8},{8,9},{9,10},{10,1... | collective-permute-start | bytes 737288 | tf_op jit(solution)/shard_map/ppermute | solution.py:77
  32.5 4.9 %collective-permute-start.9 = (f32[96,128]{1,0:T(8,128)S(1)}, f32[96,128]{1,0:T(8,128)S(1)}, u32[]{:S(2)}, u32[]{:S(2)}) collective-permute-start(f32[96,128]{1,0:T(8,128)S(1)} %get-tuple-element.52), channel_id=1, source_target_pairs={{16,63},{17,48},{18,49},{19,50},{20,51},{21,52},{22,53},{23,54},{2... | collective-permute-start | bytes 147464 | tf_op jit(solution)/shard_map/ppermute | solution.py:77
  37.4 6.6 %collective-permute-done.9.corner_left_ref = f32[96,128]{1,0:T(8,128)S(1)} collective-permute-done((f32[96,128]{1,0:T(8,128)S(1)}, f32[96,128]{1,0:T(8,128)S(1)}, u32[]{:S(2)}, u32[]{:S(2)}) %collective-permute-start.9) | collective-permute-done | bytes 49184 | tf_op jit(solution)/shard_map/ppermute | solution.py:77
  46.6 4.0 %collective-permute-start.11 = (f32[656,128]{1,0:T(8,128)S(1)}, f32[656,128]{1,0:T(8,128)S(1)}, u32[]{:S(2)}, u32[]{:S(2)}) collective-permute-start(f32[656,128]{1,0:T(8,128)S(1)} %collective-permute-done.6.got_ref), channel_id=1, source_target_pairs={{0,16},{1,17},{2,18},{3,19},{4,20},{5,21},{6,22},{7,23},{8,24},{9,... | collective-permute-start | bytes 1007624 | tf_op jit(solution)/shard_map/ppermute | solution.py:77
  53.9 3.3 %collective-permute-start.12 = (f32[128,128]{1,0:T(8,128)S(1)}, f32[128,128]{1,0:T(8,128)S(1)}, u32[]{:S(2)}, u32[]{:S(2)}) collective-permute-start(f32[128,128]{1,0:T(8,128)S(1)} %get-tuple-element.55), channel_id=1, source_target_pairs={{0,192},{1,193},{2,194},{3,195},{4,196},{5,197},{6,198},{7,199},{8... | collective-permute-start | bytes 196616 | tf_op jit(solution)/shard_map/ppermute | solution.py:77
  57.2 2.0 %collective-permute-start.15 = (f32[24,128]{1,0:T(8,128)S(1)}, f32[24,128]{1,0:T(8,128)S(1)}, u32[]{:S(2)}, u32[]{:S(2)}) collective-permute-start(f32[24,128]{1,0:T(8,128)S(1)} %get-tuple-element.56), channel_id=1, source_target_pairs={{0,255},{1,240},{2,241},{3,242},{4,243},{5,244},{6,245},{7,246},{8... | collective-permute-start | bytes 36872 | tf_op jit(solution)/shard_map/ppermute | solution.py:77
  59.8 5.1 %collective-permute-done.15.refs_6_ = f32[24,128]{1,0:T(8,128)S(1)} collective-permute-done((f32[24,128]{1,0:T(8,128)S(1)}, f32[24,128]{1,0:T(8,128)S(1)}, u32[]{:S(2)}, u32[]{:S(2)}) %collective-permute-start.15) | collective-permute-done | bytes 12320 | tf_op jit(solution)/shard_map/ppermute | solution.py:77
  64.9 2.9 %collective-permute-start.16 = (f32[128,128]{1,0:T(8,128)S(1)}, f32[128,128]{1,0:T(8,128)S(1)}, u32[]{:S(2)}, u32[]{:S(2)}) collective-permute-start(f32[128,128]{1,0:T(8,128)S(1)} %collective-permute-done.12.refs_1_), channel_id=1, source_target_pairs={{0,16},{1,17},{2,18},{3,19},{4,20},{5,21},{6,22},{7,23},{8,24},{9,... | collective-permute-start | bytes 196616 | tf_op jit(solution)/shard_map/ppermute | solution.py:77
  69.1 3.1 %collective-permute-start.18 = (f32[128,128]{1,0:T(8,128)S(1)}, f32[128,128]{1,0:T(8,128)S(1)}, u32[]{:S(2)}, u32[]{:S(2)}) collective-permute-start(f32[128,128]{1,0:T(8,128)S(1)} %get-tuple-element.63), channel_id=1, source_target_pairs={{0,192},{1,193},{2,194},{3,195},{4,196},{5,197},{6,198},{7,199},{8... | collective-permute-start | bytes 196616 | tf_op jit(solution)/shard_map/ppermute | solution.py:77
  72.3 6.1 %collective-permute-start.21 = (f32[24,128]{1,0:T(8,128)S(1)}, f32[24,128]{1,0:T(8,128)S(1)}, u32[]{:S(2)}, u32[]{:S(2)}) collective-permute-start(f32[24,128]{1,0:T(8,128)S(1)} %get-tuple-element.64), channel_id=1, source_target_pairs={{0,255},{1,240},{2,241},{3,242},{4,243},{5,244},{6,245},{7,246},{8... | collective-permute-start | bytes 36872 | tf_op jit(solution)/shard_map/ppermute | solution.py:77
  79.2 2.6 %collective-permute-done.19.refs_4_ = f32[24,128]{1,0:T(8,128)S(1)} collective-permute-done((f32[24,128]{1,0:T(8,128)S(1)}, f32[24,128]{1,0:T(8,128)S(1)}, u32[]{:S(2)}, u32[]{:S(2)}) %collective-permute-start.19) | collective-permute-done | bytes 12320 | tf_op jit(solution)/shard_map/ppermute | solution.py:77
  81.9 5.0 %collective-permute-start.22 = (f32[128,128]{1,0:T(8,128)S(1)}, f32[128,128]{1,0:T(8,128)S(1)}, u32[]{:S(2)}, u32[]{:S(2)}) collective-permute-start(f32[128,128]{1,0:T(8,128)S(1)} %collective-permute-done.18.refs_1_), channel_id=1, source_target_pairs={{0,16},{1,17},{2,18},{3,19},{4,20},{5,21},{6,22},{7,23},{8,24},{9,... | collective-permute-start | bytes 196616 | tf_op jit(solution)/shard_map/ppermute | solution.py:77
  89.3 8.1 %collective-permute-start.27 = (f32[24,128]{1,0:T(8,128)S(1)}, f32[24,128]{1,0:T(8,128)S(1)}, u32[]{:S(2)}, u32[]{:S(2)}) collective-permute-start(f32[24,128]{1,0:T(8,128)S(1)} %get-tuple-element.72), channel_id=1, source_target_pairs={{0,255},{1,240},{2,241},{3,242},{4,243},{5,244},{6,245},{7,246},{8... | collective-permute-start | bytes 36872 | tf_op jit(solution)/shard_map/ppermute | solution.py:77
  98.3 2.9 %collective-permute-done.25.refs_4_ = f32[24,128]{1,0:T(8,128)S(1)} collective-permute-done((f32[24,128]{1,0:T(8,128)S(1)}, f32[24,128]{1,0:T(8,128)S(1)}, u32[]{:S(2)}, u32[]{:S(2)}) %collective-permute-start.25) | collective-permute-done | bytes 12320 | tf_op jit(solution)/shard_map/ppermute | solution.py:77
  101.2 3.7 %collective-permute-start.28 = (f32[128,128]{1,0:T(8,128)S(1)}, f32[128,128]{1,0:T(8,128)S(1)}, u32[]{:S(2)}, u32[]{:S(2)}) collective-permute-start(f32[128,128]{1,0:T(8,128)S(1)} %collective-permute-done.24.refs_1_), channel_id=1, source_target_pairs={{0,16},{1,17},{2,18},{3,19},{4,20},{5,21},{6,22},{7,23},{8,24},{9,... | collective-permute-start | bytes 196616 | tf_op jit(solution)/shard_map/ppermute | solution.py:77
  106.3 2.7 %section.7.layers_ref = f32[17,288,128]{2,1,0:T(8,128)S(1)} custom-call(f32[34,288,128]{2,1,0:T(8,128)S(1)} %assemble.1.refs_0_, f32[128,128]{1,0:T(8,128)S(1)} %collective-permute-done.24.refs_1_, f32[128,128]{1,0:T(8,128)S(1)} %collective-permute-done.28.refs_2_, f32[64,128]{1,0:T(8,128)S(1)} %collective-permute-done.26.refs_3_, ...), custom_call_target="tpu_custom_call" | custom-call | bytes 7800000 | tf_op jit(solution)/shard_map/section/pallas_call | solution.py:88
  108.9 4.2 %smooth.1 = (f32[17,128,128]{2,1,0:T(8,128)S(1)}, f32[9,128,128]{2,1,0:T(8,128)S(1)}) custom-call(f32[17,288,128]{2,1,0:T(8,128)S(1)} %section.7.layers_ref, f32[17,288,128]{2,1,0:T(8,128)S(1)} %assemble_w.1.w_ref), custom_call_target="tpu_custom_call" | custom-call | bytes 12000000 | tf_op jit(solution)/shard_map/smooth/pallas_call | solution.py:88
  115.6 2.7 %collective-permute-start.32 = (f32[3,128,128]{2,1,0:T(8,128)S(1)}, f32[3,128,128]{2,1,0:T(8,128)S(1)}, u32[]{:S(2)}, u32[]{:S(2)}) collective-permute-start(f32[3,128,128]{2,1,0:T(8,128)S(1)} %get-tuple-element.84), channel_id=1, source_target_pairs={{0,192},{1,193},{2,194},{3,195},{4,196},{5,197},{6,198},{7,199},{8... | collective-permute-start | bytes 589832 | tf_op jit(solution)/shard_map/ppermute | solution.py:77
  118.3 3.6 %collective-permute-done.32.above_ref = f32[3,128,128]{2,1,0:T(8,128)S(1)} collective-permute-done((f32[3,128,128]{2,1,0:T(8,128)S(1)}, f32[3,128,128]{2,1,0:T(8,128)S(1)}, u32[]{:S(2)}, u32[]{:S(2)}) %collective-permute-start.32) | collective-permute-done | bytes 196640 | tf_op jit(solution)/shard_map/ppermute | solution.py:77
  121.9 3.9 %collective-permute-done.31.below_ref = f32[5,128,128]{2,1,0:T(8,128)S(1)} collective-permute-done((f32[5,128,128]{2,1,0:T(8,128)S(1)}, f32[5,128,128]{2,1,0:T(8,128)S(1)}, u32[]{:S(2)}, u32[]{:S(2)}) %collective-permute-start.31) | collective-permute-done | bytes 327712 | tf_op jit(solution)/shard_map/ppermute | solution.py:77
  (66 shorter events, 30.2 us)
Async XLA Ops:
  3.7 15.1 %collective-permute-start = (f32[3,128,128]{2,1,0:T(8,128)S(1)}, f32[3,128,128]{2,1,0:T(8,128)S(1)}, u32[]{:S(2)}, u32[]{:S(2)}) collective-permute-start(f32[3,128,128]{2,1,0:T(8,128)S(1)} %lowest.1), channel_id=1, source_target_pairs={{0,192},{1,193},{2,194},{3,195},{4,196},{5,197},{6,198},{7,199},{8... | collective-permute-start | bytes 589832 | tf_op jit(solution)/shard_map/ppermute | solution.py:77
  7.7 10.0 %collective-permute-start.1 = (f32[16,128]{1,0:T(8,128)S(1)}, f32[16,128]{1,0:T(8,128)S(1)}, u32[]{:S(2)}, u32[]{:S(2)}) collective-permute-start(f32[16,128]{1,0:T(8,128)S(1)} %get-tuple-element.45), channel_id=1, source_target_pairs={{0,16},{1,17},{2,18},{3,19},{4,20},{5,21},{6,22},{7,23},{8,24},{9,... | collective-permute-start | bytes 24584 | tf_op jit(solution)/shard_map/ppermute | solution.py:77
  8.8 8.9 %collective-permute-start.2 = (f32[16,128]{1,0:T(8,128)S(1)}, f32[16,128]{1,0:T(8,128)S(1)}, u32[]{:S(2)}, u32[]{:S(2)}) collective-permute-start(f32[16,128]{1,0:T(8,128)S(1)} %get-tuple-element.46), channel_id=1, source_target_pairs={{0,48},{1,49},{2,50},{3,51},{4,52},{5,53},{6,54},{7,55},{8,56},{9,... | collective-permute-start | bytes 24584 | tf_op jit(solution)/shard_map/ppermute | solution.py:77
  10.4 8.4 %collective-permute-start.3 = (f32[16,128]{1,0:T(8,128)S(1)}, f32[16,128]{1,0:T(8,128)S(1)}, u32[]{:S(2)}, u32[]{:S(2)}) collective-permute-start(f32[16,128]{1,0:T(8,128)S(1)} %get-tuple-element.47), channel_id=1, source_target_pairs={{0,1},{1,2},{2,3},{3,4},{4,5},{5,6},{6,7},{7,8},{8,9},{9,10},{10,1... | collective-permute-start | bytes 24584 | tf_op jit(solution)/shard_map/ppermute | solution.py:77
  13.4 5.5 %collective-permute-start.4 = (f32[16,128]{1,0:T(8,128)S(1)}, f32[16,128]{1,0:T(8,128)S(1)}, u32[]{:S(2)}, u32[]{:S(2)}) collective-permute-start(f32[16,128]{1,0:T(8,128)S(1)} %get-tuple-element.48), channel_id=1, source_target_pairs={{0,15},{1,0},{2,1},{3,2},{4,3},{5,4},{6,5},{7,6},{8,7},{9,8},{10,9... | collective-permute-start | bytes 24584 | tf_op jit(solution)/shard_map/ppermute | solution.py:77
  20.8 31.1 %collective-permute-start.5 = (f32[51,128,128]{2,1,0:T(8,128)S(1)}, f32[51,128,128]{2,1,0:T(8,128)S(1)}, u32[]{:S(2)}, u32[]{:S(2)}) collective-permute-start(f32[51,128,128]{2,1,0:T(8,128)S(1)} %all_terms.1.uvw_ref), channel_id=1, source_target_pairs={{0,16},{1,17},{2,18},{3,19},{4,20},{5,21},{6,22},{7,23},{8,24},{9,... | collective-permute-start | bytes 10027016 | tf_op jit(solution)/shard_map/ppermute | solution.py:77
  22.2 24.4 %collective-permute-start.6 = (f32[656,128]{1,0:T(8,128)S(1)}, f32[656,128]{1,0:T(8,128)S(1)}, u32[]{:S(2)}, u32[]{:S(2)}) collective-permute-start(f32[656,128]{1,0:T(8,128)S(1)} %pack_rows.1), channel_id=1, source_target_pairs={{16,32},{17,33},{18,34},{19,35},{20,36},{21,37},{22,38},{23,39},{2... | collective-permute-start | bytes 1007624 | tf_op jit(solution)/shard_map/ppermute | solution.py:77
  26.5 20.2 %collective-permute-start.7 = (f32[480,128]{1,0:T(8,128)S(1)}, f32[480,128]{1,0:T(8,128)S(1)}, u32[]{:S(2)}, u32[]{:S(2)}) collective-permute-start(f32[480,128]{1,0:T(8,128)S(1)} %get-tuple-element.50), channel_id=1, source_target_pairs={{0,1},{1,2},{2,3},{3,4},{4,5},{5,6},{6,7},{7,8},{8,9},{9,10},{10,1... | collective-permute-start | bytes 737288 | tf_op jit(solution)/shard_map/ppermute | solution.py:77
  32.5 14.1 %collective-permute-start.8 = (f32[480,128]{1,0:T(8,128)S(1)}, f32[480,128]{1,0:T(8,128)S(1)}, u32[]{:S(2)}, u32[]{:S(2)}) collective-permute-start(f32[480,128]{1,0:T(8,128)S(1)} %get-tuple-element.51), channel_id=1, source_target_pairs={{0,31},{1,16},{2,17},{3,18},{4,19},{5,20},{6,21},{7,22},{8,23},{9,... | collective-permute-start | bytes 737288 | tf_op jit(solution)/shard_map/ppermute | solution.py:77
  32.5 11.5 %collective-permute-start.9 = (f32[96,128]{1,0:T(8,128)S(1)}, f32[96,128]{1,0:T(8,128)S(1)}, u32[]{:S(2)}, u32[]{:S(2)}) collective-permute-start(f32[96,128]{1,0:T(8,128)S(1)} %get-tuple-element.52), channel_id=1, source_target_pairs={{16,63},{17,48},{18,49},{19,50},{20,51},{21,52},{22,53},{23,54},{2... | collective-permute-start | bytes 147464 | tf_op jit(solution)/shard_map/ppermute | solution.py:77
  46.6 5.3 %collective-permute-start.11 = (f32[656,128]{1,0:T(8,128)S(1)}, f32[656,128]{1,0:T(8,128)S(1)}, u32[]{:S(2)}, u32[]{:S(2)}) collective-permute-start(f32[656,128]{1,0:T(8,128)S(1)} %collective-permute-done.6.got_ref), channel_id=1, source_target_pairs={{0,16},{1,17},{2,18},{3,19},{4,20},{5,21},{6,22},{7,23},{8,24},{9,... | collective-permute-start | bytes 1007624 | tf_op jit(solution)/shard_map/ppermute | solution.py:77
  53.9 11.0 %collective-permute-start.12 = (f32[128,128]{1,0:T(8,128)S(1)}, f32[128,128]{1,0:T(8,128)S(1)}, u32[]{:S(2)}, u32[]{:S(2)}) collective-permute-start(f32[128,128]{1,0:T(8,128)S(1)} %get-tuple-element.55), channel_id=1, source_target_pairs={{0,192},{1,193},{2,194},{3,195},{4,196},{5,197},{6,198},{7,199},{8... | collective-permute-start | bytes 196616 | tf_op jit(solution)/shard_map/ppermute | solution.py:77
  57.2 7.7 %collective-permute-start.14 = (f32[64,128]{1,0:T(8,128)S(1)}, f32[64,128]{1,0:T(8,128)S(1)}, u32[]{:S(2)}, u32[]{:S(2)}) collective-permute-start(f32[64,128]{1,0:T(8,128)S(1)} %get-tuple-element.57), channel_id=1, source_target_pairs={{0,223},{1,208},{2,209},{3,210},{4,211},{5,212},{6,213},{7,214},{8... | collective-permute-start | bytes 98312 | tf_op jit(solution)/shard_map/ppermute | solution.py:77
  57.2 7.7 %collective-permute-start.15 = (f32[24,128]{1,0:T(8,128)S(1)}, f32[24,128]{1,0:T(8,128)S(1)}, u32[]{:S(2)}, u32[]{:S(2)}) collective-permute-start(f32[24,128]{1,0:T(8,128)S(1)} %get-tuple-element.56), channel_id=1, source_target_pairs={{0,255},{1,240},{2,241},{3,242},{4,243},{5,244},{6,245},{7,246},{8... | collective-permute-start | bytes 36872 | tf_op jit(solution)/shard_map/ppermute | solution.py:77
  59.2 5.7 %collective-permute-start.13 = (f32[24,128]{1,0:T(8,128)S(1)}, f32[24,128]{1,0:T(8,128)S(1)}, u32[]{:S(2)}, u32[]{:S(2)}) collective-permute-start(f32[24,128]{1,0:T(8,128)S(1)} %get-tuple-element.56), channel_id=1, source_target_pairs={{0,224},{1,225},{2,226},{3,227},{4,228},{5,229},{6,230},{7,231},{8... | collective-permute-start | bytes 36872 | tf_op jit(solution)/shard_map/ppermute | solution.py:77
  69.1 12.7 %collective-permute-start.18 = (f32[128,128]{1,0:T(8,128)S(1)}, f32[128,128]{1,0:T(8,128)S(1)}, u32[]{:S(2)}, u32[]{:S(2)}) collective-permute-start(f32[128,128]{1,0:T(8,128)S(1)} %get-tuple-element.63), channel_id=1, source_target_pairs={{0,192},{1,193},{2,194},{3,195},{4,196},{5,197},{6,198},{7,199},{8... | collective-permute-start | bytes 196616 | tf_op jit(solution)/shard_map/ppermute | solution.py:77
  72.3 9.6 %collective-permute-start.20 = (f32[64,128]{1,0:T(8,128)S(1)}, f32[64,128]{1,0:T(8,128)S(1)}, u32[]{:S(2)}, u32[]{:S(2)}) collective-permute-start(f32[64,128]{1,0:T(8,128)S(1)} %get-tuple-element.65), channel_id=1, source_target_pairs={{0,223},{1,208},{2,209},{3,210},{4,211},{5,212},{6,213},{7,214},{8... | collective-permute-start | bytes 98312 | tf_op jit(solution)/shard_map/ppermute | solution.py:77
  72.3 7.0 %collective-permute-start.21 = (f32[24,128]{1,0:T(8,128)S(1)}, f32[24,128]{1,0:T(8,128)S(1)}, u32[]{:S(2)}, u32[]{:S(2)}) collective-permute-start(f32[24,128]{1,0:T(8,128)S(1)} %get-tuple-element.64), channel_id=1, source_target_pairs={{0,255},{1,240},{2,241},{3,242},{4,243},{5,244},{6,245},{7,246},{8... | collective-permute-start | bytes 36872 | tf_op jit(solution)/shard_map/ppermute | solution.py:77
  81.9 6.2 %collective-permute-start.22 = (f32[128,128]{1,0:T(8,128)S(1)}, f32[128,128]{1,0:T(8,128)S(1)}, u32[]{:S(2)}, u32[]{:S(2)}) collective-permute-start(f32[128,128]{1,0:T(8,128)S(1)} %collective-permute-done.18.refs_1_), channel_id=1, source_target_pairs={{0,16},{1,17},{2,18},{3,19},{4,20},{5,21},{6,22},{7,23},{8,24},{9,... | collective-permute-start | bytes 196616 | tf_op jit(solution)/shard_map/ppermute | solution.py:77
  88.2 13.0 %collective-permute-start.24 = (f32[128,128]{1,0:T(8,128)S(1)}, f32[128,128]{1,0:T(8,128)S(1)}, u32[]{:S(2)}, u32[]{:S(2)}) collective-permute-start(f32[128,128]{1,0:T(8,128)S(1)} %get-tuple-element.71), channel_id=1, source_target_pairs={{0,192},{1,193},{2,194},{3,195},{4,196},{5,197},{6,198},{7,199},{8... | collective-permute-start | bytes 196616 | tf_op jit(solution)/shard_map/ppermute | solution.py:77
  89.3 11.9 %collective-permute-start.26 = (f32[64,128]{1,0:T(8,128)S(1)}, f32[64,128]{1,0:T(8,128)S(1)}, u32[]{:S(2)}, u32[]{:S(2)}) collective-permute-start(f32[64,128]{1,0:T(8,128)S(1)} %get-tuple-element.73), channel_id=1, source_target_pairs={{0,223},{1,208},{2,209},{3,210},{4,211},{5,212},{6,213},{7,214},{8... | collective-permute-start | bytes 98312 | tf_op jit(solution)/shard_map/ppermute | solution.py:77
  89.3 9.0 %collective-permute-start.27 = (f32[24,128]{1,0:T(8,128)S(1)}, f32[24,128]{1,0:T(8,128)S(1)}, u32[]{:S(2)}, u32[]{:S(2)}) collective-permute-start(f32[24,128]{1,0:T(8,128)S(1)} %get-tuple-element.72), channel_id=1, source_target_pairs={{0,255},{1,240},{2,241},{3,242},{4,243},{5,244},{6,245},{7,246},{8... | collective-permute-start | bytes 36872 | tf_op jit(solution)/shard_map/ppermute | solution.py:77
  115.5 10.2 %collective-permute-start.31 = (f32[5,128,128]{2,1,0:T(8,128)S(1)}, f32[5,128,128]{2,1,0:T(8,128)S(1)}, u32[]{:S(2)}, u32[]{:S(2)}) collective-permute-start(f32[5,128,128]{2,1,0:T(8,128)S(1)} %get-tuple-element.83), channel_id=1, source_target_pairs={{0,64},{1,65},{2,66},{3,67},{4,68},{5,69},{6,70},{7,71},{8,72},{9,... | collective-permute-start | bytes 983048 | tf_op jit(solution)/shard_map/ppermute | solution.py:77
  115.6 6.3 %collective-permute-start.32 = (f32[3,128,128]{2,1,0:T(8,128)S(1)}, f32[3,128,128]{2,1,0:T(8,128)S(1)}, u32[]{:S(2)}, u32[]{:S(2)}) collective-permute-start(f32[3,128,128]{2,1,0:T(8,128)S(1)} %get-tuple-element.84), channel_id=1, source_target_pairs={{0,192},{1,193},{2,194},{3,195},{4,196},{5,197},{6,198},{7,199},{8... | collective-permute-start | bytes 589832 | tf_op jit(solution)/shard_map/ppermute | solution.py:77
  (14 other events, 60.4 us)

commit v5 on v4

--- a/solution.py
+++ b/solution.py
@@ -213,12 +213,6 @@
     turned[pl.ds(0, 16, stride=2), :] = right_ref[...] * one_if(x < lax.axis_size("gx") - 1)
     turned[pl.ds(1, 16, stride=2), :] = left_ref[...] * one_if(x > 0)
     return power40(turned[...].T)
-
-
-def lowest(p_ref, f_ref, s_ref, out_ref):
-    out_ref[0] = p_ref[0]
-    out_ref[1] = f_ref[0]
-    out_ref[2] = s_ref[0]
 
 
 def all_terms(sizes, p_ref, f_ref, s_ref, above_ref, inner_ref, outer_ref, left_ref, right_ref, uvw_ref, powers, turned):
@@ -256,7 +250,7 @@
         rows_ref[pl.ds(at, rows), :] = plane_of(uvw_ref, name, layer)[pl.ds(start, rows), :]
 
 
-def pack(uvw_ref, same_ref, cross_ref, corner_left_ref, corner_right_ref):
+def pack(uvw_ref, same_ref, cross_ref, keep_ref, give_ref):
     c = core()
 
     def put(at, left, right):
@@ -266,8 +260,8 @@
 
     def put_corner(at, rows, left, right):
         first, last = slice(0, rows), slice(left.shape[0] - rows, left.shape[0])
-        corner_left_ref[pl.ds(at, rows), :] = jnp.where(c == 0, left[first], left[last])
-        corner_right_ref[pl.ds(at, rows), :] = jnp.where(c == 0, right[first], right[last])
+        keep_ref[pl.ds(at, rows), :] = jnp.where(c == 0, left[first], right[last])
+        give_ref[pl.ds(at, rows), :] = jnp.where(c == 0, right[first], left[last])
 
     lane = lanes(128)
     for slab in range(4):
@@ -305,6 +299,10 @@
     put_corner(88, 8, left, right)
 
 
+def pick_corner(keep_ref, got_ref, corner_ref):
+    corner_ref[...] = jnp.where((core() ^ seam()) == 1, keep_ref[...], got_ref[...])
+
+
 def slab_plane(plain, same, cross, corner):
     c = core()
     inside = one_if(jnp.logical_not(outside()))
@@ -336,7 +334,7 @@
 
 
 def assemble(
-    uvw_ref, other_ref, got_ref, shared_ref, same_ref, cross_ref, corner_left_ref, corner_right_ref, uv_ref, plain, slabs
+    uvw_ref, other_ref, got_ref, shared_ref, same_ref, cross_ref, corner_ref, uv_ref, plain, slabs
 ):
     c = core()
     for slab in range(4):
@@ -351,7 +349,7 @@
                 for value in (same_ref[here, :], cross_ref[here, :])
             )
             here = pl.ds(72, 16)
-        corner = jnp.where(c == 0, corner_right_ref[here, :], corner_left_ref[here, :])
+        corner = corner_ref[here, :]
         slot = plain.at[slab % 2]
         slab_plane(slot, same, cross, corner)
         slabs[slab] = plain_to_plane(slot)
@@ -361,7 +359,7 @@
 
 
 def assemble_w(
-    uvw_ref, other_ref, got_ref, shared_ref, same_ref, cross_ref, corner_left_ref, corner_right_ref, w_ref, plain, slabs
+    uvw_ref, other_ref, got_ref, shared_ref, same_ref, cross_ref, corner_ref, w_ref, plain, slabs
 ):
     c = core()
 
@@ -370,7 +368,7 @@
         return jnp.concatenate([value, pltpu.roll(value, 64, 1)], axis=0)
 
     here = pl.ds(88, 8)
-    corner = jnp.where(c == 0, corner_right_ref[here, :], corner_left_ref[here, :])
+    corner = corner_ref[here, :]
     corner = pltpu.roll(corner, 64 * seam(), 1)
     slab_plane(plain.at[0], unfolded(same_ref), unfolded(cross_ref), corner)
     slabs[0] = plain_to_plane(plain.at[0])
@@ -391,10 +389,16 @@
     w_ref[0] = plain_to_plane(plain.at[0])
 
 
-def five(value):
-    before = jnp.concatenate([pltpu.roll(value[PLANE - 8:], 1, 0), value[:PLANE - 8]], axis=0)
-    behind = jnp.concatenate([value[8:], pltpu.roll(value[:8], 7, 0)], axis=0)
-    return (value + before + behind) + (pltpu.roll(value, 1, 1) + pltpu.roll(value, 127, 1))
+def step_down(values, u_ref, v_ref, out_ref):
+    new = []
+    for t, value in enumerate(values):
+        before = values[t - 1] if t > 0 else pltpu.roll(values[-1], 1, 0)
+        behind = values[t + 1] if t < VECTORS - 1 else pltpu.roll(values[0], 7, 0)
+        total = (value + before) + (behind + pltpu.roll(value, 1, 1)) + pltpu.roll(value, 127, 1)
+        here = pl.ds(8 * t, 8)
+        new.append(u_ref[here, :] + v_ref[here, :] * total)
+        out_ref[here, :] = new[-1]
+    return new
 
 
 def set_carry(carry, main_ref, other_ref, outer_ref, halo_ref, halo_other_ref, halo_outer_ref):
@@ -437,22 +441,19 @@
     def _():
         if pieces:
             set_carry(carry, *pieces)
-            value = plain_to_plane(carry)
+            values = [carry[pl.ds(t, 8, stride=VECTORS), :] for t in range(VECTORS)]
         else:
-            value = jnp.zeros((PLANE, 128), F32)
-
-        def step(i, value):
-            value = uv_ref[2 * i] + uv_ref[2 * i + 1] * five(value)
-            layers_ref[LAYERS - i] = value
-            return value
-
-        value = lax.fori_loop(0, LAYERS, step, value)
-        layers_ref[0] = uv_ref[2 * LAYERS] + uv_ref[2 * LAYERS + 1] * five(value)
+            values = [jnp.zeros((8, 128), F32)] * VECTORS
+        for layer in range(LAYERS, 0, -1):
+            at = 2 * (LAYERS - layer)
+            values = step_down(values, uv_ref.at[at], uv_ref.at[at + 1], layers_ref.at[layer])
+        step_down(values, uv_ref.at[2 * LAYERS], uv_ref.at[2 * LAYERS + 1], layers_ref.at[0])
         if main_ref is None:
             return
         c = core()
         lane = lanes(128)
-        plane_to_plain(value, carry)
+        for t in range(VECTORS):
+            carry[pl.ds(t, 8, stride=VECTORS), :] = values[t]
         bottom = carry
         mine = (lane >> 6) == c
         main_ref[...] = jnp.where(mine, bottom[pl.ds(0, 128), :], pltpu.roll(bottom[pl.ds(128, 128), :], 64, 1))
@@ -478,7 +479,7 @@
     return [four[i] + values[i + 4] for i in range(len(values) - 4)]
 
 
-def smooth(layers_ref, w_ref, kept_ref, give_ref, plain, others, tent):
+def smooth(layers_ref, w_ref, kept_ref, give_ref, plains, others, tent):
     c = core()
     mine = (lanes(128) >> 6) == c
     row = lax.broadcasted_iota(jnp.int32, (256, 128), 0)
@@ -487,7 +488,7 @@
     weight = jnp.where(distance <= 2 * RADIUS, RADIUS + 1 - jnp.abs(distance - RADIUS), 0)
     tent[...] = weight.astype(F32).astype(jnp.bfloat16)
 
-    def layer(k, _):
+    def layer(k, plain):
         values = [layers_ref[k, pl.ds(8 * t, 8), :] * w_ref[k, pl.ds(8 * t, 8), :] for t in range(VECTORS)]
         first = [pltpu.roll(value, 1, 0) for value in values[VECTORS - RADIUS:]]
         last = [pltpu.roll(value, 7, 0) for value in values[:RADIUS]]
@@ -501,9 +502,9 @@
         plane_to_plain(value, plain)
         kept_ref[k] = plain[pl.ds(aligned(c * 128, 128), 128), :]
         others[k] = plain[pl.ds(aligned((1 - c) * 128, 128), 128), :]
-        return 0
-
-    lax.fori_loop(0, STEPS, layer, 0)
+
+    for k in range(STEPS):
+        layer(k, plains.at[k % 4])
     count = give_ref.shape[0]
     for k in range(count):
         second = others[k + count] if k + count < STEPS else jnp.zeros((128, 128), F32)
@@ -563,8 +564,7 @@
     def same(z, y, x):
         return (z, y, x + (-1 if y & 1 else 1))
 
-    one = pl.BlockSpec((1, 128, 128), lambda i: (0, 0, 0))
-    lowest_planes = call(lowest, shape(3, 128, 128), printed, filtered, sensitivity, in_specs=[one] * 3, grid=(1,))
+    lowest_planes = jnp.stack([printed[0], filtered[0], sensitivity[0]])
     above = moved(lowest_planes, lambda z, y, x: (z - 1, y, x))
     inner, outer, left, right = call(edges, [edge] * 4, printed, scratch=[pltpu.VMEM((128, 128), F32)])
     from_left = moved(right, lambda z, y, x: (z, y, x + 1))
@@ -579,14 +579,14 @@
     slab, corner = shape(SLAB_ROWS, 128), shape(CORNER_ROWS, 128)
     rows = call(pack_rows, shape(ROW_TOTAL, 128), uvw)
     got = moved(rows, across)
-    to_same, to_cross, corner_left, corner_right = call(pack, [slab, slab, corner, corner], after(uvw, rows))
+    to_same, to_cross, keep, give = call(pack, [slab, slab, corner, corner], after(uvw, rows))
     from_same = moved(to_same, same)
     from_cross = moved(to_cross, beside)
-    corner_right = moved(corner_right, lambda z, y, x: (z, 2 * (2 - y), x + 1) if y in (1, 2) else None)
-    corner_left = moved(corner_left, lambda z, y, x: (z, 5 - 2 * y, x - 1) if y in (1, 2) else None)
+    corner = call(pick_corner, corner, keep, to_other(give))
+    corner = moved(corner, lambda z, y, x: (z, 3 - y, x + (1 if y & 1 else -1)))
     other = to_other(uvw)
-    shared = to_other(after(got, from_same, from_cross, corner_left, corner_right))
-    parts = (uvw, other, got, shared, from_same, from_cross, corner_left, corner_right)
+    shared = to_other(after(got, from_same, from_cross, corner))
+    parts = (uvw, other, got, shared, from_same, from_cross, corner)
     stack = shape(STEPS, PLANE, 128)
     work = [pltpu.VMEM((2, PLANE, 128), F32), pltpu.VMEM((4, PLANE, 128), F32)]
     uvs = call(assemble, shape(2 * STEPS, PLANE, 128), *parts, scratch=work)
@@ -609,6 +609,9 @@
                     return (z - 1, ty, tx)
                 return to
 
+            def only(where):
+                return lambda z, y, x: where(z, y, x) if z == active else None
+
             def over(z, y, x):
                 return (z, y ^ 2, x)
 
@@ -619,7 +622,7 @@
             main = moved(main, down(lambda z, y, x: (z, y, x)))
             halo = moved(strip, down(over))
             side = moved(side, down(beside))
-            edge_piece = moved(strip, down(corner_of))
+            edge_piece = moved(strip, only(down(corner_of)))
             main, halo, side, edge_piece = lax.optimization_barrier((main, halo, side, edge_piece))
             pieces = (main, to_other(main), side, halo, to_other(halo), edge_piece)
             if ws is None:
@@ -630,7 +633,7 @@
         [shape(STEPS, 128, 128), shape(count, 128, 128)],
         layers, ws,
         scratch=[
-            pltpu.VMEM((PLANE, 128), F32), pltpu.VMEM((STEPS, 128, 128), F32), pltpu.VMEM((256, 128), jnp.bfloat16)
+            pltpu.VMEM((4, PLANE, 128), F32), pltpu.VMEM((STEPS, 128, 128), F32), pltpu.VMEM((256, 128), jnp.bfloat16)
         ],
     )
     given = to_other(given)

time: 127 us -> 120 us (0.945)
  starting transfers between devices: 73.4 us -> 68.8 us
  Pallas kernels: 16.3 us -> 12.8 us
  local copies, waits for them, and re-layouts: 3.68 us -> 6.21 us
  waiting for transfers between devices: 33.7 us -> 32.1 us
    ppermute x33, starting transfers between devices: 73.4 us -> 68.8 us  [moved(): return lax.ppermute(value, AXES, pairs)]
    pallas_call x14, Pallas kernels: 16.3 us -> 12.8 us  [call(): pl.pallas_call(kernel, out_shape=outs, scratch_shapes=list(scratch), comp...]
    slice x0 -> x3, local copies, waits for them, and re-layouts: none -> 2.53 us  [per_device(): lowest_planes = jnp.stack([printed[0], filtered[0], sensitivity[0]])]
    ppermute x33, waiting for transfers between devices: 33.7 us -> 32.1 us  [moved(): return lax.ppermute(value, AXES, pairs)]
    unnamed x10 -> x8, local copies, waits for them, and re-layouts: 3.68 us -> 3.68 us
where the time goes in v5:
time: 120 us
  starting transfers between devices  68.8 us (57%)
  waiting for transfers between devices  32.1 us (27%)
  Pallas kernels  12.8 us (11%)
  local copies, waits for them, and re-layouts  6.21 us (5%)
    ppermute x33, starting transfers between devices, moved(): return lax.ppermute(value, AXES, pairs)  68.8 us
    ppermute x33, waiting for transfers between devices, moved(): return lax.ppermute(value, AXES, pairs)  32.1 us
    pallas_call x14, Pallas kernels, call(): pl.pallas_call(kernel, out_shape=outs, scratch_shapes=list(scratch), comp...  12.8 us
    unnamed x8, local copies, waits for them, and re-layouts  3.68 us
    slice x3, local copies, waits for them, and re-layouts, per_device(): lowest_planes = jnp.stack([printed[0], filtered[0], sensitivity[0]])  2.53 us
  transfers between devices with their start and end apart: 33, of which 14 were waited for; matrix products, arithmetic and copies ran while one was open for 0% of the time, Pallas kernels for 3%

profile of v5, /device:TPU:1, one launch (start us, length us, event | category | flops | bytes accessed | tf_op | source)
XLA Modules:
  0.0 120.1 jit_solution(15744206250158603419)
XLA Ops:
  2.5 3.6 %collective-permute-start = (f32[3,128,128]{2,1,0:T(8,128)S(1)}, f32[3,128,128]{2,1,0:T(8,128)S(1)}, u32[]{:S(2)}, u32[]{:S(2)}) collective-permute-start(f32[3,128,128]{2,1,0:T(8,128)S(1)} %pad_maximum_fusion), channel_id=1, source_target_pairs={{0,192},{1,193},{2,194},{3,195},{4,196},{5,197},{6,198},{7,199},{8... | collective-permute-start | bytes 589832 | tf_op jit(solution)/shard_map/ppermute | solution.py:77
  10.5 3.0 %collective-permute-start.3 = (f32[16,128]{1,0:T(8,128)S(1)}, f32[16,128]{1,0:T(8,128)S(1)}, u32[]{:S(2)}, u32[]{:S(2)}) collective-permute-start(f32[16,128]{1,0:T(8,128)S(1)} %get-tuple-element.47), channel_id=1, source_target_pairs={{0,1},{1,2},{2,3},{3,4},{4,5},{5,6},{6,7},{7,8},{8,9},{9,10},{10,1... | collective-permute-start | bytes 24584 | tf_op jit(solution)/shard_map/ppermute | solution.py:77
  13.5 4.3 %collective-permute-start.4 = (f32[16,128]{1,0:T(8,128)S(1)}, f32[16,128]{1,0:T(8,128)S(1)}, u32[]{:S(2)}, u32[]{:S(2)}) collective-permute-start(f32[16,128]{1,0:T(8,128)S(1)} %get-tuple-element.48), channel_id=1, source_target_pairs={{0,15},{1,0},{2,1},{3,2},{4,3},{5,4},{6,5},{7,6},{8,7},{9,8},{10,9... | collective-permute-start | bytes 24584 | tf_op jit(solution)/shard_map/ppermute | solution.py:77
  21.4 2.0 %all_terms.1.uvw_ref = f32[51,128,128]{2,1,0:T(8,128)S(1)} custom-call(f32[16,128,128]{2,1,0:T(8,128)S(1)} %copy-done, f32[16,128,128]{2,1,0:T(8,128)S(1)} %copy-done.1, f32[16,128,128]{2,1,0:T(8,128)S(1)} %copy-done.2, f32[3,128,128]{2,1,0:T(8,128)S(1)} %collective-permute-done.above_ref, f32[16,128]{1,0:T(8,128)S(1)} %collective-permute-done.1.inner_ref, ...), custom_call_target="tpu_custom_call" | custom-call | bytes 7500000 | tf_op jit(solution)/shard_map/all_terms/pallas_call | solution.py:88
  24.8 2.5 %collective-permute-start.6 = (f32[656,128]{1,0:T(8,128)S(1)}, f32[656,128]{1,0:T(8,128)S(1)}, u32[]{:S(2)}, u32[]{:S(2)}) collective-permute-start(f32[656,128]{1,0:T(8,128)S(1)} %pack_rows.1), channel_id=1, source_target_pairs={{16,32},{17,33},{18,34},{19,35},{20,36},{21,37},{22,38},{23,39},{2... | collective-permute-start | bytes 1007624 | tf_op jit(solution)/shard_map/ppermute | solution.py:77
  27.2 1.7 %pack.1 = (f32[480,128]{1,0:T(8,128)S(1)}, f32[480,128]{1,0:T(8,128)S(1)}, f32[96,128]{1,0:T(8,128)S(1)}, f32[96,128]{1,0:T(8,128)S(1)}) custom-call(f32[51,128,128]{2,1,0:T(8,128)S(1)} %all_terms.1.uvw_ref), custom_call_target="tpu_custom_call" | custom-call | bytes 1500000 | tf_op jit(solution)/shard_map/pack/pallas_call | solution.py:88
  29.0 6.0 %collective-permute-start.7 = (f32[480,128]{1,0:T(8,128)S(1)}, f32[480,128]{1,0:T(8,128)S(1)}, u32[]{:S(2)}, u32[]{:S(2)}) collective-permute-start(f32[480,128]{1,0:T(8,128)S(1)} %get-tuple-element.50), channel_id=1, source_target_pairs={{0,1},{1,2},{2,3},{3,4},{4,5},{5,6},{6,7},{7,8},{8,9},{9,10},{10,1... | collective-permute-start | bytes 737288 | tf_op jit(solution)/shard_map/ppermute | solution.py:77
  37.6 9.1 %collective-permute-done.10.corner_ref = f32[96,128]{1,0:T(8,128)S(1)} collective-permute-done((f32[96,128]{1,0:T(8,128)S(1)}, f32[96,128]{1,0:T(8,128)S(1)}, u32[]{:S(2)}, u32[]{:S(2)}) %collective-permute-start.10) | collective-permute-done | bytes 49184 | tf_op jit(solution)/shard_map/ppermute | solution.py:77
  46.7 2.8 %collective-permute-start.11 = (f32[656,128]{1,0:T(8,128)S(1)}, f32[656,128]{1,0:T(8,128)S(1)}, u32[]{:S(2)}, u32[]{:S(2)}) collective-permute-start(f32[656,128]{1,0:T(8,128)S(1)} %collective-permute-done.6.got_ref), channel_id=1, source_target_pairs={{0,16},{1,17},{2,18},{3,19},{4,20},{5,21},{6,22},{7,23},{8,24},{9,... | collective-permute-start | bytes 1007624 | tf_op jit(solution)/shard_map/ppermute | solution.py:77
  50.7 2.0 %assemble.1.refs_0_ = f32[34,288,128]{2,1,0:T(8,128)S(1)} custom-call(f32[51,128,128]{2,1,0:T(8,128)S(1)} %all_terms.1.uvw_ref, f32[51,128,128]{2,1,0:T(8,128)S(1)} %collective-permute-done.5.other_ref, f32[656,128]{1,0:T(8,128)S(1)} %collective-permute-done.6.got_ref, f32[656,128]{1,0:T(8,128)S(1)} %collective-permute-done.11.shared_ref, ...), custom_call_target="tpu_custom_call" | custom-call | bytes 7500000 | tf_op jit(solution)/shard_map/assemble/pallas_call | solution.py:88
  52.7 1.9 %collective-permute-start.12 = (f32[128,128]{1,0:T(8,128)S(1)}, f32[128,128]{1,0:T(8,128)S(1)}, u32[]{:S(2)}, u32[]{:S(2)}) collective-permute-start(f32[128,128]{1,0:T(8,128)S(1)} %get-tuple-element.55), channel_id=1, source_target_pairs={{0,192},{1,193},{2,194},{3,195},{4,196},{5,197},{6,198},{7,199},{8... | collective-permute-start | bytes 196616 | tf_op jit(solution)/shard_map/ppermute | solution.py:77
  55.3 5.1 %collective-permute-start.13 = (f32[24,128]{1,0:T(8,128)S(1)}, f32[24,128]{1,0:T(8,128)S(1)}, u32[]{:S(2)}, u32[]{:S(2)}) collective-permute-start(f32[24,128]{1,0:T(8,128)S(1)} %get-tuple-element.56), channel_id=1, source_target_pairs={{0,224},{1,225},{2,226},{3,227},{4,228},{5,229},{6,230},{7,231},{8... | collective-permute-start | bytes 36872 | tf_op jit(solution)/shard_map/ppermute | solution.py:77
  61.2 5.7 %collective-permute-start.16 = (f32[128,128]{1,0:T(8,128)S(1)}, f32[128,128]{1,0:T(8,128)S(1)}, u32[]{:S(2)}, u32[]{:S(2)}) collective-permute-start(f32[128,128]{1,0:T(8,128)S(1)} %collective-permute-done.12.refs_1_), channel_id=1, source_target_pairs={{0,16},{1,17},{2,18},{3,19},{4,20},{5,21},{6,22},{7,23},{8,24},{9,... | collective-permute-start | bytes 196616 | tf_op jit(solution)/shard_map/ppermute | solution.py:77
  68.3 4.1 %collective-permute-start.18 = (f32[128,128]{1,0:T(8,128)S(1)}, f32[128,128]{1,0:T(8,128)S(1)}, u32[]{:S(2)}, u32[]{:S(2)}) collective-permute-start(f32[128,128]{1,0:T(8,128)S(1)} %get-tuple-element.63), channel_id=1, source_target_pairs={{0,192},{1,193},{2,194},{3,195},{4,196},{5,197},{6,198},{7,199},{8... | collective-permute-start | bytes 196616 | tf_op jit(solution)/shard_map/ppermute | solution.py:77
  73.1 1.7 %collective-permute-start.19 = (f32[24,128]{1,0:T(8,128)S(1)}, f32[24,128]{1,0:T(8,128)S(1)}, u32[]{:S(2)}, u32[]{:S(2)}) collective-permute-start(f32[24,128]{1,0:T(8,128)S(1)} %get-tuple-element.64), channel_id=1, source_target_pairs={{0,224},{1,225},{2,226},{3,227},{4,228},{5,229},{6,230},{7,231},{8... | collective-permute-start | bytes 36872 | tf_op jit(solution)/shard_map/ppermute | solution.py:77
  74.8 1.8 %collective-permute-done.19.refs_4_ = f32[24,128]{1,0:T(8,128)S(1)} collective-permute-done((f32[24,128]{1,0:T(8,128)S(1)}, f32[24,128]{1,0:T(8,128)S(1)}, u32[]{:S(2)}, u32[]{:S(2)}) %collective-permute-start.19) | collective-permute-done | bytes 12320 | tf_op jit(solution)/shard_map/ppermute | solution.py:77
  77.9 3.9 %collective-permute-start.22 = (f32[128,128]{1,0:T(8,128)S(1)}, f32[128,128]{1,0:T(8,128)S(1)}, u32[]{:S(2)}, u32[]{:S(2)}) collective-permute-start(f32[128,128]{1,0:T(8,128)S(1)} %collective-permute-done.18.refs_1_), channel_id=1, source_target_pairs={{0,16},{1,17},{2,18},{3,19},{4,20},{5,21},{6,22},{7,23},{8,24},{9,... | collective-permute-start | bytes 196616 | tf_op jit(solution)/shard_map/ppermute | solution.py:77
  83.2 4.6 %collective-permute-start.24 = (f32[128,128]{1,0:T(8,128)S(1)}, f32[128,128]{1,0:T(8,128)S(1)}, u32[]{:S(2)}, u32[]{:S(2)}) collective-permute-start(f32[128,128]{1,0:T(8,128)S(1)} %get-tuple-element.71), channel_id=1, source_target_pairs={{0,192},{1,193},{2,194},{3,195},{4,196},{5,197},{6,198},{7,199},{8... | collective-permute-start | bytes 196616 | tf_op jit(solution)/shard_map/ppermute | solution.py:77
  89.1 2.4 %collective-permute-start.25 = (f32[24,128]{1,0:T(8,128)S(1)}, f32[24,128]{1,0:T(8,128)S(1)}, u32[]{:S(2)}, u32[]{:S(2)}) collective-permute-start(f32[24,128]{1,0:T(8,128)S(1)} %get-tuple-element.72), channel_id=1, source_target_pairs={{0,224},{1,225},{2,226},{3,227},{4,228},{5,229},{6,230},{7,231},{8... | collective-permute-start | bytes 36872 | tf_op jit(solution)/shard_map/ppermute | solution.py:77
  91.4 4.4 %collective-permute-done.27.refs_6_ = f32[24,128]{1,0:T(8,128)S(1)} collective-permute-done((f32[24,128]{1,0:T(8,128)S(1)}, f32[24,128]{1,0:T(8,128)S(1)}, u32[]{:S(2)}, u32[]{:S(2)}) %collective-permute-start.27) | collective-permute-done | bytes 12320 | tf_op jit(solution)/shard_map/ppermute | solution.py:77
  95.9 5.3 %collective-permute-start.28 = (f32[128,128]{1,0:T(8,128)S(1)}, f32[128,128]{1,0:T(8,128)S(1)}, u32[]{:S(2)}, u32[]{:S(2)}) collective-permute-start(f32[128,128]{1,0:T(8,128)S(1)} %collective-permute-done.24.refs_1_), channel_id=1, source_target_pairs={{0,16},{1,17},{2,18},{3,19},{4,20},{5,21},{6,22},{7,23},{8,24},{9,... | collective-permute-start | bytes 196616 | tf_op jit(solution)/shard_map/ppermute | solution.py:77
  104.1 1.9 %smooth.1 = (f32[17,128,128]{2,1,0:T(8,128)S(1)}, f32[9,128,128]{2,1,0:T(8,128)S(1)}) custom-call(f32[17,288,128]{2,1,0:T(8,128)S(1)} %section.7.layers_ref, f32[17,288,128]{2,1,0:T(8,128)S(1)} %assemble_w.1.w_ref), custom_call_target="tpu_custom_call" | custom-call | bytes 12000000 | tf_op jit(solution)/shard_map/smooth/pallas_call | solution.py:88
  111.1 4.3 %collective-permute-done.32.above_ref = f32[3,128,128]{2,1,0:T(8,128)S(1)} collective-permute-done((f32[3,128,128]{2,1,0:T(8,128)S(1)}, f32[3,128,128]{2,1,0:T(8,128)S(1)}, u32[]{:S(2)}, u32[]{:S(2)}) %collective-permute-start.32) | collective-permute-done | bytes 196640 | tf_op jit(solution)/shard_map/ppermute | solution.py:77
  115.4 3.2 %collective-permute-done.31.below_ref = f32[5,128,128]{2,1,0:T(8,128)S(1)} collective-permute-done((f32[5,128,128]{2,1,0:T(8,128)S(1)}, f32[5,128,128]{2,1,0:T(8,128)S(1)}, u32[]{:S(2)}, u32[]{:S(2)}) %collective-permute-start.31) | collective-permute-done | bytes 327712 | tf_op jit(solution)/shard_map/ppermute | solution.py:77
  (68 shorter events, 32.6 us)
Async XLA Ops:
  2.5 16.4 %collective-permute-start = (f32[3,128,128]{2,1,0:T(8,128)S(1)}, f32[3,128,128]{2,1,0:T(8,128)S(1)}, u32[]{:S(2)}, u32[]{:S(2)}) collective-permute-start(f32[3,128,128]{2,1,0:T(8,128)S(1)} %pad_maximum_fusion), channel_id=1, source_target_pairs={{0,192},{1,193},{2,194},{3,195},{4,196},{5,197},{6,198},{7,199},{8... | collective-permute-start | bytes 589832 | tf_op jit(solution)/shard_map/ppermute | solution.py:77
  7.8 10.0 %collective-permute-start.1 = (f32[16,128]{1,0:T(8,128)S(1)}, f32[16,128]{1,0:T(8,128)S(1)}, u32[]{:S(2)}, u32[]{:S(2)}) collective-permute-start(f32[16,128]{1,0:T(8,128)S(1)} %get-tuple-element.45), channel_id=1, source_target_pairs={{0,16},{1,17},{2,18},{3,19},{4,20},{5,21},{6,22},{7,23},{8,24},{9,... | collective-permute-start | bytes 24584 | tf_op jit(solution)/shard_map/ppermute | solution.py:77
  8.8 8.9 %collective-permute-start.2 = (f32[16,128]{1,0:T(8,128)S(1)}, f32[16,128]{1,0:T(8,128)S(1)}, u32[]{:S(2)}, u32[]{:S(2)}) collective-permute-start(f32[16,128]{1,0:T(8,128)S(1)} %get-tuple-element.46), channel_id=1, source_target_pairs={{0,48},{1,49},{2,50},{3,51},{4,52},{5,53},{6,54},{7,55},{8,56},{9,... | collective-permute-start | bytes 24584 | tf_op jit(solution)/shard_map/ppermute | solution.py:77
  10.5 8.4 %collective-permute-start.3 = (f32[16,128]{1,0:T(8,128)S(1)}, f32[16,128]{1,0:T(8,128)S(1)}, u32[]{:S(2)}, u32[]{:S(2)}) collective-permute-start(f32[16,128]{1,0:T(8,128)S(1)} %get-tuple-element.47), channel_id=1, source_target_pairs={{0,1},{1,2},{2,3},{3,4},{4,5},{5,6},{6,7},{7,8},{8,9},{9,10},{10,1... | collective-permute-start | bytes 24584 | tf_op jit(solution)/shard_map/ppermute | solution.py:77
  13.5 5.5 %collective-permute-start.4 = (f32[16,128]{1,0:T(8,128)S(1)}, f32[16,128]{1,0:T(8,128)S(1)}, u32[]{:S(2)}, u32[]{:S(2)}) collective-permute-start(f32[16,128]{1,0:T(8,128)S(1)} %get-tuple-element.48), channel_id=1, source_target_pairs={{0,15},{1,0},{2,1},{3,2},{4,3},{5,4},{6,5},{7,6},{8,7},{9,8},{10,9... | collective-permute-start | bytes 24584 | tf_op jit(solution)/shard_map/ppermute | solution.py:77
  23.3 27.4 %collective-permute-start.5 = (f32[51,128,128]{2,1,0:T(8,128)S(1)}, f32[51,128,128]{2,1,0:T(8,128)S(1)}, u32[]{:S(2)}, u32[]{:S(2)}) collective-permute-start(f32[51,128,128]{2,1,0:T(8,128)S(1)} %all_terms.1.uvw_ref), channel_id=1, source_target_pairs={{0,16},{1,17},{2,18},{3,19},{4,20},{5,21},{6,22},{7,23},{8,24},{9,... | collective-permute-start | bytes 10027016 | tf_op jit(solution)/shard_map/ppermute | solution.py:77
  24.8 21.9 %collective-permute-start.6 = (f32[656,128]{1,0:T(8,128)S(1)}, f32[656,128]{1,0:T(8,128)S(1)}, u32[]{:S(2)}, u32[]{:S(2)}) collective-permute-start(f32[656,128]{1,0:T(8,128)S(1)} %pack_rows.1), channel_id=1, source_target_pairs={{16,32},{17,33},{18,34},{19,35},{20,36},{21,37},{22,38},{23,39},{2... | collective-permute-start | bytes 1007624 | tf_op jit(solution)/shard_map/ppermute | solution.py:77
  29.0 17.7 %collective-permute-start.7 = (f32[480,128]{1,0:T(8,128)S(1)}, f32[480,128]{1,0:T(8,128)S(1)}, u32[]{:S(2)}, u32[]{:S(2)}) collective-permute-start(f32[480,128]{1,0:T(8,128)S(1)} %get-tuple-element.50), channel_id=1, source_target_pairs={{0,1},{1,2},{2,3},{3,4},{4,5},{5,6},{6,7},{7,8},{8,9},{9,10},{10,1... | collective-permute-start | bytes 737288 | tf_op jit(solution)/shard_map/ppermute | solution.py:77
  35.0 11.7 %collective-permute-start.8 = (f32[480,128]{1,0:T(8,128)S(1)}, f32[480,128]{1,0:T(8,128)S(1)}, u32[]{:S(2)}, u32[]{:S(2)}) collective-permute-start(f32[480,128]{1,0:T(8,128)S(1)} %get-tuple-element.51), channel_id=1, source_target_pairs={{0,31},{1,16},{2,17},{3,18},{4,19},{5,20},{6,21},{7,22},{8,23},{9,... | collective-permute-start | bytes 737288 | tf_op jit(solution)/shard_map/ppermute | solution.py:77
  36.4 10.3 %collective-permute-start.10 = (f32[96,128]{1,0:T(8,128)S(1)}, f32[96,128]{1,0:T(8,128)S(1)}, u32[]{:S(2)}, u32[]{:S(2)}) collective-permute-start(f32[96,128]{1,0:T(8,128)S(1)} %pick_corner.1), channel_id=1, source_target_pairs={{0,63},{1,48},{2,49},{3,50},{4,51},{5,52},{6,53},{7,54},{8,55},{9,... | collective-permute-start | bytes 147464 | tf_op jit(solution)/shard_map/ppermute | solution.py:77
  52.7 8.5 %collective-permute-start.12 = (f32[128,128]{1,0:T(8,128)S(1)}, f32[128,128]{1,0:T(8,128)S(1)}, u32[]{:S(2)}, u32[]{:S(2)}) collective-permute-start(f32[128,128]{1,0:T(8,128)S(1)} %get-tuple-element.55), channel_id=1, source_target_pairs={{0,192},{1,193},{2,194},{3,195},{4,196},{5,197},{6,198},{7,199},{8... | collective-permute-start | bytes 196616 | tf_op jit(solution)/shard_map/ppermute | solution.py:77
  54.7 6.6 %collective-permute-start.14 = (f32[64,128]{1,0:T(8,128)S(1)}, f32[64,128]{1,0:T(8,128)S(1)}, u32[]{:S(2)}, u32[]{:S(2)}) collective-permute-start(f32[64,128]{1,0:T(8,128)S(1)} %get-tuple-element.57), channel_id=1, source_target_pairs={{0,223},{1,208},{2,209},{3,210},{4,211},{5,212},{6,213},{7,214},{8... | collective-permute-start | bytes 98312 | tf_op jit(solution)/shard_map/ppermute | solution.py:77
  54.7 5.7 %collective-permute-start.15 = (f32[24,128]{1,0:T(8,128)S(1)}, f32[24,128]{1,0:T(8,128)S(1)}, u32[]{:S(2)}, u32[]{:S(2)}) collective-permute-start(f32[24,128]{1,0:T(8,128)S(1)} %get-tuple-element.56), channel_id=1, source_target_pairs={{192,191},{193,176},{194,177},{195,178},{196,179},{197,180},{198,1... | collective-permute-start | bytes 36872 | tf_op jit(solution)/shard_map/ppermute | solution.py:77
  55.3 5.9 %collective-permute-start.13 = (f32[24,128]{1,0:T(8,128)S(1)}, f32[24,128]{1,0:T(8,128)S(1)}, u32[]{:S(2)}, u32[]{:S(2)}) collective-permute-start(f32[24,128]{1,0:T(8,128)S(1)} %get-tuple-element.56), channel_id=1, source_target_pairs={{0,224},{1,225},{2,226},{3,227},{4,228},{5,229},{6,230},{7,231},{8... | collective-permute-start | bytes 36872 | tf_op jit(solution)/shard_map/ppermute | solution.py:77
  61.2 6.9 %collective-permute-start.16 = (f32[128,128]{1,0:T(8,128)S(1)}, f32[128,128]{1,0:T(8,128)S(1)}, u32[]{:S(2)}, u32[]{:S(2)}) collective-permute-start(f32[128,128]{1,0:T(8,128)S(1)} %collective-permute-done.12.refs_1_), channel_id=1, source_target_pairs={{0,16},{1,17},{2,18},{3,19},{4,20},{5,21},{6,22},{7,23},{8,24},{9,... | collective-permute-start | bytes 196616 | tf_op jit(solution)/shard_map/ppermute | solution.py:77
  68.3 9.6 %collective-permute-start.18 = (f32[128,128]{1,0:T(8,128)S(1)}, f32[128,128]{1,0:T(8,128)S(1)}, u32[]{:S(2)}, u32[]{:S(2)}) collective-permute-start(f32[128,128]{1,0:T(8,128)S(1)} %get-tuple-element.63), channel_id=1, source_target_pairs={{0,192},{1,193},{2,194},{3,195},{4,196},{5,197},{6,198},{7,199},{8... | collective-permute-start | bytes 196616 | tf_op jit(solution)/shard_map/ppermute | solution.py:77
  72.4 5.5 %collective-permute-start.20 = (f32[64,128]{1,0:T(8,128)S(1)}, f32[64,128]{1,0:T(8,128)S(1)}, u32[]{:S(2)}, u32[]{:S(2)}) collective-permute-start(f32[64,128]{1,0:T(8,128)S(1)} %get-tuple-element.65), channel_id=1, source_target_pairs={{0,223},{1,208},{2,209},{3,210},{4,211},{5,212},{6,213},{7,214},{8... | collective-permute-start | bytes 98312 | tf_op jit(solution)/shard_map/ppermute | solution.py:77
  83.2 12.7 %collective-permute-start.24 = (f32[128,128]{1,0:T(8,128)S(1)}, f32[128,128]{1,0:T(8,128)S(1)}, u32[]{:S(2)}, u32[]{:S(2)}) collective-permute-start(f32[128,128]{1,0:T(8,128)S(1)} %get-tuple-element.71), channel_id=1, source_target_pairs={{0,192},{1,193},{2,194},{3,195},{4,196},{5,197},{6,198},{7,199},{8... | collective-permute-start | bytes 196616 | tf_op jit(solution)/shard_map/ppermute | solution.py:77
  87.8 8.1 %collective-permute-start.26 = (f32[64,128]{1,0:T(8,128)S(1)}, f32[64,128]{1,0:T(8,128)S(1)}, u32[]{:S(2)}, u32[]{:S(2)}) collective-permute-start(f32[64,128]{1,0:T(8,128)S(1)} %get-tuple-element.73), channel_id=1, source_target_pairs={{0,223},{1,208},{2,209},{3,210},{4,211},{5,212},{6,213},{7,214},{8... | collective-permute-start | bytes 98312 | tf_op jit(solution)/shard_map/ppermute | solution.py:77
  87.8 8.0 %collective-permute-start.27 = (f32[24,128]{1,0:T(8,128)S(1)}, f32[24,128]{1,0:T(8,128)S(1)}, u32[]{:S(2)}, u32[]{:S(2)}) collective-permute-start(f32[24,128]{1,0:T(8,128)S(1)} %get-tuple-element.72), channel_id=1, source_target_pairs={{64,63},{65,48},{66,49},{67,50},{68,51},{69,52},{70,53},{71,54},{7... | collective-permute-start | bytes 36872 | tf_op jit(solution)/shard_map/ppermute | solution.py:77
  89.1 6.8 %collective-permute-start.25 = (f32[24,128]{1,0:T(8,128)S(1)}, f32[24,128]{1,0:T(8,128)S(1)}, u32[]{:S(2)}, u32[]{:S(2)}) collective-permute-start(f32[24,128]{1,0:T(8,128)S(1)} %get-tuple-element.72), channel_id=1, source_target_pairs={{0,224},{1,225},{2,226},{3,227},{4,228},{5,229},{6,230},{7,231},{8... | collective-permute-start | bytes 36872 | tf_op jit(solution)/shard_map/ppermute | solution.py:77
  95.9 6.6 %collective-permute-start.28 = (f32[128,128]{1,0:T(8,128)S(1)}, f32[128,128]{1,0:T(8,128)S(1)}, u32[]{:S(2)}, u32[]{:S(2)}) collective-permute-start(f32[128,128]{1,0:T(8,128)S(1)} %collective-permute-done.24.refs_1_), channel_id=1, source_target_pairs={{0,16},{1,17},{2,18},{3,19},{4,20},{5,21},{6,22},{7,23},{8,24},{9,... | collective-permute-start | bytes 196616 | tf_op jit(solution)/shard_map/ppermute | solution.py:77
  108.4 10.2 %collective-permute-start.31 = (f32[5,128,128]{2,1,0:T(8,128)S(1)}, f32[5,128,128]{2,1,0:T(8,128)S(1)}, u32[]{:S(2)}, u32[]{:S(2)}) collective-permute-start(f32[5,128,128]{2,1,0:T(8,128)S(1)} %get-tuple-element.83), channel_id=1, source_target_pairs={{0,64},{1,65},{2,66},{3,67},{4,68},{5,69},{6,70},{7,71},{8,72},{9,... | collective-permute-start | bytes 983048 | tf_op jit(solution)/shard_map/ppermute | solution.py:77
  109.6 5.8 %collective-permute-start.32 = (f32[3,128,128]{2,1,0:T(8,128)S(1)}, f32[3,128,128]{2,1,0:T(8,128)S(1)}, u32[]{:S(2)}, u32[]{:S(2)}) collective-permute-start(f32[3,128,128]{2,1,0:T(8,128)S(1)} %get-tuple-element.84), channel_id=1, source_target_pairs={{0,192},{1,193},{2,194},{3,195},{4,196},{5,197},{6,198},{7,199},{8... | collective-permute-start | bytes 589832 | tf_op jit(solution)/shard_map/ppermute | solution.py:77
  (13 other events, 40.4 us)

commit v6 on v5

--- a/solution.py
+++ b/solution.py
@@ -150,7 +150,11 @@
     return x32 * (x4 * (x2 * x))
 
 
-def edges(p_ref, inner_ref, outer_ref, left_ref, right_ref, turned):
+def edges(p_ref, f_ref, s_ref, lowest_ref, inner_ref, outer_ref, left_ref, right_ref, turned, sems):
+    copies = [pltpu.make_async_copy(ref.at[0], lowest_ref.at[i + 1], sems.at[i]) for i, ref in enumerate((f_ref, s_ref))]
+    for copy in copies:
+        copy.start()
+    lowest_ref[0] = p_ref[0]
     lane = lanes(128)
     c = core()
     packed = jnp.zeros((128, 128), F32)
@@ -162,6 +166,8 @@
     turned[...] = packed.T
     right_ref[...] = turned[pl.ds(0, 16, stride=2), :]
     left_ref[...] = turned[pl.ds(1, 16, stride=2), :]
+    for copy in copies:
+        copy.wait()
 
 
 def norm_of(position, extent):
@@ -215,15 +221,33 @@
     return power40(turned[...].T)
 
 
-def all_terms(sizes, p_ref, f_ref, s_ref, above_ref, inner_ref, outer_ref, left_ref, right_ref, uvw_ref, powers, turned):
+def all_terms(
+    sizes, p_ref, f_hbm, s_hbm, above_ref, inner_ref, outer_ref, left_ref, right_ref,
+    uvw_ref, powers, turned, f_ref, s_ref, sems,
+):
+    def fetch(part):
+        here = pl.ds(4 * part, 4)
+        return [
+            pltpu.make_async_copy(hbm.at[here], ref.at[here], sems.at[i, part])
+            for i, (hbm, ref) in enumerate(((f_hbm, f_ref), (s_hbm, s_ref)))
+        ]
+
+    for part in range(LAYERS // 4):
+        for copy in fetch(part):
+            copy.start()
     beside = columns_beside(left_ref, right_ref, turned)
     norms = 1.0 / plane_norms(sizes)
     gz = lax.axis_index("gz")
     layer0 = gz * LAYERS
+    for copy in fetch(0):
+        copy.wait()
     uvw_ref[0] = s_ref[0]
     uvw_ref[STEPS] = power39(p_ref[0])
     uvw_ref[2 * STEPS] = norms * (1.0 / norm_of(0 * layer0, sizes[0] * LAYERS))
     for layer in range(1, STEPS):
+        if layer % 4 == 0 and layer < LAYERS:
+            for copy in fetch(layer // 4):
+                copy.wait()
         total = neighbours(p_ref[layer - 1], layer - 1, inner_ref, outer_ref, beside, powers)
         if layer < LAYERS:
             p, f, s = p_ref[layer], f_ref[layer], s_ref[layer]
@@ -401,38 +425,41 @@
     return new
 
 
-def set_carry(carry, main_ref, other_ref, outer_ref, halo_ref, halo_other_ref, halo_outer_ref):
+def set_carry(carry, main_ref, outer_ref, halo_ref, halo_outer_ref):
     c = core()
     lane = lanes(64)
     mine = (lane >> 6) == c
     inside = one_if(jnp.logical_not(outside()))
+    begin = (1 - c) * (128 - REACH)
+    beyond = (lane >= begin) & (lane < begin + REACH)
     for i in range(4):
-        rows = pl.ds(64 * (i % 2), 64)
-        own, other = main_ref[rows, :], other_ref[rows, :]
-        if i < 2:
-            value = jnp.where(mine, own, other)
-        else:
-            value = pltpu.roll(jnp.where(mine, other, own), 64, 1)
+        value = main_ref[pl.ds(64 * (i % 2), 64), :]
+        if i >= 2:
+            value = pltpu.roll(value, 64, 1)
+        inner = pltpu.roll(main_ref[pl.ds(128, 64), :], (32 * (2 - c) - 32 * i) & 127, 1)
+        value = jnp.where(mine, value, inner)
         outer = pltpu.roll(outer_ref[...], (128 - 32 * i) % 128, 1) if i else outer_ref[...]
-        outer = outer * inside
-        begin = (1 - c) * (128 - REACH)
-        value = jnp.where((lane >= begin) & (lane < begin + REACH), outer, value)
-        carry[pl.ds(64 * i, 64), :] = value
+        carry[pl.ds(64 * i, 64), :] = jnp.where(beyond, outer * inside, value)
     lane = lanes(24)
-    value = jnp.where((lane >> 6) == c, halo_ref[...], halo_other_ref[...])
-    begin = (1 - c) * (128 - REACH)
-    value = jnp.where((lane >= begin) & (lane < begin + REACH), halo_outer_ref[...] * inside, value)
+    beyond = (lane >= begin) & (lane < begin + REACH)
     carry[pl.ds(256, 32), :] = jnp.zeros((32, 128), F32)
-    carry[pl.ds(aligned(256 + 8 * seam(), 8), 24), :] = value
+    carry[pl.ds(aligned(256 + 8 * seam(), 8), 24), :] = jnp.where(beyond, halo_outer_ref[...] * inside, halo_ref[...])
+
+
+def merge(main_ref, give_ref, got_ref, down_ref, halo_ref):
+    down_ref[pl.ds(0, 128), :] = main_ref[...]
+    down_ref[pl.ds(128, 64), :] = got_ref[pl.ds(0, 64), :]
+    rows = pl.ds(64, 24)
+    halo_ref[...] = jnp.where((lanes(24) >> 6) == core(), give_ref[rows, :], got_ref[rows, :])
 
 
 def section(active, *refs):
     uv_ref, refs = refs[0], refs[1:]
     pieces, before_ref = (), None
-    if active is not None and len(refs) > 5:
-        pieces, before_ref, refs = refs[:6], refs[6], refs[7:]
-    if len(refs) == 5:
-        layers_ref, main_ref, outer_ref, halo_ref, carry = refs
+    if len(refs) > 6 or len(refs) == 5 + 2:
+        pieces, before_ref, refs = refs[:4], refs[4], refs[5:]
+    if len(refs) == 6:
+        layers_ref, main_ref, outer_ref, give_ref, strip_ref, carry = refs
     else:
         layers_ref, carry = refs
         main_ref = None
@@ -458,14 +485,18 @@
         mine = (lane >> 6) == c
         main_ref[...] = jnp.where(mine, bottom[pl.ds(0, 128), :], pltpu.roll(bottom[pl.ds(128, 128), :], 64, 1))
         lane = lanes(64)
-        slab = jnp.zeros((64, 128), F32)
+        slab = inner = jnp.zeros((64, 128), F32)
         for i in range(4):
-            rolled = bottom[pl.ds(64 * i, 64), :]
-            rolled = pltpu.roll(rolled, 32 * i, 1) if i else rolled
+            block = bottom[pl.ds(64 * i, 64), :]
+            rolled = pltpu.roll(block, 32 * i, 1) if i else block
             begin = (32 * i + 128 - c * 32) & 127
             slab = jnp.where(((lane - begin) & 127) < 32, rolled, slab)
+            inner = jnp.where((lane >> 5) == i, pltpu.roll(block, (32 * i - 32 * (1 + c)) & 127, 1), inner)
         outer_ref[...] = slab
-        halo_ref[...] = bottom[pl.ds(aligned((1 - seam()) * 232, 8), 24), :]
+        give_ref[pl.ds(0, 64), :] = inner
+        strip = bottom[pl.ds(aligned((1 - seam()) * 232, 8), 24), :]
+        give_ref[pl.ds(64, 24), :] = strip
+        strip_ref[...] = strip
 
     if before_ref is not None:
         @pl.when(lax.axis_index("gz") != active)
@@ -564,9 +595,13 @@
     def same(z, y, x):
         return (z, y, x + (-1 if y & 1 else 1))
 
-    lowest_planes = jnp.stack([printed[0], filtered[0], sensitivity[0]])
+    hbm, vmem = pl.BlockSpec(memory_space=pltpu.HBM), pl.BlockSpec(memory_space=pltpu.VMEM)
+    lowest_planes, inner, outer, left, right = call(
+        edges, [shape(3, 128, 128)] + [edge] * 4, printed, filtered, sensitivity,
+        in_specs=[vmem, hbm, hbm],
+        scratch=[pltpu.VMEM((128, 128), F32), pltpu.SemaphoreType.DMA((2,))],
+    )
     above = moved(lowest_planes, lambda z, y, x: (z - 1, y, x))
-    inner, outer, left, right = call(edges, [edge] * 4, printed, scratch=[pltpu.VMEM((128, 128), F32)])
     from_left = moved(right, lambda z, y, x: (z, y, x + 1))
     from_right = moved(left, lambda z, y, x: (z, y, x - 1))
     outer = moved(outer, lambda z, y, x: (z, y ^ 3, x))
@@ -574,7 +609,12 @@
     uvw = call(
         functools.partial(all_terms, sizes), shape(3 * STEPS, 128, 128),
         printed, filtered, sensitivity, above, inner, outer, from_left, from_right,
-        scratch=[pltpu.VMEM((144, 128), F32), pltpu.VMEM((128, 128), F32)],
+        in_specs=[vmem, hbm, hbm] + [vmem] * 5,
+        scratch=[
+            pltpu.VMEM((144, 128), F32), pltpu.VMEM((128, 128), F32),
+            pltpu.VMEM((LAYERS, 128, 128), F32), pltpu.VMEM((LAYERS, 128, 128), F32),
+            pltpu.SemaphoreType.DMA((2, LAYERS // 4)),
+        ],
     )
     slab, corner = shape(SLAB_ROWS, 128), shape(CORNER_ROWS, 128)
     rows = call(pack_rows, shape(ROW_TOTAL, 128), uvw)
@@ -595,22 +635,19 @@
     for active in range(depth - 1, -1, -1):
         outs = [stack]
         if active > 0:
-            outs = outs + [plane, shape(64, 128), shape(24, 128)]
+            outs = outs + [plane, shape(64, 128), shape(88, 128), shape(24, 128)]
         layers, *sent = call(
             functools.partial(section, active), outs, uvs, *pieces, *before, scratch=[pltpu.VMEM((PLANE, 128), F32)]
         )
         before = (layers,)
         if active > 0:
-            main, side, strip = sent
+            main, side, give, strip = sent
 
             def down(where):
                 def to(z, y, x):
                     _, ty, tx = where(z, y, x)
-                    return (z - 1, ty, tx)
+                    return (z - 1, ty, tx) if z == active else None
                 return to
-
-            def only(where):
-                return lambda z, y, x: where(z, y, x) if z == active else None
 
             def over(z, y, x):
                 return (z, y ^ 2, x)
@@ -619,12 +656,12 @@
                 _, ty, tx = beside(z, y, x)
                 return (z, ty ^ 2, tx)
 
+            side = moved(side, down(beside))
+            edge_piece = moved(strip, down(corner_of))
+            main, halo = call(merge, [shape(192, 128), shape(24, 128)], main, give, to_other(give))
             main = moved(main, down(lambda z, y, x: (z, y, x)))
-            halo = moved(strip, down(over))
-            side = moved(side, down(beside))
-            edge_piece = moved(strip, only(down(corner_of)))
-            main, halo, side, edge_piece = lax.optimization_barrier((main, halo, side, edge_piece))
-            pieces = (main, to_other(main), side, halo, to_other(halo), edge_piece)
+            halo = moved(halo, down(over))
+            pieces = (main, side, halo, edge_piece)
             if ws is None:
                 ws = call(assemble_w, stack, after(uvw, side), *parts[1:], scratch=work)
     count = STEPS // 2 + 1

time: 120 us -> 107 us (0.89)
  starting transfers between devices: 68.8 us -> 43.9 us
  waiting for transfers between devices: 32.1 us -> 44.3 us
  local copies, waits for them, and re-layouts: 6.21 us -> 3.68 us
    ppermute x33 -> x30, starting transfers between devices: 68.8 us -> 43.9 us  [moved(): return lax.ppermute(value, AXES, pairs)]
    ppermute x33 -> x30, waiting for transfers between devices: 32.1 us -> 44.3 us  [moved(): return lax.ppermute(value, AXES, pairs)]
    slice x3 -> x0, local copies, waits for them, and re-layouts: 2.53 us -> none  [per_device(): lowest_planes = jnp.stack([printed[0], filtered[0], sensitivity[0]])]
    pallas_call x14 -> x17, Pallas kernels: 12.8 us -> 13.8 us  [call(): pl.pallas_call(kernel, out_shape=outs, scratch_shapes=list(scratch), comp...]
  transfers between devices with their start and end apart: 33 -> 30, of which waited for: 14 -> 12; matrix products, arithmetic and copies ran while one was open for 0% -> 0% of each run, Pallas kernels for 3% -> 3%
where the time goes in v6:
time: 107 us; the launch traced here: 106 us
  waiting for transfers between devices  44.3 us (41%)
  starting transfers between devices  43.9 us (41%)
  Pallas kernels  13.8 us (13%)
  local copies, waits for them, and re-layouts  3.68 us (3%)
    ppermute x30, waiting for transfers between devices, moved(): return lax.ppermute(value, AXES, pairs)  44.3 us
    ppermute x30, starting transfers between devices, moved(): return lax.ppermute(value, AXES, pairs)  43.9 us
    pallas_call x17, Pallas kernels, call(): pl.pallas_call(kernel, out_shape=outs, scratch_shapes=list(scratch), comp...  13.8 us
    unnamed x8, local copies, waits for them, and re-layouts  3.68 us
  transfers between devices with their start and end apart: 30, of which 12 were waited for; matrix products, arithmetic and copies ran while one was open for 0% of the time, Pallas kernels for 3%

profile of v6, /device:TPU:1, one launch (start us, length us, event | category | flops | bytes accessed | tf_op | source)
XLA Modules:
  0.0 106.0 jit_solution(12847100384073833129)
XLA Ops:
  4.3 3.6 %collective-permute-start = (f32[3,128,128]{2,1,0:T(8,128)S(1)}, f32[3,128,128]{2,1,0:T(8,128)S(1)}, u32[]{:S(2)}, u32[]{:S(2)}) collective-permute-start(f32[3,128,128]{2,1,0:T(8,128)S(1)} %get-tuple-element.43), channel_id=1, source_target_pairs={{0,192},{1,193},{2,194},{3,195},{4,196},{5,197},{6,198},{7,199},{8... | collective-permute-start | bytes 589832 | tf_op jit(solution)/shard_map/ppermute | solution.py:77
  8.8 1.5 %collective-permute-start.2 = (f32[16,128]{1,0:T(8,128)S(1)}, f32[16,128]{1,0:T(8,128)S(1)}, u32[]{:S(2)}, u32[]{:S(2)}) collective-permute-start(f32[16,128]{1,0:T(8,128)S(1)} %get-tuple-element.45), channel_id=1, source_target_pairs={{0,48},{1,49},{2,50},{3,51},{4,52},{5,53},{6,54},{7,55},{8,56},{9,... | collective-permute-start | bytes 24584 | tf_op jit(solution)/shard_map/ppermute | solution.py:77
  10.4 3.0 %collective-permute-start.3 = (f32[16,128]{1,0:T(8,128)S(1)}, f32[16,128]{1,0:T(8,128)S(1)}, u32[]{:S(2)}, u32[]{:S(2)}) collective-permute-start(f32[16,128]{1,0:T(8,128)S(1)} %get-tuple-element.46), channel_id=1, source_target_pairs={{0,1},{1,2},{2,3},{3,4},{4,5},{5,6},{6,7},{7,8},{8,9},{9,10},{10,1... | collective-permute-start | bytes 24584 | tf_op jit(solution)/shard_map/ppermute | solution.py:77
  13.4 4.3 %collective-permute-start.4 = (f32[16,128]{1,0:T(8,128)S(1)}, f32[16,128]{1,0:T(8,128)S(1)}, u32[]{:S(2)}, u32[]{:S(2)}) collective-permute-start(f32[16,128]{1,0:T(8,128)S(1)} %get-tuple-element.47), channel_id=1, source_target_pairs={{0,15},{1,0},{2,1},{3,2},{4,3},{5,4},{6,5},{7,6},{8,7},{9,8},{10,9... | collective-permute-start | bytes 24584 | tf_op jit(solution)/shard_map/ppermute | solution.py:77
  18.8 2.4 %all_terms.1.uvw_ref = f32[51,128,128]{2,1,0:T(8,128)S(1)} custom-call(f32[16,128,128]{2,1,0:T(8,128)S(1)} %copy-done, f32[16,128,128]{2,1,0:T(8,128)S(1)} %copy-done.1, f32[16,128,128]{2,1,0:T(8,128)S(1)} %copy-done.2, f32[3,128,128]{2,1,0:T(8,128)S(1)} %collective-permute-done.above_ref, f32[16,128]{1,0:T(8,128)S(1)} %collective-permute-done.1.inner_ref, ...), custom_call_target="tpu_custom_call" | custom-call | bytes 7500000 | tf_op jit(solution)/shard_map/all_terms/pallas_call | solution.py:88
  21.3 1.5 %collective-permute-start.5 = (f32[51,128,128]{2,1,0:T(8,128)S(1)}, f32[51,128,128]{2,1,0:T(8,128)S(1)}, u32[]{:S(2)}, u32[]{:S(2)}) collective-permute-start(f32[51,128,128]{2,1,0:T(8,128)S(1)} %all_terms.1.uvw_ref), channel_id=1, source_target_pairs={{0,16},{1,17},{2,18},{3,19},{4,20},{5,21},{6,22},{7,23},{8,24},{9,... | collective-permute-start | bytes 10027016 | tf_op jit(solution)/shard_map/ppermute | solution.py:77
  22.8 2.5 %collective-permute-start.6 = (f32[656,128]{1,0:T(8,128)S(1)}, f32[656,128]{1,0:T(8,128)S(1)}, u32[]{:S(2)}, u32[]{:S(2)}) collective-permute-start(f32[656,128]{1,0:T(8,128)S(1)} %pack_rows.1), channel_id=1, source_target_pairs={{16,32},{17,33},{18,34},{19,35},{20,36},{21,37},{22,38},{23,39},{2... | collective-permute-start | bytes 1007624 | tf_op jit(solution)/shard_map/ppermute | solution.py:77
  25.2 1.7 %pack.1 = (f32[480,128]{1,0:T(8,128)S(1)}, f32[480,128]{1,0:T(8,128)S(1)}, f32[96,128]{1,0:T(8,128)S(1)}, f32[96,128]{1,0:T(8,128)S(1)}) custom-call(f32[51,128,128]{2,1,0:T(8,128)S(1)} %all_terms.1.uvw_ref), custom_call_target="tpu_custom_call" | custom-call | bytes 1500000 | tf_op jit(solution)/shard_map/pack/pallas_call | solution.py:88
  27.0 6.0 %collective-permute-start.7 = (f32[480,128]{1,0:T(8,128)S(1)}, f32[480,128]{1,0:T(8,128)S(1)}, u32[]{:S(2)}, u32[]{:S(2)}) collective-permute-start(f32[480,128]{1,0:T(8,128)S(1)} %get-tuple-element.49), channel_id=1, source_target_pairs={{0,1},{1,2},{2,3},{3,4},{4,5},{5,6},{6,7},{7,8},{8,9},{9,10},{10,1... | collective-permute-start | bytes 737288 | tf_op jit(solution)/shard_map/ppermute | solution.py:77
  35.6 9.1 %collective-permute-done.10.corner_ref = f32[96,128]{1,0:T(8,128)S(1)} collective-permute-done((f32[96,128]{1,0:T(8,128)S(1)}, f32[96,128]{1,0:T(8,128)S(1)}, u32[]{:S(2)}, u32[]{:S(2)}) %collective-permute-start.10) | collective-permute-done | bytes 49184 | tf_op jit(solution)/shard_map/ppermute | solution.py:77
  44.7 2.8 %collective-permute-start.11 = (f32[656,128]{1,0:T(8,128)S(1)}, f32[656,128]{1,0:T(8,128)S(1)}, u32[]{:S(2)}, u32[]{:S(2)}) collective-permute-start(f32[656,128]{1,0:T(8,128)S(1)} %collective-permute-done.6.got_ref), channel_id=1, source_target_pairs={{0,16},{1,17},{2,18},{3,19},{4,20},{5,21},{6,22},{7,23},{8,24},{9,... | collective-permute-start | bytes 1007624 | tf_op jit(solution)/shard_map/ppermute | solution.py:77
  48.8 2.0 %assemble.1.refs_0_ = f32[34,288,128]{2,1,0:T(8,128)S(1)} custom-call(f32[51,128,128]{2,1,0:T(8,128)S(1)} %all_terms.1.uvw_ref, f32[51,128,128]{2,1,0:T(8,128)S(1)} %collective-permute-done.5.other_ref, f32[656,128]{1,0:T(8,128)S(1)} %collective-permute-done.6.got_ref, f32[656,128]{1,0:T(8,128)S(1)} %collective-permute-done.11.shared_ref, ...), custom_call_target="tpu_custom_call" | custom-call | bytes 7500000 | tf_op jit(solution)/shard_map/assemble/pallas_call | solution.py:88
  60.6 1.3 %collective-permute-start.23 = (f32[192,128]{1,0:T(8,128)S(1)}, f32[192,128]{1,0:T(8,128)S(1)}, u32[]{:S(2)}, u32[]{:S(2)}) collective-permute-start(f32[192,128]{1,0:T(8,128)S(1)} %get-tuple-element.70), channel_id=1, source_target_pairs={{64,0},{65,1},{66,2},{67,3},{68,4},{69,5},{70,6},{71,7},{72,8},{73... | collective-permute-start | bytes 294920 | tf_op jit(solution)/shard_map/ppermute | solution.py:77
  61.9 1.3 %collective-permute-start.24 = (f32[64,128]{1,0:T(8,128)S(1)}, f32[64,128]{1,0:T(8,128)S(1)}, u32[]{:S(2)}, u32[]{:S(2)}) collective-permute-start(f32[64,128]{1,0:T(8,128)S(1)} %get-tuple-element.71), channel_id=1, source_target_pairs={{64,31},{65,16},{66,17},{67,18},{68,19},{69,20},{70,21},{71,22},{7... | collective-permute-start | bytes 98312 | tf_op jit(solution)/shard_map/ppermute | solution.py:77
  67.0 18.2 %collective-permute-done.26.refs_4_ = f32[24,128]{1,0:T(8,128)S(1)} collective-permute-done((f32[24,128]{1,0:T(8,128)S(1)}, f32[24,128]{1,0:T(8,128)S(1)}, u32[]{:S(2)}, u32[]{:S(2)}) %collective-permute-start.26) | collective-permute-done | bytes 12320 | tf_op jit(solution)/shard_map/ppermute | solution.py:77
  85.2 2.0 %collective-permute-done.25.refs_3_ = f32[24,128]{1,0:T(8,128)S(1)} collective-permute-done((f32[24,128]{1,0:T(8,128)S(1)}, f32[24,128]{1,0:T(8,128)S(1)}, u32[]{:S(2)}, u32[]{:S(2)}) %collective-permute-start.25) | collective-permute-done | bytes 12320 | tf_op jit(solution)/shard_map/ppermute | solution.py:77
  87.2 1.8 %section.7.layers_ref = f32[17,288,128]{2,1,0:T(8,128)S(1)} custom-call(f32[34,288,128]{2,1,0:T(8,128)S(1)} %assemble.1.refs_0_, f32[192,128]{1,0:T(8,128)S(1)} %collective-permute-done.23.refs_1_, f32[64,128]{1,0:T(8,128)S(1)} %collective-permute-done.24.refs_2_, f32[24,128]{1,0:T(8,128)S(1)} %collective-permute-done.25.refs_3_, ...), custom_call_target="tpu_custom_call" | custom-call | bytes 7800000 | tf_op jit(solution)/shard_map/section/pallas_call | solution.py:88
  89.0 1.9 %smooth.1 = (f32[17,128,128]{2,1,0:T(8,128)S(1)}, f32[9,128,128]{2,1,0:T(8,128)S(1)}) custom-call(f32[17,288,128]{2,1,0:T(8,128)S(1)} %section.7.layers_ref, f32[17,288,128]{2,1,0:T(8,128)S(1)} %assemble_w.1.w_ref), custom_call_target="tpu_custom_call" | custom-call | bytes 12000000 | tf_op jit(solution)/shard_map/smooth/pallas_call | solution.py:88
  90.9 1.5 %collective-permute-start.27 = (f32[9,128,128]{2,1,0:T(8,128)S(1)}, f32[9,128,128]{2,1,0:T(8,128)S(1)}, u32[]{:S(2)}, u32[]{:S(2)}) collective-permute-start(f32[9,128,128]{2,1,0:T(8,128)S(1)} %get-tuple-element.77), channel_id=1, source_target_pairs={{0,16},{1,17},{2,18},{3,19},{4,20},{5,21},{6,22},{7,23},{8,24},{9,... | collective-permute-start | bytes 1769480 | tf_op jit(solution)/shard_map/ppermute | solution.py:77
  92.4 1.6 %collective-permute-done.27.got_ref = f32[9,128,128]{2,1,0:T(8,128)S(1)} collective-permute-done((f32[9,128,128]{2,1,0:T(8,128)S(1)}, f32[9,128,128]{2,1,0:T(8,128)S(1)}, u32[]{:S(2)}, u32[]{:S(2)}) %collective-permute-start.27) | collective-permute-done | bytes 589856 | tf_op jit(solution)/shard_map/ppermute | solution.py:77
  94.3 2.7 %collective-permute-start.29 = (f32[3,128,128]{2,1,0:T(8,128)S(1)}, f32[3,128,128]{2,1,0:T(8,128)S(1)}, u32[]{:S(2)}, u32[]{:S(2)}) collective-permute-start(f32[3,128,128]{2,1,0:T(8,128)S(1)} %get-tuple-element.80), channel_id=1, source_target_pairs={{0,192},{1,193},{2,194},{3,195},{4,196},{5,197},{6,198},{7,199},{8... | collective-permute-start | bytes 589832 | tf_op jit(solution)/shard_map/ppermute | solution.py:77
  97.0 3.6 %collective-permute-done.29.above_ref = f32[3,128,128]{2,1,0:T(8,128)S(1)} collective-permute-done((f32[3,128,128]{2,1,0:T(8,128)S(1)}, f32[3,128,128]{2,1,0:T(8,128)S(1)}, u32[]{:S(2)}, u32[]{:S(2)}) %collective-permute-start.29) | collective-permute-done | bytes 196640 | tf_op jit(solution)/shard_map/ppermute | solution.py:77
  100.6 3.9 %collective-permute-done.28.below_ref = f32[5,128,128]{2,1,0:T(8,128)S(1)} collective-permute-done((f32[5,128,128]{2,1,0:T(8,128)S(1)}, f32[5,128,128]{2,1,0:T(8,128)S(1)}, u32[]{:S(2)}, u32[]{:S(2)}) %collective-permute-start.28) | collective-permute-done | bytes 327712 | tf_op jit(solution)/shard_map/ppermute | solution.py:77
  104.5 1.5 %finish.1 = f32[16,128,128]{2,1,0:T(8,128)} custom-call(f32[17,128,128]{2,1,0:T(8,128)S(1)} %get-tuple-element.78.tile_ref, f32[5,128,128]{2,1,0:T(8,128)S(1)} %collective-permute-done.28.below_ref, f32[3,128,128]{2,1,0:T(8,128)S(1)} %collective-permute-done.29.above_ref, s32[16,128,128]{2,1,0:T(8,128)S(1)} %copy-done.3), custom_call_target="tpu_custom_call" | custom-call | bytes 9000000 | tf_op jit(solution)/shard_map/finish/pallas_call | solution.py:88
  (61 shorter events, 24.0 us)
Async XLA Ops:
  4.3 14.6 %collective-permute-start = (f32[3,128,128]{2,1,0:T(8,128)S(1)}, f32[3,128,128]{2,1,0:T(8,128)S(1)}, u32[]{:S(2)}, u32[]{:S(2)}) collective-permute-start(f32[3,128,128]{2,1,0:T(8,128)S(1)} %get-tuple-element.43), channel_id=1, source_target_pairs={{0,192},{1,193},{2,194},{3,195},{4,196},{5,197},{6,198},{7,199},{8... | collective-permute-start | bytes 589832 | tf_op jit(solution)/shard_map/ppermute | solution.py:77
  7.9 9.8 %collective-permute-start.1 = (f32[16,128]{1,0:T(8,128)S(1)}, f32[16,128]{1,0:T(8,128)S(1)}, u32[]{:S(2)}, u32[]{:S(2)}) collective-permute-start(f32[16,128]{1,0:T(8,128)S(1)} %get-tuple-element.44), channel_id=1, source_target_pairs={{0,16},{1,17},{2,18},{3,19},{4,20},{5,21},{6,22},{7,23},{8,24},{9,... | collective-permute-start | bytes 24584 | tf_op jit(solution)/shard_map/ppermute | solution.py:77
  8.8 8.9 %collective-permute-start.2 = (f32[16,128]{1,0:T(8,128)S(1)}, f32[16,128]{1,0:T(8,128)S(1)}, u32[]{:S(2)}, u32[]{:S(2)}) collective-permute-start(f32[16,128]{1,0:T(8,128)S(1)} %get-tuple-element.45), channel_id=1, source_target_pairs={{0,48},{1,49},{2,50},{3,51},{4,52},{5,53},{6,54},{7,55},{8,56},{9,... | collective-permute-start | bytes 24584 | tf_op jit(solution)/shard_map/ppermute | solution.py:77
  10.4 8.4 %collective-permute-start.3 = (f32[16,128]{1,0:T(8,128)S(1)}, f32[16,128]{1,0:T(8,128)S(1)}, u32[]{:S(2)}, u32[]{:S(2)}) collective-permute-start(f32[16,128]{1,0:T(8,128)S(1)} %get-tuple-element.46), channel_id=1, source_target_pairs={{0,1},{1,2},{2,3},{3,4},{4,5},{5,6},{6,7},{7,8},{8,9},{9,10},{10,1... | collective-permute-start | bytes 24584 | tf_op jit(solution)/shard_map/ppermute | solution.py:77
  13.4 5.5 %collective-permute-start.4 = (f32[16,128]{1,0:T(8,128)S(1)}, f32[16,128]{1,0:T(8,128)S(1)}, u32[]{:S(2)}, u32[]{:S(2)}) collective-permute-start(f32[16,128]{1,0:T(8,128)S(1)} %get-tuple-element.47), channel_id=1, source_target_pairs={{0,15},{1,0},{2,1},{3,2},{4,3},{5,4},{6,5},{7,6},{8,7},{9,8},{10,9... | collective-permute-start | bytes 24584 | tf_op jit(solution)/shard_map/ppermute | solution.py:77
  21.3 27.5 %collective-permute-start.5 = (f32[51,128,128]{2,1,0:T(8,128)S(1)}, f32[51,128,128]{2,1,0:T(8,128)S(1)}, u32[]{:S(2)}, u32[]{:S(2)}) collective-permute-start(f32[51,128,128]{2,1,0:T(8,128)S(1)} %all_terms.1.uvw_ref), channel_id=1, source_target_pairs={{0,16},{1,17},{2,18},{3,19},{4,20},{5,21},{6,22},{7,23},{8,24},{9,... | collective-permute-start | bytes 10027016 | tf_op jit(solution)/shard_map/ppermute | solution.py:77
  22.8 21.9 %collective-permute-start.6 = (f32[656,128]{1,0:T(8,128)S(1)}, f32[656,128]{1,0:T(8,128)S(1)}, u32[]{:S(2)}, u32[]{:S(2)}) collective-permute-start(f32[656,128]{1,0:T(8,128)S(1)} %pack_rows.1), channel_id=1, source_target_pairs={{16,32},{17,33},{18,34},{19,35},{20,36},{21,37},{22,38},{23,39},{2... | collective-permute-start | bytes 1007624 | tf_op jit(solution)/shard_map/ppermute | solution.py:77
  27.0 17.7 %collective-permute-start.7 = (f32[480,128]{1,0:T(8,128)S(1)}, f32[480,128]{1,0:T(8,128)S(1)}, u32[]{:S(2)}, u32[]{:S(2)}) collective-permute-start(f32[480,128]{1,0:T(8,128)S(1)} %get-tuple-element.49), channel_id=1, source_target_pairs={{0,1},{1,2},{2,3},{3,4},{4,5},{5,6},{6,7},{7,8},{8,9},{9,10},{10,1... | collective-permute-start | bytes 737288 | tf_op jit(solution)/shard_map/ppermute | solution.py:77
  33.0 11.7 %collective-permute-start.8 = (f32[480,128]{1,0:T(8,128)S(1)}, f32[480,128]{1,0:T(8,128)S(1)}, u32[]{:S(2)}, u32[]{:S(2)}) collective-permute-start(f32[480,128]{1,0:T(8,128)S(1)} %get-tuple-element.50), channel_id=1, source_target_pairs={{0,31},{1,16},{2,17},{3,18},{4,19},{5,20},{6,21},{7,22},{8,23},{9,... | collective-permute-start | bytes 737288 | tf_op jit(solution)/shard_map/ppermute | solution.py:77
  33.0 1.4 %collective-permute-start.9 = (f32[96,128]{1,0:T(8,128)S(1)}, f32[96,128]{1,0:T(8,128)S(1)}, u32[]{:S(2)}, u32[]{:S(2)}) collective-permute-start(f32[96,128]{1,0:T(8,128)S(1)} %get-tuple-element.52), channel_id=1, source_target_pairs={{0,16},{1,17},{2,18},{3,19},{4,20},{5,21},{6,22},{7,23},{8,24},{9,... | collective-permute-start | bytes 147464 | tf_op jit(solution)/shard_map/ppermute | solution.py:77
  34.4 10.3 %collective-permute-start.10 = (f32[96,128]{1,0:T(8,128)S(1)}, f32[96,128]{1,0:T(8,128)S(1)}, u32[]{:S(2)}, u32[]{:S(2)}) collective-permute-start(f32[96,128]{1,0:T(8,128)S(1)} %pick_corner.1), channel_id=1, source_target_pairs={{0,63},{1,48},{2,49},{3,50},{4,51},{5,52},{6,53},{7,54},{8,55},{9,... | collective-permute-start | bytes 147464 | tf_op jit(solution)/shard_map/ppermute | solution.py:77
  44.7 4.0 %collective-permute-start.11 = (f32[656,128]{1,0:T(8,128)S(1)}, f32[656,128]{1,0:T(8,128)S(1)}, u32[]{:S(2)}, u32[]{:S(2)}) collective-permute-start(f32[656,128]{1,0:T(8,128)S(1)} %collective-permute-done.6.got_ref), channel_id=1, source_target_pairs={{0,16},{1,17},{2,18},{3,19},{4,20},{5,21},{6,22},{7,23},{8,24},{9,... | collective-permute-start | bytes 1007624 | tf_op jit(solution)/shard_map/ppermute | solution.py:77
  50.7 1.4 %collective-permute-start.12 = (f32[88,128]{1,0:T(8,128)S(1)}, f32[88,128]{1,0:T(8,128)S(1)}, u32[]{:S(2)}, u32[]{:S(2)}) collective-permute-start(f32[88,128]{1,0:T(8,128)S(1)} %get-tuple-element.55.give_ref), channel_id=1, source_target_pairs={{0,16},{1,17},{2,18},{3,19},{4,20},{5,21},{6,22},{7,23},{8,24},{9,... | collective-permute-start | bytes 135176 | tf_op jit(solution)/shard_map/ppermute | solution.py:77
  52.1 2.7 %collective-permute-start.13 = (f32[192,128]{1,0:T(8,128)S(1)}, f32[192,128]{1,0:T(8,128)S(1)}, u32[]{:S(2)}, u32[]{:S(2)}) collective-permute-start(f32[192,128]{1,0:T(8,128)S(1)} %get-tuple-element.56), channel_id=1, source_target_pairs={{192,128},{193,129},{194,130},{195,131},{196,132},{197,133},{198,1... | collective-permute-start | bytes 294920 | tf_op jit(solution)/shard_map/ppermute | solution.py:77
  52.8 2.0 %collective-permute-start.14 = (f32[64,128]{1,0:T(8,128)S(1)}, f32[64,128]{1,0:T(8,128)S(1)}, u32[]{:S(2)}, u32[]{:S(2)}) collective-permute-start(f32[64,128]{1,0:T(8,128)S(1)} %get-tuple-element.57), channel_id=1, source_target_pairs={{192,159},{193,144},{194,145},{195,146},{196,147},{197,148},{198,1... | collective-permute-start | bytes 98312 | tf_op jit(solution)/shard_map/ppermute | solution.py:77
  56.4 2.7 %collective-permute-start.18 = (f32[192,128]{1,0:T(8,128)S(1)}, f32[192,128]{1,0:T(8,128)S(1)}, u32[]{:S(2)}, u32[]{:S(2)}) collective-permute-start(f32[192,128]{1,0:T(8,128)S(1)} %get-tuple-element.63), channel_id=1, source_target_pairs={{128,64},{129,65},{130,66},{131,67},{132,68},{133,69},{134,70},{13... | collective-permute-start | bytes 294920 | tf_op jit(solution)/shard_map/ppermute | solution.py:77
  57.0 2.0 %collective-permute-start.19 = (f32[64,128]{1,0:T(8,128)S(1)}, f32[64,128]{1,0:T(8,128)S(1)}, u32[]{:S(2)}, u32[]{:S(2)}) collective-permute-start(f32[64,128]{1,0:T(8,128)S(1)} %get-tuple-element.64), channel_id=1, source_target_pairs={{128,95},{129,80},{130,81},{131,82},{132,83},{133,84},{134,85},{13... | collective-permute-start | bytes 98312 | tf_op jit(solution)/shard_map/ppermute | solution.py:77
  60.6 26.6 %collective-permute-start.23 = (f32[192,128]{1,0:T(8,128)S(1)}, f32[192,128]{1,0:T(8,128)S(1)}, u32[]{:S(2)}, u32[]{:S(2)}) collective-permute-start(f32[192,128]{1,0:T(8,128)S(1)} %get-tuple-element.70), channel_id=1, source_target_pairs={{64,0},{65,1},{66,2},{67,3},{68,4},{69,5},{70,6},{71,7},{72,8},{73... | collective-permute-start | bytes 294920 | tf_op jit(solution)/shard_map/ppermute | solution.py:77
  61.9 23.3 %collective-permute-start.24 = (f32[64,128]{1,0:T(8,128)S(1)}, f32[64,128]{1,0:T(8,128)S(1)}, u32[]{:S(2)}, u32[]{:S(2)}) collective-permute-start(f32[64,128]{1,0:T(8,128)S(1)} %get-tuple-element.71), channel_id=1, source_target_pairs={{64,31},{65,16},{66,17},{67,18},{68,19},{69,20},{70,21},{71,22},{7... | collective-permute-start | bytes 98312 | tf_op jit(solution)/shard_map/ppermute | solution.py:77
  63.2 22.0 %collective-permute-start.26 = (f32[24,128]{1,0:T(8,128)S(1)}, f32[24,128]{1,0:T(8,128)S(1)}, u32[]{:S(2)}, u32[]{:S(2)}) collective-permute-start(f32[24,128]{1,0:T(8,128)S(1)} %get-tuple-element.73), channel_id=1, source_target_pairs={{64,63},{65,48},{66,49},{67,50},{68,51},{69,52},{70,53},{71,54},{7... | collective-permute-start | bytes 36872 | tf_op jit(solution)/shard_map/ppermute | solution.py:77
  64.5 22.7 %collective-permute-start.25 = (f32[24,128]{1,0:T(8,128)S(1)}, f32[24,128]{1,0:T(8,128)S(1)}, u32[]{:S(2)}, u32[]{:S(2)}) collective-permute-start(f32[24,128]{1,0:T(8,128)S(1)} %get-tuple-element.72), channel_id=1, source_target_pairs={{64,32},{65,33},{66,34},{67,35},{68,36},{69,37},{70,38},{71,39},{7... | collective-permute-start | bytes 36872 | tf_op jit(solution)/shard_map/ppermute | solution.py:77
  90.9 3.1 %collective-permute-start.27 = (f32[9,128,128]{2,1,0:T(8,128)S(1)}, f32[9,128,128]{2,1,0:T(8,128)S(1)}, u32[]{:S(2)}, u32[]{:S(2)}) collective-permute-start(f32[9,128,128]{2,1,0:T(8,128)S(1)} %get-tuple-element.77), channel_id=1, source_target_pairs={{0,16},{1,17},{2,18},{3,19},{4,20},{5,21},{6,22},{7,23},{8,24},{9,... | collective-permute-start | bytes 1769480 | tf_op jit(solution)/shard_map/ppermute | solution.py:77
  94.2 10.2 %collective-permute-start.28 = (f32[5,128,128]{2,1,0:T(8,128)S(1)}, f32[5,128,128]{2,1,0:T(8,128)S(1)}, u32[]{:S(2)}, u32[]{:S(2)}) collective-permute-start(f32[5,128,128]{2,1,0:T(8,128)S(1)} %get-tuple-element.79), channel_id=1, source_target_pairs={{0,64},{1,65},{2,66},{3,67},{4,68},{5,69},{6,70},{7,71},{8,72},{9,... | collective-permute-start | bytes 983048 | tf_op jit(solution)/shard_map/ppermute | solution.py:77
  94.3 6.3 %collective-permute-start.29 = (f32[3,128,128]{2,1,0:T(8,128)S(1)}, f32[3,128,128]{2,1,0:T(8,128)S(1)}, u32[]{:S(2)}, u32[]{:S(2)}) collective-permute-start(f32[3,128,128]{2,1,0:T(8,128)S(1)} %get-tuple-element.80), channel_id=1, source_target_pairs={{0,192},{1,193},{2,194},{3,195},{4,196},{5,197},{6,198},{7,199},{8... | collective-permute-start | bytes 589832 | tf_op jit(solution)/shard_map/ppermute | solution.py:77
  (10 other events, 25.9 us)

commit v7 on v6

--- a/solution.py
+++ b/solution.py
@@ -20,6 +20,7 @@
 PLANE = 288
 VECTORS = PLANE // 8
 REACH = RADIUS + STEPS
+LOW = LAYERS - RADIUS
 SLABS = ((16, 15, 14, 3), (13, 12, 11, 8, 0), (10, 9, 7, 6, 5, 2), (4, 1))
 FOLDED = 32
 SLAB_ROWS = 3 * 128 + FOLDED + 64
@@ -34,7 +35,8 @@
     return -(-width_of(layer) // 8) * 8
 
 
-MICROSECONDS = {"all_terms": 2.5, "assemble": 2.5, "section": 2.6, "smooth": 4.0, "finish": 3.0, "ends": 1.0}
+MICROSECONDS = {"all_terms": 2.5, "assemble": 2.5, "section": 1.5, "section_rest": 3.0, "smooth_rest": 3.0, "finish": 3.0}
+VMEM_LIMIT = {"edges": (64 << 20) - (64 << 10)}
 
 
 def strips():
@@ -89,7 +91,7 @@
         kernel,
         out_shape=outs,
         scratch_shapes=list(scratch),
-        compiler_params=pltpu.CompilerParams(vmem_limit_bytes=40 * 1024 * 1024),
+        compiler_params=pltpu.CompilerParams(vmem_limit_bytes=VMEM_LIMIT.get(name, 40 << 20)),
         cost_estimate=pl.CostEstimate(flops=0, bytes_accessed=int(MICROSECONDS.get(name, 0.5) * 3e6), transcendentals=0),
         name=name,
         **more,
@@ -150,15 +152,17 @@
     return x32 * (x4 * (x2 * x))
 
 
-def edges(p_ref, f_ref, s_ref, lowest_ref, inner_ref, outer_ref, left_ref, right_ref, turned, sems):
-    copies = [pltpu.make_async_copy(ref.at[0], lowest_ref.at[i + 1], sems.at[i]) for i, ref in enumerate((f_ref, s_ref))]
-    for copy in copies:
+def edges(p_hbm, f_hbm, s_hbm, lowest_ref, inner_ref, outer_ref, left_ref, right_ref, turned, p_ref, sems):
+    planes = [pltpu.make_async_copy(p_hbm.at[pl.ds(4 * i, 4)], p_ref.at[pl.ds(4 * i, 4)], sems.at[i]) for i in range(4)]
+    copies = [pltpu.make_async_copy(ref.at[0], lowest_ref.at[i + 1], sems.at[4 + i]) for i, ref in enumerate((f_hbm, s_hbm))]
+    for copy in planes + copies:
         copy.start()
-    lowest_ref[0] = p_ref[0]
     lane = lanes(128)
     c = core()
     packed = jnp.zeros((128, 128), F32)
     for layer in range(LAYERS):
+        if layer % 4 == 0:
+            planes[layer // 4].wait()
         inner_ref[pl.ds(layer, 1), :] = p_ref[layer, pl.ds(127 * (1 - c), 1), :]
         outer_ref[pl.ds(layer, 1), :] = p_ref[layer, pl.ds(127 * c, 1), :]
         rolled = pltpu.roll(p_ref[layer], 2 * layer + 1, 1)
@@ -166,8 +170,13 @@
     turned[...] = packed.T
     right_ref[...] = turned[pl.ds(0, 16, stride=2), :]
     left_ref[...] = turned[pl.ds(1, 16, stride=2), :]
+    lowest_ref[0] = p_ref[0]
     for copy in copies:
         copy.wait()
+
+
+def early(p_ref, f_ref, s_ref, out_ref):
+    out_ref[...] = p_ref[0, pl.ds(0, 8), :] + f_ref[0, pl.ds(0, 8), :] + s_ref[0, pl.ds(0, 8), :]
 
 
 def norm_of(position, extent):
@@ -222,32 +231,16 @@
 
 
 def all_terms(
-    sizes, p_ref, f_hbm, s_hbm, above_ref, inner_ref, outer_ref, left_ref, right_ref,
-    uvw_ref, powers, turned, f_ref, s_ref, sems,
+    sizes, p_ref, f_ref, s_ref, above_ref, inner_ref, outer_ref, left_ref, right_ref, early_ref, uvw_ref, powers, turned
 ):
-    def fetch(part):
-        here = pl.ds(4 * part, 4)
-        return [
-            pltpu.make_async_copy(hbm.at[here], ref.at[here], sems.at[i, part])
-            for i, (hbm, ref) in enumerate(((f_hbm, f_ref), (s_hbm, s_ref)))
-        ]
-
-    for part in range(LAYERS // 4):
-        for copy in fetch(part):
-            copy.start()
     beside = columns_beside(left_ref, right_ref, turned)
     norms = 1.0 / plane_norms(sizes)
     gz = lax.axis_index("gz")
     layer0 = gz * LAYERS
-    for copy in fetch(0):
-        copy.wait()
     uvw_ref[0] = s_ref[0]
     uvw_ref[STEPS] = power39(p_ref[0])
     uvw_ref[2 * STEPS] = norms * (1.0 / norm_of(0 * layer0, sizes[0] * LAYERS))
     for layer in range(1, STEPS):
-        if layer % 4 == 0 and layer < LAYERS:
-            for copy in fetch(layer // 4):
-                copy.wait()
         total = neighbours(p_ref[layer - 1], layer - 1, inner_ref, outer_ref, beside, powers)
         if layer < LAYERS:
             p, f, s = p_ref[layer], f_ref[layer], s_ref[layer]
@@ -433,11 +426,14 @@
     begin = (1 - c) * (128 - REACH)
     beyond = (lane >= begin) & (lane < begin + REACH)
     for i in range(4):
-        value = main_ref[pl.ds(64 * (i % 2), 64), :]
-        if i >= 2:
-            value = pltpu.roll(value, 64, 1)
-        inner = pltpu.roll(main_ref[pl.ds(128, 64), :], (32 * (2 - c) - 32 * i) & 127, 1)
-        value = jnp.where(mine, value, inner)
+        if main_ref.shape[0] == 256:
+            value = main_ref[pl.ds(64 * i, 64), :]
+        else:
+            value = main_ref[pl.ds(64 * (i % 2), 64), :]
+            if i >= 2:
+                value = pltpu.roll(value, 64, 1)
+            inner = pltpu.roll(main_ref[pl.ds(128, 64), :], (32 * (2 - c) - 32 * i) & 127, 1)
+            value = jnp.where(mine, value, inner)
         outer = pltpu.roll(outer_ref[...], (128 - 32 * i) % 128, 1) if i else outer_ref[...]
         carry[pl.ds(64 * i, 64), :] = jnp.where(beyond, outer * inside, value)
     lane = lanes(24)
@@ -446,57 +442,63 @@
     carry[pl.ds(aligned(256 + 8 * seam(), 8), 24), :] = jnp.where(beyond, halo_outer_ref[...] * inside, halo_ref[...])
 
 
-def merge(main_ref, give_ref, got_ref, down_ref, halo_ref):
-    down_ref[pl.ds(0, 128), :] = main_ref[...]
-    down_ref[pl.ds(128, 64), :] = got_ref[pl.ds(0, 64), :]
-    rows = pl.ds(64, 24)
-    halo_ref[...] = jnp.where((lanes(24) >> 6) == core(), give_ref[rows, :], got_ref[rows, :])
-
-
-def section(active, *refs):
+def merge(give_ref, got_ref, down_ref, halo_ref):
+    mine = (lanes(128) >> 6) == core()
+    rows = pl.ds(0, 128)
+    own, other = give_ref[rows, :], got_ref[rows, :]
+    down_ref[rows, :] = jnp.where(mine, own, other)
+    down_ref[pl.ds(128, 128), :] = pltpu.roll(jnp.where(mine, other, own), 64, 1)
+    rows = pl.ds(128, 24)
+    halo_ref[...] = jnp.where(mine[:24], give_ref[rows, :], got_ref[rows, :])
+
+
+def load_carry(pieces, carry):
+    set_carry(carry, *pieces)
+    return [carry[pl.ds(t, 8, stride=VECTORS), :] for t in range(VECTORS)]
+
+
+def run_down(values, uv_ref, layers_ref, first, last, base=0):
+    for layer in range(first, last - 1, -1):
+        at = 2 * (LAYERS - layer)
+        values = step_down(values, uv_ref.at[at], uv_ref.at[at + 1], layers_ref.at[layer - base])
+    return values
+
+
+def section(active, shared, *refs):
     uv_ref, refs = refs[0], refs[1:]
     pieces, before_ref = (), None
-    if len(refs) > 6 or len(refs) == 5 + 2:
+    if len(refs) > 5:
         pieces, before_ref, refs = refs[:4], refs[4], refs[5:]
-    if len(refs) == 6:
-        layers_ref, main_ref, outer_ref, give_ref, strip_ref, carry = refs
-    else:
-        layers_ref, carry = refs
-        main_ref = None
+    layers_ref, down_ref, outer_ref, strip_ref, carry = refs
 
     @pl.when(lax.axis_index("gz") == active)
     def _():
-        if pieces:
-            set_carry(carry, *pieces)
-            values = [carry[pl.ds(t, 8, stride=VECTORS), :] for t in range(VECTORS)]
-        else:
-            values = [jnp.zeros((8, 128), F32)] * VECTORS
-        for layer in range(LAYERS, 0, -1):
-            at = 2 * (LAYERS - layer)
-            values = step_down(values, uv_ref.at[at], uv_ref.at[at + 1], layers_ref.at[layer])
-        step_down(values, uv_ref.at[2 * LAYERS], uv_ref.at[2 * LAYERS + 1], layers_ref.at[0])
-        if main_ref is None:
-            return
-        c = core()
-        lane = lanes(128)
+        values = load_carry(pieces, carry) if pieces else [jnp.zeros((8, 128), F32)] * VECTORS
+        values = run_down(values, uv_ref, layers_ref, LAYERS, 1)
+        layers_ref[0] = layers_ref[1]
         for t in range(VECTORS):
             carry[pl.ds(t, 8, stride=VECTORS), :] = values[t]
-        bottom = carry
-        mine = (lane >> 6) == c
-        main_ref[...] = jnp.where(mine, bottom[pl.ds(0, 128), :], pltpu.roll(bottom[pl.ds(128, 128), :], 64, 1))
+        c = core()
+        mine = (lanes(128) >> 6) == c
+        down_ref[pl.ds(0, 128), :] = jnp.where(
+            mine, carry[pl.ds(0, 128), :], pltpu.roll(carry[pl.ds(128, 128), :], 64, 1)
+        )
         lane = lanes(64)
         slab = inner = jnp.zeros((64, 128), F32)
         for i in range(4):
-            block = bottom[pl.ds(64 * i, 64), :]
+            block = carry[pl.ds(64 * i, 64), :]
             rolled = pltpu.roll(block, 32 * i, 1) if i else block
             begin = (32 * i + 128 - c * 32) & 127
             slab = jnp.where(((lane - begin) & 127) < 32, rolled, slab)
-            inner = jnp.where((lane >> 5) == i, pltpu.roll(block, (32 * i - 32 * (1 + c)) & 127, 1), inner)
+            if not shared:
+                inner = jnp.where((lane >> 5) == i, pltpu.roll(block, (32 * i - 32 * (2 - c)) & 127, 1), inner)
         outer_ref[...] = slab
-        give_ref[pl.ds(0, 64), :] = inner
-        strip = bottom[pl.ds(aligned((1 - seam()) * 232, 8), 24), :]
-        give_ref[pl.ds(64, 24), :] = strip
+        strip = carry[pl.ds(aligned((1 - seam()) * 232, 8), 24), :]
         strip_ref[...] = strip
+        if shared:
+            down_ref[pl.ds(128, 24), :] = strip
+        else:
+            down_ref[pl.ds(128, 64), :] = inner
 
     if before_ref is not None:
         @pl.when(lax.axis_index("gz") != active)
@@ -504,23 +506,44 @@
             layers_ref[...] = before_ref[...]
 
 
+def section_top(uv_ref, main_ref, outer_ref, halo_ref, halo_outer_ref, before_ref, top_ref, carry):
+    @pl.when(lax.axis_index("gz") == 0)
+    def _():
+        values = load_carry((main_ref, outer_ref, halo_ref, halo_outer_ref), carry)
+        run_down(values, uv_ref, top_ref, LAYERS, LOW, LOW)
+
+    @pl.when(lax.axis_index("gz") != 0)
+    def _():
+        top_ref[...] = before_ref[pl.ds(LOW, STEPS - LOW)]
+
+
+def section_rest(uv_ref, top_ref, before_ref, layers_ref):
+    @pl.when(lax.axis_index("gz") == 0)
+    def _():
+        values = [top_ref[0, pl.ds(8 * t, 8), :] for t in range(VECTORS)]
+        run_down(values, uv_ref, layers_ref, LOW - 1, 0)
+
+    @pl.when(lax.axis_index("gz") != 0)
+    def _():
+        layers_ref[...] = before_ref[pl.ds(0, LOW)]
+
+
 def box(values):
     two = [values[i] + values[i + 1] for i in range(len(values) - 1)]
     four = [two[i] + two[i + 2] for i in range(len(two) - 2)]
     return [four[i] + values[i + 4] for i in range(len(values) - 4)]
 
 
-def smooth(layers_ref, w_ref, kept_ref, give_ref, plains, others, tent):
-    c = core()
-    mine = (lanes(128) >> 6) == c
+def smooth(layers, kept_ref, plains, others, tent):
+    c = core()
     row = lax.broadcasted_iota(jnp.int32, (256, 128), 0)
     col = lax.broadcasted_iota(jnp.int32, (256, 128), 1)
     distance = (row - col + RADIUS) & 127
     weight = jnp.where(distance <= 2 * RADIUS, RADIUS + 1 - jnp.abs(distance - RADIUS), 0)
     tent[...] = weight.astype(F32).astype(jnp.bfloat16)
-
-    def layer(k, plain):
-        values = [layers_ref[k, pl.ds(8 * t, 8), :] * w_ref[k, pl.ds(8 * t, 8), :] for t in range(VECTORS)]
+    for k, (layer_ref, w_ref) in enumerate(layers):
+        plain = plains.at[k % 4]
+        values = [layer_ref[pl.ds(8 * t, 8), :] * w_ref[pl.ds(8 * t, 8), :] for t in range(VECTORS)]
         first = [pltpu.roll(value, 1, 0) for value in values[VECTORS - RADIUS:]]
         last = [pltpu.roll(value, 7, 0) for value in values[:RADIUS]]
         total = jnp.concatenate(box(box(first + values + last)), axis=0)
@@ -534,36 +557,54 @@
         kept_ref[k] = plain[pl.ds(aligned(c * 128, 128), 128), :]
         others[k] = plain[pl.ds(aligned((1 - c) * 128, 128), 128), :]
 
-    for k in range(STEPS):
-        layer(k, plains.at[k % 4])
-    count = give_ref.shape[0]
+
+def pair_up(others, first, count, give_ref):
+    mine = (lanes(128) >> 6) == core()
     for k in range(count):
-        second = others[k + count] if k + count < STEPS else jnp.zeros((128, 128), F32)
-        give_ref[k] = jnp.where(mine, others[k], pltpu.roll(second, 64, 1))
-
-
-def ends(kept_ref, got_ref, out_ref, top_ref, bottom_ref):
+        give_ref[k] = jnp.where(mine, others[first + k], pltpu.roll(others[first + count + k], 64, 1))
+
+
+def smooth_first(top_ref, before_ref, w_ref, kept_ref, give_ref, plains, others, tent):
+    layers = [(top_ref.at[k], w_ref.at[LOW + k]) for k in range(STEPS - LOW)]
+    layers += [(before_ref.at[k], w_ref.at[k]) for k in range(1, RADIUS)]
+    smooth(layers, kept_ref, plains, others, tent)
+    pair_up(others, 0, 4, give_ref)
+
+
+def smooth_rest(layers_ref, w_ref, kept_ref, give_ref, give_more_ref, plains, others, tent):
+    smooth([(layers_ref.at[k], w_ref.at[k]) for k in range(LOW)], kept_ref, plains, others, tent)
+    pair_up(others, 0, 3, give_ref)
+    pair_up(others, 6, 3, give_more_ref)
+
+
+def whole(kept, got, second):
     mine = (lanes(128) >> 6) == core()
-    count = got_ref.shape[0]
-    for k in range(STEPS):
-        other = got_ref[k] if k < count else pltpu.roll(got_ref[k - count], 64, 1)
-        out_ref[k] = jnp.where(mine, kept_ref[k], other)
-    top_ref[...] = out_ref[pl.ds(STEPS - RADIUS - 1, RADIUS + 1)]
-    bottom_ref[...] = out_ref[pl.ds(1, RADIUS - 1)]
-
-
-def finish(tile_ref, below_ref, above_ref, passive_ref, out_ref):
+    return jnp.where(mine, kept, pltpu.roll(got, 64, 1) if second else got)
+
+
+def ends(kept_ref, got_ref, top_ref, bottom_ref):
+    for k in range(8):
+        value = whole(kept_ref[k], got_ref[k % 4], k >= 4)
+        if k < STEPS - LOW:
+            top_ref[k] = value
+        else:
+            bottom_ref[k - (STEPS - LOW)] = value
+
+
+def finish(kept_ref, got_ref, got_more_ref, top_ref, below_ref, above_ref, passive_ref, out_ref, tile):
     gz = lax.axis_index("gz")
-    has_below, has_above = one_if(gz > 0), one_if(gz < lax.axis_size("gz") - 1)
+    for k in range(LOW):
+        got = got_ref if k < 6 else got_more_ref
+        tile[k] = whole(kept_ref[k], got[k % 3], k % 6 >= 3)
 
     def layer(k):
         if k < 0:
-            return below_ref[k + RADIUS] * has_below
+            return jnp.where(gz > 0, below_ref[k + RADIUS], 0.0)
         if k == 0:
-            return jnp.where(gz == 0, tile_ref[0], below_ref[RADIUS])
+            return jnp.where(gz == 0, tile[0], below_ref[RADIUS])
         if k > LAYERS:
-            return above_ref[k - STEPS] * has_above
-        return tile_ref[k]
+            return jnp.where(gz < lax.axis_size("gz") - 1, above_ref[k - STEPS], 0.0)
+        return tile[k] if k < LOW else top_ref[k - LOW]
 
     for k in range(LAYERS):
         total = layer(k) * 5.0
@@ -595,25 +636,23 @@
     def same(z, y, x):
         return (z, y, x + (-1 if y & 1 else 1))
 
-    hbm, vmem = pl.BlockSpec(memory_space=pltpu.HBM), pl.BlockSpec(memory_space=pltpu.VMEM)
+    hbm = pl.BlockSpec(memory_space=pltpu.HBM)
     lowest_planes, inner, outer, left, right = call(
         edges, [shape(3, 128, 128)] + [edge] * 4, printed, filtered, sensitivity,
-        in_specs=[vmem, hbm, hbm],
-        scratch=[pltpu.VMEM((128, 128), F32), pltpu.SemaphoreType.DMA((2,))],
+        in_specs=[hbm] * 3,
+        scratch=[pltpu.VMEM((128, 128), F32), pltpu.VMEM((LAYERS, 128, 128), F32), pltpu.SemaphoreType.DMA((6,))],
     )
     above = moved(lowest_planes, lambda z, y, x: (z - 1, y, x))
     from_left = moved(right, lambda z, y, x: (z, y, x + 1))
     from_right = moved(left, lambda z, y, x: (z, y, x - 1))
     outer = moved(outer, lambda z, y, x: (z, y ^ 3, x))
     inner = to_other(inner)
+    ready = call(early, shape(8, 128), printed, filtered, after(sensitivity, left))
     uvw = call(
         functools.partial(all_terms, sizes), shape(3 * STEPS, 128, 128),
-        printed, filtered, sensitivity, above, inner, outer, from_left, from_right,
-        in_specs=[vmem, hbm, hbm] + [vmem] * 5,
+        printed, filtered, sensitivity, above, inner, outer, from_left, from_right, ready,
         scratch=[
             pltpu.VMEM((144, 128), F32), pltpu.VMEM((128, 128), F32),
-            pltpu.VMEM((LAYERS, 128, 128), F32), pltpu.VMEM((LAYERS, 128, 128), F32),
-            pltpu.SemaphoreType.DMA((2, LAYERS // 4)),
         ],
     )
     slab, corner = shape(SLAB_ROWS, 128), shape(CORNER_ROWS, 128)
@@ -632,54 +671,64 @@
     uvs = call(assemble, shape(2 * STEPS, PLANE, 128), *parts, scratch=work)
     ws = None
     pieces, before = (), ()
-    for active in range(depth - 1, -1, -1):
-        outs = [stack]
-        if active > 0:
-            outs = outs + [plane, shape(64, 128), shape(88, 128), shape(24, 128)]
-        layers, *sent = call(
-            functools.partial(section, active), outs, uvs, *pieces, *before, scratch=[pltpu.VMEM((PLANE, 128), F32)]
+    whole_stack = [pltpu.VMEM((PLANE, 128), F32)]
+    for active in range(depth - 1, 0, -1):
+        swap = (depth - 1 - active) % 2 == 1
+        layers, main, side, strip = call(
+            functools.partial(section, active, swap),
+            [stack, shape(152 if swap else 192, 128), shape(64, 128), shape(24, 128)],
+            uvs, *pieces, *before, scratch=whole_stack,
         )
         before = (layers,)
-        if active > 0:
-            main, side, give, strip = sent
-
-            def down(where):
-                def to(z, y, x):
-                    _, ty, tx = where(z, y, x)
-                    return (z - 1, ty, tx) if z == active else None
-                return to
-
-            def over(z, y, x):
-                return (z, y ^ 2, x)
-
-            def corner_of(z, y, x):
-                _, ty, tx = beside(z, y, x)
-                return (z, ty ^ 2, tx)
-
-            side = moved(side, down(beside))
-            edge_piece = moved(strip, down(corner_of))
-            main, halo = call(merge, [shape(192, 128), shape(24, 128)], main, give, to_other(give))
-            main = moved(main, down(lambda z, y, x: (z, y, x)))
-            halo = moved(halo, down(over))
-            pieces = (main, side, halo, edge_piece)
-            if ws is None:
-                ws = call(assemble_w, stack, after(uvw, side), *parts[1:], scratch=work)
-    count = STEPS // 2 + 1
+
+        def down(where):
+            def to(z, y, x):
+                _, ty, tx = where(z, y, x)
+                return (z - 1, ty, tx) if z == active else None
+            return to
+
+        def over(z, y, x):
+            return (z, y ^ 2, x)
+
+        def corner_of(z, y, x):
+            _, ty, tx = beside(z, y, x)
+            return (z, ty ^ 2, tx)
+
+        side = moved(side, down(beside))
+        edge_piece = moved(strip, down(corner_of))
+        halo = strip
+        if swap:
+            main, halo = call(merge, [shape(256, 128), shape(24, 128)], main, to_other(main))
+        main = moved(main, down(lambda z, y, x: (z, y, x)))
+        halo = moved(halo, down(over))
+        pieces = (main, side, halo, edge_piece)
+        if ws is None:
+            ws = call(assemble_w, stack, after(uvw, side), *parts[1:], scratch=work)
+    top_layers = call(
+        section_top, shape(STEPS - LOW, PLANE, 128), uvs, *pieces, layers, scratch=whole_stack
+    )
+
+    def work_for(count):
+        return [
+            pltpu.VMEM((4, PLANE, 128), F32), pltpu.VMEM((count, 128, 128), F32), pltpu.VMEM((256, 128), jnp.bfloat16)
+        ]
+
     kept, given = call(
-        smooth,
-        [shape(STEPS, 128, 128), shape(count, 128, 128)],
-        layers, ws,
-        scratch=[
-            pltpu.VMEM((4, PLANE, 128), F32), pltpu.VMEM((STEPS, 128, 128), F32), pltpu.VMEM((256, 128), jnp.bfloat16)
-        ],
+        smooth_first, [shape(8, 128, 128), shape(4, 128, 128)], top_layers, layers, ws, scratch=work_for(8)
     )
-    given = to_other(given)
-    tile, top, bottom = call(
-        ends, [shape(STEPS, 128, 128), shape(RADIUS + 1, 128, 128), shape(RADIUS - 1, 128, 128)], kept, given
-    )
+    top, bottom = call(ends, [shape(RADIUS + 1, 128, 128), shape(RADIUS - 1, 128, 128)], kept, to_other(given))
     below = moved(top, lambda z, y, x: (z + 1, y, x))
     over = moved(bottom, lambda z, y, x: (z - 1, y, x))
-    return call(finish, shape(LAYERS, 128, 128), tile, below, over, passive)
+    rest = call(section_rest, shape(LOW, PLANE, 128), uvs, after(top_layers, top), layers)
+    third = shape(3, 128, 128)
+    kept, given, given_more = call(
+        smooth_rest, [shape(LOW, 128, 128), third, third], rest, ws, scratch=work_for(LOW)
+    )
+    return call(
+        finish, shape(LAYERS, 128, 128),
+        kept, to_other(given), to_other(given_more), top, below, over, passive,
+        scratch=[pltpu.VMEM((LOW, 128, 128), F32)],
+    )
 
 
 def solution(mesh):

time: 107 us -> 105 us (0.981)
  waiting for transfers between devices: 44.3 us -> 41.6 us
  Pallas kernels: 13.8 us -> 15.8 us
  starting transfers between devices: 43.9 us -> 42.1 us
    ppermute x30, waiting for transfers between devices: 44.3 us -> 41.6 us  [moved(): return lax.ppermute(value, AXES, pairs)]
    pallas_call x17 -> x18, Pallas kernels: 13.8 us -> 15.8 us  [call(): pl.pallas_call(kernel, out_shape=outs, scratch_shapes=list(scratch), comp...]
    ppermute x30, starting transfers between devices: 43.9 us -> 42.1 us  [moved(): return lax.ppermute(value, AXES, pairs)]
    unnamed x8 -> x12, local copies, waits for them, and re-layouts: 3.68 us -> 3.69 us
  transfers between devices with their start and end apart: 30 -> 30, of which waited for: 12 -> 11; matrix products, arithmetic and copies ran while one was open for 0% -> 0% of each run, Pallas kernels for 3% -> 6%
where the time goes in v7:
time: 105 us; the launch traced here: 104 us
  starting transfers between devices  42.1 us (40%)
  waiting for transfers between devices  41.6 us (40%)
  Pallas kernels  15.8 us (15%)
  local copies, waits for them, and re-layouts  3.69 us (4%)
    ppermute x30, starting transfers between devices, moved(): return lax.ppermute(value, AXES, pairs)  42.1 us
    ppermute x30, waiting for transfers between devices, moved(): return lax.ppermute(value, AXES, pairs)  41.6 us
    pallas_call x18, Pallas kernels, call(): pl.pallas_call(kernel, out_shape=outs, scratch_shapes=list(scratch), comp...  15.8 us
    unnamed x12, local copies, waits for them, and re-layouts  3.69 us
  transfers between devices with their start and end apart: 30, of which 11 were waited for; matrix products, arithmetic and copies ran while one was open for 0% of the time, Pallas kernels for 6%

profile of v7, /device:TPU:1, one launch (start us, length us, event | category | flops | bytes accessed | tf_op | source)
XLA Modules:
  0.0 103.5 jit_solution(7697089256394313179)
XLA Ops:
  0.0 2.3 %edges.1 = (f32[3,128,128]{2,1,0:T(8,128)}, f32[16,128]{1,0:T(8,128)}, f32[16,128]{1,0:T(8,128)}, f32[16,128]{1,0:T(8,128)}, f32[16,128]{1,0:T(8,128)}) custom-call(f32[16,128,128]{2,1,0:T(8,128)} %p_ref.3, f32[16,128,128]{2,1,0:T(8,128)} %f_ref.3, f32[16,128,128]{2,1,0:T(8,128)} %s_ref.2), custom_call_target="tpu_custom_call" | custom-call | bytes 1500000 | tf_op jit(solution)/shard_map/edges/pallas_call | solution.py:90
  2.3 3.6 %collective-permute-start = (f32[3,128,128]{2,1,0:T(8,128)}, f32[3,128,128]{2,1,0:T(8,128)S(1)}, u32[]{:S(2)}, u32[]{:S(2)}) collective-permute-start(f32[3,128,128]{2,1,0:T(8,128)} %get-tuple-element.40), channel_id=1, source_target_pairs={{0,192},{1,193},{2,194},{3,195},{4,196},{5,197},{6,198},{7,199},{8... | collective-permute-start | bytes 589832 | tf_op jit(solution)/shard_map/ppermute | solution.py:79
  6.0 8.2 %collective-permute-start.4 = (f32[16,128]{1,0:T(8,128)}, f32[16,128]{1,0:T(8,128)S(1)}, u32[]{:S(2)}, u32[]{:S(2)}) collective-permute-start(f32[16,128]{1,0:T(8,128)} %get-tuple-element.44), channel_id=1, source_target_pairs={{0,15},{1,0},{2,1},{3,2},{4,3},{5,4},{6,5},{7,6},{8,7},{9,8},{10,9... | collective-permute-start | bytes 24584 | tf_op jit(solution)/shard_map/ppermute | solution.py:79
  19.8 3.2 %collective-permute-done.3.left_ref = f32[16,128]{1,0:T(8,128)S(1)} collective-permute-done((f32[16,128]{1,0:T(8,128)}, f32[16,128]{1,0:T(8,128)S(1)}, u32[]{:S(2)}, u32[]{:S(2)}) %collective-permute-start.3) | collective-permute-done | bytes 8224 | tf_op jit(solution)/shard_map/ppermute | solution.py:79
  23.0 2.0 %all_terms.1.uvw_ref = f32[51,128,128]{2,1,0:T(8,128)S(1)} custom-call(f32[16,128,128]{2,1,0:T(8,128)S(1)} %copy-done.2, f32[16,128,128]{2,1,0:T(8,128)S(1)} %copy-done.3, f32[16,128,128]{2,1,0:T(8,128)S(1)} %copy-done.4, f32[3,128,128]{2,1,0:T(8,128)S(1)} %collective-permute-done.above_ref, f32[16,128]{1,0:T(8,128)S(1)} %collective-permute-done.1.inner_ref, ...), custom_call_target="tpu_custom_call" | custom-call | bytes 7500000 | tf_op jit(solution)/shard_map/all_terms/pallas_call | solution.py:90
  25.0 1.7 %collective-permute-start.5 = (f32[51,128,128]{2,1,0:T(8,128)S(1)}, f32[51,128,128]{2,1,0:T(8,128)S(1)}, u32[]{:S(2)}, u32[]{:S(2)}) collective-permute-start(f32[51,128,128]{2,1,0:T(8,128)S(1)} %all_terms.1.uvw_ref), channel_id=1, source_target_pairs={{0,16},{1,17},{2,18},{3,19},{4,20},{5,21},{6,22},{7,23},{8,24},{9,... | collective-permute-start | bytes 10027016 | tf_op jit(solution)/shard_map/ppermute | solution.py:79
  26.7 2.5 %collective-permute-start.6 = (f32[656,128]{1,0:T(8,128)S(1)}, f32[656,128]{1,0:T(8,128)S(1)}, u32[]{:S(2)}, u32[]{:S(2)}) collective-permute-start(f32[656,128]{1,0:T(8,128)S(1)} %pack_rows.1), channel_id=1, source_target_pairs={{16,32},{17,33},{18,34},{19,35},{20,36},{21,37},{22,38},{23,39},{2... | collective-permute-start | bytes 1007624 | tf_op jit(solution)/shard_map/ppermute | solution.py:79
  29.3 1.7 %pack.1 = (f32[480,128]{1,0:T(8,128)S(1)}, f32[480,128]{1,0:T(8,128)S(1)}, f32[96,128]{1,0:T(8,128)S(1)}, f32[96,128]{1,0:T(8,128)S(1)}) custom-call(f32[51,128,128]{2,1,0:T(8,128)S(1)} %all_terms.1.uvw_ref), custom_call_target="tpu_custom_call" | custom-call | bytes 1500000 | tf_op jit(solution)/shard_map/pack/pallas_call | solution.py:90
  31.0 1.7 %collective-permute-start.7 = (f32[480,128]{1,0:T(8,128)S(1)}, f32[480,128]{1,0:T(8,128)S(1)}, u32[]{:S(2)}, u32[]{:S(2)}) collective-permute-start(f32[480,128]{1,0:T(8,128)S(1)} %get-tuple-element.47), channel_id=1, source_target_pairs={{0,1},{1,2},{2,3},{3,4},{4,5},{5,6},{6,7},{7,8},{8,9},{9,10},{10,1... | collective-permute-start | bytes 737288 | tf_op jit(solution)/shard_map/ppermute | solution.py:79
  35.3 9.7 %collective-permute-done.10.corner_ref = f32[96,128]{1,0:T(8,128)S(1)} collective-permute-done((f32[96,128]{1,0:T(8,128)S(1)}, f32[96,128]{1,0:T(8,128)S(1)}, u32[]{:S(2)}, u32[]{:S(2)}) %collective-permute-start.10) | collective-permute-done | bytes 49184 | tf_op jit(solution)/shard_map/ppermute | solution.py:79
  45.4 4.2 %collective-permute-start.11 = (f32[656,128]{1,0:T(8,128)S(1)}, f32[656,128]{1,0:T(8,128)S(1)}, u32[]{:S(2)}, u32[]{:S(2)}) collective-permute-start(f32[656,128]{1,0:T(8,128)S(1)} %collective-permute-done.6.got_ref), channel_id=1, source_target_pairs={{0,16},{1,17},{2,18},{3,19},{4,20},{5,21},{6,22},{7,23},{8,24},{9,... | collective-permute-start | bytes 1007624 | tf_op jit(solution)/shard_map/ppermute | solution.py:79
  49.6 1.3 %collective-permute-done.11.shared_ref = f32[656,128]{1,0:T(8,128)S(1)} collective-permute-done((f32[656,128]{1,0:T(8,128)S(1)}, f32[656,128]{1,0:T(8,128)S(1)}, u32[]{:S(2)}, u32[]{:S(2)}) %collective-permute-start.11) | collective-permute-done | bytes 335904 | tf_op jit(solution)/shard_map/ppermute | solution.py:79
  50.9 2.0 %assemble.1.refs_0_.uv_ref = f32[34,288,128]{2,1,0:T(8,128)S(1)} custom-call(f32[51,128,128]{2,1,0:T(8,128)S(1)} %all_terms.1.uvw_ref, f32[51,128,128]{2,1,0:T(8,128)S(1)} %collective-permute-done.5.other_ref, f32[656,128]{1,0:T(8,128)S(1)} %collective-permute-done.6.got_ref, f32[656,128]{1,0:T(8,128)S(1)} %collective-permute-done.11.shared_ref, ...), custom_call_target="tpu_custom_call" | custom-call | bytes 7500000 | tf_op jit(solution)/shard_map/assemble/pallas_call | solution.py:90
  60.2 1.6 %collective-permute-start.21 = (f32[192,128]{1,0:T(8,128)S(1)}, f32[192,128]{1,0:T(8,128)S(1)}, u32[]{:S(2)}, u32[]{:S(2)}) collective-permute-start(f32[192,128]{1,0:T(8,128)S(1)} %get-tuple-element.62), channel_id=1, source_target_pairs={{64,0},{65,1},{66,2},{67,3},{68,4},{69,5},{70,6},{71,7},{72,8},{73... | collective-permute-start | bytes 294920 | tf_op jit(solution)/shard_map/ppermute | solution.py:79
  61.8 1.3 %collective-permute-start.22 = (f32[64,128]{1,0:T(8,128)S(1)}, f32[64,128]{1,0:T(8,128)S(1)}, u32[]{:S(2)}, u32[]{:S(2)}) collective-permute-start(f32[64,128]{1,0:T(8,128)S(1)} %get-tuple-element.63), channel_id=1, source_target_pairs={{64,31},{65,16},{66,17},{67,18},{68,19},{69,20},{70,21},{71,22},{7... | collective-permute-start | bytes 98312 | tf_op jit(solution)/shard_map/ppermute | solution.py:79
  63.1 1.3 %collective-permute-start.23 = (f32[24,128]{1,0:T(8,128)S(1)}, f32[24,128]{1,0:T(8,128)S(1)}, u32[]{:S(2)}, u32[]{:S(2)}) collective-permute-start(f32[24,128]{1,0:T(8,128)S(1)} %get-tuple-element.64), channel_id=1, source_target_pairs={{64,32},{65,33},{66,34},{67,35},{68,36},{69,37},{70,38},{71,39},{7... | collective-permute-start | bytes 36872 | tf_op jit(solution)/shard_map/ppermute | solution.py:79
  64.4 1.3 %collective-permute-start.24 = (f32[24,128]{1,0:T(8,128)S(1)}, f32[24,128]{1,0:T(8,128)S(1)}, u32[]{:S(2)}, u32[]{:S(2)}) collective-permute-start(f32[24,128]{1,0:T(8,128)S(1)} %get-tuple-element.64), channel_id=1, source_target_pairs={{64,63},{65,48},{66,49},{67,50},{68,51},{69,52},{70,53},{71,54},{7... | collective-permute-start | bytes 36872 | tf_op jit(solution)/shard_map/ppermute | solution.py:79
  66.9 16.6 %collective-permute-done.23.halo_ref = f32[24,128]{1,0:T(8,128)S(1)} collective-permute-done((f32[24,128]{1,0:T(8,128)S(1)}, f32[24,128]{1,0:T(8,128)S(1)}, u32[]{:S(2)}, u32[]{:S(2)}) %collective-permute-start.23) | collective-permute-done | bytes 12320 | tf_op jit(solution)/shard_map/ppermute | solution.py:79
  83.5 2.3 %collective-permute-done.24.halo_outer_ref = f32[24,128]{1,0:T(8,128)S(1)} collective-permute-done((f32[24,128]{1,0:T(8,128)S(1)}, f32[24,128]{1,0:T(8,128)S(1)}, u32[]{:S(2)}, u32[]{:S(2)}) %collective-permute-start.24) | collective-permute-done | bytes 12320 | tf_op jit(solution)/shard_map/ppermute | solution.py:79
  87.6 2.9 %collective-permute-start.25 = (f32[4,128,128]{2,1,0:T(8,128)S(1)}, f32[4,128,128]{2,1,0:T(8,128)S(1)}, u32[]{:S(2)}, u32[]{:S(2)}) collective-permute-start(f32[4,128,128]{2,1,0:T(8,128)S(1)} %get-tuple-element.68), channel_id=1, source_target_pairs={{0,16},{1,17},{2,18},{3,19},{4,20},{5,21},{6,22},{7,23},{8,24},{9,... | collective-permute-start | bytes 786440 | tf_op jit(solution)/shard_map/ppermute | solution.py:79
  93.1 1.5 %smooth_rest.1 = (f32[12,128,128]{2,1,0:T(8,128)S(1)}, f32[3,128,128]{2,1,0:T(8,128)S(1)}, f32[3,128,128]{2,1,0:T(8,128)S(1)}) custom-call(f32[12,288,128]{2,1,0:T(8,128)S(1)} %section_rest.1.layers_ref, f32[17,288,128]{2,1,0:T(8,128)S(1)} %assemble_w.1.w_ref), custom_call_target="tpu_custom_call" | custom-call | bytes 9000000 | tf_op jit(solution)/shard_map/smooth_rest/pallas_call | solution.py:90
  95.2 1.8 %collective-permute-start.29 = (f32[3,128,128]{2,1,0:T(8,128)S(1)}, f32[3,128,128]{2,1,0:T(8,128)S(1)}, u32[]{:S(2)}, u32[]{:S(2)}) collective-permute-start(f32[3,128,128]{2,1,0:T(8,128)S(1)} %get-tuple-element.74), channel_id=1, source_target_pairs={{0,192},{1,193},{2,194},{3,195},{4,196},{5,197},{6,198},{7,199},{8... | collective-permute-start | bytes 589832 | tf_op jit(solution)/shard_map/ppermute | solution.py:79
  97.0 4.3 %collective-permute-done.29.above_ref = f32[3,128,128]{2,1,0:T(8,128)S(1)} collective-permute-done((f32[3,128,128]{2,1,0:T(8,128)S(1)}, f32[3,128,128]{2,1,0:T(8,128)S(1)}, u32[]{:S(2)}, u32[]{:S(2)}) %collective-permute-start.29) | collective-permute-done | bytes 196640 | tf_op jit(solution)/shard_map/ppermute | solution.py:79
  102.0 1.5 %finish.1 = f32[16,128,128]{2,1,0:T(8,128)} custom-call(f32[12,128,128]{2,1,0:T(8,128)S(1)} %get-tuple-element.71.kept_ref, f32[3,128,128]{2,1,0:T(8,128)S(1)} %collective-permute-done.26.got_ref, f32[3,128,128]{2,1,0:T(8,128)S(1)} %collective-permute-done.27.got_more_ref, f32[5,128,128]{2,1,0:T(8,128)S(1)} %get-tuple-element.69.top_ref, ...), custom_call_target="tpu_custom_call" | custom-call | bytes 9000000 | tf_op jit(solution)/shard_map/finish/pallas_call | solution.py:90
  (66 shorter events, 22.6 us)
Async XLA Ops:
  2.3 20.7 %collective-permute-start = (f32[3,128,128]{2,1,0:T(8,128)}, f32[3,128,128]{2,1,0:T(8,128)S(1)}, u32[]{:S(2)}, u32[]{:S(2)}) collective-permute-start(f32[3,128,128]{2,1,0:T(8,128)} %get-tuple-element.40), channel_id=1, source_target_pairs={{0,192},{1,193},{2,194},{3,195},{4,196},{5,197},{6,198},{7,199},{8... | collective-permute-start | bytes 589832 | tf_op jit(solution)/shard_map/ppermute | solution.py:79
  6.0 13.8 %collective-permute-start.4 = (f32[16,128]{1,0:T(8,128)}, f32[16,128]{1,0:T(8,128)S(1)}, u32[]{:S(2)}, u32[]{:S(2)}) collective-permute-start(f32[16,128]{1,0:T(8,128)} %get-tuple-element.44), channel_id=1, source_target_pairs={{0,15},{1,0},{2,1},{3,2},{4,3},{5,4},{6,5},{7,6},{8,7},{9,8},{10,9... | collective-permute-start | bytes 24584 | tf_op jit(solution)/shard_map/ppermute | solution.py:79
  14.2 5.6 %collective-permute-start.1 = (f32[16,128]{1,0:T(8,128)}, f32[16,128]{1,0:T(8,128)S(1)}, u32[]{:S(2)}, u32[]{:S(2)}) collective-permute-start(f32[16,128]{1,0:T(8,128)} %get-tuple-element.41), channel_id=1, source_target_pairs={{0,16},{1,17},{2,18},{3,19},{4,20},{5,21},{6,22},{7,23},{8,24},{9,... | collective-permute-start | bytes 24584 | tf_op jit(solution)/shard_map/ppermute | solution.py:79
  15.4 4.3 %collective-permute-start.2 = (f32[16,128]{1,0:T(8,128)}, f32[16,128]{1,0:T(8,128)S(1)}, u32[]{:S(2)}, u32[]{:S(2)}) collective-permute-start(f32[16,128]{1,0:T(8,128)} %get-tuple-element.42), channel_id=1, source_target_pairs={{0,48},{1,49},{2,50},{3,51},{4,52},{5,53},{6,54},{7,55},{8,56},{9,... | collective-permute-start | bytes 24584 | tf_op jit(solution)/shard_map/ppermute | solution.py:79
  16.1 6.9 %collective-permute-start.3 = (f32[16,128]{1,0:T(8,128)}, f32[16,128]{1,0:T(8,128)S(1)}, u32[]{:S(2)}, u32[]{:S(2)}) collective-permute-start(f32[16,128]{1,0:T(8,128)} %get-tuple-element.43), channel_id=1, source_target_pairs={{0,1},{1,2},{2,3},{3,4},{4,5},{5,6},{6,7},{7,8},{8,9},{9,10},{10,1... | collective-permute-start | bytes 24584 | tf_op jit(solution)/shard_map/ppermute | solution.py:79
  25.0 25.9 %collective-permute-start.5 = (f32[51,128,128]{2,1,0:T(8,128)S(1)}, f32[51,128,128]{2,1,0:T(8,128)S(1)}, u32[]{:S(2)}, u32[]{:S(2)}) collective-permute-start(f32[51,128,128]{2,1,0:T(8,128)S(1)} %all_terms.1.uvw_ref), channel_id=1, source_target_pairs={{0,16},{1,17},{2,18},{3,19},{4,20},{5,21},{6,22},{7,23},{8,24},{9,... | collective-permute-start | bytes 10027016 | tf_op jit(solution)/shard_map/ppermute | solution.py:79
  26.7 18.7 %collective-permute-start.6 = (f32[656,128]{1,0:T(8,128)S(1)}, f32[656,128]{1,0:T(8,128)S(1)}, u32[]{:S(2)}, u32[]{:S(2)}) collective-permute-start(f32[656,128]{1,0:T(8,128)S(1)} %pack_rows.1), channel_id=1, source_target_pairs={{16,32},{17,33},{18,34},{19,35},{20,36},{21,37},{22,38},{23,39},{2... | collective-permute-start | bytes 1007624 | tf_op jit(solution)/shard_map/ppermute | solution.py:79
  31.0 13.9 %collective-permute-start.7 = (f32[480,128]{1,0:T(8,128)S(1)}, f32[480,128]{1,0:T(8,128)S(1)}, u32[]{:S(2)}, u32[]{:S(2)}) collective-permute-start(f32[480,128]{1,0:T(8,128)S(1)} %get-tuple-element.47), channel_id=1, source_target_pairs={{0,1},{1,2},{2,3},{3,4},{4,5},{5,6},{6,7},{7,8},{8,9},{9,10},{10,1... | collective-permute-start | bytes 737288 | tf_op jit(solution)/shard_map/ppermute | solution.py:79
  32.7 12.7 %collective-permute-start.8 = (f32[480,128]{1,0:T(8,128)S(1)}, f32[480,128]{1,0:T(8,128)S(1)}, u32[]{:S(2)}, u32[]{:S(2)}) collective-permute-start(f32[480,128]{1,0:T(8,128)S(1)} %get-tuple-element.48), channel_id=1, source_target_pairs={{0,31},{1,16},{2,17},{3,18},{4,19},{5,20},{6,21},{7,22},{8,23},{9,... | collective-permute-start | bytes 737288 | tf_op jit(solution)/shard_map/ppermute | solution.py:79
  34.1 10.9 %collective-permute-start.10 = (f32[96,128]{1,0:T(8,128)S(1)}, f32[96,128]{1,0:T(8,128)S(1)}, u32[]{:S(2)}, u32[]{:S(2)}) collective-permute-start(f32[96,128]{1,0:T(8,128)S(1)} %pick_corner.1), channel_id=1, source_target_pairs={{0,63},{1,48},{2,49},{3,50},{4,51},{5,52},{6,53},{7,54},{8,55},{9,... | collective-permute-start | bytes 147464 | tf_op jit(solution)/shard_map/ppermute | solution.py:79
  45.4 5.4 %collective-permute-start.11 = (f32[656,128]{1,0:T(8,128)S(1)}, f32[656,128]{1,0:T(8,128)S(1)}, u32[]{:S(2)}, u32[]{:S(2)}) collective-permute-start(f32[656,128]{1,0:T(8,128)S(1)} %collective-permute-done.6.got_ref), channel_id=1, source_target_pairs={{0,16},{1,17},{2,18},{3,19},{4,20},{5,21},{6,22},{7,23},{8,24},{9,... | collective-permute-start | bytes 1007624 | tf_op jit(solution)/shard_map/ppermute | solution.py:79
  52.9 2.7 %collective-permute-start.12 = (f32[192,128]{1,0:T(8,128)S(1)}, f32[192,128]{1,0:T(8,128)S(1)}, u32[]{:S(2)}, u32[]{:S(2)}) collective-permute-start(f32[192,128]{1,0:T(8,128)S(1)} %get-tuple-element.52), channel_id=1, source_target_pairs={{192,128},{193,129},{194,130},{195,131},{196,132},{197,133},{198,1... | collective-permute-start | bytes 294920 | tf_op jit(solution)/shard_map/ppermute | solution.py:79
  53.6 2.0 %collective-permute-start.13 = (f32[64,128]{1,0:T(8,128)S(1)}, f32[64,128]{1,0:T(8,128)S(1)}, u32[]{:S(2)}, u32[]{:S(2)}) collective-permute-start(f32[64,128]{1,0:T(8,128)S(1)} %get-tuple-element.53), channel_id=1, source_target_pairs={{192,159},{193,144},{194,145},{195,146},{196,147},{197,148},{198,1... | collective-permute-start | bytes 98312 | tf_op jit(solution)/shard_map/ppermute | solution.py:79
  57.3 2.7 %collective-permute-start.17 = (f32[256,128]{1,0:T(8,128)S(1)}, f32[256,128]{1,0:T(8,128)S(1)}, u32[]{:S(2)}, u32[]{:S(2)}) collective-permute-start(f32[256,128]{1,0:T(8,128)S(1)} %get-tuple-element.57), channel_id=1, source_target_pairs={{128,64},{129,65},{130,66},{131,67},{132,68},{133,69},{134,70},{13... | collective-permute-start | bytes 393224 | tf_op jit(solution)/shard_map/ppermute | solution.py:79
  58.0 2.0 %collective-permute-start.18 = (f32[64,128]{1,0:T(8,128)S(1)}, f32[64,128]{1,0:T(8,128)S(1)}, u32[]{:S(2)}, u32[]{:S(2)}) collective-permute-start(f32[64,128]{1,0:T(8,128)S(1)} %get-tuple-element.58), channel_id=1, source_target_pairs={{128,95},{129,80},{130,81},{131,82},{132,83},{133,84},{134,85},{13... | collective-permute-start | bytes 98312 | tf_op jit(solution)/shard_map/ppermute | solution.py:79
  60.2 25.6 %collective-permute-start.21 = (f32[192,128]{1,0:T(8,128)S(1)}, f32[192,128]{1,0:T(8,128)S(1)}, u32[]{:S(2)}, u32[]{:S(2)}) collective-permute-start(f32[192,128]{1,0:T(8,128)S(1)} %get-tuple-element.62), channel_id=1, source_target_pairs={{64,0},{65,1},{66,2},{67,3},{68,4},{69,5},{70,6},{71,7},{72,8},{73... | collective-permute-start | bytes 294920 | tf_op jit(solution)/shard_map/ppermute | solution.py:79
  61.8 24.1 %collective-permute-start.22 = (f32[64,128]{1,0:T(8,128)S(1)}, f32[64,128]{1,0:T(8,128)S(1)}, u32[]{:S(2)}, u32[]{:S(2)}) collective-permute-start(f32[64,128]{1,0:T(8,128)S(1)} %get-tuple-element.63), channel_id=1, source_target_pairs={{64,31},{65,16},{66,17},{67,18},{68,19},{69,20},{70,21},{71,22},{7... | collective-permute-start | bytes 98312 | tf_op jit(solution)/shard_map/ppermute | solution.py:79
  63.1 20.4 %collective-permute-start.23 = (f32[24,128]{1,0:T(8,128)S(1)}, f32[24,128]{1,0:T(8,128)S(1)}, u32[]{:S(2)}, u32[]{:S(2)}) collective-permute-start(f32[24,128]{1,0:T(8,128)S(1)} %get-tuple-element.64), channel_id=1, source_target_pairs={{64,32},{65,33},{66,34},{67,35},{68,36},{69,37},{70,38},{71,39},{7... | collective-permute-start | bytes 36872 | tf_op jit(solution)/shard_map/ppermute | solution.py:79
  64.4 21.5 %collective-permute-start.24 = (f32[24,128]{1,0:T(8,128)S(1)}, f32[24,128]{1,0:T(8,128)S(1)}, u32[]{:S(2)}, u32[]{:S(2)}) collective-permute-start(f32[24,128]{1,0:T(8,128)S(1)} %get-tuple-element.64), channel_id=1, source_target_pairs={{64,63},{65,48},{66,49},{67,50},{68,51},{69,52},{70,53},{71,54},{7... | collective-permute-start | bytes 36872 | tf_op jit(solution)/shard_map/ppermute | solution.py:79
  87.6 4.0 %collective-permute-start.25 = (f32[4,128,128]{2,1,0:T(8,128)S(1)}, f32[4,128,128]{2,1,0:T(8,128)S(1)}, u32[]{:S(2)}, u32[]{:S(2)}) collective-permute-start(f32[4,128,128]{2,1,0:T(8,128)S(1)} %get-tuple-element.68), channel_id=1, source_target_pairs={{0,16},{1,17},{2,18},{3,19},{4,20},{5,21},{6,22},{7,23},{8,24},{9,... | collective-permute-start | bytes 786440 | tf_op jit(solution)/shard_map/ppermute | solution.py:79
  91.7 10.2 %collective-permute-start.28 = (f32[5,128,128]{2,1,0:T(8,128)S(1)}, f32[5,128,128]{2,1,0:T(8,128)S(1)}, u32[]{:S(2)}, u32[]{:S(2)}) collective-permute-start(f32[5,128,128]{2,1,0:T(8,128)S(1)} %get-tuple-element.69.top_ref), channel_id=1, source_target_pairs={{0,64},{1,65},{2,66},{3,67},{4,68},{5,69},{6,70},{7,71},{8,72},{9,... | collective-permute-start | bytes 983048 | tf_op jit(solution)/shard_map/ppermute | solution.py:79
  94.6 2.4 %collective-permute-start.26 = (f32[3,128,128]{2,1,0:T(8,128)S(1)}, f32[3,128,128]{2,1,0:T(8,128)S(1)}, u32[]{:S(2)}, u32[]{:S(2)}) collective-permute-start(f32[3,128,128]{2,1,0:T(8,128)S(1)} %get-tuple-element.72), channel_id=1, source_target_pairs={{0,16},{1,17},{2,18},{3,19},{4,20},{5,21},{6,22},{7,23},{8,24},{9,... | collective-permute-start | bytes 589832 | tf_op jit(solution)/shard_map/ppermute | solution.py:79
  95.1 1.9 %collective-permute-start.27 = (f32[3,128,128]{2,1,0:T(8,128)S(1)}, f32[3,128,128]{2,1,0:T(8,128)S(1)}, u32[]{:S(2)}, u32[]{:S(2)}) collective-permute-start(f32[3,128,128]{2,1,0:T(8,128)S(1)} %get-tuple-element.73), channel_id=1, source_target_pairs={{0,16},{1,17},{2,18},{3,19},{4,20},{5,21},{6,22},{7,23},{8,24},{9,... | collective-permute-start | bytes 589832 | tf_op jit(solution)/shard_map/ppermute | solution.py:79
  95.2 6.1 %collective-permute-start.29 = (f32[3,128,128]{2,1,0:T(8,128)S(1)}, f32[3,128,128]{2,1,0:T(8,128)S(1)}, u32[]{:S(2)}, u32[]{:S(2)}) collective-permute-start(f32[3,128,128]{2,1,0:T(8,128)S(1)} %get-tuple-element.74), channel_id=1, source_target_pairs={{0,192},{1,193},{2,194},{3,195},{4,196},{5,197},{6,198},{7,199},{8... | collective-permute-start | bytes 589832 | tf_op jit(solution)/shard_map/ppermute | solution.py:79
  (12 other events, 27.0 us)

commit v8 on v7

--- a/solution.py
+++ b/solution.py
@@ -24,7 +24,8 @@
 SLABS = ((16, 15, 14, 3), (13, 12, 11, 8, 0), (10, 9, 7, 6, 5, 2), (4, 1))
 FOLDED = 32
 SLAB_ROWS = 3 * 128 + FOLDED + 64
-CORNER_ROWS = 3 * 24 + 16 + 8
+CORNERS = ((0, 24), (24, 24), (48, 16), (64, 8), (72, 8))
+CORNER_ROWS = 80
 
 
 def width_of(layer):
@@ -36,7 +37,7 @@
 
 
 MICROSECONDS = {"all_terms": 2.5, "assemble": 2.5, "section": 1.5, "section_rest": 3.0, "smooth_rest": 3.0, "finish": 3.0}
-VMEM_LIMIT = {"edges": (64 << 20) - (64 << 10)}
+VMEM_LIMIT = {"edges": 52 << 20}
 
 
 def strips():
@@ -231,17 +232,32 @@
 
 
 def all_terms(
-    sizes, p_ref, f_ref, s_ref, above_ref, inner_ref, outer_ref, left_ref, right_ref, early_ref, uvw_ref, powers, turned
+    sizes, p_ref, f_ref, s_ref, above_ref, inner_ref, outer_ref, left_ref, right_ref, early_ref,
+    uvw_ref, rows_ref, same_ref, cross_ref, keep_ref, give_ref, powers, turned, w_slabs,
 ):
+    c = core()
     beside = columns_beside(left_ref, right_ref, turned)
     norms = 1.0 / plane_norms(sizes)
     gz = lax.axis_index("gz")
     layer0 = gz * LAYERS
-    uvw_ref[0] = s_ref[0]
-    uvw_ref[STEPS] = power39(p_ref[0])
-    uvw_ref[2 * STEPS] = norms * (1.0 / norm_of(0 * layer0, sizes[0] * LAYERS))
-    for layer in range(1, STEPS):
-        total = neighbours(p_ref[layer - 1], layer - 1, inner_ref, outer_ref, beside, powers)
+    lane = lanes(128)
+    half_lane = lanes(64)
+
+    def put(slab, at, left, right):
+        count = left.shape[0]
+        same_ref[pl.ds(at, count), :] = jnp.where(c == 0, right, left)
+        cross_ref[pl.ds(at, count), :] = jnp.where(c == 0, left, right)
+
+    def put_corner(slab, left, right):
+        at, rows = CORNERS[slab]
+        first, last = slice(0, rows), slice(left.shape[0] - rows, left.shape[0])
+        keep_ref[pl.ds(at, rows), :] = jnp.where(c == 0, left[first], right[last])
+        give_ref[pl.ds(at, rows), :] = jnp.where(c == 0, right[first], left[last])
+
+    def terms_of(layer, slot):
+        if layer == 0:
+            return s_ref[0], power39(p_ref[0]), norms * (1.0 / norm_of(0 * layer0, sizes[0] * LAYERS))
+        total = neighbours(p_ref[layer - 1], layer - 1, inner_ref, outer_ref, beside, powers.at[slot])
         if layer < LAYERS:
             p, f, s = p_ref[layer], f_ref[layer], s_ref[layer]
         else:
@@ -250,70 +266,54 @@
         if layer == LAYERS:
             there = one_if(gz < sizes[0] - 1)
             u, v = u * there, v * there
-        norm_z = norm_of(layer0 + layer, sizes[0] * LAYERS)
-        uvw_ref[layer] = u
-        uvw_ref[STEPS + layer] = v
-        uvw_ref[2 * STEPS + layer] = low * inverse * (norms * (1.0 / norm_z))
-
-
-def plane_of(uvw_ref, name, layer):
-    return uvw_ref.at[STEPS * "uvw".index(name) + layer]
-
-
-def pack_rows(uvw_ref, rows_ref):
-    c = core()
-    for (name, layer), (at, rows) in ROW_PLACES.items():
-        start = aligned(c * (128 - rows), 8)
-        rows_ref[pl.ds(at, rows), :] = plane_of(uvw_ref, name, layer)[pl.ds(start, rows), :]
-
-
-def pack(uvw_ref, same_ref, cross_ref, keep_ref, give_ref):
-    c = core()
-
-    def put(at, left, right):
-        count = left.shape[0]
-        same_ref[pl.ds(at, count), :] = jnp.where(c == 0, right, left)
-        cross_ref[pl.ds(at, count), :] = jnp.where(c == 0, left, right)
-
-    def put_corner(at, rows, left, right):
-        first, last = slice(0, rows), slice(left.shape[0] - rows, left.shape[0])
-        keep_ref[pl.ds(at, rows), :] = jnp.where(c == 0, left[first], right[last])
-        give_ref[pl.ds(at, rows), :] = jnp.where(c == 0, right[first], left[last])
-
-    lane = lanes(128)
-    for slab in range(4):
+        return u, v, low * inverse * (norms * (1.0 / norm_of(layer0 + layer, sizes[0] * LAYERS)))
+
+    w_slabs[...] = jnp.zeros(w_slabs.shape, F32)
+    count = 0
+    for slab, layers in enumerate(SLABS):
         left = right = jnp.zeros((128, 128), F32)
-        for name, layer, where, at in strips():
-            if where == slab:
-                width = width_of(layer)
-                plane = plane_of(uvw_ref, name, layer)[...]
+        at = 0
+        for layer in layers:
+            u, v, w = terms_of(layer, count % 2)
+            count += 1
+            uvw_ref[layer] = u
+            uvw_ref[STEPS + layer] = v
+            uvw_ref[2 * STEPS + layer] = w
+            width = width_of(layer)
+            for plane in (u, v):
                 inside = (lane >= at) & (lane < at + width)
                 left = jnp.where(inside, pltpu.roll(plane, at, 1) if at else plane, left)
                 right = jnp.where(inside, pltpu.roll(plane, (at + width) % 128, 1), right)
+                at += width
+            if layer == 0:
+                continue
+            for half in range(2):
+                plane = w[64 * half:64 * half + 64]
+                begin = 64 * half + RADIUS * (layer - 1)
+                inside = (half_lane >= begin) & (half_lane < begin + RADIUS)
+                moved_left = pltpu.roll(plane, begin, 1) if begin else plane
+                w_slabs[0] = jnp.where(inside, moved_left, w_slabs[0])
+                w_slabs[1] = jnp.where(inside, pltpu.roll(plane, (begin + RADIUS) % 128, 1), w_slabs[1])
+        put_corner(slab, left, right)
         if slab < 3:
-            put(128 * slab, left, right)
-            put_corner(24 * slab, 24, left, right)
+            put(slab, 128 * slab, left, right)
             continue
-        put_corner(72, 16, left, right)
         folded = []
         for value in (left, right):
             total = value[:FOLDED]
             for i in range(1, 4):
                 total = total + pltpu.roll(value[FOLDED * i:FOLDED * (i + 1)], FOLDED * i, 1)
             folded.append(total)
-        put(384, *folded)
-    lane = lanes(64)
-    left = right = jnp.zeros((64, 128), F32)
-    for layer in range(1, STEPS):
-        ref = plane_of(uvw_ref, "w", layer)
-        for half in range(2):
-            plane = ref[pl.ds(64 * half, 64), :]
-            at = 64 * half + RADIUS * (layer - 1)
-            inside = (lane >= at) & (lane < at + RADIUS)
-            left = jnp.where(inside, pltpu.roll(plane, at, 1) if at else plane, left)
-            right = jnp.where(inside, pltpu.roll(plane, (at + RADIUS) % 128, 1), right)
-    put(384 + FOLDED, left, right)
-    put_corner(88, 8, left, right)
+        put(slab, 384, *folded)
+    put(4, 384 + FOLDED, w_slabs[0], w_slabs[1])
+    put_corner(4, w_slabs[0], w_slabs[1])
+    for (name, layer), (at, rows) in ROW_PLACES.items():
+        start = aligned(c * (128 - rows), 8)
+        rows_ref[pl.ds(at, rows), :] = plane_of(uvw_ref, name, layer)[pl.ds(start, rows), :]
+
+
+def plane_of(uvw_ref, name, layer):
+    return uvw_ref.at[STEPS * "uvw".index(name) + layer]
 
 
 def pick_corner(keep_ref, got_ref, corner_ref):
@@ -358,14 +358,14 @@
         if slab < 3:
             here = pl.ds(128 * slab, 128)
             same, cross = same_ref[here, :], cross_ref[here, :]
-            here = pl.ds(24 * slab, 24)
+            here = pl.ds(*CORNERS[slab])
         else:
             here = pl.ds(384, FOLDED)
             same, cross = (
                 jnp.concatenate([value] + [pltpu.roll(value, 128 - FOLDED * i, 1) for i in range(1, 4)], axis=0)
                 for value in (same_ref[here, :], cross_ref[here, :])
             )
-            here = pl.ds(72, 16)
+            here = pl.ds(*CORNERS[3])
         corner = corner_ref[here, :]
         slot = plain.at[slab % 2]
         slab_plane(slot, same, cross, corner)
@@ -384,7 +384,7 @@
         value = ref[pl.ds(384 + FOLDED, 64), :]
         return jnp.concatenate([value, pltpu.roll(value, 64, 1)], axis=0)
 
-    here = pl.ds(88, 8)
+    here = pl.ds(*CORNERS[4])
     corner = corner_ref[here, :]
     corner = pltpu.roll(corner, 64 * seam(), 1)
     slab_plane(plain.at[0], unfolded(same_ref), unfolded(cross_ref), corner)
@@ -648,17 +648,14 @@
     outer = moved(outer, lambda z, y, x: (z, y ^ 3, x))
     inner = to_other(inner)
     ready = call(early, shape(8, 128), printed, filtered, after(sensitivity, left))
-    uvw = call(
-        functools.partial(all_terms, sizes), shape(3 * STEPS, 128, 128),
+    slab, corner = shape(SLAB_ROWS, 128), shape(CORNER_ROWS, 128)
+    uvw, rows, to_same, to_cross, keep, give = call(
+        functools.partial(all_terms, sizes),
+        [shape(3 * STEPS, 128, 128), shape(ROW_TOTAL, 128), slab, slab, corner, corner],
         printed, filtered, sensitivity, above, inner, outer, from_left, from_right, ready,
-        scratch=[
-            pltpu.VMEM((144, 128), F32), pltpu.VMEM((128, 128), F32),
-        ],
+        scratch=[pltpu.VMEM((2, 144, 128), F32), pltpu.VMEM((128, 128), F32), pltpu.VMEM((2, 64, 128), F32)],
     )
-    slab, corner = shape(SLAB_ROWS, 128), shape(CORNER_ROWS, 128)
-    rows = call(pack_rows, shape(ROW_TOTAL, 128), uvw)
     got = moved(rows, across)
-    to_same, to_cross, keep, give = call(pack, [slab, slab, corner, corner], after(uvw, rows))
     from_same = moved(to_same, same)
     from_cross = moved(to_cross, beside)
     corner = call(pick_corner, corner, keep, to_other(give))

time: 105 us -> 106 us (level)
  waiting for transfers between devices: 41.6 us -> 47.9 us
  starting transfers between devices: 42.1 us -> 39.2 us
  local copies, waits for them, and re-layouts: 3.69 us -> 1.25 us
    ppermute x30, waiting for transfers between devices: 41.6 us -> 47.9 us  [moved(): return lax.ppermute(value, AXES, pairs)]
    ppermute x30, starting transfers between devices: 42.1 us -> 39.2 us  [moved(): return lax.ppermute(value, AXES, pairs)]
    unnamed x12, local copies, waits for them, and re-layouts: 3.69 us -> 1.25 us
    pallas_call x18 -> x16, Pallas kernels: 15.8 us -> 15.3 us  [call(): pl.pallas_call(kernel, out_shape=outs, scratch_shapes=list(scratch), comp...]
  transfers between devices with their start and end apart: 30 -> 30, of which waited for: 11 -> 13; matrix products, arithmetic and copies ran while one was open for 0% -> 0% of each run, Pallas kernels for 6% -> 4%
where the time goes in v8:
time: 106 us; the launch traced here: 104 us
  waiting for transfers between devices  47.9 us (45%)
  starting transfers between devices  39.2 us (37%)
  Pallas kernels  15.3 us (14%)
  local copies, waits for them, and re-layouts  1.25 us (1%)
    ppermute x30, waiting for transfers between devices, moved(): return lax.ppermute(value, AXES, pairs)  47.9 us
    ppermute x30, starting transfers between devices, moved(): return lax.ppermute(value, AXES, pairs)  39.2 us
    pallas_call x16, Pallas kernels, call(): pl.pallas_call(kernel, out_shape=outs, scratch_shapes=list(scratch), comp...  15.3 us
  transfers between devices with their start and end apart: 30, of which 13 were waited for; matrix products, arithmetic and copies ran while one was open for 0% of the time, Pallas kernels for 4%

profile of v8, /device:TPU:1, one launch (start us, length us, event | category | flops | bytes accessed | tf_op | source)
XLA Modules:
  0.0 104.0 jit_solution(8967439460635644948)
XLA Ops:
  2.4 3.6 %collective-permute-start = (f32[3,128,128]{2,1,0:T(8,128)S(1)}, f32[3,128,128]{2,1,0:T(8,128)S(1)}, u32[]{:S(2)}, u32[]{:S(2)}) collective-permute-start(f32[3,128,128]{2,1,0:T(8,128)S(1)} %get-tuple-element.41), channel_id=1, source_target_pairs={{0,192},{1,193},{2,194},{3,195},{4,196},{5,197},{6,198},{7,199},{8... | collective-permute-start | bytes 589832 | tf_op jit(solution)/shard_map/ppermute | solution.py:80
  6.0 8.2 %collective-permute-start.4 = (f32[16,128]{1,0:T(8,128)S(1)}, f32[16,128]{1,0:T(8,128)S(1)}, u32[]{:S(2)}, u32[]{:S(2)}) collective-permute-start(f32[16,128]{1,0:T(8,128)S(1)} %get-tuple-element.45), channel_id=1, source_target_pairs={{0,15},{1,0},{2,1},{3,2},{4,3},{5,4},{6,5},{7,6},{8,7},{9,8},{10,9... | collective-permute-start | bytes 24584 | tf_op jit(solution)/shard_map/ppermute | solution.py:80
  14.2 1.2 %collective-permute-start.1 = (f32[16,128]{1,0:T(8,128)S(1)}, f32[16,128]{1,0:T(8,128)S(1)}, u32[]{:S(2)}, u32[]{:S(2)}) collective-permute-start(f32[16,128]{1,0:T(8,128)S(1)} %get-tuple-element.42), channel_id=1, source_target_pairs={{0,16},{1,17},{2,18},{3,19},{4,20},{5,21},{6,22},{7,23},{8,24},{9,... | collective-permute-start | bytes 24584 | tf_op jit(solution)/shard_map/ppermute | solution.py:80
  16.3 2.2 %collective-permute-done.2.outer_ref = f32[16,128]{1,0:T(8,128)S(1)} collective-permute-done((f32[16,128]{1,0:T(8,128)S(1)}, f32[16,128]{1,0:T(8,128)S(1)}, u32[]{:S(2)}, u32[]{:S(2)}) %collective-permute-start.2) | collective-permute-done | bytes 8224 | tf_op jit(solution)/shard_map/ppermute | solution.py:80
  18.5 4.3 %collective-permute-done.3.left_ref = f32[16,128]{1,0:T(8,128)S(1)} collective-permute-done((f32[16,128]{1,0:T(8,128)S(1)}, f32[16,128]{1,0:T(8,128)S(1)}, u32[]{:S(2)}, u32[]{:S(2)}) %collective-permute-start.3) | collective-permute-done | bytes 8224 | tf_op jit(solution)/shard_map/ppermute | solution.py:80
  22.8 4.3 %all_terms.1 = (f32[51,128,128]{2,1,0:T(8,128)S(1)}, f32[656,128]{1,0:T(8,128)S(1)}, f32[480,128]{1,0:T(8,128)S(1)}, f32[480,128]{1,0:T(8,128)S(1)}, f32[80,128]{1,0:T(8,128)S(1)}, /*index=5*/f32[80,128]{1,0:T(8,128)S(1)}) custom-call(f32[16,128,128]{2,1,0:T(8,128)S(1)} %copy-done.2, f32[16,128,128]{2,1,0:T(8,128)S(1)} %copy-done.3, ...), custom_call_target="tpu_custom_call" | custom-call | bytes 7500000 | tf_op jit(solution)/shard_map/all_terms/pallas_call | solution.py:91
  27.1 1.7 %collective-permute-start.5 = (f32[51,128,128]{2,1,0:T(8,128)S(1)}, f32[51,128,128]{2,1,0:T(8,128)S(1)}, u32[]{:S(2)}, u32[]{:S(2)}) collective-permute-start(f32[51,128,128]{2,1,0:T(8,128)S(1)} %get-tuple-element.68.uvw_ref), channel_id=1, source_target_pairs={{0,16},{1,17},{2,18},{3,19},{4,20},{5,21},{6,22},{7,23},{8,24},{9,... | collective-permute-start | bytes 10027016 | tf_op jit(solution)/shard_map/ppermute | solution.py:80
  28.9 2.5 %collective-permute-start.6 = (f32[656,128]{1,0:T(8,128)S(1)}, f32[656,128]{1,0:T(8,128)S(1)}, u32[]{:S(2)}, u32[]{:S(2)}) collective-permute-start(f32[656,128]{1,0:T(8,128)S(1)} %get-tuple-element.48), channel_id=1, source_target_pairs={{16,32},{17,33},{18,34},{19,35},{20,36},{21,37},{22,38},{23,39},{2... | collective-permute-start | bytes 1007624 | tf_op jit(solution)/shard_map/ppermute | solution.py:80
  31.7 2.8 %collective-permute-done.9.got_ref = f32[80,128]{1,0:T(8,128)S(1)} collective-permute-done((f32[80,128]{1,0:T(8,128)S(1)}, f32[80,128]{1,0:T(8,128)S(1)}, u32[]{:S(2)}, u32[]{:S(2)}) %collective-permute-start.9) | collective-permute-done | bytes 40992 | tf_op jit(solution)/shard_map/ppermute | solution.py:80
  34.6 10.8 %collective-permute-done.10.corner_ref = f32[80,128]{1,0:T(8,128)S(1)} collective-permute-done((f32[80,128]{1,0:T(8,128)S(1)}, f32[80,128]{1,0:T(8,128)S(1)}, u32[]{:S(2)}, u32[]{:S(2)}) %collective-permute-start.10) | collective-permute-done | bytes 40992 | tf_op jit(solution)/shard_map/ppermute | solution.py:80
  45.9 4.5 %collective-permute-start.11 = (f32[656,128]{1,0:T(8,128)S(1)}, f32[656,128]{1,0:T(8,128)S(1)}, u32[]{:S(2)}, u32[]{:S(2)}) collective-permute-start(f32[656,128]{1,0:T(8,128)S(1)} %collective-permute-done.6.got_ref), channel_id=1, source_target_pairs={{0,16},{1,17},{2,18},{3,19},{4,20},{5,21},{6,22},{7,23},{8,24},{9,... | collective-permute-start | bytes 1007624 | tf_op jit(solution)/shard_map/ppermute | solution.py:80
  50.4 1.3 %collective-permute-done.11.shared_ref = f32[656,128]{1,0:T(8,128)S(1)} collective-permute-done((f32[656,128]{1,0:T(8,128)S(1)}, f32[656,128]{1,0:T(8,128)S(1)}, u32[]{:S(2)}, u32[]{:S(2)}) %collective-permute-start.11) | collective-permute-done | bytes 335904 | tf_op jit(solution)/shard_map/ppermute | solution.py:80
  51.7 2.0 %assemble.1.refs_0_.uv_ref = f32[34,288,128]{2,1,0:T(8,128)S(1)} custom-call(f32[51,128,128]{2,1,0:T(8,128)S(1)} %get-tuple-element.68.uvw_ref, f32[51,128,128]{2,1,0:T(8,128)S(1)} %collective-permute-done.5.other_ref, f32[656,128]{1,0:T(8,128)S(1)} %collective-permute-done.6.got_ref, f32[656,128]{1,0:T(8,128)S(1)} %collective-permute-done.11.shared_ref, ...), custom_call_target="tpu_custom_call" | custom-call | bytes 7500000 | tf_op jit(solution)/shard_map/assemble/pallas_call | solution.py:91
  61.1 1.6 %collective-permute-start.21 = (f32[192,128]{1,0:T(8,128)S(1)}, f32[192,128]{1,0:T(8,128)S(1)}, u32[]{:S(2)}, u32[]{:S(2)}) collective-permute-start(f32[192,128]{1,0:T(8,128)S(1)} %get-tuple-element.64), channel_id=1, source_target_pairs={{64,0},{65,1},{66,2},{67,3},{68,4},{69,5},{70,6},{71,7},{72,8},{73... | collective-permute-start | bytes 294920 | tf_op jit(solution)/shard_map/ppermute | solution.py:80
  62.6 1.3 %collective-permute-start.22 = (f32[64,128]{1,0:T(8,128)S(1)}, f32[64,128]{1,0:T(8,128)S(1)}, u32[]{:S(2)}, u32[]{:S(2)}) collective-permute-start(f32[64,128]{1,0:T(8,128)S(1)} %get-tuple-element.65), channel_id=1, source_target_pairs={{64,31},{65,16},{66,17},{67,18},{68,19},{69,20},{70,21},{71,22},{7... | collective-permute-start | bytes 98312 | tf_op jit(solution)/shard_map/ppermute | solution.py:80
  63.9 1.3 %collective-permute-start.23 = (f32[24,128]{1,0:T(8,128)S(1)}, f32[24,128]{1,0:T(8,128)S(1)}, u32[]{:S(2)}, u32[]{:S(2)}) collective-permute-start(f32[24,128]{1,0:T(8,128)S(1)} %get-tuple-element.66), channel_id=1, source_target_pairs={{64,32},{65,33},{66,34},{67,35},{68,36},{69,37},{70,38},{71,39},{7... | collective-permute-start | bytes 36872 | tf_op jit(solution)/shard_map/ppermute | solution.py:80
  65.2 1.3 %collective-permute-start.24 = (f32[24,128]{1,0:T(8,128)S(1)}, f32[24,128]{1,0:T(8,128)S(1)}, u32[]{:S(2)}, u32[]{:S(2)}) collective-permute-start(f32[24,128]{1,0:T(8,128)S(1)} %get-tuple-element.66), channel_id=1, source_target_pairs={{64,63},{65,48},{66,49},{67,50},{68,51},{69,52},{70,53},{71,54},{7... | collective-permute-start | bytes 36872 | tf_op jit(solution)/shard_map/ppermute | solution.py:80
  67.8 16.5 %collective-permute-done.23.halo_ref = f32[24,128]{1,0:T(8,128)S(1)} collective-permute-done((f32[24,128]{1,0:T(8,128)S(1)}, f32[24,128]{1,0:T(8,128)S(1)}, u32[]{:S(2)}, u32[]{:S(2)}) %collective-permute-start.23) | collective-permute-done | bytes 12320 | tf_op jit(solution)/shard_map/ppermute | solution.py:80
  84.3 2.3 %collective-permute-done.24.halo_outer_ref = f32[24,128]{1,0:T(8,128)S(1)} collective-permute-done((f32[24,128]{1,0:T(8,128)S(1)}, f32[24,128]{1,0:T(8,128)S(1)}, u32[]{:S(2)}, u32[]{:S(2)}) %collective-permute-start.24) | collective-permute-done | bytes 12320 | tf_op jit(solution)/shard_map/ppermute | solution.py:80
  88.3 2.7 %collective-permute-start.25 = (f32[4,128,128]{2,1,0:T(8,128)S(1)}, f32[4,128,128]{2,1,0:T(8,128)S(1)}, u32[]{:S(2)}, u32[]{:S(2)}) collective-permute-start(f32[4,128,128]{2,1,0:T(8,128)S(1)} %get-tuple-element.70), channel_id=1, source_target_pairs={{0,16},{1,17},{2,18},{3,19},{4,20},{5,21},{6,22},{7,23},{8,24},{9,... | collective-permute-start | bytes 786440 | tf_op jit(solution)/shard_map/ppermute | solution.py:80
  93.6 1.5 %smooth_rest.1 = (f32[12,128,128]{2,1,0:T(8,128)S(1)}, f32[3,128,128]{2,1,0:T(8,128)S(1)}, f32[3,128,128]{2,1,0:T(8,128)S(1)}) custom-call(f32[12,288,128]{2,1,0:T(8,128)S(1)} %section_rest.1.layers_ref, f32[17,288,128]{2,1,0:T(8,128)S(1)} %assemble_w.1.w_ref), custom_call_target="tpu_custom_call" | custom-call | bytes 9000000 | tf_op jit(solution)/shard_map/smooth_rest/pallas_call | solution.py:91
  95.8 1.8 %collective-permute-start.29 = (f32[3,128,128]{2,1,0:T(8,128)S(1)}, f32[3,128,128]{2,1,0:T(8,128)S(1)}, u32[]{:S(2)}, u32[]{:S(2)}) collective-permute-start(f32[3,128,128]{2,1,0:T(8,128)S(1)} %get-tuple-element.76), channel_id=1, source_target_pairs={{0,192},{1,193},{2,194},{3,195},{4,196},{5,197},{6,198},{7,199},{8... | collective-permute-start | bytes 589832 | tf_op jit(solution)/shard_map/ppermute | solution.py:80
  97.6 4.3 %collective-permute-done.29.above_ref = f32[3,128,128]{2,1,0:T(8,128)S(1)} collective-permute-done((f32[3,128,128]{2,1,0:T(8,128)S(1)}, f32[3,128,128]{2,1,0:T(8,128)S(1)}, u32[]{:S(2)}, u32[]{:S(2)}) %collective-permute-start.29) | collective-permute-done | bytes 196640 | tf_op jit(solution)/shard_map/ppermute | solution.py:80
  102.5 1.5 %finish.1 = f32[16,128,128]{2,1,0:T(8,128)} custom-call(f32[12,128,128]{2,1,0:T(8,128)S(1)} %get-tuple-element.73.kept_ref, f32[3,128,128]{2,1,0:T(8,128)S(1)} %collective-permute-done.26.got_ref, f32[3,128,128]{2,1,0:T(8,128)S(1)} %collective-permute-done.27.got_more_ref, f32[5,128,128]{2,1,0:T(8,128)S(1)} %get-tuple-element.71.top_ref, ...), custom_call_target="tpu_custom_call" | custom-call | bytes 9000000 | tf_op jit(solution)/shard_map/finish/pallas_call | solution.py:91
  (64 shorter events, 18.0 us)
Async XLA Ops:
  2.4 20.4 %collective-permute-start = (f32[3,128,128]{2,1,0:T(8,128)S(1)}, f32[3,128,128]{2,1,0:T(8,128)S(1)}, u32[]{:S(2)}, u32[]{:S(2)}) collective-permute-start(f32[3,128,128]{2,1,0:T(8,128)S(1)} %get-tuple-element.41), channel_id=1, source_target_pairs={{0,192},{1,193},{2,194},{3,195},{4,196},{5,197},{6,198},{7,199},{8... | collective-permute-start | bytes 589832 | tf_op jit(solution)/shard_map/ppermute | solution.py:80
  6.0 10.1 %collective-permute-start.4 = (f32[16,128]{1,0:T(8,128)S(1)}, f32[16,128]{1,0:T(8,128)S(1)}, u32[]{:S(2)}, u32[]{:S(2)}) collective-permute-start(f32[16,128]{1,0:T(8,128)S(1)} %get-tuple-element.45), channel_id=1, source_target_pairs={{0,15},{1,0},{2,1},{3,2},{4,3},{5,4},{6,5},{7,6},{8,7},{9,8},{10,9... | collective-permute-start | bytes 24584 | tf_op jit(solution)/shard_map/ppermute | solution.py:80
  14.2 2.1 %collective-permute-start.1 = (f32[16,128]{1,0:T(8,128)S(1)}, f32[16,128]{1,0:T(8,128)S(1)}, u32[]{:S(2)}, u32[]{:S(2)}) collective-permute-start(f32[16,128]{1,0:T(8,128)S(1)} %get-tuple-element.42), channel_id=1, source_target_pairs={{0,16},{1,17},{2,18},{3,19},{4,20},{5,21},{6,22},{7,23},{8,24},{9,... | collective-permute-start | bytes 24584 | tf_op jit(solution)/shard_map/ppermute | solution.py:80
  15.5 3.1 %collective-permute-start.2 = (f32[16,128]{1,0:T(8,128)S(1)}, f32[16,128]{1,0:T(8,128)S(1)}, u32[]{:S(2)}, u32[]{:S(2)}) collective-permute-start(f32[16,128]{1,0:T(8,128)S(1)} %get-tuple-element.43), channel_id=1, source_target_pairs={{0,48},{1,49},{2,50},{3,51},{4,52},{5,53},{6,54},{7,55},{8,56},{9,... | collective-permute-start | bytes 24584 | tf_op jit(solution)/shard_map/ppermute | solution.py:80
  16.1 6.7 %collective-permute-start.3 = (f32[16,128]{1,0:T(8,128)S(1)}, f32[16,128]{1,0:T(8,128)S(1)}, u32[]{:S(2)}, u32[]{:S(2)}) collective-permute-start(f32[16,128]{1,0:T(8,128)S(1)} %get-tuple-element.44), channel_id=1, source_target_pairs={{0,1},{1,2},{2,3},{3,4},{4,5},{5,6},{6,7},{7,8},{8,9},{9,10},{10,1... | collective-permute-start | bytes 24584 | tf_op jit(solution)/shard_map/ppermute | solution.py:80
  27.1 24.6 %collective-permute-start.5 = (f32[51,128,128]{2,1,0:T(8,128)S(1)}, f32[51,128,128]{2,1,0:T(8,128)S(1)}, u32[]{:S(2)}, u32[]{:S(2)}) collective-permute-start(f32[51,128,128]{2,1,0:T(8,128)S(1)} %get-tuple-element.68.uvw_ref), channel_id=1, source_target_pairs={{0,16},{1,17},{2,18},{3,19},{4,20},{5,21},{6,22},{7,23},{8,24},{9,... | collective-permute-start | bytes 10027016 | tf_op jit(solution)/shard_map/ppermute | solution.py:80
  28.9 17.0 %collective-permute-start.6 = (f32[656,128]{1,0:T(8,128)S(1)}, f32[656,128]{1,0:T(8,128)S(1)}, u32[]{:S(2)}, u32[]{:S(2)}) collective-permute-start(f32[656,128]{1,0:T(8,128)S(1)} %get-tuple-element.48), channel_id=1, source_target_pairs={{16,32},{17,33},{18,34},{19,35},{20,36},{21,37},{22,38},{23,39},{2... | collective-permute-start | bytes 1007624 | tf_op jit(solution)/shard_map/ppermute | solution.py:80
  31.4 14.0 %collective-permute-start.7 = (f32[480,128]{1,0:T(8,128)S(1)}, f32[480,128]{1,0:T(8,128)S(1)}, u32[]{:S(2)}, u32[]{:S(2)}) collective-permute-start(f32[480,128]{1,0:T(8,128)S(1)} %get-tuple-element.49), channel_id=1, source_target_pairs={{0,1},{1,2},{2,3},{3,4},{4,5},{5,6},{6,7},{7,8},{8,9},{9,10},{10,1... | collective-permute-start | bytes 737288 | tf_op jit(solution)/shard_map/ppermute | solution.py:80
  31.5 14.4 %collective-permute-start.8 = (f32[480,128]{1,0:T(8,128)S(1)}, f32[480,128]{1,0:T(8,128)S(1)}, u32[]{:S(2)}, u32[]{:S(2)}) collective-permute-start(f32[480,128]{1,0:T(8,128)S(1)} %get-tuple-element.50), channel_id=1, source_target_pairs={{0,31},{1,16},{2,17},{3,18},{4,19},{5,20},{6,21},{7,22},{8,23},{9,... | collective-permute-start | bytes 737288 | tf_op jit(solution)/shard_map/ppermute | solution.py:80
  31.6 2.9 %collective-permute-start.9 = (f32[80,128]{1,0:T(8,128)S(1)}, f32[80,128]{1,0:T(8,128)S(1)}, u32[]{:S(2)}, u32[]{:S(2)}) collective-permute-start(f32[80,128]{1,0:T(8,128)S(1)} %get-tuple-element.52), channel_id=1, source_target_pairs={{0,16},{1,17},{2,18},{3,19},{4,20},{5,21},{6,22},{7,23},{8,24},{9,... | collective-permute-start | bytes 122888 | tf_op jit(solution)/shard_map/ppermute | solution.py:80
  34.5 10.9 %collective-permute-start.10 = (f32[80,128]{1,0:T(8,128)S(1)}, f32[80,128]{1,0:T(8,128)S(1)}, u32[]{:S(2)}, u32[]{:S(2)}) collective-permute-start(f32[80,128]{1,0:T(8,128)S(1)} %pick_corner.1), channel_id=1, source_target_pairs={{0,63},{1,48},{2,49},{3,50},{4,51},{5,52},{6,53},{7,54},{8,55},{9,... | collective-permute-start | bytes 122888 | tf_op jit(solution)/shard_map/ppermute | solution.py:80
  45.9 5.8 %collective-permute-start.11 = (f32[656,128]{1,0:T(8,128)S(1)}, f32[656,128]{1,0:T(8,128)S(1)}, u32[]{:S(2)}, u32[]{:S(2)}) collective-permute-start(f32[656,128]{1,0:T(8,128)S(1)} %collective-permute-done.6.got_ref), channel_id=1, source_target_pairs={{0,16},{1,17},{2,18},{3,19},{4,20},{5,21},{6,22},{7,23},{8,24},{9,... | collective-permute-start | bytes 1007624 | tf_op jit(solution)/shard_map/ppermute | solution.py:80
  53.7 2.7 %collective-permute-start.12 = (f32[192,128]{1,0:T(8,128)S(1)}, f32[192,128]{1,0:T(8,128)S(1)}, u32[]{:S(2)}, u32[]{:S(2)}) collective-permute-start(f32[192,128]{1,0:T(8,128)S(1)} %get-tuple-element.54), channel_id=1, source_target_pairs={{192,128},{193,129},{194,130},{195,131},{196,132},{197,133},{198,1... | collective-permute-start | bytes 294920 | tf_op jit(solution)/shard_map/ppermute | solution.py:80
  54.4 2.0 %collective-permute-start.13 = (f32[64,128]{1,0:T(8,128)S(1)}, f32[64,128]{1,0:T(8,128)S(1)}, u32[]{:S(2)}, u32[]{:S(2)}) collective-permute-start(f32[64,128]{1,0:T(8,128)S(1)} %get-tuple-element.55), channel_id=1, source_target_pairs={{192,159},{193,144},{194,145},{195,146},{196,147},{197,148},{198,1... | collective-permute-start | bytes 98312 | tf_op jit(solution)/shard_map/ppermute | solution.py:80
  58.2 2.7 %collective-permute-start.17 = (f32[256,128]{1,0:T(8,128)S(1)}, f32[256,128]{1,0:T(8,128)S(1)}, u32[]{:S(2)}, u32[]{:S(2)}) collective-permute-start(f32[256,128]{1,0:T(8,128)S(1)} %get-tuple-element.59), channel_id=1, source_target_pairs={{128,64},{129,65},{130,66},{131,67},{132,68},{133,69},{134,70},{13... | collective-permute-start | bytes 393224 | tf_op jit(solution)/shard_map/ppermute | solution.py:80
  58.8 2.0 %collective-permute-start.18 = (f32[64,128]{1,0:T(8,128)S(1)}, f32[64,128]{1,0:T(8,128)S(1)}, u32[]{:S(2)}, u32[]{:S(2)}) collective-permute-start(f32[64,128]{1,0:T(8,128)S(1)} %get-tuple-element.60), channel_id=1, source_target_pairs={{128,95},{129,80},{130,81},{131,82},{132,83},{133,84},{134,85},{13... | collective-permute-start | bytes 98312 | tf_op jit(solution)/shard_map/ppermute | solution.py:80
  61.1 25.5 %collective-permute-start.21 = (f32[192,128]{1,0:T(8,128)S(1)}, f32[192,128]{1,0:T(8,128)S(1)}, u32[]{:S(2)}, u32[]{:S(2)}) collective-permute-start(f32[192,128]{1,0:T(8,128)S(1)} %get-tuple-element.64), channel_id=1, source_target_pairs={{64,0},{65,1},{66,2},{67,3},{68,4},{69,5},{70,6},{71,7},{72,8},{73... | collective-permute-start | bytes 294920 | tf_op jit(solution)/shard_map/ppermute | solution.py:80
  62.6 23.9 %collective-permute-start.22 = (f32[64,128]{1,0:T(8,128)S(1)}, f32[64,128]{1,0:T(8,128)S(1)}, u32[]{:S(2)}, u32[]{:S(2)}) collective-permute-start(f32[64,128]{1,0:T(8,128)S(1)} %get-tuple-element.65), channel_id=1, source_target_pairs={{64,31},{65,16},{66,17},{67,18},{68,19},{69,20},{70,21},{71,22},{7... | collective-permute-start | bytes 98312 | tf_op jit(solution)/shard_map/ppermute | solution.py:80
  63.9 20.3 %collective-permute-start.23 = (f32[24,128]{1,0:T(8,128)S(1)}, f32[24,128]{1,0:T(8,128)S(1)}, u32[]{:S(2)}, u32[]{:S(2)}) collective-permute-start(f32[24,128]{1,0:T(8,128)S(1)} %get-tuple-element.66), channel_id=1, source_target_pairs={{64,32},{65,33},{66,34},{67,35},{68,36},{69,37},{70,38},{71,39},{7... | collective-permute-start | bytes 36872 | tf_op jit(solution)/shard_map/ppermute | solution.py:80
  65.2 21.3 %collective-permute-start.24 = (f32[24,128]{1,0:T(8,128)S(1)}, f32[24,128]{1,0:T(8,128)S(1)}, u32[]{:S(2)}, u32[]{:S(2)}) collective-permute-start(f32[24,128]{1,0:T(8,128)S(1)} %get-tuple-element.66), channel_id=1, source_target_pairs={{64,63},{65,48},{66,49},{67,50},{68,51},{69,52},{70,53},{71,54},{7... | collective-permute-start | bytes 36872 | tf_op jit(solution)/shard_map/ppermute | solution.py:80
  88.3 3.8 %collective-permute-start.25 = (f32[4,128,128]{2,1,0:T(8,128)S(1)}, f32[4,128,128]{2,1,0:T(8,128)S(1)}, u32[]{:S(2)}, u32[]{:S(2)}) collective-permute-start(f32[4,128,128]{2,1,0:T(8,128)S(1)} %get-tuple-element.70), channel_id=1, source_target_pairs={{0,16},{1,17},{2,18},{3,19},{4,20},{5,21},{6,22},{7,23},{8,24},{9,... | collective-permute-start | bytes 786440 | tf_op jit(solution)/shard_map/ppermute | solution.py:80
  92.3 10.2 %collective-permute-start.28 = (f32[5,128,128]{2,1,0:T(8,128)S(1)}, f32[5,128,128]{2,1,0:T(8,128)S(1)}, u32[]{:S(2)}, u32[]{:S(2)}) collective-permute-start(f32[5,128,128]{2,1,0:T(8,128)S(1)} %get-tuple-element.71.top_ref), channel_id=1, source_target_pairs={{0,64},{1,65},{2,66},{3,67},{4,68},{5,69},{6,70},{7,71},{8,72},{9,... | collective-permute-start | bytes 983048 | tf_op jit(solution)/shard_map/ppermute | solution.py:80
  95.2 2.4 %collective-permute-start.26 = (f32[3,128,128]{2,1,0:T(8,128)S(1)}, f32[3,128,128]{2,1,0:T(8,128)S(1)}, u32[]{:S(2)}, u32[]{:S(2)}) collective-permute-start(f32[3,128,128]{2,1,0:T(8,128)S(1)} %get-tuple-element.74), channel_id=1, source_target_pairs={{0,16},{1,17},{2,18},{3,19},{4,20},{5,21},{6,22},{7,23},{8,24},{9,... | collective-permute-start | bytes 589832 | tf_op jit(solution)/shard_map/ppermute | solution.py:80
  95.8 6.1 %collective-permute-start.29 = (f32[3,128,128]{2,1,0:T(8,128)S(1)}, f32[3,128,128]{2,1,0:T(8,128)S(1)}, u32[]{:S(2)}, u32[]{:S(2)}) collective-permute-start(f32[3,128,128]{2,1,0:T(8,128)S(1)} %get-tuple-element.76), channel_id=1, source_target_pairs={{0,192},{1,193},{2,194},{3,195},{4,196},{5,197},{6,198},{7,199},{8... | collective-permute-start | bytes 589832 | tf_op jit(solution)/shard_map/ppermute | solution.py:80
  (12 other events, 55.0 us)

commit v9 on v7

--- a/solution.py
+++ b/solution.py
@@ -24,7 +24,8 @@
 SLABS = ((16, 15, 14, 3), (13, 12, 11, 8, 0), (10, 9, 7, 6, 5, 2), (4, 1))
 FOLDED = 32
 SLAB_ROWS = 3 * 128 + FOLDED + 64
-CORNER_ROWS = 3 * 24 + 16 + 8
+CORNERS = ((0, 24), (24, 24), (48, 16), (64, 8), (72, 8))
+CORNER_ROWS = 80
 
 
 def width_of(layer):
@@ -36,7 +37,7 @@
 
 
 MICROSECONDS = {"all_terms": 2.5, "assemble": 2.5, "section": 1.5, "section_rest": 3.0, "smooth_rest": 3.0, "finish": 3.0}
-VMEM_LIMIT = {"edges": (64 << 20) - (64 << 10)}
+VMEM_LIMIT = {"edges": 52 << 20}
 
 
 def strips():
@@ -275,7 +276,8 @@
         same_ref[pl.ds(at, count), :] = jnp.where(c == 0, right, left)
         cross_ref[pl.ds(at, count), :] = jnp.where(c == 0, left, right)
 
-    def put_corner(at, rows, left, right):
+    def put_corner(slab, left, right):
+        at, rows = CORNERS[slab]
         first, last = slice(0, rows), slice(left.shape[0] - rows, left.shape[0])
         keep_ref[pl.ds(at, rows), :] = jnp.where(c == 0, left[first], right[last])
         give_ref[pl.ds(at, rows), :] = jnp.where(c == 0, right[first], left[last])
@@ -292,9 +294,9 @@
                 right = jnp.where(inside, pltpu.roll(plane, (at + width) % 128, 1), right)
         if slab < 3:
             put(128 * slab, left, right)
-            put_corner(24 * slab, 24, left, right)
+            put_corner(slab, left, right)
             continue
-        put_corner(72, 16, left, right)
+        put_corner(slab, left, right)
         folded = []
         for value in (left, right):
             total = value[:FOLDED]
@@ -313,7 +315,12 @@
             left = jnp.where(inside, pltpu.roll(plane, at, 1) if at else plane, left)
             right = jnp.where(inside, pltpu.roll(plane, (at + RADIUS) % 128, 1), right)
     put(384 + FOLDED, left, right)
-    put_corner(88, 8, left, right)
+    put_corner(4, left, right)
+
+
+def join(own_ref, other_ref, out_ref):
+    out_ref[pl.ds(0, SLAB_ROWS), :] = own_ref[...]
+    out_ref[pl.ds(SLAB_ROWS, SLAB_ROWS), :] = other_ref[...]
 
 
 def pick_corner(keep_ref, got_ref, corner_ref):
@@ -351,21 +358,22 @@
 
 
 def assemble(
-    uvw_ref, other_ref, got_ref, shared_ref, same_ref, cross_ref, corner_ref, uv_ref, plain, slabs
+    uvw_ref, other_ref, got_ref, shared_ref, came_ref, corner_ref, uv_ref, plain, slabs
 ):
     c = core()
+    cross_ref, same_ref = (came_ref.at[pl.ds(SLAB_ROWS * i, SLAB_ROWS)] for i in range(2))
     for slab in range(4):
         if slab < 3:
             here = pl.ds(128 * slab, 128)
             same, cross = same_ref[here, :], cross_ref[here, :]
-            here = pl.ds(24 * slab, 24)
+            here = pl.ds(*CORNERS[slab])
         else:
             here = pl.ds(384, FOLDED)
             same, cross = (
                 jnp.concatenate([value] + [pltpu.roll(value, 128 - FOLDED * i, 1) for i in range(1, 4)], axis=0)
                 for value in (same_ref[here, :], cross_ref[here, :])
             )
-            here = pl.ds(72, 16)
+            here = pl.ds(*CORNERS[3])
         corner = corner_ref[here, :]
         slot = plain.at[slab % 2]
         slab_plane(slot, same, cross, corner)
@@ -376,15 +384,16 @@
 
 
 def assemble_w(
-    uvw_ref, other_ref, got_ref, shared_ref, same_ref, cross_ref, corner_ref, w_ref, plain, slabs
+    uvw_ref, other_ref, got_ref, shared_ref, came_ref, corner_ref, w_ref, plain, slabs
 ):
     c = core()
+    cross_ref, same_ref = (came_ref.at[pl.ds(SLAB_ROWS * i, SLAB_ROWS)] for i in range(2))
 
     def unfolded(ref):
         value = ref[pl.ds(384 + FOLDED, 64), :]
         return jnp.concatenate([value, pltpu.roll(value, 64, 1)], axis=0)
 
-    here = pl.ds(88, 8)
+    here = pl.ds(*CORNERS[4])
     corner = corner_ref[here, :]
     corner = pltpu.roll(corner, 64 * seam(), 1)
     slab_plane(plain.at[0], unfolded(same_ref), unfolded(cross_ref), corner)
@@ -633,9 +642,6 @@
     def beside(z, y, x):
         return (z, y ^ 1, x + (1 if y & 1 else -1))
 
-    def same(z, y, x):
-        return (z, y, x + (-1 if y & 1 else 1))
-
     hbm = pl.BlockSpec(memory_space=pltpu.HBM)
     lowest_planes, inner, outer, left, right = call(
         edges, [shape(3, 128, 128)] + [edge] * 4, printed, filtered, sensitivity,
@@ -659,13 +665,12 @@
     rows = call(pack_rows, shape(ROW_TOTAL, 128), uvw)
     got = moved(rows, across)
     to_same, to_cross, keep, give = call(pack, [slab, slab, corner, corner], after(uvw, rows))
-    from_same = moved(to_same, same)
-    from_cross = moved(to_cross, beside)
+    came = moved(call(join, shape(2 * SLAB_ROWS, 128), to_cross, to_other(to_same)), beside)
     corner = call(pick_corner, corner, keep, to_other(give))
     corner = moved(corner, lambda z, y, x: (z, 3 - y, x + (1 if y & 1 else -1)))
     other = to_other(uvw)
-    shared = to_other(after(got, from_same, from_cross, corner))
-    parts = (uvw, other, got, shared, from_same, from_cross, corner)
+    shared = to_other(after(got, came, corner))
+    parts = (uvw, other, got, shared, came, corner)
     stack = shape(STEPS, PLANE, 128)
     work = [pltpu.VMEM((2, PLANE, 128), F32), pltpu.VMEM((4, PLANE, 128), F32)]
     uvs = call(assemble, shape(2 * STEPS, PLANE, 128), *parts, scratch=work)

time: 105 us -> 109 us (1.038)
  waiting for transfers between devices: 41.6 us -> 54.3 us
  starting transfers between devices: 42.1 us -> 36.9 us
  local copies, waits for them, and re-layouts: 3.69 us -> 1.25 us
    ppermute x30, waiting for transfers between devices: 41.6 us -> 54.3 us  [moved(): return lax.ppermute(value, AXES, pairs)]
    ppermute x30, starting transfers between devices: 42.1 us -> 36.9 us  [moved(): return lax.ppermute(value, AXES, pairs)]
    unnamed x12, local copies, waits for them, and re-layouts: 3.69 us -> 1.25 us
    pallas_call x18 -> x19, Pallas kernels: 15.8 us -> 14.8 us  [call(): pl.pallas_call(kernel, out_shape=outs, scratch_shapes=list(scratch), comp...]
  transfers between devices with their start and end apart: 30 -> 30, of which waited for: 11 -> 13; matrix products, arithmetic and copies ran while one was open for 0% -> 0% of each run, Pallas kernels for 6% -> 5%
where the time goes in v9:
time: 109 us; the launch traced here: 108 us
  waiting for transfers between devices  54.3 us (50%)
  starting transfers between devices  36.9 us (34%)
  Pallas kernels  14.8 us (14%)
  local copies, waits for them, and re-layouts  1.25 us (1%)
    ppermute x30, waiting for transfers between devices, moved(): return lax.ppermute(value, AXES, pairs)  54.3 us
    ppermute x30, starting transfers between devices, moved(): return lax.ppermute(value, AXES, pairs)  36.9 us
    pallas_call x19, Pallas kernels, call(): pl.pallas_call(kernel, out_shape=outs, scratch_shapes=list(scratch), comp...  14.8 us
  transfers between devices with their start and end apart: 30, of which 13 were waited for; matrix products, arithmetic and copies ran while one was open for 0% of the time, Pallas kernels for 5%

profile of v9, /device:TPU:1, one launch (start us, length us, event | category | flops | bytes accessed | tf_op | source)
XLA Modules:
  0.0 107.7 jit_solution(296817425954609157)
XLA Ops:
  2.4 3.6 %collective-permute-start = (f32[3,128,128]{2,1,0:T(8,128)S(1)}, f32[3,128,128]{2,1,0:T(8,128)S(1)}, u32[]{:S(2)}, u32[]{:S(2)}) collective-permute-start(f32[3,128,128]{2,1,0:T(8,128)S(1)} %get-tuple-element.40), channel_id=1, source_target_pairs={{0,192},{1,193},{2,194},{3,195},{4,196},{5,197},{6,198},{7,199},{8... | collective-permute-start | bytes 589832 | tf_op jit(solution)/shard_map/ppermute | solution.py:80
  6.0 8.2 %collective-permute-start.4 = (f32[16,128]{1,0:T(8,128)S(1)}, f32[16,128]{1,0:T(8,128)S(1)}, u32[]{:S(2)}, u32[]{:S(2)}) collective-permute-start(f32[16,128]{1,0:T(8,128)S(1)} %get-tuple-element.44), channel_id=1, source_target_pairs={{0,15},{1,0},{2,1},{3,2},{4,3},{5,4},{6,5},{7,6},{8,7},{9,8},{10,9... | collective-permute-start | bytes 24584 | tf_op jit(solution)/shard_map/ppermute | solution.py:80
  16.3 2.2 %collective-permute-done.2.outer_ref = f32[16,128]{1,0:T(8,128)S(1)} collective-permute-done((f32[16,128]{1,0:T(8,128)S(1)}, f32[16,128]{1,0:T(8,128)S(1)}, u32[]{:S(2)}, u32[]{:S(2)}) %collective-permute-start.2) | collective-permute-done | bytes 8224 | tf_op jit(solution)/shard_map/ppermute | solution.py:80
  18.5 4.3 %collective-permute-done.3.left_ref = f32[16,128]{1,0:T(8,128)S(1)} collective-permute-done((f32[16,128]{1,0:T(8,128)S(1)}, f32[16,128]{1,0:T(8,128)S(1)}, u32[]{:S(2)}, u32[]{:S(2)}) %collective-permute-start.3) | collective-permute-done | bytes 8224 | tf_op jit(solution)/shard_map/ppermute | solution.py:80
  22.8 2.0 %all_terms.1.uvw_ref = f32[51,128,128]{2,1,0:T(8,128)S(1)} custom-call(f32[16,128,128]{2,1,0:T(8,128)S(1)} %copy-done.2, f32[16,128,128]{2,1,0:T(8,128)S(1)} %copy-done.3, f32[16,128,128]{2,1,0:T(8,128)S(1)} %copy-done.4, f32[3,128,128]{2,1,0:T(8,128)S(1)} %collective-permute-done.above_ref, f32[16,128]{1,0:T(8,128)S(1)} %collective-permute-done.1.inner_ref, ...), custom_call_target="tpu_custom_call" | custom-call | bytes 7500000 | tf_op jit(solution)/shard_map/all_terms/pallas_call | solution.py:91
  24.8 1.7 %collective-permute-start.5 = (f32[51,128,128]{2,1,0:T(8,128)S(1)}, f32[51,128,128]{2,1,0:T(8,128)S(1)}, u32[]{:S(2)}, u32[]{:S(2)}) collective-permute-start(f32[51,128,128]{2,1,0:T(8,128)S(1)} %all_terms.1.uvw_ref), channel_id=1, source_target_pairs={{0,16},{1,17},{2,18},{3,19},{4,20},{5,21},{6,22},{7,23},{8,24},{9,... | collective-permute-start | bytes 10027016 | tf_op jit(solution)/shard_map/ppermute | solution.py:80
  26.6 1.8 %pack.1 = (f32[480,128]{1,0:T(8,128)S(1)}, f32[480,128]{1,0:T(8,128)S(1)}, f32[80,128]{1,0:T(8,128)S(1)}, f32[80,128]{1,0:T(8,128)S(1)}) custom-call(f32[51,128,128]{2,1,0:T(8,128)S(1)} %all_terms.1.uvw_ref), custom_call_target="tpu_custom_call" | custom-call | bytes 1500000 | tf_op jit(solution)/shard_map/pack/pallas_call | solution.py:91
  28.5 4.0 %collective-permute-done.7.other_ref = f32[480,128]{1,0:T(8,128)S(1)} collective-permute-done((f32[480,128]{1,0:T(8,128)S(1)}, f32[480,128]{1,0:T(8,128)S(1)}, u32[]{:S(2)}, u32[]{:S(2)}) %collective-permute-start.7) | collective-permute-done | bytes 245792 | tf_op jit(solution)/shard_map/ppermute | solution.py:80
  32.6 2.9 %collective-permute-start.6 = (f32[656,128]{1,0:T(8,128)S(1)}, f32[656,128]{1,0:T(8,128)S(1)}, u32[]{:S(2)}, u32[]{:S(2)}) collective-permute-start(f32[656,128]{1,0:T(8,128)S(1)} %pack_rows.1), channel_id=1, source_target_pairs={{16,32},{17,33},{18,34},{19,35},{20,36},{21,37},{22,38},{23,39},{2... | collective-permute-start | bytes 1007624 | tf_op jit(solution)/shard_map/ppermute | solution.py:80
  36.8 2.2 %collective-permute-start.10 = (f32[80,128]{1,0:T(8,128)S(1)}, f32[80,128]{1,0:T(8,128)S(1)}, u32[]{:S(2)}, u32[]{:S(2)}) collective-permute-start(f32[80,128]{1,0:T(8,128)S(1)} %pick_corner.1), channel_id=1, source_target_pairs={{0,63},{1,48},{2,49},{3,50},{4,51},{5,52},{6,53},{7,54},{8,55},{9,... | collective-permute-start | bytes 122888 | tf_op jit(solution)/shard_map/ppermute | solution.py:80
  39.0 12.6 %collective-permute-done.10.corner_ref = f32[80,128]{1,0:T(8,128)S(1)} collective-permute-done((f32[80,128]{1,0:T(8,128)S(1)}, f32[80,128]{1,0:T(8,128)S(1)}, u32[]{:S(2)}, u32[]{:S(2)}) %collective-permute-start.10) | collective-permute-done | bytes 40992 | tf_op jit(solution)/shard_map/ppermute | solution.py:80
  51.6 1.6 %collective-permute-done.11.shared_ref = f32[656,128]{1,0:T(8,128)S(1)} collective-permute-done((f32[656,128]{1,0:T(8,128)S(1)}, f32[656,128]{1,0:T(8,128)S(1)}, u32[]{:S(2)}, u32[]{:S(2)}) %collective-permute-start.11) | collective-permute-done | bytes 335904 | tf_op jit(solution)/shard_map/ppermute | solution.py:80
  53.2 2.1 %assemble.1.refs_0_.uv_ref = f32[34,288,128]{2,1,0:T(8,128)S(1)} custom-call(f32[51,128,128]{2,1,0:T(8,128)S(1)} %all_terms.1.uvw_ref, f32[51,128,128]{2,1,0:T(8,128)S(1)} %collective-permute-done.5.other_ref, f32[656,128]{1,0:T(8,128)S(1)} %collective-permute-done.6.got_ref, f32[656,128]{1,0:T(8,128)S(1)} %collective-permute-done.11.shared_ref, ...), custom_call_target="tpu_custom_call" | custom-call | bytes 7500000 | tf_op jit(solution)/shard_map/assemble/pallas_call | solution.py:91
  62.6 1.6 %collective-permute-start.21 = (f32[192,128]{1,0:T(8,128)S(1)}, f32[192,128]{1,0:T(8,128)S(1)}, u32[]{:S(2)}, u32[]{:S(2)}) collective-permute-start(f32[192,128]{1,0:T(8,128)S(1)} %get-tuple-element.62), channel_id=1, source_target_pairs={{64,0},{65,1},{66,2},{67,3},{68,4},{69,5},{70,6},{71,7},{72,8},{73... | collective-permute-start | bytes 294920 | tf_op jit(solution)/shard_map/ppermute | solution.py:80
  64.2 1.3 %collective-permute-start.22 = (f32[64,128]{1,0:T(8,128)S(1)}, f32[64,128]{1,0:T(8,128)S(1)}, u32[]{:S(2)}, u32[]{:S(2)}) collective-permute-start(f32[64,128]{1,0:T(8,128)S(1)} %get-tuple-element.63), channel_id=1, source_target_pairs={{64,31},{65,16},{66,17},{67,18},{68,19},{69,20},{70,21},{71,22},{7... | collective-permute-start | bytes 98312 | tf_op jit(solution)/shard_map/ppermute | solution.py:80
  65.5 1.3 %collective-permute-start.23 = (f32[24,128]{1,0:T(8,128)S(1)}, f32[24,128]{1,0:T(8,128)S(1)}, u32[]{:S(2)}, u32[]{:S(2)}) collective-permute-start(f32[24,128]{1,0:T(8,128)S(1)} %get-tuple-element.64), channel_id=1, source_target_pairs={{64,32},{65,33},{66,34},{67,35},{68,36},{69,37},{70,38},{71,39},{7... | collective-permute-start | bytes 36872 | tf_op jit(solution)/shard_map/ppermute | solution.py:80
  66.8 1.3 %collective-permute-start.24 = (f32[24,128]{1,0:T(8,128)S(1)}, f32[24,128]{1,0:T(8,128)S(1)}, u32[]{:S(2)}, u32[]{:S(2)}) collective-permute-start(f32[24,128]{1,0:T(8,128)S(1)} %get-tuple-element.64), channel_id=1, source_target_pairs={{64,63},{65,48},{66,49},{67,50},{68,51},{69,52},{70,53},{71,54},{7... | collective-permute-start | bytes 36872 | tf_op jit(solution)/shard_map/ppermute | solution.py:80
  69.3 18.7 %collective-permute-done.23.halo_ref = f32[24,128]{1,0:T(8,128)S(1)} collective-permute-done((f32[24,128]{1,0:T(8,128)S(1)}, f32[24,128]{1,0:T(8,128)S(1)}, u32[]{:S(2)}, u32[]{:S(2)}) %collective-permute-start.23) | collective-permute-done | bytes 12320 | tf_op jit(solution)/shard_map/ppermute | solution.py:80
  88.0 2.3 %collective-permute-done.24.halo_outer_ref = f32[24,128]{1,0:T(8,128)S(1)} collective-permute-done((f32[24,128]{1,0:T(8,128)S(1)}, f32[24,128]{1,0:T(8,128)S(1)}, u32[]{:S(2)}, u32[]{:S(2)}) %collective-permute-start.24) | collective-permute-done | bytes 12320 | tf_op jit(solution)/shard_map/ppermute | solution.py:80
  92.0 2.7 %collective-permute-start.25 = (f32[4,128,128]{2,1,0:T(8,128)S(1)}, f32[4,128,128]{2,1,0:T(8,128)S(1)}, u32[]{:S(2)}, u32[]{:S(2)}) collective-permute-start(f32[4,128,128]{2,1,0:T(8,128)S(1)} %get-tuple-element.68), channel_id=1, source_target_pairs={{0,16},{1,17},{2,18},{3,19},{4,20},{5,21},{6,22},{7,23},{8,24},{9,... | collective-permute-start | bytes 786440 | tf_op jit(solution)/shard_map/ppermute | solution.py:80
  97.3 1.5 %smooth_rest.1 = (f32[12,128,128]{2,1,0:T(8,128)S(1)}, f32[3,128,128]{2,1,0:T(8,128)S(1)}, f32[3,128,128]{2,1,0:T(8,128)S(1)}) custom-call(f32[12,288,128]{2,1,0:T(8,128)S(1)} %section_rest.1.layers_ref, f32[17,288,128]{2,1,0:T(8,128)S(1)} %assemble_w.1.w_ref), custom_call_target="tpu_custom_call" | custom-call | bytes 9000000 | tf_op jit(solution)/shard_map/smooth_rest/pallas_call | solution.py:91
  99.4 1.8 %collective-permute-start.29 = (f32[3,128,128]{2,1,0:T(8,128)S(1)}, f32[3,128,128]{2,1,0:T(8,128)S(1)}, u32[]{:S(2)}, u32[]{:S(2)}) collective-permute-start(f32[3,128,128]{2,1,0:T(8,128)S(1)} %get-tuple-element.74), channel_id=1, source_target_pairs={{0,192},{1,193},{2,194},{3,195},{4,196},{5,197},{6,198},{7,199},{8... | collective-permute-start | bytes 589832 | tf_op jit(solution)/shard_map/ppermute | solution.py:80
  101.2 4.3 %collective-permute-done.29.above_ref = f32[3,128,128]{2,1,0:T(8,128)S(1)} collective-permute-done((f32[3,128,128]{2,1,0:T(8,128)S(1)}, f32[3,128,128]{2,1,0:T(8,128)S(1)}, u32[]{:S(2)}, u32[]{:S(2)}) %collective-permute-start.29) | collective-permute-done | bytes 196640 | tf_op jit(solution)/shard_map/ppermute | solution.py:80
  106.2 1.5 %finish.1 = f32[16,128,128]{2,1,0:T(8,128)} custom-call(f32[12,128,128]{2,1,0:T(8,128)S(1)} %get-tuple-element.71.kept_ref, f32[3,128,128]{2,1,0:T(8,128)S(1)} %collective-permute-done.26.got_ref, f32[3,128,128]{2,1,0:T(8,128)S(1)} %collective-permute-done.27.got_more_ref, f32[5,128,128]{2,1,0:T(8,128)S(1)} %get-tuple-element.69.top_ref, ...), custom_call_target="tpu_custom_call" | custom-call | bytes 9000000 | tf_op jit(solution)/shard_map/finish/pallas_call | solution.py:91
  (67 shorter events, 19.9 us)
Async XLA Ops:
  2.4 20.4 %collective-permute-start = (f32[3,128,128]{2,1,0:T(8,128)S(1)}, f32[3,128,128]{2,1,0:T(8,128)S(1)}, u32[]{:S(2)}, u32[]{:S(2)}) collective-permute-start(f32[3,128,128]{2,1,0:T(8,128)S(1)} %get-tuple-element.40), channel_id=1, source_target_pairs={{0,192},{1,193},{2,194},{3,195},{4,196},{5,197},{6,198},{7,199},{8... | collective-permute-start | bytes 589832 | tf_op jit(solution)/shard_map/ppermute | solution.py:80
  6.0 10.1 %collective-permute-start.4 = (f32[16,128]{1,0:T(8,128)S(1)}, f32[16,128]{1,0:T(8,128)S(1)}, u32[]{:S(2)}, u32[]{:S(2)}) collective-permute-start(f32[16,128]{1,0:T(8,128)S(1)} %get-tuple-element.44), channel_id=1, source_target_pairs={{0,15},{1,0},{2,1},{3,2},{4,3},{5,4},{6,5},{7,6},{8,7},{9,8},{10,9... | collective-permute-start | bytes 24584 | tf_op jit(solution)/shard_map/ppermute | solution.py:80
  14.2 2.1 %collective-permute-start.1 = (f32[16,128]{1,0:T(8,128)S(1)}, f32[16,128]{1,0:T(8,128)S(1)}, u32[]{:S(2)}, u32[]{:S(2)}) collective-permute-start(f32[16,128]{1,0:T(8,128)S(1)} %get-tuple-element.41), channel_id=1, source_target_pairs={{0,16},{1,17},{2,18},{3,19},{4,20},{5,21},{6,22},{7,23},{8,24},{9,... | collective-permute-start | bytes 24584 | tf_op jit(solution)/shard_map/ppermute | solution.py:80
  15.5 3.1 %collective-permute-start.2 = (f32[16,128]{1,0:T(8,128)S(1)}, f32[16,128]{1,0:T(8,128)S(1)}, u32[]{:S(2)}, u32[]{:S(2)}) collective-permute-start(f32[16,128]{1,0:T(8,128)S(1)} %get-tuple-element.42), channel_id=1, source_target_pairs={{0,48},{1,49},{2,50},{3,51},{4,52},{5,53},{6,54},{7,55},{8,56},{9,... | collective-permute-start | bytes 24584 | tf_op jit(solution)/shard_map/ppermute | solution.py:80
  16.1 6.7 %collective-permute-start.3 = (f32[16,128]{1,0:T(8,128)S(1)}, f32[16,128]{1,0:T(8,128)S(1)}, u32[]{:S(2)}, u32[]{:S(2)}) collective-permute-start(f32[16,128]{1,0:T(8,128)S(1)} %get-tuple-element.43), channel_id=1, source_target_pairs={{0,1},{1,2},{2,3},{3,4},{4,5},{5,6},{6,7},{7,8},{8,9},{9,10},{10,1... | collective-permute-start | bytes 24584 | tf_op jit(solution)/shard_map/ppermute | solution.py:80
  24.8 28.4 %collective-permute-start.5 = (f32[51,128,128]{2,1,0:T(8,128)S(1)}, f32[51,128,128]{2,1,0:T(8,128)S(1)}, u32[]{:S(2)}, u32[]{:S(2)}) collective-permute-start(f32[51,128,128]{2,1,0:T(8,128)S(1)} %all_terms.1.uvw_ref), channel_id=1, source_target_pairs={{0,16},{1,17},{2,18},{3,19},{4,20},{5,21},{6,22},{7,23},{8,24},{9,... | collective-permute-start | bytes 10027016 | tf_op jit(solution)/shard_map/ppermute | solution.py:80
  28.4 4.1 %collective-permute-start.7 = (f32[480,128]{1,0:T(8,128)S(1)}, f32[480,128]{1,0:T(8,128)S(1)}, u32[]{:S(2)}, u32[]{:S(2)}) collective-permute-start(f32[480,128]{1,0:T(8,128)S(1)} %get-tuple-element.48), channel_id=1, source_target_pairs={{0,16},{1,17},{2,18},{3,19},{4,20},{5,21},{6,22},{7,23},{8,24},{9,... | collective-permute-start | bytes 737288 | tf_op jit(solution)/shard_map/ppermute | solution.py:80
  32.5 19.1 %collective-permute-start.8 = (f32[960,128]{1,0:T(8,128)S(1)}, f32[960,128]{1,0:T(8,128)S(1)}, u32[]{:S(2)}, u32[]{:S(2)}) collective-permute-start(f32[960,128]{1,0:T(8,128)S(1)} %join.1), channel_id=1, source_target_pairs={{0,31},{1,16},{2,17},{3,18},{4,19},{5,20},{6,21},{7,22},{8,23},{9,... | collective-permute-start | bytes 1474568 | tf_op jit(solution)/shard_map/ppermute | solution.py:80
  32.6 19.0 %collective-permute-start.6 = (f32[656,128]{1,0:T(8,128)S(1)}, f32[656,128]{1,0:T(8,128)S(1)}, u32[]{:S(2)}, u32[]{:S(2)}) collective-permute-start(f32[656,128]{1,0:T(8,128)S(1)} %pack_rows.1), channel_id=1, source_target_pairs={{16,32},{17,33},{18,34},{19,35},{20,36},{21,37},{22,38},{23,39},{2... | collective-permute-start | bytes 1007624 | tf_op jit(solution)/shard_map/ppermute | solution.py:80
  36.8 14.7 %collective-permute-start.10 = (f32[80,128]{1,0:T(8,128)S(1)}, f32[80,128]{1,0:T(8,128)S(1)}, u32[]{:S(2)}, u32[]{:S(2)}) collective-permute-start(f32[80,128]{1,0:T(8,128)S(1)} %pick_corner.1), channel_id=1, source_target_pairs={{0,63},{1,48},{2,49},{3,50},{4,51},{5,52},{6,53},{7,54},{8,55},{9,... | collective-permute-start | bytes 122888 | tf_op jit(solution)/shard_map/ppermute | solution.py:80
  51.6 1.6 %collective-permute-start.11 = (f32[656,128]{1,0:T(8,128)S(1)}, f32[656,128]{1,0:T(8,128)S(1)}, u32[]{:S(2)}, u32[]{:S(2)}) collective-permute-start(f32[656,128]{1,0:T(8,128)S(1)} %collective-permute-done.6.got_ref), channel_id=1, source_target_pairs={{0,16},{1,17},{2,18},{3,19},{4,20},{5,21},{6,22},{7,23},{8,24},{9,... | collective-permute-start | bytes 1007624 | tf_op jit(solution)/shard_map/ppermute | solution.py:80
  55.3 2.7 %collective-permute-start.12 = (f32[192,128]{1,0:T(8,128)S(1)}, f32[192,128]{1,0:T(8,128)S(1)}, u32[]{:S(2)}, u32[]{:S(2)}) collective-permute-start(f32[192,128]{1,0:T(8,128)S(1)} %get-tuple-element.52), channel_id=1, source_target_pairs={{192,128},{193,129},{194,130},{195,131},{196,132},{197,133},{198,1... | collective-permute-start | bytes 294920 | tf_op jit(solution)/shard_map/ppermute | solution.py:80
  56.0 2.0 %collective-permute-start.13 = (f32[64,128]{1,0:T(8,128)S(1)}, f32[64,128]{1,0:T(8,128)S(1)}, u32[]{:S(2)}, u32[]{:S(2)}) collective-permute-start(f32[64,128]{1,0:T(8,128)S(1)} %get-tuple-element.53), channel_id=1, source_target_pairs={{192,159},{193,144},{194,145},{195,146},{196,147},{197,148},{198,1... | collective-permute-start | bytes 98312 | tf_op jit(solution)/shard_map/ppermute | solution.py:80
  59.7 2.7 %collective-permute-start.17 = (f32[256,128]{1,0:T(8,128)S(1)}, f32[256,128]{1,0:T(8,128)S(1)}, u32[]{:S(2)}, u32[]{:S(2)}) collective-permute-start(f32[256,128]{1,0:T(8,128)S(1)} %get-tuple-element.57), channel_id=1, source_target_pairs={{128,64},{129,65},{130,66},{131,67},{132,68},{133,69},{134,70},{13... | collective-permute-start | bytes 393224 | tf_op jit(solution)/shard_map/ppermute | solution.py:80
  60.4 2.0 %collective-permute-start.18 = (f32[64,128]{1,0:T(8,128)S(1)}, f32[64,128]{1,0:T(8,128)S(1)}, u32[]{:S(2)}, u32[]{:S(2)}) collective-permute-start(f32[64,128]{1,0:T(8,128)S(1)} %get-tuple-element.58), channel_id=1, source_target_pairs={{128,95},{129,80},{130,81},{131,82},{132,83},{133,84},{134,85},{13... | collective-permute-start | bytes 98312 | tf_op jit(solution)/shard_map/ppermute | solution.py:80
  62.6 27.7 %collective-permute-start.21 = (f32[192,128]{1,0:T(8,128)S(1)}, f32[192,128]{1,0:T(8,128)S(1)}, u32[]{:S(2)}, u32[]{:S(2)}) collective-permute-start(f32[192,128]{1,0:T(8,128)S(1)} %get-tuple-element.62), channel_id=1, source_target_pairs={{64,0},{65,1},{66,2},{67,3},{68,4},{69,5},{70,6},{71,7},{72,8},{73... | collective-permute-start | bytes 294920 | tf_op jit(solution)/shard_map/ppermute | solution.py:80
  64.2 26.1 %collective-permute-start.22 = (f32[64,128]{1,0:T(8,128)S(1)}, f32[64,128]{1,0:T(8,128)S(1)}, u32[]{:S(2)}, u32[]{:S(2)}) collective-permute-start(f32[64,128]{1,0:T(8,128)S(1)} %get-tuple-element.63), channel_id=1, source_target_pairs={{64,31},{65,16},{66,17},{67,18},{68,19},{69,20},{70,21},{71,22},{7... | collective-permute-start | bytes 98312 | tf_op jit(solution)/shard_map/ppermute | solution.py:80
  65.5 22.5 %collective-permute-start.23 = (f32[24,128]{1,0:T(8,128)S(1)}, f32[24,128]{1,0:T(8,128)S(1)}, u32[]{:S(2)}, u32[]{:S(2)}) collective-permute-start(f32[24,128]{1,0:T(8,128)S(1)} %get-tuple-element.64), channel_id=1, source_target_pairs={{64,32},{65,33},{66,34},{67,35},{68,36},{69,37},{70,38},{71,39},{7... | collective-permute-start | bytes 36872 | tf_op jit(solution)/shard_map/ppermute | solution.py:80
  66.8 23.5 %collective-permute-start.24 = (f32[24,128]{1,0:T(8,128)S(1)}, f32[24,128]{1,0:T(8,128)S(1)}, u32[]{:S(2)}, u32[]{:S(2)}) collective-permute-start(f32[24,128]{1,0:T(8,128)S(1)} %get-tuple-element.64), channel_id=1, source_target_pairs={{64,63},{65,48},{66,49},{67,50},{68,51},{69,52},{70,53},{71,54},{7... | collective-permute-start | bytes 36872 | tf_op jit(solution)/shard_map/ppermute | solution.py:80
  92.0 3.8 %collective-permute-start.25 = (f32[4,128,128]{2,1,0:T(8,128)S(1)}, f32[4,128,128]{2,1,0:T(8,128)S(1)}, u32[]{:S(2)}, u32[]{:S(2)}) collective-permute-start(f32[4,128,128]{2,1,0:T(8,128)S(1)} %get-tuple-element.68), channel_id=1, source_target_pairs={{0,16},{1,17},{2,18},{3,19},{4,20},{5,21},{6,22},{7,23},{8,24},{9,... | collective-permute-start | bytes 786440 | tf_op jit(solution)/shard_map/ppermute | solution.py:80
  96.0 10.2 %collective-permute-start.28 = (f32[5,128,128]{2,1,0:T(8,128)S(1)}, f32[5,128,128]{2,1,0:T(8,128)S(1)}, u32[]{:S(2)}, u32[]{:S(2)}) collective-permute-start(f32[5,128,128]{2,1,0:T(8,128)S(1)} %get-tuple-element.69.top_ref), channel_id=1, source_target_pairs={{0,64},{1,65},{2,66},{3,67},{4,68},{5,69},{6,70},{7,71},{8,72},{9,... | collective-permute-start | bytes 983048 | tf_op jit(solution)/shard_map/ppermute | solution.py:80
  98.8 2.4 %collective-permute-start.26 = (f32[3,128,128]{2,1,0:T(8,128)S(1)}, f32[3,128,128]{2,1,0:T(8,128)S(1)}, u32[]{:S(2)}, u32[]{:S(2)}) collective-permute-start(f32[3,128,128]{2,1,0:T(8,128)S(1)} %get-tuple-element.72), channel_id=1, source_target_pairs={{0,16},{1,17},{2,18},{3,19},{4,20},{5,21},{6,22},{7,23},{8,24},{9,... | collective-permute-start | bytes 589832 | tf_op jit(solution)/shard_map/ppermute | solution.py:80
  99.3 1.9 %collective-permute-start.27 = (f32[3,128,128]{2,1,0:T(8,128)S(1)}, f32[3,128,128]{2,1,0:T(8,128)S(1)}, u32[]{:S(2)}, u32[]{:S(2)}) collective-permute-start(f32[3,128,128]{2,1,0:T(8,128)S(1)} %get-tuple-element.73), channel_id=1, source_target_pairs={{0,16},{1,17},{2,18},{3,19},{4,20},{5,21},{6,22},{7,23},{8,24},{9,... | collective-permute-start | bytes 589832 | tf_op jit(solution)/shard_map/ppermute | solution.py:80
  99.4 6.1 %collective-permute-start.29 = (f32[3,128,128]{2,1,0:T(8,128)S(1)}, f32[3,128,128]{2,1,0:T(8,128)S(1)}, u32[]{:S(2)}, u32[]{:S(2)}) collective-permute-start(f32[3,128,128]{2,1,0:T(8,128)S(1)} %get-tuple-element.74), channel_id=1, source_target_pairs={{0,192},{1,193},{2,194},{3,195},{4,196},{5,197},{6,198},{7,199},{8... | collective-permute-start | bytes 589832 | tf_op jit(solution)/shard_map/ppermute | solution.py:80
  (12 other events, 54.3 us)

commit v10 on v9

--- a/solution.py
+++ b/solution.py
@@ -153,7 +153,7 @@
     return x32 * (x4 * (x2 * x))
 
 
-def edges(p_hbm, f_hbm, s_hbm, lowest_ref, inner_ref, outer_ref, left_ref, right_ref, turned, p_ref, sems):
+def edges(p_hbm, f_hbm, s_hbm, lowest_ref, inner_ref, outer_ref, along_ref, back_ref, turned, p_ref, sems):
     planes = [pltpu.make_async_copy(p_hbm.at[pl.ds(4 * i, 4)], p_ref.at[pl.ds(4 * i, 4)], sems.at[i]) for i in range(4)]
     copies = [pltpu.make_async_copy(ref.at[0], lowest_ref.at[i + 1], sems.at[4 + i]) for i, ref in enumerate((f_hbm, s_hbm))]
     for copy in planes + copies:
@@ -169,8 +169,9 @@
         rolled = pltpu.roll(p_ref[layer], 2 * layer + 1, 1)
         packed = jnp.where((lane >> 1) == layer, rolled, packed)
     turned[...] = packed.T
-    right_ref[...] = turned[pl.ds(0, 16, stride=2), :]
-    left_ref[...] = turned[pl.ds(1, 16, stride=2), :]
+    right, left = turned[pl.ds(0, 16, stride=2), :], turned[pl.ds(1, 16, stride=2), :]
+    along_ref[...] = jnp.where(c == 0, right, left)
+    back_ref[...] = jnp.where(c == 0, left, right)
     lowest_ref[0] = p_ref[0]
     for copy in copies:
         copy.wait()
@@ -223,18 +224,21 @@
     return (own + right) + left + (powers[pl.ds(7, 128), :] + powers[pl.ds(9, 128), :])
 
 
-def columns_beside(left_ref, right_ref, turned):
+def columns_beside(along_ref, back_ref, turned):
     x = lax.axis_index("gx")
     turned[...] = jnp.zeros((128, 128), F32)
-    turned[pl.ds(0, 16, stride=2), :] = right_ref[...] * one_if(x < lax.axis_size("gx") - 1)
-    turned[pl.ds(1, 16, stride=2), :] = left_ref[...] * one_if(x > 0)
+    first = core() == 0
+    right = jnp.where(first, back_ref[...], along_ref[...])
+    left = jnp.where(first, along_ref[...], back_ref[...])
+    turned[pl.ds(0, 16, stride=2), :] = right * one_if(x < lax.axis_size("gx") - 1)
+    turned[pl.ds(1, 16, stride=2), :] = left * one_if(x > 0)
     return power40(turned[...].T)
 
 
 def all_terms(
-    sizes, p_ref, f_ref, s_ref, above_ref, inner_ref, outer_ref, left_ref, right_ref, early_ref, uvw_ref, powers, turned
+    sizes, p_ref, f_ref, s_ref, above_ref, inner_ref, outer_ref, along_ref, back_ref, early_ref, uvw_ref, powers, turned
 ):
-    beside = columns_beside(left_ref, right_ref, turned)
+    beside = columns_beside(along_ref, back_ref, turned)
     norms = 1.0 / plane_norms(sizes)
     gz = lax.axis_index("gz")
     layer0 = gz * LAYERS
@@ -318,11 +322,6 @@
     put_corner(4, left, right)
 
 
-def join(own_ref, other_ref, out_ref):
-    out_ref[pl.ds(0, SLAB_ROWS), :] = own_ref[...]
-    out_ref[pl.ds(SLAB_ROWS, SLAB_ROWS), :] = other_ref[...]
-
-
 def pick_corner(keep_ref, got_ref, corner_ref):
     corner_ref[...] = jnp.where((core() ^ seam()) == 1, keep_ref[...], got_ref[...])
 
@@ -358,10 +357,9 @@
 
 
 def assemble(
-    uvw_ref, other_ref, got_ref, shared_ref, came_ref, corner_ref, uv_ref, plain, slabs
+    uvw_ref, other_ref, got_ref, shared_ref, same_ref, cross_ref, corner_ref, uv_ref, plain, slabs
 ):
     c = core()
-    cross_ref, same_ref = (came_ref.at[pl.ds(SLAB_ROWS * i, SLAB_ROWS)] for i in range(2))
     for slab in range(4):
         if slab < 3:
             here = pl.ds(128 * slab, 128)
@@ -384,10 +382,9 @@
 
 
 def assemble_w(
-    uvw_ref, other_ref, got_ref, shared_ref, came_ref, corner_ref, w_ref, plain, slabs
+    uvw_ref, other_ref, got_ref, shared_ref, same_ref, cross_ref, corner_ref, w_ref, plain, slabs
 ):
     c = core()
-    cross_ref, same_ref = (came_ref.at[pl.ds(SLAB_ROWS * i, SLAB_ROWS)] for i in range(2))
 
     def unfolded(ref):
         value = ref[pl.ds(384 + FOLDED, 64), :]
@@ -639,24 +636,39 @@
     def across(z, y, x):
         return (z, y ^ 3, x) if y in (1, 2) else None
 
+    def on_grid(x):
+        return 0 <= x < sizes[2]
+
     def beside(z, y, x):
-        return (z, y ^ 1, x + (1 if y & 1 else -1))
+        to = x + (1 if y & 1 else -1)
+        return (z, y ^ 1, to) if on_grid(to) else (z, y ^ 2, x)
+
+    def same(z, y, x):
+        to = x + (-1 if y & 1 else 1)
+        return (z, y, to) if on_grid(to) else (z, y ^ 1, x)
+
+    def opposite(z, y, x):
+        to = x + (1 if y & 1 else -1)
+        return (z, y, to) if on_grid(to) else (z, y ^ 1, x)
+
+    def across_beside(z, y, x):
+        to = x + (1 if y & 1 else -1)
+        return (z, 3 - y, to) if on_grid(to) else (z, y ^ 2, x)
 
     hbm = pl.BlockSpec(memory_space=pltpu.HBM)
-    lowest_planes, inner, outer, left, right = call(
+    lowest_planes, inner, outer, along, back = call(
         edges, [shape(3, 128, 128)] + [edge] * 4, printed, filtered, sensitivity,
         in_specs=[hbm] * 3,
         scratch=[pltpu.VMEM((128, 128), F32), pltpu.VMEM((LAYERS, 128, 128), F32), pltpu.SemaphoreType.DMA((6,))],
     )
     above = moved(lowest_planes, lambda z, y, x: (z - 1, y, x))
-    from_left = moved(right, lambda z, y, x: (z, y, x + 1))
-    from_right = moved(left, lambda z, y, x: (z, y, x - 1))
+    along, back = moved(along, same), moved(back, opposite)
     outer = moved(outer, lambda z, y, x: (z, y ^ 3, x))
     inner = to_other(inner)
-    ready = call(early, shape(8, 128), printed, filtered, after(sensitivity, left))
+    ready = call(early, shape(8, 128), printed, filtered, after(sensitivity, inner))
     uvw = call(
         functools.partial(all_terms, sizes), shape(3 * STEPS, 128, 128),
-        printed, filtered, sensitivity, above, inner, outer, from_left, from_right, ready,
+        printed, filtered, sensitivity, above, inner, outer, along, back, ready,
         scratch=[
             pltpu.VMEM((144, 128), F32), pltpu.VMEM((128, 128), F32),
         ],
@@ -665,12 +677,13 @@
     rows = call(pack_rows, shape(ROW_TOTAL, 128), uvw)
     got = moved(rows, across)
     to_same, to_cross, keep, give = call(pack, [slab, slab, corner, corner], after(uvw, rows))
-    came = moved(call(join, shape(2 * SLAB_ROWS, 128), to_cross, to_other(to_same)), beside)
+    from_same = moved(to_same, same)
+    from_cross = moved(to_cross, beside)
     corner = call(pick_corner, corner, keep, to_other(give))
-    corner = moved(corner, lambda z, y, x: (z, 3 - y, x + (1 if y & 1 else -1)))
+    corner = moved(corner, across_beside)
     other = to_other(uvw)
-    shared = to_other(after(got, came, corner))
-    parts = (uvw, other, got, shared, came, corner)
+    shared = to_other(after(got, from_same, from_cross, corner))
+    parts = (uvw, other, got, shared, from_same, from_cross, corner)
     stack = shape(STEPS, PLANE, 128)
     work = [pltpu.VMEM((2, PLANE, 128), F32), pltpu.VMEM((4, PLANE, 128), F32)]
     uvs = call(assemble, shape(2 * STEPS, PLANE, 128), *parts, scratch=work)
@@ -688,18 +701,21 @@
 
         def down(where):
             def to(z, y, x):
-                _, ty, tx = where(z, y, x)
-                return (z - 1, ty, tx) if z == active else None
+                target = where(z, y, x) if z == active else None
+                return target and (z - 1,) + target[1:]
             return to
 
         def over(z, y, x):
             return (z, y ^ 2, x)
 
+        def beyond(z, y, x):
+            return beside(z, y, x) if on_grid(x + (1 if y & 1 else -1)) else None
+
         def corner_of(z, y, x):
-            _, ty, tx = beside(z, y, x)
-            return (z, ty ^ 2, tx)
-
-        side = moved(side, down(beside))
+            target = beyond(z, y, x)
+            return target and (z, target[1] ^ 2, target[2])
+
+        side = moved(side, down(beyond))
         edge_piece = moved(strip, down(corner_of))
         halo = strip
         if swap:

time: 109 us -> 96.4 us (0.88)
  waiting for transfers between devices: 54.3 us -> 41.2 us
    ppermute x30, waiting for transfers between devices: 54.3 us -> 41.2 us  [moved(): return lax.ppermute(value, AXES, pairs)]
    pallas_call x19 -> x18, Pallas kernels: 14.8 us -> 14.8 us  [call(): pl.pallas_call(kernel, out_shape=outs, scratch_shapes=list(scratch), comp...]
  transfers between devices with their start and end apart: 30 -> 30, of which waited for: 13 -> 11; matrix products, arithmetic and copies ran while one was open for 0% -> 0% of each run, Pallas kernels for 5% -> 6%
where the time goes in v10:
time: 96.4 us; the launch traced here: 94.8 us
  waiting for transfers between devices  41.2 us (43%)
  starting transfers between devices  37.2 us (39%)
  Pallas kernels  14.8 us (15%)
  local copies, waits for them, and re-layouts  1.25 us (1%)
    ppermute x30, waiting for transfers between devices, moved(): return lax.ppermute(value, AXES, pairs)  41.2 us
    ppermute x30, starting transfers between devices, moved(): return lax.ppermute(value, AXES, pairs)  37.2 us
    pallas_call x18, Pallas kernels, call(): pl.pallas_call(kernel, out_shape=outs, scratch_shapes=list(scratch), comp...  14.8 us
  transfers between devices with their start and end apart: 30, of which 11 were waited for; matrix products, arithmetic and copies ran while one was open for 0% of the time, Pallas kernels for 6%

profile of v10, /device:TPU:1, one launch (start us, length us, event | category | flops | bytes accessed | tf_op | source)
XLA Modules:
  0.0 94.8 jit_solution(4532473406924895274)
XLA Ops:
  2.4 3.6 %collective-permute-start = (f32[3,128,128]{2,1,0:T(8,128)S(1)}, f32[3,128,128]{2,1,0:T(8,128)S(1)}, u32[]{:S(2)}, u32[]{:S(2)}) collective-permute-start(f32[3,128,128]{2,1,0:T(8,128)S(1)} %get-tuple-element.40), channel_id=1, source_target_pairs={{0,192},{1,193},{2,194},{3,195},{4,196},{5,197},{6,198},{7,199},{8... | collective-permute-start | bytes 589832 | tf_op jit(solution)/shard_map/ppermute | solution.py:80
  7.0 1.5 %collective-permute-start.2 = (f32[16,128]{1,0:T(8,128)S(1)}, f32[16,128]{1,0:T(8,128)S(1)}, u32[]{:S(2)}, u32[]{:S(2)}) collective-permute-start(f32[16,128]{1,0:T(8,128)S(1)} %get-tuple-element.42), channel_id=1, source_target_pairs={{0,48},{1,49},{2,50},{3,51},{4,52},{5,53},{6,54},{7,55},{8,56},{9,... | collective-permute-start | bytes 24584 | tf_op jit(solution)/shard_map/ppermute | solution.py:80
  9.0 2.5 %collective-permute-start.4 = (f32[16,128]{1,0:T(8,128)S(1)}, f32[16,128]{1,0:T(8,128)S(1)}, u32[]{:S(2)}, u32[]{:S(2)}) collective-permute-start(f32[16,128]{1,0:T(8,128)S(1)} %get-tuple-element.44), channel_id=1, source_target_pairs={{0,16},{1,0},{2,1},{3,2},{4,3},{5,4},{6,5},{7,6},{8,7},{9,8},{10,9... | collective-permute-start | bytes 24584 | tf_op jit(solution)/shard_map/ppermute | solution.py:80
  12.9 2.0 %all_terms.1.uvw_ref = f32[51,128,128]{2,1,0:T(8,128)S(1)} custom-call(f32[16,128,128]{2,1,0:T(8,128)S(1)} %copy-done.2, f32[16,128,128]{2,1,0:T(8,128)S(1)} %copy-done.3, f32[16,128,128]{2,1,0:T(8,128)S(1)} %copy-done.4, f32[3,128,128]{2,1,0:T(8,128)S(1)} %collective-permute-done.above_ref, f32[16,128]{1,0:T(8,128)S(1)} %collective-permute-done.1.inner_ref, ...), custom_call_target="tpu_custom_call" | custom-call | bytes 7500000 | tf_op jit(solution)/shard_map/all_terms/pallas_call | solution.py:91
  14.9 4.6 %collective-permute-start.5 = (f32[51,128,128]{2,1,0:T(8,128)S(1)}, f32[51,128,128]{2,1,0:T(8,128)S(1)}, u32[]{:S(2)}, u32[]{:S(2)}) collective-permute-start(f32[51,128,128]{2,1,0:T(8,128)S(1)} %all_terms.1.uvw_ref), channel_id=1, source_target_pairs={{0,16},{1,17},{2,18},{3,19},{4,20},{5,21},{6,22},{7,23},{8,24},{9,... | collective-permute-start | bytes 10027016 | tf_op jit(solution)/shard_map/ppermute | solution.py:80
  19.6 2.5 %collective-permute-start.6 = (f32[656,128]{1,0:T(8,128)S(1)}, f32[656,128]{1,0:T(8,128)S(1)}, u32[]{:S(2)}, u32[]{:S(2)}) collective-permute-start(f32[656,128]{1,0:T(8,128)S(1)} %pack_rows.1), channel_id=1, source_target_pairs={{16,32},{17,33},{18,34},{19,35},{20,36},{21,37},{22,38},{23,39},{2... | collective-permute-start | bytes 1007624 | tf_op jit(solution)/shard_map/ppermute | solution.py:80
  22.1 1.8 %pack.1 = (f32[480,128]{1,0:T(8,128)S(1)}, f32[480,128]{1,0:T(8,128)S(1)}, f32[80,128]{1,0:T(8,128)S(1)}, f32[80,128]{1,0:T(8,128)S(1)}) custom-call(f32[51,128,128]{2,1,0:T(8,128)S(1)} %all_terms.1.uvw_ref), custom_call_target="tpu_custom_call" | custom-call | bytes 1500000 | tf_op jit(solution)/shard_map/pack/pallas_call | solution.py:91
  24.0 2.1 %collective-permute-start.8 = (f32[480,128]{1,0:T(8,128)S(1)}, f32[480,128]{1,0:T(8,128)S(1)}, u32[]{:S(2)}, u32[]{:S(2)}) collective-permute-start(f32[480,128]{1,0:T(8,128)S(1)} %get-tuple-element.48), channel_id=1, source_target_pairs={{0,32},{1,16},{2,17},{3,18},{4,19},{5,20},{6,21},{7,22},{8,23},{9,... | collective-permute-start | bytes 737288 | tf_op jit(solution)/shard_map/ppermute | solution.py:80
  26.2 3.5 %collective-permute-start.9 = (f32[80,128]{1,0:T(8,128)S(1)}, f32[80,128]{1,0:T(8,128)S(1)}, u32[]{:S(2)}, u32[]{:S(2)}) collective-permute-start(f32[80,128]{1,0:T(8,128)S(1)} %get-tuple-element.50), channel_id=1, source_target_pairs={{0,16},{1,17},{2,18},{3,19},{4,20},{5,21},{6,22},{7,23},{8,24},{9,... | collective-permute-start | bytes 122888 | tf_op jit(solution)/shard_map/ppermute | solution.py:80
  30.5 1.6 %collective-permute-start.10 = (f32[80,128]{1,0:T(8,128)S(1)}, f32[80,128]{1,0:T(8,128)S(1)}, u32[]{:S(2)}, u32[]{:S(2)}) collective-permute-start(f32[80,128]{1,0:T(8,128)S(1)} %pick_corner.1), channel_id=1, source_target_pairs={{0,32},{1,48},{2,49},{3,50},{4,51},{5,52},{6,53},{7,54},{8,55},{9,... | collective-permute-start | bytes 122888 | tf_op jit(solution)/shard_map/ppermute | solution.py:80
  32.1 9.8 %collective-permute-done.10.corner_ref = f32[80,128]{1,0:T(8,128)S(1)} collective-permute-done((f32[80,128]{1,0:T(8,128)S(1)}, f32[80,128]{1,0:T(8,128)S(1)}, u32[]{:S(2)}, u32[]{:S(2)}) %collective-permute-start.10) | collective-permute-done | bytes 40992 | tf_op jit(solution)/shard_map/ppermute | solution.py:80
  42.3 1.6 %collective-permute-done.11.shared_ref = f32[656,128]{1,0:T(8,128)S(1)} collective-permute-done((f32[656,128]{1,0:T(8,128)S(1)}, f32[656,128]{1,0:T(8,128)S(1)}, u32[]{:S(2)}, u32[]{:S(2)}) %collective-permute-start.11) | collective-permute-done | bytes 335904 | tf_op jit(solution)/shard_map/ppermute | solution.py:80
  43.9 2.0 %assemble.1.refs_0_.uv_ref = f32[34,288,128]{2,1,0:T(8,128)S(1)} custom-call(f32[51,128,128]{2,1,0:T(8,128)S(1)} %all_terms.1.uvw_ref, f32[51,128,128]{2,1,0:T(8,128)S(1)} %collective-permute-done.5.other_ref, f32[656,128]{1,0:T(8,128)S(1)} %collective-permute-done.6.got_ref, f32[656,128]{1,0:T(8,128)S(1)} %collective-permute-done.11.shared_ref, ...), custom_call_target="tpu_custom_call" | custom-call | bytes 7500000 | tf_op jit(solution)/shard_map/assemble/pallas_call | solution.py:91
  53.3 1.6 %collective-permute-start.21 = (f32[192,128]{1,0:T(8,128)S(1)}, f32[192,128]{1,0:T(8,128)S(1)}, u32[]{:S(2)}, u32[]{:S(2)}) collective-permute-start(f32[192,128]{1,0:T(8,128)S(1)} %get-tuple-element.62), channel_id=1, source_target_pairs={{64,0},{65,1},{66,2},{67,3},{68,4},{69,5},{70,6},{71,7},{72,8},{73... | collective-permute-start | bytes 294920 | tf_op jit(solution)/shard_map/ppermute | solution.py:80
  54.8 1.3 %collective-permute-start.22 = (f32[64,128]{1,0:T(8,128)S(1)}, f32[64,128]{1,0:T(8,128)S(1)}, u32[]{:S(2)}, u32[]{:S(2)}) collective-permute-start(f32[64,128]{1,0:T(8,128)S(1)} %get-tuple-element.63), channel_id=1, source_target_pairs={{65,16},{66,17},{67,18},{68,19},{69,20},{70,21},{71,22},{72,23},{7... | collective-permute-start | bytes 98312 | tf_op jit(solution)/shard_map/ppermute | solution.py:80
  56.1 1.3 %collective-permute-start.23 = (f32[24,128]{1,0:T(8,128)S(1)}, f32[24,128]{1,0:T(8,128)S(1)}, u32[]{:S(2)}, u32[]{:S(2)}) collective-permute-start(f32[24,128]{1,0:T(8,128)S(1)} %get-tuple-element.64), channel_id=1, source_target_pairs={{64,32},{65,33},{66,34},{67,35},{68,36},{69,37},{70,38},{71,39},{7... | collective-permute-start | bytes 36872 | tf_op jit(solution)/shard_map/ppermute | solution.py:80
  57.4 1.3 %collective-permute-start.24 = (f32[24,128]{1,0:T(8,128)S(1)}, f32[24,128]{1,0:T(8,128)S(1)}, u32[]{:S(2)}, u32[]{:S(2)}) collective-permute-start(f32[24,128]{1,0:T(8,128)S(1)} %get-tuple-element.64), channel_id=1, source_target_pairs={{65,48},{66,49},{67,50},{68,51},{69,52},{70,53},{71,54},{72,55},{7... | collective-permute-start | bytes 36872 | tf_op jit(solution)/shard_map/ppermute | solution.py:80
  59.9 14.8 %collective-permute-done.23.halo_ref = f32[24,128]{1,0:T(8,128)S(1)} collective-permute-done((f32[24,128]{1,0:T(8,128)S(1)}, f32[24,128]{1,0:T(8,128)S(1)}, u32[]{:S(2)}, u32[]{:S(2)}) %collective-permute-start.23) | collective-permute-done | bytes 12320 | tf_op jit(solution)/shard_map/ppermute | solution.py:80
  74.7 4.6 %collective-permute-done.24.halo_outer_ref = f32[24,128]{1,0:T(8,128)S(1)} collective-permute-done((f32[24,128]{1,0:T(8,128)S(1)}, f32[24,128]{1,0:T(8,128)S(1)}, u32[]{:S(2)}, u32[]{:S(2)}) %collective-permute-start.24) | collective-permute-done | bytes 12320 | tf_op jit(solution)/shard_map/ppermute | solution.py:80
  81.1 1.5 %collective-permute-done.25.got_ref = f32[4,128,128]{2,1,0:T(8,128)S(1)} collective-permute-done((f32[4,128,128]{2,1,0:T(8,128)S(1)}, f32[4,128,128]{2,1,0:T(8,128)S(1)}, u32[]{:S(2)}, u32[]{:S(2)}) %collective-permute-start.25) | collective-permute-done | bytes 262176 | tf_op jit(solution)/shard_map/ppermute | solution.py:80
  84.2 1.5 %smooth_rest.1 = (f32[12,128,128]{2,1,0:T(8,128)S(1)}, f32[3,128,128]{2,1,0:T(8,128)S(1)}, f32[3,128,128]{2,1,0:T(8,128)S(1)}) custom-call(f32[12,288,128]{2,1,0:T(8,128)S(1)} %section_rest.1.layers_ref, f32[17,288,128]{2,1,0:T(8,128)S(1)} %assemble_w.1.w_ref), custom_call_target="tpu_custom_call" | custom-call | bytes 9000000 | tf_op jit(solution)/shard_map/smooth_rest/pallas_call | solution.py:91
  86.3 1.6 %collective-permute-start.29 = (f32[3,128,128]{2,1,0:T(8,128)S(1)}, f32[3,128,128]{2,1,0:T(8,128)S(1)}, u32[]{:S(2)}, u32[]{:S(2)}) collective-permute-start(f32[3,128,128]{2,1,0:T(8,128)S(1)} %get-tuple-element.74), channel_id=1, source_target_pairs={{0,192},{1,193},{2,194},{3,195},{4,196},{5,197},{6,198},{7,199},{8... | collective-permute-start | bytes 589832 | tf_op jit(solution)/shard_map/ppermute | solution.py:80
  87.9 4.8 %collective-permute-done.29.above_ref = f32[3,128,128]{2,1,0:T(8,128)S(1)} collective-permute-done((f32[3,128,128]{2,1,0:T(8,128)S(1)}, f32[3,128,128]{2,1,0:T(8,128)S(1)}, u32[]{:S(2)}, u32[]{:S(2)}) %collective-permute-start.29) | collective-permute-done | bytes 196640 | tf_op jit(solution)/shard_map/ppermute | solution.py:80
  93.3 1.5 %finish.1 = f32[16,128,128]{2,1,0:T(8,128)} custom-call(f32[12,128,128]{2,1,0:T(8,128)S(1)} %get-tuple-element.71.kept_ref, f32[3,128,128]{2,1,0:T(8,128)S(1)} %collective-permute-done.26.got_ref, f32[3,128,128]{2,1,0:T(8,128)S(1)} %collective-permute-done.27.got_more_ref, f32[5,128,128]{2,1,0:T(8,128)S(1)} %get-tuple-element.69.top_ref, ...), custom_call_target="tpu_custom_call" | custom-call | bytes 9000000 | tf_op jit(solution)/shard_map/finish/pallas_call | solution.py:91
  (66 shorter events, 19.4 us)
Async XLA Ops:
  2.4 10.6 %collective-permute-start = (f32[3,128,128]{2,1,0:T(8,128)S(1)}, f32[3,128,128]{2,1,0:T(8,128)S(1)}, u32[]{:S(2)}, u32[]{:S(2)}) collective-permute-start(f32[3,128,128]{2,1,0:T(8,128)S(1)} %get-tuple-element.40), channel_id=1, source_target_pairs={{0,192},{1,193},{2,194},{3,195},{4,196},{5,197},{6,198},{7,199},{8... | collective-permute-start | bytes 589832 | tf_op jit(solution)/shard_map/ppermute | solution.py:80
  6.0 5.5 %collective-permute-start.1 = (f32[16,128]{1,0:T(8,128)S(1)}, f32[16,128]{1,0:T(8,128)S(1)}, u32[]{:S(2)}, u32[]{:S(2)}) collective-permute-start(f32[16,128]{1,0:T(8,128)S(1)} %get-tuple-element.41), channel_id=1, source_target_pairs={{0,16},{1,17},{2,18},{3,19},{4,20},{5,21},{6,22},{7,23},{8,24},{9,... | collective-permute-start | bytes 24584 | tf_op jit(solution)/shard_map/ppermute | solution.py:80
  7.0 4.5 %collective-permute-start.2 = (f32[16,128]{1,0:T(8,128)S(1)}, f32[16,128]{1,0:T(8,128)S(1)}, u32[]{:S(2)}, u32[]{:S(2)}) collective-permute-start(f32[16,128]{1,0:T(8,128)S(1)} %get-tuple-element.42), channel_id=1, source_target_pairs={{0,48},{1,49},{2,50},{3,51},{4,52},{5,53},{6,54},{7,55},{8,56},{9,... | collective-permute-start | bytes 24584 | tf_op jit(solution)/shard_map/ppermute | solution.py:80
  8.5 4.0 %collective-permute-start.3 = (f32[16,128]{1,0:T(8,128)S(1)}, f32[16,128]{1,0:T(8,128)S(1)}, u32[]{:S(2)}, u32[]{:S(2)}) collective-permute-start(f32[16,128]{1,0:T(8,128)S(1)} %get-tuple-element.43), channel_id=1, source_target_pairs={{0,1},{1,2},{2,3},{3,4},{4,5},{5,6},{6,7},{7,8},{8,9},{9,10},{10,1... | collective-permute-start | bytes 24584 | tf_op jit(solution)/shard_map/ppermute | solution.py:80
  9.0 3.9 %collective-permute-start.4 = (f32[16,128]{1,0:T(8,128)S(1)}, f32[16,128]{1,0:T(8,128)S(1)}, u32[]{:S(2)}, u32[]{:S(2)}) collective-permute-start(f32[16,128]{1,0:T(8,128)S(1)} %get-tuple-element.44), channel_id=1, source_target_pairs={{0,16},{1,0},{2,1},{3,2},{4,3},{5,4},{6,5},{7,6},{8,7},{9,8},{10,9... | collective-permute-start | bytes 24584 | tf_op jit(solution)/shard_map/ppermute | solution.py:80
  14.9 29.0 %collective-permute-start.5 = (f32[51,128,128]{2,1,0:T(8,128)S(1)}, f32[51,128,128]{2,1,0:T(8,128)S(1)}, u32[]{:S(2)}, u32[]{:S(2)}) collective-permute-start(f32[51,128,128]{2,1,0:T(8,128)S(1)} %all_terms.1.uvw_ref), channel_id=1, source_target_pairs={{0,16},{1,17},{2,18},{3,19},{4,20},{5,21},{6,22},{7,23},{8,24},{9,... | collective-permute-start | bytes 10027016 | tf_op jit(solution)/shard_map/ppermute | solution.py:80
  19.6 22.4 %collective-permute-start.6 = (f32[656,128]{1,0:T(8,128)S(1)}, f32[656,128]{1,0:T(8,128)S(1)}, u32[]{:S(2)}, u32[]{:S(2)}) collective-permute-start(f32[656,128]{1,0:T(8,128)S(1)} %pack_rows.1), channel_id=1, source_target_pairs={{16,32},{17,33},{18,34},{19,35},{20,36},{21,37},{22,38},{23,39},{2... | collective-permute-start | bytes 1007624 | tf_op jit(solution)/shard_map/ppermute | solution.py:80
  23.9 18.0 %collective-permute-start.7 = (f32[480,128]{1,0:T(8,128)S(1)}, f32[480,128]{1,0:T(8,128)S(1)}, u32[]{:S(2)}, u32[]{:S(2)}) collective-permute-start(f32[480,128]{1,0:T(8,128)S(1)} %get-tuple-element.47), channel_id=1, source_target_pairs={{0,1},{1,2},{2,3},{3,4},{4,5},{5,6},{6,7},{7,8},{8,9},{9,10},{10,1... | collective-permute-start | bytes 737288 | tf_op jit(solution)/shard_map/ppermute | solution.py:80
  24.0 17.9 %collective-permute-start.8 = (f32[480,128]{1,0:T(8,128)S(1)}, f32[480,128]{1,0:T(8,128)S(1)}, u32[]{:S(2)}, u32[]{:S(2)}) collective-permute-start(f32[480,128]{1,0:T(8,128)S(1)} %get-tuple-element.48), channel_id=1, source_target_pairs={{0,32},{1,16},{2,17},{3,18},{4,19},{5,20},{6,21},{7,22},{8,23},{9,... | collective-permute-start | bytes 737288 | tf_op jit(solution)/shard_map/ppermute | solution.py:80
  26.2 4.3 %collective-permute-start.9 = (f32[80,128]{1,0:T(8,128)S(1)}, f32[80,128]{1,0:T(8,128)S(1)}, u32[]{:S(2)}, u32[]{:S(2)}) collective-permute-start(f32[80,128]{1,0:T(8,128)S(1)} %get-tuple-element.50), channel_id=1, source_target_pairs={{0,16},{1,17},{2,18},{3,19},{4,20},{5,21},{6,22},{7,23},{8,24},{9,... | collective-permute-start | bytes 122888 | tf_op jit(solution)/shard_map/ppermute | solution.py:80
  30.5 11.4 %collective-permute-start.10 = (f32[80,128]{1,0:T(8,128)S(1)}, f32[80,128]{1,0:T(8,128)S(1)}, u32[]{:S(2)}, u32[]{:S(2)}) collective-permute-start(f32[80,128]{1,0:T(8,128)S(1)} %pick_corner.1), channel_id=1, source_target_pairs={{0,32},{1,48},{2,49},{3,50},{4,51},{5,52},{6,53},{7,54},{8,55},{9,... | collective-permute-start | bytes 122888 | tf_op jit(solution)/shard_map/ppermute | solution.py:80
  42.0 1.9 %collective-permute-start.11 = (f32[656,128]{1,0:T(8,128)S(1)}, f32[656,128]{1,0:T(8,128)S(1)}, u32[]{:S(2)}, u32[]{:S(2)}) collective-permute-start(f32[656,128]{1,0:T(8,128)S(1)} %collective-permute-done.6.got_ref), channel_id=1, source_target_pairs={{0,16},{1,17},{2,18},{3,19},{4,20},{5,21},{6,22},{7,23},{8,24},{9,... | collective-permute-start | bytes 1007624 | tf_op jit(solution)/shard_map/ppermute | solution.py:80
  46.0 2.7 %collective-permute-start.12 = (f32[192,128]{1,0:T(8,128)S(1)}, f32[192,128]{1,0:T(8,128)S(1)}, u32[]{:S(2)}, u32[]{:S(2)}) collective-permute-start(f32[192,128]{1,0:T(8,128)S(1)} %get-tuple-element.52), channel_id=1, source_target_pairs={{192,128},{193,129},{194,130},{195,131},{196,132},{197,133},{198,1... | collective-permute-start | bytes 294920 | tf_op jit(solution)/shard_map/ppermute | solution.py:80
  46.6 2.0 %collective-permute-start.13 = (f32[64,128]{1,0:T(8,128)S(1)}, f32[64,128]{1,0:T(8,128)S(1)}, u32[]{:S(2)}, u32[]{:S(2)}) collective-permute-start(f32[64,128]{1,0:T(8,128)S(1)} %get-tuple-element.53), channel_id=1, source_target_pairs={{193,144},{194,145},{195,146},{196,147},{197,148},{198,149},{199,1... | collective-permute-start | bytes 98312 | tf_op jit(solution)/shard_map/ppermute | solution.py:80
  50.3 2.7 %collective-permute-start.17 = (f32[256,128]{1,0:T(8,128)S(1)}, f32[256,128]{1,0:T(8,128)S(1)}, u32[]{:S(2)}, u32[]{:S(2)}) collective-permute-start(f32[256,128]{1,0:T(8,128)S(1)} %get-tuple-element.57), channel_id=1, source_target_pairs={{128,64},{129,65},{130,66},{131,67},{132,68},{133,69},{134,70},{13... | collective-permute-start | bytes 393224 | tf_op jit(solution)/shard_map/ppermute | solution.py:80
  51.0 2.0 %collective-permute-start.18 = (f32[64,128]{1,0:T(8,128)S(1)}, f32[64,128]{1,0:T(8,128)S(1)}, u32[]{:S(2)}, u32[]{:S(2)}) collective-permute-start(f32[64,128]{1,0:T(8,128)S(1)} %get-tuple-element.58), channel_id=1, source_target_pairs={{129,80},{130,81},{131,82},{132,83},{133,84},{134,85},{135,86},{13... | collective-permute-start | bytes 98312 | tf_op jit(solution)/shard_map/ppermute | solution.py:80
  53.3 26.1 %collective-permute-start.21 = (f32[192,128]{1,0:T(8,128)S(1)}, f32[192,128]{1,0:T(8,128)S(1)}, u32[]{:S(2)}, u32[]{:S(2)}) collective-permute-start(f32[192,128]{1,0:T(8,128)S(1)} %get-tuple-element.62), channel_id=1, source_target_pairs={{64,0},{65,1},{66,2},{67,3},{68,4},{69,5},{70,6},{71,7},{72,8},{73... | collective-permute-start | bytes 294920 | tf_op jit(solution)/shard_map/ppermute | solution.py:80
  54.8 24.5 %collective-permute-start.22 = (f32[64,128]{1,0:T(8,128)S(1)}, f32[64,128]{1,0:T(8,128)S(1)}, u32[]{:S(2)}, u32[]{:S(2)}) collective-permute-start(f32[64,128]{1,0:T(8,128)S(1)} %get-tuple-element.63), channel_id=1, source_target_pairs={{65,16},{66,17},{67,18},{68,19},{69,20},{70,21},{71,22},{72,23},{7... | collective-permute-start | bytes 98312 | tf_op jit(solution)/shard_map/ppermute | solution.py:80
  56.1 18.6 %collective-permute-start.23 = (f32[24,128]{1,0:T(8,128)S(1)}, f32[24,128]{1,0:T(8,128)S(1)}, u32[]{:S(2)}, u32[]{:S(2)}) collective-permute-start(f32[24,128]{1,0:T(8,128)S(1)} %get-tuple-element.64), channel_id=1, source_target_pairs={{64,32},{65,33},{66,34},{67,35},{68,36},{69,37},{70,38},{71,39},{7... | collective-permute-start | bytes 36872 | tf_op jit(solution)/shard_map/ppermute | solution.py:80
  57.4 21.9 %collective-permute-start.24 = (f32[24,128]{1,0:T(8,128)S(1)}, f32[24,128]{1,0:T(8,128)S(1)}, u32[]{:S(2)}, u32[]{:S(2)}) collective-permute-start(f32[24,128]{1,0:T(8,128)S(1)} %get-tuple-element.64), channel_id=1, source_target_pairs={{65,48},{66,49},{67,50},{68,51},{69,52},{70,53},{71,54},{72,55},{7... | collective-permute-start | bytes 36872 | tf_op jit(solution)/shard_map/ppermute | solution.py:80
  82.8 10.5 %collective-permute-start.28 = (f32[5,128,128]{2,1,0:T(8,128)S(1)}, f32[5,128,128]{2,1,0:T(8,128)S(1)}, u32[]{:S(2)}, u32[]{:S(2)}) collective-permute-start(f32[5,128,128]{2,1,0:T(8,128)S(1)} %get-tuple-element.69.top_ref), channel_id=1, source_target_pairs={{0,64},{1,65},{2,66},{3,67},{4,68},{5,69},{6,70},{7,71},{8,72},{9,... | collective-permute-start | bytes 983048 | tf_op jit(solution)/shard_map/ppermute | solution.py:80
  85.7 2.2 %collective-permute-start.26 = (f32[3,128,128]{2,1,0:T(8,128)S(1)}, f32[3,128,128]{2,1,0:T(8,128)S(1)}, u32[]{:S(2)}, u32[]{:S(2)}) collective-permute-start(f32[3,128,128]{2,1,0:T(8,128)S(1)} %get-tuple-element.72), channel_id=1, source_target_pairs={{0,16},{1,17},{2,18},{3,19},{4,20},{5,21},{6,22},{7,23},{8,24},{9,... | collective-permute-start | bytes 589832 | tf_op jit(solution)/shard_map/ppermute | solution.py:80
  85.9 1.9 %collective-permute-start.27 = (f32[3,128,128]{2,1,0:T(8,128)S(1)}, f32[3,128,128]{2,1,0:T(8,128)S(1)}, u32[]{:S(2)}, u32[]{:S(2)}) collective-permute-start(f32[3,128,128]{2,1,0:T(8,128)S(1)} %get-tuple-element.73), channel_id=1, source_target_pairs={{0,16},{1,17},{2,18},{3,19},{4,20},{5,21},{6,22},{7,23},{8,24},{9,... | collective-permute-start | bytes 589832 | tf_op jit(solution)/shard_map/ppermute | solution.py:80
  86.3 6.4 %collective-permute-start.29 = (f32[3,128,128]{2,1,0:T(8,128)S(1)}, f32[3,128,128]{2,1,0:T(8,128)S(1)}, u32[]{:S(2)}, u32[]{:S(2)}) collective-permute-start(f32[3,128,128]{2,1,0:T(8,128)S(1)} %get-tuple-element.74), channel_id=1, source_target_pairs={{0,192},{1,193},{2,194},{3,195},{4,196},{5,197},{6,198},{7,199},{8... | collective-permute-start | bytes 589832 | tf_op jit(solution)/shard_map/ppermute | solution.py:80
  (12 other events, 45.6 us)

commit v11 on v10

--- a/solution.py
+++ b/solution.py
@@ -738,8 +738,8 @@
         smooth_first, [shape(8, 128, 128), shape(4, 128, 128)], top_layers, layers, ws, scratch=work_for(8)
     )
     top, bottom = call(ends, [shape(RADIUS + 1, 128, 128), shape(RADIUS - 1, 128, 128)], kept, to_other(given))
-    below = moved(top, lambda z, y, x: (z + 1, y, x))
-    over = moved(bottom, lambda z, y, x: (z - 1, y, x))
+    below = moved(top, lambda z, y, x: (z + 1, y, x) if z < depth - 1 else None)
+    over = moved(bottom, lambda z, y, x: (z - 1, y, x) if z > 0 else None)
     rest = call(section_rest, shape(LOW, PLANE, 128), uvs, after(top_layers, top), layers)
     third = shape(3, 128, 128)
     kept, given, given_more = call(

time: 96.4 us -> 98.9 us (1.026)
  waiting for transfers between devices: 41.2 us -> 42.7 us
  starting transfers between devices: 37.2 us -> 38.2 us
    ppermute x30, waiting for transfers between devices: 41.2 us -> 42.7 us  [moved(): return lax.ppermute(value, AXES, pairs)]
  transfers between devices with their start and end apart: 30 -> 30, of which waited for: 11 -> 10; matrix products, arithmetic and copies ran while one was open for 0% -> 0% of each run, Pallas kernels for 6% -> 6%
where the time goes in v11:
time: 98.9 us; the launch traced here: 97.3 us
  waiting for transfers between devices  42.7 us (43%)
  starting transfers between devices  38.2 us (39%)
  Pallas kernels  14.8 us (15%)
  local copies, waits for them, and re-layouts  1.25 us (1%)
    ppermute x30, waiting for transfers between devices, moved(): return lax.ppermute(value, AXES, pairs)  42.7 us
    ppermute x30, starting transfers between devices, moved(): return lax.ppermute(value, AXES, pairs)  38.2 us
    pallas_call x18, Pallas kernels, call(): pl.pallas_call(kernel, out_shape=outs, scratch_shapes=list(scratch), comp...  14.8 us
  transfers between devices with their start and end apart: 30, of which 10 were waited for; matrix products, arithmetic and copies ran while one was open for 0% of the time, Pallas kernels for 6%

profile of v11, /device:TPU:1, one launch (start us, length us, event | category | flops | bytes accessed | tf_op | source)
XLA Modules:
  0.0 97.3 jit_solution(8366094163494380101)
XLA Ops:
  2.4 3.6 %collective-permute-start = (f32[3,128,128]{2,1,0:T(8,128)S(1)}, f32[3,128,128]{2,1,0:T(8,128)S(1)}, u32[]{:S(2)}, u32[]{:S(2)}) collective-permute-start(f32[3,128,128]{2,1,0:T(8,128)S(1)} %get-tuple-element.40), channel_id=1, source_target_pairs={{0,192},{1,193},{2,194},{3,195},{4,196},{5,197},{6,198},{7,199},{8... | collective-permute-start | bytes 589832 | tf_op jit(solution)/shard_map/ppermute | solution.py:80
  7.0 1.5 %collective-permute-start.2 = (f32[16,128]{1,0:T(8,128)S(1)}, f32[16,128]{1,0:T(8,128)S(1)}, u32[]{:S(2)}, u32[]{:S(2)}) collective-permute-start(f32[16,128]{1,0:T(8,128)S(1)} %get-tuple-element.42), channel_id=1, source_target_pairs={{0,48},{1,49},{2,50},{3,51},{4,52},{5,53},{6,54},{7,55},{8,56},{9,... | collective-permute-start | bytes 24584 | tf_op jit(solution)/shard_map/ppermute | solution.py:80
  9.0 2.5 %collective-permute-start.4 = (f32[16,128]{1,0:T(8,128)S(1)}, f32[16,128]{1,0:T(8,128)S(1)}, u32[]{:S(2)}, u32[]{:S(2)}) collective-permute-start(f32[16,128]{1,0:T(8,128)S(1)} %get-tuple-element.44), channel_id=1, source_target_pairs={{0,16},{1,0},{2,1},{3,2},{4,3},{5,4},{6,5},{7,6},{8,7},{9,8},{10,9... | collective-permute-start | bytes 24584 | tf_op jit(solution)/shard_map/ppermute | solution.py:80
  12.9 2.0 %all_terms.1.uvw_ref = f32[51,128,128]{2,1,0:T(8,128)S(1)} custom-call(f32[16,128,128]{2,1,0:T(8,128)S(1)} %copy-done.2, f32[16,128,128]{2,1,0:T(8,128)S(1)} %copy-done.3, f32[16,128,128]{2,1,0:T(8,128)S(1)} %copy-done.4, f32[3,128,128]{2,1,0:T(8,128)S(1)} %collective-permute-done.above_ref, f32[16,128]{1,0:T(8,128)S(1)} %collective-permute-done.1.inner_ref, ...), custom_call_target="tpu_custom_call" | custom-call | bytes 7500000 | tf_op jit(solution)/shard_map/all_terms/pallas_call | solution.py:91
  14.9 4.6 %collective-permute-start.5 = (f32[51,128,128]{2,1,0:T(8,128)S(1)}, f32[51,128,128]{2,1,0:T(8,128)S(1)}, u32[]{:S(2)}, u32[]{:S(2)}) collective-permute-start(f32[51,128,128]{2,1,0:T(8,128)S(1)} %all_terms.1.uvw_ref), channel_id=1, source_target_pairs={{0,16},{1,17},{2,18},{3,19},{4,20},{5,21},{6,22},{7,23},{8,24},{9,... | collective-permute-start | bytes 10027016 | tf_op jit(solution)/shard_map/ppermute | solution.py:80
  19.6 2.5 %collective-permute-start.6 = (f32[656,128]{1,0:T(8,128)S(1)}, f32[656,128]{1,0:T(8,128)S(1)}, u32[]{:S(2)}, u32[]{:S(2)}) collective-permute-start(f32[656,128]{1,0:T(8,128)S(1)} %pack_rows.1), channel_id=1, source_target_pairs={{16,32},{17,33},{18,34},{19,35},{20,36},{21,37},{22,38},{23,39},{2... | collective-permute-start | bytes 1007624 | tf_op jit(solution)/shard_map/ppermute | solution.py:80
  22.1 1.8 %pack.1 = (f32[480,128]{1,0:T(8,128)S(1)}, f32[480,128]{1,0:T(8,128)S(1)}, f32[80,128]{1,0:T(8,128)S(1)}, f32[80,128]{1,0:T(8,128)S(1)}) custom-call(f32[51,128,128]{2,1,0:T(8,128)S(1)} %all_terms.1.uvw_ref), custom_call_target="tpu_custom_call" | custom-call | bytes 1500000 | tf_op jit(solution)/shard_map/pack/pallas_call | solution.py:91
  24.0 2.1 %collective-permute-start.8 = (f32[480,128]{1,0:T(8,128)S(1)}, f32[480,128]{1,0:T(8,128)S(1)}, u32[]{:S(2)}, u32[]{:S(2)}) collective-permute-start(f32[480,128]{1,0:T(8,128)S(1)} %get-tuple-element.48), channel_id=1, source_target_pairs={{0,32},{1,16},{2,17},{3,18},{4,19},{5,20},{6,21},{7,22},{8,23},{9,... | collective-permute-start | bytes 737288 | tf_op jit(solution)/shard_map/ppermute | solution.py:80
  26.2 3.5 %collective-permute-start.9 = (f32[80,128]{1,0:T(8,128)S(1)}, f32[80,128]{1,0:T(8,128)S(1)}, u32[]{:S(2)}, u32[]{:S(2)}) collective-permute-start(f32[80,128]{1,0:T(8,128)S(1)} %get-tuple-element.50), channel_id=1, source_target_pairs={{0,16},{1,17},{2,18},{3,19},{4,20},{5,21},{6,22},{7,23},{8,24},{9,... | collective-permute-start | bytes 122888 | tf_op jit(solution)/shard_map/ppermute | solution.py:80
  30.5 1.6 %collective-permute-start.10 = (f32[80,128]{1,0:T(8,128)S(1)}, f32[80,128]{1,0:T(8,128)S(1)}, u32[]{:S(2)}, u32[]{:S(2)}) collective-permute-start(f32[80,128]{1,0:T(8,128)S(1)} %pick_corner.1), channel_id=1, source_target_pairs={{0,32},{1,48},{2,49},{3,50},{4,51},{5,52},{6,53},{7,54},{8,55},{9,... | collective-permute-start | bytes 122888 | tf_op jit(solution)/shard_map/ppermute | solution.py:80
  32.1 9.8 %collective-permute-done.10.corner_ref = f32[80,128]{1,0:T(8,128)S(1)} collective-permute-done((f32[80,128]{1,0:T(8,128)S(1)}, f32[80,128]{1,0:T(8,128)S(1)}, u32[]{:S(2)}, u32[]{:S(2)}) %collective-permute-start.10) | collective-permute-done | bytes 40992 | tf_op jit(solution)/shard_map/ppermute | solution.py:80
  42.3 1.6 %collective-permute-done.11.shared_ref = f32[656,128]{1,0:T(8,128)S(1)} collective-permute-done((f32[656,128]{1,0:T(8,128)S(1)}, f32[656,128]{1,0:T(8,128)S(1)}, u32[]{:S(2)}, u32[]{:S(2)}) %collective-permute-start.11) | collective-permute-done | bytes 335904 | tf_op jit(solution)/shard_map/ppermute | solution.py:80
  43.9 2.0 %assemble.1.refs_0_.uv_ref = f32[34,288,128]{2,1,0:T(8,128)S(1)} custom-call(f32[51,128,128]{2,1,0:T(8,128)S(1)} %all_terms.1.uvw_ref, f32[51,128,128]{2,1,0:T(8,128)S(1)} %collective-permute-done.5.other_ref, f32[656,128]{1,0:T(8,128)S(1)} %collective-permute-done.6.got_ref, f32[656,128]{1,0:T(8,128)S(1)} %collective-permute-done.11.shared_ref, ...), custom_call_target="tpu_custom_call" | custom-call | bytes 7500000 | tf_op jit(solution)/shard_map/assemble/pallas_call | solution.py:91
  53.3 1.6 %collective-permute-start.21 = (f32[192,128]{1,0:T(8,128)S(1)}, f32[192,128]{1,0:T(8,128)S(1)}, u32[]{:S(2)}, u32[]{:S(2)}) collective-permute-start(f32[192,128]{1,0:T(8,128)S(1)} %get-tuple-element.62), channel_id=1, source_target_pairs={{64,0},{65,1},{66,2},{67,3},{68,4},{69,5},{70,6},{71,7},{72,8},{73... | collective-permute-start | bytes 294920 | tf_op jit(solution)/shard_map/ppermute | solution.py:80
  54.8 1.3 %collective-permute-start.22 = (f32[64,128]{1,0:T(8,128)S(1)}, f32[64,128]{1,0:T(8,128)S(1)}, u32[]{:S(2)}, u32[]{:S(2)}) collective-permute-start(f32[64,128]{1,0:T(8,128)S(1)} %get-tuple-element.63), channel_id=1, source_target_pairs={{65,16},{66,17},{67,18},{68,19},{69,20},{70,21},{71,22},{72,23},{7... | collective-permute-start | bytes 98312 | tf_op jit(solution)/shard_map/ppermute | solution.py:80
  56.1 1.3 %collective-permute-start.23 = (f32[24,128]{1,0:T(8,128)S(1)}, f32[24,128]{1,0:T(8,128)S(1)}, u32[]{:S(2)}, u32[]{:S(2)}) collective-permute-start(f32[24,128]{1,0:T(8,128)S(1)} %get-tuple-element.64), channel_id=1, source_target_pairs={{64,32},{65,33},{66,34},{67,35},{68,36},{69,37},{70,38},{71,39},{7... | collective-permute-start | bytes 36872 | tf_op jit(solution)/shard_map/ppermute | solution.py:80
  57.4 1.3 %collective-permute-start.24 = (f32[24,128]{1,0:T(8,128)S(1)}, f32[24,128]{1,0:T(8,128)S(1)}, u32[]{:S(2)}, u32[]{:S(2)}) collective-permute-start(f32[24,128]{1,0:T(8,128)S(1)} %get-tuple-element.64), channel_id=1, source_target_pairs={{65,48},{66,49},{67,50},{68,51},{69,52},{70,53},{71,54},{72,55},{7... | collective-permute-start | bytes 36872 | tf_op jit(solution)/shard_map/ppermute | solution.py:80
  59.9 14.8 %collective-permute-done.23.halo_ref = f32[24,128]{1,0:T(8,128)S(1)} collective-permute-done((f32[24,128]{1,0:T(8,128)S(1)}, f32[24,128]{1,0:T(8,128)S(1)}, u32[]{:S(2)}, u32[]{:S(2)}) %collective-permute-start.23) | collective-permute-done | bytes 12320 | tf_op jit(solution)/shard_map/ppermute | solution.py:80
  74.7 4.6 %collective-permute-done.24.halo_outer_ref = f32[24,128]{1,0:T(8,128)S(1)} collective-permute-done((f32[24,128]{1,0:T(8,128)S(1)}, f32[24,128]{1,0:T(8,128)S(1)}, u32[]{:S(2)}, u32[]{:S(2)}) %collective-permute-start.24) | collective-permute-done | bytes 12320 | tf_op jit(solution)/shard_map/ppermute | solution.py:80
  81.1 1.5 %collective-permute-done.25.got_ref = f32[4,128,128]{2,1,0:T(8,128)S(1)} collective-permute-done((f32[4,128,128]{2,1,0:T(8,128)S(1)}, f32[4,128,128]{2,1,0:T(8,128)S(1)}, u32[]{:S(2)}, u32[]{:S(2)}) %collective-permute-start.25) | collective-permute-done | bytes 262176 | tf_op jit(solution)/shard_map/ppermute | solution.py:80
  82.8 1.3 %collective-permute-start.28 = (f32[5,128,128]{2,1,0:T(8,128)S(1)}, f32[5,128,128]{2,1,0:T(8,128)S(1)}, u32[]{:S(2)}, u32[]{:S(2)}) collective-permute-start(f32[5,128,128]{2,1,0:T(8,128)S(1)} %get-tuple-element.69.top_ref), channel_id=1, source_target_pairs={{0,64},{1,65},{2,66},{3,67},{4,68},{5,69},{6,70},{7,71},{8,72},{9,... | collective-permute-start | bytes 983048 | tf_op jit(solution)/shard_map/ppermute | solution.py:80
  85.4 1.5 %smooth_rest.1 = (f32[12,128,128]{2,1,0:T(8,128)S(1)}, f32[3,128,128]{2,1,0:T(8,128)S(1)}, f32[3,128,128]{2,1,0:T(8,128)S(1)}) custom-call(f32[12,288,128]{2,1,0:T(8,128)S(1)} %section_rest.1.layers_ref, f32[17,288,128]{2,1,0:T(8,128)S(1)} %assemble_w.1.w_ref), custom_call_target="tpu_custom_call" | custom-call | bytes 9000000 | tf_op jit(solution)/shard_map/smooth_rest/pallas_call | solution.py:91
  88.8 6.9 %collective-permute-done.29.above_ref = f32[3,128,128]{2,1,0:T(8,128)S(1)} collective-permute-done((f32[3,128,128]{2,1,0:T(8,128)S(1)}, f32[3,128,128]{2,1,0:T(8,128)S(1)}, u32[]{:S(2)}, u32[]{:S(2)}) %collective-permute-start.29) | collective-permute-done | bytes 196640 | tf_op jit(solution)/shard_map/ppermute | solution.py:80
  95.8 1.5 %finish.1 = f32[16,128,128]{2,1,0:T(8,128)} custom-call(f32[12,128,128]{2,1,0:T(8,128)S(1)} %get-tuple-element.71.kept_ref, f32[3,128,128]{2,1,0:T(8,128)S(1)} %collective-permute-done.26.got_ref, f32[3,128,128]{2,1,0:T(8,128)S(1)} %collective-permute-done.27.got_more_ref, f32[5,128,128]{2,1,0:T(8,128)S(1)} %get-tuple-element.69.top_ref, ...), custom_call_target="tpu_custom_call" | custom-call | bytes 9000000 | tf_op jit(solution)/shard_map/finish/pallas_call | solution.py:91
  (66 shorter events, 20.0 us)
Async XLA Ops:
  2.4 10.6 %collective-permute-start = (f32[3,128,128]{2,1,0:T(8,128)S(1)}, f32[3,128,128]{2,1,0:T(8,128)S(1)}, u32[]{:S(2)}, u32[]{:S(2)}) collective-permute-start(f32[3,128,128]{2,1,0:T(8,128)S(1)} %get-tuple-element.40), channel_id=1, source_target_pairs={{0,192},{1,193},{2,194},{3,195},{4,196},{5,197},{6,198},{7,199},{8... | collective-permute-start | bytes 589832 | tf_op jit(solution)/shard_map/ppermute | solution.py:80
  6.0 5.5 %collective-permute-start.1 = (f32[16,128]{1,0:T(8,128)S(1)}, f32[16,128]{1,0:T(8,128)S(1)}, u32[]{:S(2)}, u32[]{:S(2)}) collective-permute-start(f32[16,128]{1,0:T(8,128)S(1)} %get-tuple-element.41), channel_id=1, source_target_pairs={{0,16},{1,17},{2,18},{3,19},{4,20},{5,21},{6,22},{7,23},{8,24},{9,... | collective-permute-start | bytes 24584 | tf_op jit(solution)/shard_map/ppermute | solution.py:80
  7.0 4.5 %collective-permute-start.2 = (f32[16,128]{1,0:T(8,128)S(1)}, f32[16,128]{1,0:T(8,128)S(1)}, u32[]{:S(2)}, u32[]{:S(2)}) collective-permute-start(f32[16,128]{1,0:T(8,128)S(1)} %get-tuple-element.42), channel_id=1, source_target_pairs={{0,48},{1,49},{2,50},{3,51},{4,52},{5,53},{6,54},{7,55},{8,56},{9,... | collective-permute-start | bytes 24584 | tf_op jit(solution)/shard_map/ppermute | solution.py:80
  8.5 4.0 %collective-permute-start.3 = (f32[16,128]{1,0:T(8,128)S(1)}, f32[16,128]{1,0:T(8,128)S(1)}, u32[]{:S(2)}, u32[]{:S(2)}) collective-permute-start(f32[16,128]{1,0:T(8,128)S(1)} %get-tuple-element.43), channel_id=1, source_target_pairs={{0,1},{1,2},{2,3},{3,4},{4,5},{5,6},{6,7},{7,8},{8,9},{9,10},{10,1... | collective-permute-start | bytes 24584 | tf_op jit(solution)/shard_map/ppermute | solution.py:80
  9.0 3.9 %collective-permute-start.4 = (f32[16,128]{1,0:T(8,128)S(1)}, f32[16,128]{1,0:T(8,128)S(1)}, u32[]{:S(2)}, u32[]{:S(2)}) collective-permute-start(f32[16,128]{1,0:T(8,128)S(1)} %get-tuple-element.44), channel_id=1, source_target_pairs={{0,16},{1,0},{2,1},{3,2},{4,3},{5,4},{6,5},{7,6},{8,7},{9,8},{10,9... | collective-permute-start | bytes 24584 | tf_op jit(solution)/shard_map/ppermute | solution.py:80
  14.9 29.0 %collective-permute-start.5 = (f32[51,128,128]{2,1,0:T(8,128)S(1)}, f32[51,128,128]{2,1,0:T(8,128)S(1)}, u32[]{:S(2)}, u32[]{:S(2)}) collective-permute-start(f32[51,128,128]{2,1,0:T(8,128)S(1)} %all_terms.1.uvw_ref), channel_id=1, source_target_pairs={{0,16},{1,17},{2,18},{3,19},{4,20},{5,21},{6,22},{7,23},{8,24},{9,... | collective-permute-start | bytes 10027016 | tf_op jit(solution)/shard_map/ppermute | solution.py:80
  19.6 22.4 %collective-permute-start.6 = (f32[656,128]{1,0:T(8,128)S(1)}, f32[656,128]{1,0:T(8,128)S(1)}, u32[]{:S(2)}, u32[]{:S(2)}) collective-permute-start(f32[656,128]{1,0:T(8,128)S(1)} %pack_rows.1), channel_id=1, source_target_pairs={{16,32},{17,33},{18,34},{19,35},{20,36},{21,37},{22,38},{23,39},{2... | collective-permute-start | bytes 1007624 | tf_op jit(solution)/shard_map/ppermute | solution.py:80
  23.9 18.0 %collective-permute-start.7 = (f32[480,128]{1,0:T(8,128)S(1)}, f32[480,128]{1,0:T(8,128)S(1)}, u32[]{:S(2)}, u32[]{:S(2)}) collective-permute-start(f32[480,128]{1,0:T(8,128)S(1)} %get-tuple-element.47), channel_id=1, source_target_pairs={{0,1},{1,2},{2,3},{3,4},{4,5},{5,6},{6,7},{7,8},{8,9},{9,10},{10,1... | collective-permute-start | bytes 737288 | tf_op jit(solution)/shard_map/ppermute | solution.py:80
  24.0 17.9 %collective-permute-start.8 = (f32[480,128]{1,0:T(8,128)S(1)}, f32[480,128]{1,0:T(8,128)S(1)}, u32[]{:S(2)}, u32[]{:S(2)}) collective-permute-start(f32[480,128]{1,0:T(8,128)S(1)} %get-tuple-element.48), channel_id=1, source_target_pairs={{0,32},{1,16},{2,17},{3,18},{4,19},{5,20},{6,21},{7,22},{8,23},{9,... | collective-permute-start | bytes 737288 | tf_op jit(solution)/shard_map/ppermute | solution.py:80
  26.2 4.3 %collective-permute-start.9 = (f32[80,128]{1,0:T(8,128)S(1)}, f32[80,128]{1,0:T(8,128)S(1)}, u32[]{:S(2)}, u32[]{:S(2)}) collective-permute-start(f32[80,128]{1,0:T(8,128)S(1)} %get-tuple-element.50), channel_id=1, source_target_pairs={{0,16},{1,17},{2,18},{3,19},{4,20},{5,21},{6,22},{7,23},{8,24},{9,... | collective-permute-start | bytes 122888 | tf_op jit(solution)/shard_map/ppermute | solution.py:80
  30.5 11.4 %collective-permute-start.10 = (f32[80,128]{1,0:T(8,128)S(1)}, f32[80,128]{1,0:T(8,128)S(1)}, u32[]{:S(2)}, u32[]{:S(2)}) collective-permute-start(f32[80,128]{1,0:T(8,128)S(1)} %pick_corner.1), channel_id=1, source_target_pairs={{0,32},{1,48},{2,49},{3,50},{4,51},{5,52},{6,53},{7,54},{8,55},{9,... | collective-permute-start | bytes 122888 | tf_op jit(solution)/shard_map/ppermute | solution.py:80
  42.0 1.9 %collective-permute-start.11 = (f32[656,128]{1,0:T(8,128)S(1)}, f32[656,128]{1,0:T(8,128)S(1)}, u32[]{:S(2)}, u32[]{:S(2)}) collective-permute-start(f32[656,128]{1,0:T(8,128)S(1)} %collective-permute-done.6.got_ref), channel_id=1, source_target_pairs={{0,16},{1,17},{2,18},{3,19},{4,20},{5,21},{6,22},{7,23},{8,24},{9,... | collective-permute-start | bytes 1007624 | tf_op jit(solution)/shard_map/ppermute | solution.py:80
  46.0 2.7 %collective-permute-start.12 = (f32[192,128]{1,0:T(8,128)S(1)}, f32[192,128]{1,0:T(8,128)S(1)}, u32[]{:S(2)}, u32[]{:S(2)}) collective-permute-start(f32[192,128]{1,0:T(8,128)S(1)} %get-tuple-element.52), channel_id=1, source_target_pairs={{192,128},{193,129},{194,130},{195,131},{196,132},{197,133},{198,1... | collective-permute-start | bytes 294920 | tf_op jit(solution)/shard_map/ppermute | solution.py:80
  46.6 2.0 %collective-permute-start.13 = (f32[64,128]{1,0:T(8,128)S(1)}, f32[64,128]{1,0:T(8,128)S(1)}, u32[]{:S(2)}, u32[]{:S(2)}) collective-permute-start(f32[64,128]{1,0:T(8,128)S(1)} %get-tuple-element.53), channel_id=1, source_target_pairs={{193,144},{194,145},{195,146},{196,147},{197,148},{198,149},{199,1... | collective-permute-start | bytes 98312 | tf_op jit(solution)/shard_map/ppermute | solution.py:80
  50.3 2.7 %collective-permute-start.17 = (f32[256,128]{1,0:T(8,128)S(1)}, f32[256,128]{1,0:T(8,128)S(1)}, u32[]{:S(2)}, u32[]{:S(2)}) collective-permute-start(f32[256,128]{1,0:T(8,128)S(1)} %get-tuple-element.57), channel_id=1, source_target_pairs={{128,64},{129,65},{130,66},{131,67},{132,68},{133,69},{134,70},{13... | collective-permute-start | bytes 393224 | tf_op jit(solution)/shard_map/ppermute | solution.py:80
  51.0 2.0 %collective-permute-start.18 = (f32[64,128]{1,0:T(8,128)S(1)}, f32[64,128]{1,0:T(8,128)S(1)}, u32[]{:S(2)}, u32[]{:S(2)}) collective-permute-start(f32[64,128]{1,0:T(8,128)S(1)} %get-tuple-element.58), channel_id=1, source_target_pairs={{129,80},{130,81},{131,82},{132,83},{133,84},{134,85},{135,86},{13... | collective-permute-start | bytes 98312 | tf_op jit(solution)/shard_map/ppermute | solution.py:80
  53.3 26.1 %collective-permute-start.21 = (f32[192,128]{1,0:T(8,128)S(1)}, f32[192,128]{1,0:T(8,128)S(1)}, u32[]{:S(2)}, u32[]{:S(2)}) collective-permute-start(f32[192,128]{1,0:T(8,128)S(1)} %get-tuple-element.62), channel_id=1, source_target_pairs={{64,0},{65,1},{66,2},{67,3},{68,4},{69,5},{70,6},{71,7},{72,8},{73... | collective-permute-start | bytes 294920 | tf_op jit(solution)/shard_map/ppermute | solution.py:80
  54.8 24.5 %collective-permute-start.22 = (f32[64,128]{1,0:T(8,128)S(1)}, f32[64,128]{1,0:T(8,128)S(1)}, u32[]{:S(2)}, u32[]{:S(2)}) collective-permute-start(f32[64,128]{1,0:T(8,128)S(1)} %get-tuple-element.63), channel_id=1, source_target_pairs={{65,16},{66,17},{67,18},{68,19},{69,20},{70,21},{71,22},{72,23},{7... | collective-permute-start | bytes 98312 | tf_op jit(solution)/shard_map/ppermute | solution.py:80
  56.1 18.6 %collective-permute-start.23 = (f32[24,128]{1,0:T(8,128)S(1)}, f32[24,128]{1,0:T(8,128)S(1)}, u32[]{:S(2)}, u32[]{:S(2)}) collective-permute-start(f32[24,128]{1,0:T(8,128)S(1)} %get-tuple-element.64), channel_id=1, source_target_pairs={{64,32},{65,33},{66,34},{67,35},{68,36},{69,37},{70,38},{71,39},{7... | collective-permute-start | bytes 36872 | tf_op jit(solution)/shard_map/ppermute | solution.py:80
  57.4 21.9 %collective-permute-start.24 = (f32[24,128]{1,0:T(8,128)S(1)}, f32[24,128]{1,0:T(8,128)S(1)}, u32[]{:S(2)}, u32[]{:S(2)}) collective-permute-start(f32[24,128]{1,0:T(8,128)S(1)} %get-tuple-element.64), channel_id=1, source_target_pairs={{65,48},{66,49},{67,50},{68,51},{69,52},{70,53},{71,54},{72,55},{7... | collective-permute-start | bytes 36872 | tf_op jit(solution)/shard_map/ppermute | solution.py:80
  82.8 12.9 %collective-permute-start.28 = (f32[5,128,128]{2,1,0:T(8,128)S(1)}, f32[5,128,128]{2,1,0:T(8,128)S(1)}, u32[]{:S(2)}, u32[]{:S(2)}) collective-permute-start(f32[5,128,128]{2,1,0:T(8,128)S(1)} %get-tuple-element.69.top_ref), channel_id=1, source_target_pairs={{0,64},{1,65},{2,66},{3,67},{4,68},{5,69},{6,70},{7,71},{8,72},{9,... | collective-permute-start | bytes 983048 | tf_op jit(solution)/shard_map/ppermute | solution.py:80
  86.9 1.9 %collective-permute-start.26 = (f32[3,128,128]{2,1,0:T(8,128)S(1)}, f32[3,128,128]{2,1,0:T(8,128)S(1)}, u32[]{:S(2)}, u32[]{:S(2)}) collective-permute-start(f32[3,128,128]{2,1,0:T(8,128)S(1)} %get-tuple-element.72), channel_id=1, source_target_pairs={{0,16},{1,17},{2,18},{3,19},{4,20},{5,21},{6,22},{7,23},{8,24},{9,... | collective-permute-start | bytes 589832 | tf_op jit(solution)/shard_map/ppermute | solution.py:80
  87.1 1.7 %collective-permute-start.27 = (f32[3,128,128]{2,1,0:T(8,128)S(1)}, f32[3,128,128]{2,1,0:T(8,128)S(1)}, u32[]{:S(2)}, u32[]{:S(2)}) collective-permute-start(f32[3,128,128]{2,1,0:T(8,128)S(1)} %get-tuple-element.73), channel_id=1, source_target_pairs={{0,16},{1,17},{2,18},{3,19},{4,20},{5,21},{6,22},{7,23},{8,24},{9,... | collective-permute-start | bytes 589832 | tf_op jit(solution)/shard_map/ppermute | solution.py:80
  87.5 8.2 %collective-permute-start.29 = (f32[3,128,128]{2,1,0:T(8,128)S(1)}, f32[3,128,128]{2,1,0:T(8,128)S(1)}, u32[]{:S(2)}, u32[]{:S(2)}) collective-permute-start(f32[3,128,128]{2,1,0:T(8,128)S(1)} %get-tuple-element.74), channel_id=1, source_target_pairs={{64,0},{65,1},{66,2},{67,3},{68,4},{69,5},{70,6},{71,7},{72,8},{73... | collective-permute-start | bytes 589832 | tf_op jit(solution)/shard_map/ppermute | solution.py:80
  (12 other events, 46.9 us)

commit v12 on v10

--- a/solution.py
+++ b/solution.py
@@ -577,10 +577,10 @@
     pair_up(others, 0, 4, give_ref)
 
 
-def smooth_rest(layers_ref, w_ref, kept_ref, give_ref, give_more_ref, plains, others, tent):
+def smooth_rest(layers_ref, w_ref, kept_ref, first_ref, second_ref, third_ref, plains, others, tent):
     smooth([(layers_ref.at[k], w_ref.at[k]) for k in range(LOW)], kept_ref, plains, others, tent)
-    pair_up(others, 0, 3, give_ref)
-    pair_up(others, 6, 3, give_more_ref)
+    for i, give_ref in enumerate((first_ref, second_ref, third_ref)):
+        pair_up(others, 4 * i, 2, give_ref)
 
 
 def whole(kept, got, second):
@@ -597,11 +597,11 @@
             bottom_ref[k - (STEPS - LOW)] = value
 
 
-def finish(kept_ref, got_ref, got_more_ref, top_ref, below_ref, above_ref, passive_ref, out_ref, tile):
+def finish(kept_ref, first_ref, second_ref, third_ref, top_ref, below_ref, above_ref, passive_ref, out_ref, tile):
     gz = lax.axis_index("gz")
     for k in range(LOW):
-        got = got_ref if k < 6 else got_more_ref
-        tile[k] = whole(kept_ref[k], got[k % 3], k % 6 >= 3)
+        got = (first_ref, second_ref, third_ref)[k // 4]
+        tile[k] = whole(kept_ref[k], got[k % 2], k % 4 >= 2)
 
     def layer(k):
         if k < 0:
@@ -741,13 +741,13 @@
     below = moved(top, lambda z, y, x: (z + 1, y, x))
     over = moved(bottom, lambda z, y, x: (z - 1, y, x))
     rest = call(section_rest, shape(LOW, PLANE, 128), uvs, after(top_layers, top), layers)
-    third = shape(3, 128, 128)
-    kept, given, given_more = call(
-        smooth_rest, [shape(LOW, 128, 128), third, third], rest, ws, scratch=work_for(LOW)
+    third = shape(2, 128, 128)
+    kept, *given = call(
+        smooth_rest, [shape(LOW, 128, 128), third, third, third], rest, ws, scratch=work_for(LOW)
     )
     return call(
         finish, shape(LAYERS, 128, 128),
-        kept, to_other(given), to_other(given_more), top, below, over, passive,
+        kept, *(to_other(part) for part in given), top, below, over, passive,
         scratch=[pltpu.VMEM((LOW, 128, 128), F32)],
     )
 

time: 96.4 us -> 96.4 us (level)
  starting transfers between devices: 37.2 us -> 39 us
  waiting for transfers between devices: 41.2 us -> 39.6 us
    ppermute x30 -> x31, starting transfers between devices: 37.2 us -> 39 us  [moved(): return lax.ppermute(value, AXES, pairs)]
    ppermute x30 -> x31, waiting for transfers between devices: 41.2 us -> 39.6 us  [moved(): return lax.ppermute(value, AXES, pairs)]
  transfers between devices with their start and end apart: 30 -> 31, of which waited for: 11 -> 13; matrix products, arithmetic and copies ran while one was open for 0% -> 0% of each run, Pallas kernels for 6% -> 6%
where the time goes in v12:
time: 96.4 us; the launch traced here: 94.8 us
  waiting for transfers between devices  39.6 us (41%)
  starting transfers between devices  39 us (40%)
  Pallas kernels  14.5 us (15%)
  local copies, waits for them, and re-layouts  1.25 us (1%)
    ppermute x31, waiting for transfers between devices, moved(): return lax.ppermute(value, AXES, pairs)  39.6 us
    ppermute x31, starting transfers between devices, moved(): return lax.ppermute(value, AXES, pairs)  39 us
    pallas_call x18, Pallas kernels, call(): pl.pallas_call(kernel, out_shape=outs, scratch_shapes=list(scratch), comp...  14.5 us
  transfers between devices with their start and end apart: 31, of which 13 were waited for; matrix products, arithmetic and copies ran while one was open for 0% of the time, Pallas kernels for 6%

profile of v12, /device:TPU:1, one launch (start us, length us, event | category | flops | bytes accessed | tf_op | source)
XLA Modules:
  0.0 94.8 jit_solution(8272660571289873669)
XLA Ops:
  2.4 3.6 %collective-permute-start = (f32[3,128,128]{2,1,0:T(8,128)S(1)}, f32[3,128,128]{2,1,0:T(8,128)S(1)}, u32[]{:S(2)}, u32[]{:S(2)}) collective-permute-start(f32[3,128,128]{2,1,0:T(8,128)S(1)} %get-tuple-element.41), channel_id=1, source_target_pairs={{0,192},{1,193},{2,194},{3,195},{4,196},{5,197},{6,198},{7,199},{8... | collective-permute-start | bytes 589832 | tf_op jit(solution)/shard_map/ppermute | solution.py:80
  7.0 1.5 %collective-permute-start.2 = (f32[16,128]{1,0:T(8,128)S(1)}, f32[16,128]{1,0:T(8,128)S(1)}, u32[]{:S(2)}, u32[]{:S(2)}) collective-permute-start(f32[16,128]{1,0:T(8,128)S(1)} %get-tuple-element.43), channel_id=1, source_target_pairs={{0,48},{1,49},{2,50},{3,51},{4,52},{5,53},{6,54},{7,55},{8,56},{9,... | collective-permute-start | bytes 24584 | tf_op jit(solution)/shard_map/ppermute | solution.py:80
  9.0 2.5 %collective-permute-start.4 = (f32[16,128]{1,0:T(8,128)S(1)}, f32[16,128]{1,0:T(8,128)S(1)}, u32[]{:S(2)}, u32[]{:S(2)}) collective-permute-start(f32[16,128]{1,0:T(8,128)S(1)} %get-tuple-element.45), channel_id=1, source_target_pairs={{0,16},{1,0},{2,1},{3,2},{4,3},{5,4},{6,5},{7,6},{8,7},{9,8},{10,9... | collective-permute-start | bytes 24584 | tf_op jit(solution)/shard_map/ppermute | solution.py:80
  12.9 2.0 %all_terms.1.uvw_ref = f32[51,128,128]{2,1,0:T(8,128)S(1)} custom-call(f32[16,128,128]{2,1,0:T(8,128)S(1)} %copy-done.2, f32[16,128,128]{2,1,0:T(8,128)S(1)} %copy-done.3, f32[16,128,128]{2,1,0:T(8,128)S(1)} %copy-done.4, f32[3,128,128]{2,1,0:T(8,128)S(1)} %collective-permute-done.above_ref, f32[16,128]{1,0:T(8,128)S(1)} %collective-permute-done.1.inner_ref, ...), custom_call_target="tpu_custom_call" | custom-call | bytes 7500000 | tf_op jit(solution)/shard_map/all_terms/pallas_call | solution.py:91
  14.9 4.6 %collective-permute-start.5 = (f32[51,128,128]{2,1,0:T(8,128)S(1)}, f32[51,128,128]{2,1,0:T(8,128)S(1)}, u32[]{:S(2)}, u32[]{:S(2)}) collective-permute-start(f32[51,128,128]{2,1,0:T(8,128)S(1)} %all_terms.1.uvw_ref), channel_id=1, source_target_pairs={{0,16},{1,17},{2,18},{3,19},{4,20},{5,21},{6,22},{7,23},{8,24},{9,... | collective-permute-start | bytes 10027016 | tf_op jit(solution)/shard_map/ppermute | solution.py:80
  19.6 2.5 %collective-permute-start.6 = (f32[656,128]{1,0:T(8,128)S(1)}, f32[656,128]{1,0:T(8,128)S(1)}, u32[]{:S(2)}, u32[]{:S(2)}) collective-permute-start(f32[656,128]{1,0:T(8,128)S(1)} %pack_rows.1), channel_id=1, source_target_pairs={{16,32},{17,33},{18,34},{19,35},{20,36},{21,37},{22,38},{23,39},{2... | collective-permute-start | bytes 1007624 | tf_op jit(solution)/shard_map/ppermute | solution.py:80
  22.1 1.8 %pack.1 = (f32[480,128]{1,0:T(8,128)S(1)}, f32[480,128]{1,0:T(8,128)S(1)}, f32[80,128]{1,0:T(8,128)S(1)}, f32[80,128]{1,0:T(8,128)S(1)}) custom-call(f32[51,128,128]{2,1,0:T(8,128)S(1)} %all_terms.1.uvw_ref), custom_call_target="tpu_custom_call" | custom-call | bytes 1500000 | tf_op jit(solution)/shard_map/pack/pallas_call | solution.py:91
  24.0 2.1 %collective-permute-start.8 = (f32[480,128]{1,0:T(8,128)S(1)}, f32[480,128]{1,0:T(8,128)S(1)}, u32[]{:S(2)}, u32[]{:S(2)}) collective-permute-start(f32[480,128]{1,0:T(8,128)S(1)} %get-tuple-element.49), channel_id=1, source_target_pairs={{0,32},{1,16},{2,17},{3,18},{4,19},{5,20},{6,21},{7,22},{8,23},{9,... | collective-permute-start | bytes 737288 | tf_op jit(solution)/shard_map/ppermute | solution.py:80
  26.2 3.5 %collective-permute-start.9 = (f32[80,128]{1,0:T(8,128)S(1)}, f32[80,128]{1,0:T(8,128)S(1)}, u32[]{:S(2)}, u32[]{:S(2)}) collective-permute-start(f32[80,128]{1,0:T(8,128)S(1)} %get-tuple-element.51), channel_id=1, source_target_pairs={{0,16},{1,17},{2,18},{3,19},{4,20},{5,21},{6,22},{7,23},{8,24},{9,... | collective-permute-start | bytes 122888 | tf_op jit(solution)/shard_map/ppermute | solution.py:80
  30.5 1.6 %collective-permute-start.10 = (f32[80,128]{1,0:T(8,128)S(1)}, f32[80,128]{1,0:T(8,128)S(1)}, u32[]{:S(2)}, u32[]{:S(2)}) collective-permute-start(f32[80,128]{1,0:T(8,128)S(1)} %pick_corner.1), channel_id=1, source_target_pairs={{0,32},{1,48},{2,49},{3,50},{4,51},{5,52},{6,53},{7,54},{8,55},{9,... | collective-permute-start | bytes 122888 | tf_op jit(solution)/shard_map/ppermute | solution.py:80
  32.1 9.8 %collective-permute-done.10.corner_ref = f32[80,128]{1,0:T(8,128)S(1)} collective-permute-done((f32[80,128]{1,0:T(8,128)S(1)}, f32[80,128]{1,0:T(8,128)S(1)}, u32[]{:S(2)}, u32[]{:S(2)}) %collective-permute-start.10) | collective-permute-done | bytes 40992 | tf_op jit(solution)/shard_map/ppermute | solution.py:80
  42.3 1.6 %collective-permute-done.11.shared_ref = f32[656,128]{1,0:T(8,128)S(1)} collective-permute-done((f32[656,128]{1,0:T(8,128)S(1)}, f32[656,128]{1,0:T(8,128)S(1)}, u32[]{:S(2)}, u32[]{:S(2)}) %collective-permute-start.11) | collective-permute-done | bytes 335904 | tf_op jit(solution)/shard_map/ppermute | solution.py:80
  43.9 2.0 %assemble.1.refs_0_.uv_ref = f32[34,288,128]{2,1,0:T(8,128)S(1)} custom-call(f32[51,128,128]{2,1,0:T(8,128)S(1)} %all_terms.1.uvw_ref, f32[51,128,128]{2,1,0:T(8,128)S(1)} %collective-permute-done.5.other_ref, f32[656,128]{1,0:T(8,128)S(1)} %collective-permute-done.6.got_ref, f32[656,128]{1,0:T(8,128)S(1)} %collective-permute-done.11.shared_ref, ...), custom_call_target="tpu_custom_call" | custom-call | bytes 7500000 | tf_op jit(solution)/shard_map/assemble/pallas_call | solution.py:91
  53.3 1.6 %collective-permute-start.21 = (f32[192,128]{1,0:T(8,128)S(1)}, f32[192,128]{1,0:T(8,128)S(1)}, u32[]{:S(2)}, u32[]{:S(2)}) collective-permute-start(f32[192,128]{1,0:T(8,128)S(1)} %get-tuple-element.63), channel_id=1, source_target_pairs={{64,0},{65,1},{66,2},{67,3},{68,4},{69,5},{70,6},{71,7},{72,8},{73... | collective-permute-start | bytes 294920 | tf_op jit(solution)/shard_map/ppermute | solution.py:80
  54.8 1.3 %collective-permute-start.22 = (f32[64,128]{1,0:T(8,128)S(1)}, f32[64,128]{1,0:T(8,128)S(1)}, u32[]{:S(2)}, u32[]{:S(2)}) collective-permute-start(f32[64,128]{1,0:T(8,128)S(1)} %get-tuple-element.64), channel_id=1, source_target_pairs={{65,16},{66,17},{67,18},{68,19},{69,20},{70,21},{71,22},{72,23},{7... | collective-permute-start | bytes 98312 | tf_op jit(solution)/shard_map/ppermute | solution.py:80
  56.1 1.3 %collective-permute-start.23 = (f32[24,128]{1,0:T(8,128)S(1)}, f32[24,128]{1,0:T(8,128)S(1)}, u32[]{:S(2)}, u32[]{:S(2)}) collective-permute-start(f32[24,128]{1,0:T(8,128)S(1)} %get-tuple-element.65), channel_id=1, source_target_pairs={{64,32},{65,33},{66,34},{67,35},{68,36},{69,37},{70,38},{71,39},{7... | collective-permute-start | bytes 36872 | tf_op jit(solution)/shard_map/ppermute | solution.py:80
  57.4 1.3 %collective-permute-start.24 = (f32[24,128]{1,0:T(8,128)S(1)}, f32[24,128]{1,0:T(8,128)S(1)}, u32[]{:S(2)}, u32[]{:S(2)}) collective-permute-start(f32[24,128]{1,0:T(8,128)S(1)} %get-tuple-element.65), channel_id=1, source_target_pairs={{65,48},{66,49},{67,50},{68,51},{69,52},{70,53},{71,54},{72,55},{7... | collective-permute-start | bytes 36872 | tf_op jit(solution)/shard_map/ppermute | solution.py:80
  59.9 14.8 %collective-permute-done.23.halo_ref = f32[24,128]{1,0:T(8,128)S(1)} collective-permute-done((f32[24,128]{1,0:T(8,128)S(1)}, f32[24,128]{1,0:T(8,128)S(1)}, u32[]{:S(2)}, u32[]{:S(2)}) %collective-permute-start.23) | collective-permute-done | bytes 12320 | tf_op jit(solution)/shard_map/ppermute | solution.py:80
  74.7 4.6 %collective-permute-done.24.halo_outer_ref = f32[24,128]{1,0:T(8,128)S(1)} collective-permute-done((f32[24,128]{1,0:T(8,128)S(1)}, f32[24,128]{1,0:T(8,128)S(1)}, u32[]{:S(2)}, u32[]{:S(2)}) %collective-permute-start.24) | collective-permute-done | bytes 12320 | tf_op jit(solution)/shard_map/ppermute | solution.py:80
  81.1 1.5 %collective-permute-done.25.got_ref = f32[4,128,128]{2,1,0:T(8,128)S(1)} collective-permute-done((f32[4,128,128]{2,1,0:T(8,128)S(1)}, f32[4,128,128]{2,1,0:T(8,128)S(1)}, u32[]{:S(2)}, u32[]{:S(2)}) %collective-permute-start.25) | collective-permute-done | bytes 262176 | tf_op jit(solution)/shard_map/ppermute | solution.py:80
  82.9 2.7 %collective-permute-start.30 = (f32[3,128,128]{2,1,0:T(8,128)S(1)}, f32[3,128,128]{2,1,0:T(8,128)S(1)}, u32[]{:S(2)}, u32[]{:S(2)}) collective-permute-start(f32[3,128,128]{2,1,0:T(8,128)S(1)} %get-tuple-element.76), channel_id=1, source_target_pairs={{0,192},{1,193},{2,194},{3,195},{4,196},{5,197},{6,198},{7,199},{8... | collective-permute-start | bytes 589832 | tf_op jit(solution)/shard_map/ppermute | solution.py:80
  86.6 1.5 %smooth_rest.1 = (f32[12,128,128]{2,1,0:T(8,128)S(1)}, f32[2,128,128]{2,1,0:T(8,128)S(1)}, f32[2,128,128]{2,1,0:T(8,128)S(1)}, f32[2,128,128]{2,1,0:T(8,128)S(1)}) custom-call(f32[12,288,128]{2,1,0:T(8,128)S(1)} %section_rest.1.layers_ref, f32[17,288,128]{2,1,0:T(8,128)S(1)} %assemble_w.1.w_ref), custom_call_target="tpu_custom_call" | custom-call | bytes 9000000 | tf_op jit(solution)/shard_map/smooth_rest/pallas_call | solution.py:91
  90.4 2.8 %collective-permute-done.29.below_ref = f32[5,128,128]{2,1,0:T(8,128)S(1)} collective-permute-done((f32[5,128,128]{2,1,0:T(8,128)S(1)}, f32[5,128,128]{2,1,0:T(8,128)S(1)}, u32[]{:S(2)}, u32[]{:S(2)}) %collective-permute-start.29) | collective-permute-done | bytes 327712 | tf_op jit(solution)/shard_map/ppermute | solution.py:80
  93.3 1.6 %finish.1 = f32[16,128,128]{2,1,0:T(8,128)} custom-call(f32[12,128,128]{2,1,0:T(8,128)S(1)} %get-tuple-element.72.kept_ref, f32[2,128,128]{2,1,0:T(8,128)S(1)} %collective-permute-done.26.first_ref, f32[2,128,128]{2,1,0:T(8,128)S(1)} %collective-permute-done.27.second_ref, f32[2,128,128]{2,1,0:T(8,128)S(1)} %collective-permute-done.28.third_ref, ...), custom_call_target="tpu_custom_call" | custom-call | bytes 9000000 | tf_op jit(solution)/shard_map/finish/pallas_call | solution.py:91
  (68 shorter events, 20.3 us)
Async XLA Ops:
  2.4 10.6 %collective-permute-start = (f32[3,128,128]{2,1,0:T(8,128)S(1)}, f32[3,128,128]{2,1,0:T(8,128)S(1)}, u32[]{:S(2)}, u32[]{:S(2)}) collective-permute-start(f32[3,128,128]{2,1,0:T(8,128)S(1)} %get-tuple-element.41), channel_id=1, source_target_pairs={{0,192},{1,193},{2,194},{3,195},{4,196},{5,197},{6,198},{7,199},{8... | collective-permute-start | bytes 589832 | tf_op jit(solution)/shard_map/ppermute | solution.py:80
  6.0 5.5 %collective-permute-start.1 = (f32[16,128]{1,0:T(8,128)S(1)}, f32[16,128]{1,0:T(8,128)S(1)}, u32[]{:S(2)}, u32[]{:S(2)}) collective-permute-start(f32[16,128]{1,0:T(8,128)S(1)} %get-tuple-element.42), channel_id=1, source_target_pairs={{0,16},{1,17},{2,18},{3,19},{4,20},{5,21},{6,22},{7,23},{8,24},{9,... | collective-permute-start | bytes 24584 | tf_op jit(solution)/shard_map/ppermute | solution.py:80
  7.0 4.5 %collective-permute-start.2 = (f32[16,128]{1,0:T(8,128)S(1)}, f32[16,128]{1,0:T(8,128)S(1)}, u32[]{:S(2)}, u32[]{:S(2)}) collective-permute-start(f32[16,128]{1,0:T(8,128)S(1)} %get-tuple-element.43), channel_id=1, source_target_pairs={{0,48},{1,49},{2,50},{3,51},{4,52},{5,53},{6,54},{7,55},{8,56},{9,... | collective-permute-start | bytes 24584 | tf_op jit(solution)/shard_map/ppermute | solution.py:80
  8.5 4.0 %collective-permute-start.3 = (f32[16,128]{1,0:T(8,128)S(1)}, f32[16,128]{1,0:T(8,128)S(1)}, u32[]{:S(2)}, u32[]{:S(2)}) collective-permute-start(f32[16,128]{1,0:T(8,128)S(1)} %get-tuple-element.44), channel_id=1, source_target_pairs={{0,1},{1,2},{2,3},{3,4},{4,5},{5,6},{6,7},{7,8},{8,9},{9,10},{10,1... | collective-permute-start | bytes 24584 | tf_op jit(solution)/shard_map/ppermute | solution.py:80
  9.0 3.9 %collective-permute-start.4 = (f32[16,128]{1,0:T(8,128)S(1)}, f32[16,128]{1,0:T(8,128)S(1)}, u32[]{:S(2)}, u32[]{:S(2)}) collective-permute-start(f32[16,128]{1,0:T(8,128)S(1)} %get-tuple-element.45), channel_id=1, source_target_pairs={{0,16},{1,0},{2,1},{3,2},{4,3},{5,4},{6,5},{7,6},{8,7},{9,8},{10,9... | collective-permute-start | bytes 24584 | tf_op jit(solution)/shard_map/ppermute | solution.py:80
  14.9 29.0 %collective-permute-start.5 = (f32[51,128,128]{2,1,0:T(8,128)S(1)}, f32[51,128,128]{2,1,0:T(8,128)S(1)}, u32[]{:S(2)}, u32[]{:S(2)}) collective-permute-start(f32[51,128,128]{2,1,0:T(8,128)S(1)} %all_terms.1.uvw_ref), channel_id=1, source_target_pairs={{0,16},{1,17},{2,18},{3,19},{4,20},{5,21},{6,22},{7,23},{8,24},{9,... | collective-permute-start | bytes 10027016 | tf_op jit(solution)/shard_map/ppermute | solution.py:80
  19.6 22.4 %collective-permute-start.6 = (f32[656,128]{1,0:T(8,128)S(1)}, f32[656,128]{1,0:T(8,128)S(1)}, u32[]{:S(2)}, u32[]{:S(2)}) collective-permute-start(f32[656,128]{1,0:T(8,128)S(1)} %pack_rows.1), channel_id=1, source_target_pairs={{16,32},{17,33},{18,34},{19,35},{20,36},{21,37},{22,38},{23,39},{2... | collective-permute-start | bytes 1007624 | tf_op jit(solution)/shard_map/ppermute | solution.py:80
  23.9 18.0 %collective-permute-start.7 = (f32[480,128]{1,0:T(8,128)S(1)}, f32[480,128]{1,0:T(8,128)S(1)}, u32[]{:S(2)}, u32[]{:S(2)}) collective-permute-start(f32[480,128]{1,0:T(8,128)S(1)} %get-tuple-element.48), channel_id=1, source_target_pairs={{0,1},{1,2},{2,3},{3,4},{4,5},{5,6},{6,7},{7,8},{8,9},{9,10},{10,1... | collective-permute-start | bytes 737288 | tf_op jit(solution)/shard_map/ppermute | solution.py:80
  24.0 17.9 %collective-permute-start.8 = (f32[480,128]{1,0:T(8,128)S(1)}, f32[480,128]{1,0:T(8,128)S(1)}, u32[]{:S(2)}, u32[]{:S(2)}) collective-permute-start(f32[480,128]{1,0:T(8,128)S(1)} %get-tuple-element.49), channel_id=1, source_target_pairs={{0,32},{1,16},{2,17},{3,18},{4,19},{5,20},{6,21},{7,22},{8,23},{9,... | collective-permute-start | bytes 737288 | tf_op jit(solution)/shard_map/ppermute | solution.py:80
  26.2 4.3 %collective-permute-start.9 = (f32[80,128]{1,0:T(8,128)S(1)}, f32[80,128]{1,0:T(8,128)S(1)}, u32[]{:S(2)}, u32[]{:S(2)}) collective-permute-start(f32[80,128]{1,0:T(8,128)S(1)} %get-tuple-element.51), channel_id=1, source_target_pairs={{0,16},{1,17},{2,18},{3,19},{4,20},{5,21},{6,22},{7,23},{8,24},{9,... | collective-permute-start | bytes 122888 | tf_op jit(solution)/shard_map/ppermute | solution.py:80
  30.5 11.4 %collective-permute-start.10 = (f32[80,128]{1,0:T(8,128)S(1)}, f32[80,128]{1,0:T(8,128)S(1)}, u32[]{:S(2)}, u32[]{:S(2)}) collective-permute-start(f32[80,128]{1,0:T(8,128)S(1)} %pick_corner.1), channel_id=1, source_target_pairs={{0,32},{1,48},{2,49},{3,50},{4,51},{5,52},{6,53},{7,54},{8,55},{9,... | collective-permute-start | bytes 122888 | tf_op jit(solution)/shard_map/ppermute | solution.py:80
  42.0 1.9 %collective-permute-start.11 = (f32[656,128]{1,0:T(8,128)S(1)}, f32[656,128]{1,0:T(8,128)S(1)}, u32[]{:S(2)}, u32[]{:S(2)}) collective-permute-start(f32[656,128]{1,0:T(8,128)S(1)} %collective-permute-done.6.got_ref), channel_id=1, source_target_pairs={{0,16},{1,17},{2,18},{3,19},{4,20},{5,21},{6,22},{7,23},{8,24},{9,... | collective-permute-start | bytes 1007624 | tf_op jit(solution)/shard_map/ppermute | solution.py:80
  46.0 2.7 %collective-permute-start.12 = (f32[192,128]{1,0:T(8,128)S(1)}, f32[192,128]{1,0:T(8,128)S(1)}, u32[]{:S(2)}, u32[]{:S(2)}) collective-permute-start(f32[192,128]{1,0:T(8,128)S(1)} %get-tuple-element.53), channel_id=1, source_target_pairs={{192,128},{193,129},{194,130},{195,131},{196,132},{197,133},{198,1... | collective-permute-start | bytes 294920 | tf_op jit(solution)/shard_map/ppermute | solution.py:80
  46.6 2.0 %collective-permute-start.13 = (f32[64,128]{1,0:T(8,128)S(1)}, f32[64,128]{1,0:T(8,128)S(1)}, u32[]{:S(2)}, u32[]{:S(2)}) collective-permute-start(f32[64,128]{1,0:T(8,128)S(1)} %get-tuple-element.54), channel_id=1, source_target_pairs={{193,144},{194,145},{195,146},{196,147},{197,148},{198,149},{199,1... | collective-permute-start | bytes 98312 | tf_op jit(solution)/shard_map/ppermute | solution.py:80
  50.3 2.7 %collective-permute-start.17 = (f32[256,128]{1,0:T(8,128)S(1)}, f32[256,128]{1,0:T(8,128)S(1)}, u32[]{:S(2)}, u32[]{:S(2)}) collective-permute-start(f32[256,128]{1,0:T(8,128)S(1)} %get-tuple-element.58), channel_id=1, source_target_pairs={{128,64},{129,65},{130,66},{131,67},{132,68},{133,69},{134,70},{13... | collective-permute-start | bytes 393224 | tf_op jit(solution)/shard_map/ppermute | solution.py:80
  51.0 2.0 %collective-permute-start.18 = (f32[64,128]{1,0:T(8,128)S(1)}, f32[64,128]{1,0:T(8,128)S(1)}, u32[]{:S(2)}, u32[]{:S(2)}) collective-permute-start(f32[64,128]{1,0:T(8,128)S(1)} %get-tuple-element.59), channel_id=1, source_target_pairs={{129,80},{130,81},{131,82},{132,83},{133,84},{134,85},{135,86},{13... | collective-permute-start | bytes 98312 | tf_op jit(solution)/shard_map/ppermute | solution.py:80
  53.3 26.1 %collective-permute-start.21 = (f32[192,128]{1,0:T(8,128)S(1)}, f32[192,128]{1,0:T(8,128)S(1)}, u32[]{:S(2)}, u32[]{:S(2)}) collective-permute-start(f32[192,128]{1,0:T(8,128)S(1)} %get-tuple-element.63), channel_id=1, source_target_pairs={{64,0},{65,1},{66,2},{67,3},{68,4},{69,5},{70,6},{71,7},{72,8},{73... | collective-permute-start | bytes 294920 | tf_op jit(solution)/shard_map/ppermute | solution.py:80
  54.8 24.5 %collective-permute-start.22 = (f32[64,128]{1,0:T(8,128)S(1)}, f32[64,128]{1,0:T(8,128)S(1)}, u32[]{:S(2)}, u32[]{:S(2)}) collective-permute-start(f32[64,128]{1,0:T(8,128)S(1)} %get-tuple-element.64), channel_id=1, source_target_pairs={{65,16},{66,17},{67,18},{68,19},{69,20},{70,21},{71,22},{72,23},{7... | collective-permute-start | bytes 98312 | tf_op jit(solution)/shard_map/ppermute | solution.py:80
  56.1 18.6 %collective-permute-start.23 = (f32[24,128]{1,0:T(8,128)S(1)}, f32[24,128]{1,0:T(8,128)S(1)}, u32[]{:S(2)}, u32[]{:S(2)}) collective-permute-start(f32[24,128]{1,0:T(8,128)S(1)} %get-tuple-element.65), channel_id=1, source_target_pairs={{64,32},{65,33},{66,34},{67,35},{68,36},{69,37},{70,38},{71,39},{7... | collective-permute-start | bytes 36872 | tf_op jit(solution)/shard_map/ppermute | solution.py:80
  57.4 21.9 %collective-permute-start.24 = (f32[24,128]{1,0:T(8,128)S(1)}, f32[24,128]{1,0:T(8,128)S(1)}, u32[]{:S(2)}, u32[]{:S(2)}) collective-permute-start(f32[24,128]{1,0:T(8,128)S(1)} %get-tuple-element.65), channel_id=1, source_target_pairs={{65,48},{66,49},{67,50},{68,51},{69,52},{70,53},{71,54},{72,55},{7... | collective-permute-start | bytes 36872 | tf_op jit(solution)/shard_map/ppermute | solution.py:80
  81.0 1.6 %collective-permute-start.25 = (f32[4,128,128]{2,1,0:T(8,128)S(1)}, f32[4,128,128]{2,1,0:T(8,128)S(1)}, u32[]{:S(2)}, u32[]{:S(2)}) collective-permute-start(f32[4,128,128]{2,1,0:T(8,128)S(1)} %get-tuple-element.69), channel_id=1, source_target_pairs={{0,16},{1,17},{2,18},{3,19},{4,20},{5,21},{6,22},{7,23},{8,24},{9,... | collective-permute-start | bytes 786440 | tf_op jit(solution)/shard_map/ppermute | solution.py:80
  82.8 10.5 %collective-permute-start.29 = (f32[5,128,128]{2,1,0:T(8,128)S(1)}, f32[5,128,128]{2,1,0:T(8,128)S(1)}, u32[]{:S(2)}, u32[]{:S(2)}) collective-permute-start(f32[5,128,128]{2,1,0:T(8,128)S(1)} %get-tuple-element.70.top_ref), channel_id=1, source_target_pairs={{0,64},{1,65},{2,66},{3,67},{4,68},{5,69},{6,70},{7,71},{8,72},{9,... | collective-permute-start | bytes 983048 | tf_op jit(solution)/shard_map/ppermute | solution.py:80
  82.9 7.5 %collective-permute-start.30 = (f32[3,128,128]{2,1,0:T(8,128)S(1)}, f32[3,128,128]{2,1,0:T(8,128)S(1)}, u32[]{:S(2)}, u32[]{:S(2)}) collective-permute-start(f32[3,128,128]{2,1,0:T(8,128)S(1)} %get-tuple-element.76), channel_id=1, source_target_pairs={{0,192},{1,193},{2,194},{3,195},{4,196},{5,197},{6,198},{7,199},{8... | collective-permute-start | bytes 589832 | tf_op jit(solution)/shard_map/ppermute | solution.py:80
  88.1 1.8 %collective-permute-start.26 = (f32[2,128,128]{2,1,0:T(8,128)S(1)}, f32[2,128,128]{2,1,0:T(8,128)S(1)}, u32[]{:S(2)}, u32[]{:S(2)}) collective-permute-start(f32[2,128,128]{2,1,0:T(8,128)S(1)} %get-tuple-element.73), channel_id=1, source_target_pairs={{0,16},{1,17},{2,18},{3,19},{4,20},{5,21},{6,22},{7,23},{8,24},{9,... | collective-permute-start | bytes 393224 | tf_op jit(solution)/shard_map/ppermute | solution.py:80
  (13 other events, 44.4 us)

commit v13 on v10

--- a/solution.py
+++ b/solution.py
@@ -661,7 +661,7 @@
         in_specs=[hbm] * 3,
         scratch=[pltpu.VMEM((128, 128), F32), pltpu.VMEM((LAYERS, 128, 128), F32), pltpu.SemaphoreType.DMA((6,))],
     )
-    above = moved(lowest_planes, lambda z, y, x: (z - 1, y, x))
+    above = moved(lowest_planes, lambda z, y, x: (z - 1, y, x) if z > 0 else None)
     along, back = moved(along, same), moved(back, opposite)
     outer = moved(outer, lambda z, y, x: (z, y ^ 3, x))
     inner = to_other(inner)

time: 96.4 us -> 98.3 us (1.020)
  waiting for transfers between devices: 41.2 us -> 44.8 us
  starting transfers between devices: 37.2 us -> 35.6 us
    ppermute x30, waiting for transfers between devices: 41.2 us -> 44.8 us  [moved(): return lax.ppermute(value, AXES, pairs)]
    ppermute x30, starting transfers between devices: 37.2 us -> 35.6 us  [moved(): return lax.ppermute(value, AXES, pairs)]
  transfers between devices with their start and end apart: 30 -> 30, of which waited for: 11 -> 12; matrix products, arithmetic and copies ran while one was open for 0% -> 0% of each run, Pallas kernels for 6% -> 6%
where the time goes in v13:
time: 98.3 us; the launch traced here: 96.8 us
  waiting for transfers between devices  44.8 us (46%)
  starting transfers between devices  35.6 us (36%)
  Pallas kernels  14.8 us (15%)
  local copies, waits for them, and re-layouts  1.25 us (1%)
    ppermute x30, waiting for transfers between devices, moved(): return lax.ppermute(value, AXES, pairs)  44.8 us
    ppermute x30, starting transfers between devices, moved(): return lax.ppermute(value, AXES, pairs)  35.6 us
    pallas_call x18, Pallas kernels, call(): pl.pallas_call(kernel, out_shape=outs, scratch_shapes=list(scratch), comp...  14.8 us
  transfers between devices with their start and end apart: 30, of which 12 were waited for; matrix products, arithmetic and copies ran while one was open for 0% of the time, Pallas kernels for 6%

profile of v13, /device:TPU:1, one launch (start us, length us, event | category | flops | bytes accessed | tf_op | source)
XLA Modules:
  0.0 96.8 jit_solution(17236326951422486798)
XLA Ops:
  2.4 1.3 %collective-permute-start = (f32[3,128,128]{2,1,0:T(8,128)S(1)}, f32[3,128,128]{2,1,0:T(8,128)S(1)}, u32[]{:S(2)}, u32[]{:S(2)}) collective-permute-start(f32[3,128,128]{2,1,0:T(8,128)S(1)} %get-tuple-element.40), channel_id=1, source_target_pairs={{64,0},{65,1},{66,2},{67,3},{68,4},{69,5},{70,6},{71,7},{72,8},{73... | collective-permute-start | bytes 589832 | tf_op jit(solution)/shard_map/ppermute | solution.py:80
  3.7 3.3 %collective-permute-start.1 = (f32[16,128]{1,0:T(8,128)S(1)}, f32[16,128]{1,0:T(8,128)S(1)}, u32[]{:S(2)}, u32[]{:S(2)}) collective-permute-start(f32[16,128]{1,0:T(8,128)S(1)} %get-tuple-element.41), channel_id=1, source_target_pairs={{0,16},{1,17},{2,18},{3,19},{4,20},{5,21},{6,22},{7,23},{8,24},{9,... | collective-permute-start | bytes 24584 | tf_op jit(solution)/shard_map/ppermute | solution.py:80
  7.3 2.6 %collective-permute-start.4 = (f32[16,128]{1,0:T(8,128)S(1)}, f32[16,128]{1,0:T(8,128)S(1)}, u32[]{:S(2)}, u32[]{:S(2)}) collective-permute-start(f32[16,128]{1,0:T(8,128)S(1)} %get-tuple-element.44), channel_id=1, source_target_pairs={{0,16},{1,0},{2,1},{3,2},{4,3},{5,4},{6,5},{7,6},{8,7},{9,8},{10,9... | collective-permute-start | bytes 24584 | tf_op jit(solution)/shard_map/ppermute | solution.py:80
  11.3 2.0 %all_terms.1.uvw_ref = f32[51,128,128]{2,1,0:T(8,128)S(1)} custom-call(f32[16,128,128]{2,1,0:T(8,128)S(1)} %copy-done.2, f32[16,128,128]{2,1,0:T(8,128)S(1)} %copy-done.3, f32[16,128,128]{2,1,0:T(8,128)S(1)} %copy-done.4, f32[3,128,128]{2,1,0:T(8,128)S(1)} %collective-permute-done.above_ref, f32[16,128]{1,0:T(8,128)S(1)} %collective-permute-done.1.inner_ref, ...), custom_call_target="tpu_custom_call" | custom-call | bytes 7500000 | tf_op jit(solution)/shard_map/all_terms/pallas_call | solution.py:91
  13.2 4.6 %collective-permute-start.5 = (f32[51,128,128]{2,1,0:T(8,128)S(1)}, f32[51,128,128]{2,1,0:T(8,128)S(1)}, u32[]{:S(2)}, u32[]{:S(2)}) collective-permute-start(f32[51,128,128]{2,1,0:T(8,128)S(1)} %all_terms.1.uvw_ref), channel_id=1, source_target_pairs={{0,16},{1,17},{2,18},{3,19},{4,20},{5,21},{6,22},{7,23},{8,24},{9,... | collective-permute-start | bytes 10027016 | tf_op jit(solution)/shard_map/ppermute | solution.py:80
  17.9 2.5 %collective-permute-start.6 = (f32[656,128]{1,0:T(8,128)S(1)}, f32[656,128]{1,0:T(8,128)S(1)}, u32[]{:S(2)}, u32[]{:S(2)}) collective-permute-start(f32[656,128]{1,0:T(8,128)S(1)} %pack_rows.1), channel_id=1, source_target_pairs={{16,32},{17,33},{18,34},{19,35},{20,36},{21,37},{22,38},{23,39},{2... | collective-permute-start | bytes 1007624 | tf_op jit(solution)/shard_map/ppermute | solution.py:80
  20.5 1.8 %pack.1 = (f32[480,128]{1,0:T(8,128)S(1)}, f32[480,128]{1,0:T(8,128)S(1)}, f32[80,128]{1,0:T(8,128)S(1)}, f32[80,128]{1,0:T(8,128)S(1)}) custom-call(f32[51,128,128]{2,1,0:T(8,128)S(1)} %all_terms.1.uvw_ref), custom_call_target="tpu_custom_call" | custom-call | bytes 1500000 | tf_op jit(solution)/shard_map/pack/pallas_call | solution.py:91
  22.3 2.1 %collective-permute-start.8 = (f32[480,128]{1,0:T(8,128)S(1)}, f32[480,128]{1,0:T(8,128)S(1)}, u32[]{:S(2)}, u32[]{:S(2)}) collective-permute-start(f32[480,128]{1,0:T(8,128)S(1)} %get-tuple-element.48), channel_id=1, source_target_pairs={{0,32},{1,16},{2,17},{3,18},{4,19},{5,20},{6,21},{7,22},{8,23},{9,... | collective-permute-start | bytes 737288 | tf_op jit(solution)/shard_map/ppermute | solution.py:80
  24.5 3.5 %collective-permute-start.9 = (f32[80,128]{1,0:T(8,128)S(1)}, f32[80,128]{1,0:T(8,128)S(1)}, u32[]{:S(2)}, u32[]{:S(2)}) collective-permute-start(f32[80,128]{1,0:T(8,128)S(1)} %get-tuple-element.50), channel_id=1, source_target_pairs={{0,16},{1,17},{2,18},{3,19},{4,20},{5,21},{6,22},{7,23},{8,24},{9,... | collective-permute-start | bytes 122888 | tf_op jit(solution)/shard_map/ppermute | solution.py:80
  28.8 1.6 %collective-permute-start.10 = (f32[80,128]{1,0:T(8,128)S(1)}, f32[80,128]{1,0:T(8,128)S(1)}, u32[]{:S(2)}, u32[]{:S(2)}) collective-permute-start(f32[80,128]{1,0:T(8,128)S(1)} %pick_corner.1), channel_id=1, source_target_pairs={{0,32},{1,48},{2,49},{3,50},{4,51},{5,52},{6,53},{7,54},{8,55},{9,... | collective-permute-start | bytes 122888 | tf_op jit(solution)/shard_map/ppermute | solution.py:80
  30.5 9.8 %collective-permute-done.10.corner_ref = f32[80,128]{1,0:T(8,128)S(1)} collective-permute-done((f32[80,128]{1,0:T(8,128)S(1)}, f32[80,128]{1,0:T(8,128)S(1)}, u32[]{:S(2)}, u32[]{:S(2)}) %collective-permute-start.10) | collective-permute-done | bytes 40992 | tf_op jit(solution)/shard_map/ppermute | solution.py:80
  40.6 1.6 %collective-permute-done.11.shared_ref = f32[656,128]{1,0:T(8,128)S(1)} collective-permute-done((f32[656,128]{1,0:T(8,128)S(1)}, f32[656,128]{1,0:T(8,128)S(1)}, u32[]{:S(2)}, u32[]{:S(2)}) %collective-permute-start.11) | collective-permute-done | bytes 335904 | tf_op jit(solution)/shard_map/ppermute | solution.py:80
  42.2 2.0 %assemble.1.refs_0_.uv_ref = f32[34,288,128]{2,1,0:T(8,128)S(1)} custom-call(f32[51,128,128]{2,1,0:T(8,128)S(1)} %all_terms.1.uvw_ref, f32[51,128,128]{2,1,0:T(8,128)S(1)} %collective-permute-done.5.other_ref, f32[656,128]{1,0:T(8,128)S(1)} %collective-permute-done.6.got_ref, f32[656,128]{1,0:T(8,128)S(1)} %collective-permute-done.11.shared_ref, ...), custom_call_target="tpu_custom_call" | custom-call | bytes 7500000 | tf_op jit(solution)/shard_map/assemble/pallas_call | solution.py:91
  51.6 1.6 %collective-permute-start.21 = (f32[192,128]{1,0:T(8,128)S(1)}, f32[192,128]{1,0:T(8,128)S(1)}, u32[]{:S(2)}, u32[]{:S(2)}) collective-permute-start(f32[192,128]{1,0:T(8,128)S(1)} %get-tuple-element.62), channel_id=1, source_target_pairs={{64,0},{65,1},{66,2},{67,3},{68,4},{69,5},{70,6},{71,7},{72,8},{73... | collective-permute-start | bytes 294920 | tf_op jit(solution)/shard_map/ppermute | solution.py:80
  53.1 1.3 %collective-permute-start.22 = (f32[64,128]{1,0:T(8,128)S(1)}, f32[64,128]{1,0:T(8,128)S(1)}, u32[]{:S(2)}, u32[]{:S(2)}) collective-permute-start(f32[64,128]{1,0:T(8,128)S(1)} %get-tuple-element.63), channel_id=1, source_target_pairs={{65,16},{66,17},{67,18},{68,19},{69,20},{70,21},{71,22},{72,23},{7... | collective-permute-start | bytes 98312 | tf_op jit(solution)/shard_map/ppermute | solution.py:80
  54.4 1.3 %collective-permute-start.23 = (f32[24,128]{1,0:T(8,128)S(1)}, f32[24,128]{1,0:T(8,128)S(1)}, u32[]{:S(2)}, u32[]{:S(2)}) collective-permute-start(f32[24,128]{1,0:T(8,128)S(1)} %get-tuple-element.64), channel_id=1, source_target_pairs={{64,32},{65,33},{66,34},{67,35},{68,36},{69,37},{70,38},{71,39},{7... | collective-permute-start | bytes 36872 | tf_op jit(solution)/shard_map/ppermute | solution.py:80
  55.7 1.3 %collective-permute-start.24 = (f32[24,128]{1,0:T(8,128)S(1)}, f32[24,128]{1,0:T(8,128)S(1)}, u32[]{:S(2)}, u32[]{:S(2)}) collective-permute-start(f32[24,128]{1,0:T(8,128)S(1)} %get-tuple-element.64), channel_id=1, source_target_pairs={{65,48},{66,49},{67,50},{68,51},{69,52},{70,53},{71,54},{72,55},{7... | collective-permute-start | bytes 36872 | tf_op jit(solution)/shard_map/ppermute | solution.py:80
  58.3 18.4 %collective-permute-done.23.halo_ref = f32[24,128]{1,0:T(8,128)S(1)} collective-permute-done((f32[24,128]{1,0:T(8,128)S(1)}, f32[24,128]{1,0:T(8,128)S(1)}, u32[]{:S(2)}, u32[]{:S(2)}) %collective-permute-start.23) | collective-permute-done | bytes 12320 | tf_op jit(solution)/shard_map/ppermute | solution.py:80
  76.7 4.6 %collective-permute-done.24.halo_outer_ref = f32[24,128]{1,0:T(8,128)S(1)} collective-permute-done((f32[24,128]{1,0:T(8,128)S(1)}, f32[24,128]{1,0:T(8,128)S(1)}, u32[]{:S(2)}, u32[]{:S(2)}) %collective-permute-start.24) | collective-permute-done | bytes 12320 | tf_op jit(solution)/shard_map/ppermute | solution.py:80
  83.1 1.5 %collective-permute-done.25.got_ref = f32[4,128,128]{2,1,0:T(8,128)S(1)} collective-permute-done((f32[4,128,128]{2,1,0:T(8,128)S(1)}, f32[4,128,128]{2,1,0:T(8,128)S(1)}, u32[]{:S(2)}, u32[]{:S(2)}) %collective-permute-start.25) | collective-permute-done | bytes 262176 | tf_op jit(solution)/shard_map/ppermute | solution.py:80
  86.1 1.5 %smooth_rest.1 = (f32[12,128,128]{2,1,0:T(8,128)S(1)}, f32[3,128,128]{2,1,0:T(8,128)S(1)}, f32[3,128,128]{2,1,0:T(8,128)S(1)}) custom-call(f32[12,288,128]{2,1,0:T(8,128)S(1)} %section_rest.1.layers_ref, f32[17,288,128]{2,1,0:T(8,128)S(1)} %assemble_w.1.w_ref), custom_call_target="tpu_custom_call" | custom-call | bytes 9000000 | tf_op jit(solution)/shard_map/smooth_rest/pallas_call | solution.py:91
  88.2 1.6 %collective-permute-start.29 = (f32[3,128,128]{2,1,0:T(8,128)S(1)}, f32[3,128,128]{2,1,0:T(8,128)S(1)}, u32[]{:S(2)}, u32[]{:S(2)}) collective-permute-start(f32[3,128,128]{2,1,0:T(8,128)S(1)} %get-tuple-element.74), channel_id=1, source_target_pairs={{0,192},{1,193},{2,194},{3,195},{4,196},{5,197},{6,198},{7,199},{8... | collective-permute-start | bytes 589832 | tf_op jit(solution)/shard_map/ppermute | solution.py:80
  89.8 4.8 %collective-permute-done.29.above_ref = f32[3,128,128]{2,1,0:T(8,128)S(1)} collective-permute-done((f32[3,128,128]{2,1,0:T(8,128)S(1)}, f32[3,128,128]{2,1,0:T(8,128)S(1)}, u32[]{:S(2)}, u32[]{:S(2)}) %collective-permute-start.29) | collective-permute-done | bytes 196640 | tf_op jit(solution)/shard_map/ppermute | solution.py:80
  95.2 1.5 %finish.1 = f32[16,128,128]{2,1,0:T(8,128)} custom-call(f32[12,128,128]{2,1,0:T(8,128)S(1)} %get-tuple-element.71.kept_ref, f32[3,128,128]{2,1,0:T(8,128)S(1)} %collective-permute-done.26.got_ref, f32[3,128,128]{2,1,0:T(8,128)S(1)} %collective-permute-done.27.got_more_ref, f32[5,128,128]{2,1,0:T(8,128)S(1)} %get-tuple-element.69.top_ref, ...), custom_call_target="tpu_custom_call" | custom-call | bytes 9000000 | tf_op jit(solution)/shard_map/finish/pallas_call | solution.py:91
  (66 shorter events, 18.2 us)
Async XLA Ops:
  2.4 8.9 %collective-permute-start = (f32[3,128,128]{2,1,0:T(8,128)S(1)}, f32[3,128,128]{2,1,0:T(8,128)S(1)}, u32[]{:S(2)}, u32[]{:S(2)}) collective-permute-start(f32[3,128,128]{2,1,0:T(8,128)S(1)} %get-tuple-element.40), channel_id=1, source_target_pairs={{64,0},{65,1},{66,2},{67,3},{68,4},{69,5},{70,6},{71,7},{72,8},{73... | collective-permute-start | bytes 589832 | tf_op jit(solution)/shard_map/ppermute | solution.py:80
  3.7 6.2 %collective-permute-start.1 = (f32[16,128]{1,0:T(8,128)S(1)}, f32[16,128]{1,0:T(8,128)S(1)}, u32[]{:S(2)}, u32[]{:S(2)}) collective-permute-start(f32[16,128]{1,0:T(8,128)S(1)} %get-tuple-element.41), channel_id=1, source_target_pairs={{0,16},{1,17},{2,18},{3,19},{4,20},{5,21},{6,22},{7,23},{8,24},{9,... | collective-permute-start | bytes 24584 | tf_op jit(solution)/shard_map/ppermute | solution.py:80
  7.0 3.1 %collective-permute-start.2 = (f32[16,128]{1,0:T(8,128)S(1)}, f32[16,128]{1,0:T(8,128)S(1)}, u32[]{:S(2)}, u32[]{:S(2)}) collective-permute-start(f32[16,128]{1,0:T(8,128)S(1)} %get-tuple-element.42), channel_id=1, source_target_pairs={{0,48},{1,49},{2,50},{3,51},{4,52},{5,53},{6,54},{7,55},{8,56},{9,... | collective-permute-start | bytes 24584 | tf_op jit(solution)/shard_map/ppermute | solution.py:80
  7.0 3.9 %collective-permute-start.3 = (f32[16,128]{1,0:T(8,128)S(1)}, f32[16,128]{1,0:T(8,128)S(1)}, u32[]{:S(2)}, u32[]{:S(2)}) collective-permute-start(f32[16,128]{1,0:T(8,128)S(1)} %get-tuple-element.43), channel_id=1, source_target_pairs={{0,1},{1,2},{2,3},{3,4},{4,5},{5,6},{6,7},{7,8},{8,9},{9,10},{10,1... | collective-permute-start | bytes 24584 | tf_op jit(solution)/shard_map/ppermute | solution.py:80
  7.3 3.9 %collective-permute-start.4 = (f32[16,128]{1,0:T(8,128)S(1)}, f32[16,128]{1,0:T(8,128)S(1)}, u32[]{:S(2)}, u32[]{:S(2)}) collective-permute-start(f32[16,128]{1,0:T(8,128)S(1)} %get-tuple-element.44), channel_id=1, source_target_pairs={{0,16},{1,0},{2,1},{3,2},{4,3},{5,4},{6,5},{7,6},{8,7},{9,8},{10,9... | collective-permute-start | bytes 24584 | tf_op jit(solution)/shard_map/ppermute | solution.py:80
  13.2 29.0 %collective-permute-start.5 = (f32[51,128,128]{2,1,0:T(8,128)S(1)}, f32[51,128,128]{2,1,0:T(8,128)S(1)}, u32[]{:S(2)}, u32[]{:S(2)}) collective-permute-start(f32[51,128,128]{2,1,0:T(8,128)S(1)} %all_terms.1.uvw_ref), channel_id=1, source_target_pairs={{0,16},{1,17},{2,18},{3,19},{4,20},{5,21},{6,22},{7,23},{8,24},{9,... | collective-permute-start | bytes 10027016 | tf_op jit(solution)/shard_map/ppermute | solution.py:80
  17.9 22.4 %collective-permute-start.6 = (f32[656,128]{1,0:T(8,128)S(1)}, f32[656,128]{1,0:T(8,128)S(1)}, u32[]{:S(2)}, u32[]{:S(2)}) collective-permute-start(f32[656,128]{1,0:T(8,128)S(1)} %pack_rows.1), channel_id=1, source_target_pairs={{16,32},{17,33},{18,34},{19,35},{20,36},{21,37},{22,38},{23,39},{2... | collective-permute-start | bytes 1007624 | tf_op jit(solution)/shard_map/ppermute | solution.py:80
  22.2 18.0 %collective-permute-start.7 = (f32[480,128]{1,0:T(8,128)S(1)}, f32[480,128]{1,0:T(8,128)S(1)}, u32[]{:S(2)}, u32[]{:S(2)}) collective-permute-start(f32[480,128]{1,0:T(8,128)S(1)} %get-tuple-element.47), channel_id=1, source_target_pairs={{0,1},{1,2},{2,3},{3,4},{4,5},{5,6},{6,7},{7,8},{8,9},{9,10},{10,1... | collective-permute-start | bytes 737288 | tf_op jit(solution)/shard_map/ppermute | solution.py:80
  22.3 17.9 %collective-permute-start.8 = (f32[480,128]{1,0:T(8,128)S(1)}, f32[480,128]{1,0:T(8,128)S(1)}, u32[]{:S(2)}, u32[]{:S(2)}) collective-permute-start(f32[480,128]{1,0:T(8,128)S(1)} %get-tuple-element.48), channel_id=1, source_target_pairs={{0,32},{1,16},{2,17},{3,18},{4,19},{5,20},{6,21},{7,22},{8,23},{9,... | collective-permute-start | bytes 737288 | tf_op jit(solution)/shard_map/ppermute | solution.py:80
  24.5 4.4 %collective-permute-start.9 = (f32[80,128]{1,0:T(8,128)S(1)}, f32[80,128]{1,0:T(8,128)S(1)}, u32[]{:S(2)}, u32[]{:S(2)}) collective-permute-start(f32[80,128]{1,0:T(8,128)S(1)} %get-tuple-element.50), channel_id=1, source_target_pairs={{0,16},{1,17},{2,18},{3,19},{4,20},{5,21},{6,22},{7,23},{8,24},{9,... | collective-permute-start | bytes 122888 | tf_op jit(solution)/shard_map/ppermute | solution.py:80
  28.8 11.4 %collective-permute-start.10 = (f32[80,128]{1,0:T(8,128)S(1)}, f32[80,128]{1,0:T(8,128)S(1)}, u32[]{:S(2)}, u32[]{:S(2)}) collective-permute-start(f32[80,128]{1,0:T(8,128)S(1)} %pick_corner.1), channel_id=1, source_target_pairs={{0,32},{1,48},{2,49},{3,50},{4,51},{5,52},{6,53},{7,54},{8,55},{9,... | collective-permute-start | bytes 122888 | tf_op jit(solution)/shard_map/ppermute | solution.py:80
  40.3 1.9 %collective-permute-start.11 = (f32[656,128]{1,0:T(8,128)S(1)}, f32[656,128]{1,0:T(8,128)S(1)}, u32[]{:S(2)}, u32[]{:S(2)}) collective-permute-start(f32[656,128]{1,0:T(8,128)S(1)} %collective-permute-done.6.got_ref), channel_id=1, source_target_pairs={{0,16},{1,17},{2,18},{3,19},{4,20},{5,21},{6,22},{7,23},{8,24},{9,... | collective-permute-start | bytes 1007624 | tf_op jit(solution)/shard_map/ppermute | solution.py:80
  44.3 2.7 %collective-permute-start.12 = (f32[192,128]{1,0:T(8,128)S(1)}, f32[192,128]{1,0:T(8,128)S(1)}, u32[]{:S(2)}, u32[]{:S(2)}) collective-permute-start(f32[192,128]{1,0:T(8,128)S(1)} %get-tuple-element.52), channel_id=1, source_target_pairs={{192,128},{193,129},{194,130},{195,131},{196,132},{197,133},{198,1... | collective-permute-start | bytes 294920 | tf_op jit(solution)/shard_map/ppermute | solution.py:80
  45.0 2.0 %collective-permute-start.13 = (f32[64,128]{1,0:T(8,128)S(1)}, f32[64,128]{1,0:T(8,128)S(1)}, u32[]{:S(2)}, u32[]{:S(2)}) collective-permute-start(f32[64,128]{1,0:T(8,128)S(1)} %get-tuple-element.53), channel_id=1, source_target_pairs={{193,144},{194,145},{195,146},{196,147},{197,148},{198,149},{199,1... | collective-permute-start | bytes 98312 | tf_op jit(solution)/shard_map/ppermute | solution.py:80
  48.6 2.7 %collective-permute-start.17 = (f32[256,128]{1,0:T(8,128)S(1)}, f32[256,128]{1,0:T(8,128)S(1)}, u32[]{:S(2)}, u32[]{:S(2)}) collective-permute-start(f32[256,128]{1,0:T(8,128)S(1)} %get-tuple-element.57), channel_id=1, source_target_pairs={{128,64},{129,65},{130,66},{131,67},{132,68},{133,69},{134,70},{13... | collective-permute-start | bytes 393224 | tf_op jit(solution)/shard_map/ppermute | solution.py:80
  49.3 2.0 %collective-permute-start.18 = (f32[64,128]{1,0:T(8,128)S(1)}, f32[64,128]{1,0:T(8,128)S(1)}, u32[]{:S(2)}, u32[]{:S(2)}) collective-permute-start(f32[64,128]{1,0:T(8,128)S(1)} %get-tuple-element.58), channel_id=1, source_target_pairs={{129,80},{130,81},{131,82},{132,83},{133,84},{134,85},{135,86},{13... | collective-permute-start | bytes 98312 | tf_op jit(solution)/shard_map/ppermute | solution.py:80
  51.6 29.7 %collective-permute-start.21 = (f32[192,128]{1,0:T(8,128)S(1)}, f32[192,128]{1,0:T(8,128)S(1)}, u32[]{:S(2)}, u32[]{:S(2)}) collective-permute-start(f32[192,128]{1,0:T(8,128)S(1)} %get-tuple-element.62), channel_id=1, source_target_pairs={{64,0},{65,1},{66,2},{67,3},{68,4},{69,5},{70,6},{71,7},{72,8},{73... | collective-permute-start | bytes 294920 | tf_op jit(solution)/shard_map/ppermute | solution.py:80
  53.1 28.1 %collective-permute-start.22 = (f32[64,128]{1,0:T(8,128)S(1)}, f32[64,128]{1,0:T(8,128)S(1)}, u32[]{:S(2)}, u32[]{:S(2)}) collective-permute-start(f32[64,128]{1,0:T(8,128)S(1)} %get-tuple-element.63), channel_id=1, source_target_pairs={{65,16},{66,17},{67,18},{68,19},{69,20},{70,21},{71,22},{72,23},{7... | collective-permute-start | bytes 98312 | tf_op jit(solution)/shard_map/ppermute | solution.py:80
  54.4 22.3 %collective-permute-start.23 = (f32[24,128]{1,0:T(8,128)S(1)}, f32[24,128]{1,0:T(8,128)S(1)}, u32[]{:S(2)}, u32[]{:S(2)}) collective-permute-start(f32[24,128]{1,0:T(8,128)S(1)} %get-tuple-element.64), channel_id=1, source_target_pairs={{64,32},{65,33},{66,34},{67,35},{68,36},{69,37},{70,38},{71,39},{7... | collective-permute-start | bytes 36872 | tf_op jit(solution)/shard_map/ppermute | solution.py:80
  55.7 25.5 %collective-permute-start.24 = (f32[24,128]{1,0:T(8,128)S(1)}, f32[24,128]{1,0:T(8,128)S(1)}, u32[]{:S(2)}, u32[]{:S(2)}) collective-permute-start(f32[24,128]{1,0:T(8,128)S(1)} %get-tuple-element.64), channel_id=1, source_target_pairs={{65,48},{66,49},{67,50},{68,51},{69,52},{70,53},{71,54},{72,55},{7... | collective-permute-start | bytes 36872 | tf_op jit(solution)/shard_map/ppermute | solution.py:80
  84.8 10.5 %collective-permute-start.28 = (f32[5,128,128]{2,1,0:T(8,128)S(1)}, f32[5,128,128]{2,1,0:T(8,128)S(1)}, u32[]{:S(2)}, u32[]{:S(2)}) collective-permute-start(f32[5,128,128]{2,1,0:T(8,128)S(1)} %get-tuple-element.69.top_ref), channel_id=1, source_target_pairs={{0,64},{1,65},{2,66},{3,67},{4,68},{5,69},{6,70},{7,71},{8,72},{9,... | collective-permute-start | bytes 983048 | tf_op jit(solution)/shard_map/ppermute | solution.py:80
  87.7 2.2 %collective-permute-start.26 = (f32[3,128,128]{2,1,0:T(8,128)S(1)}, f32[3,128,128]{2,1,0:T(8,128)S(1)}, u32[]{:S(2)}, u32[]{:S(2)}) collective-permute-start(f32[3,128,128]{2,1,0:T(8,128)S(1)} %get-tuple-element.72), channel_id=1, source_target_pairs={{0,16},{1,17},{2,18},{3,19},{4,20},{5,21},{6,22},{7,23},{8,24},{9,... | collective-permute-start | bytes 589832 | tf_op jit(solution)/shard_map/ppermute | solution.py:80
  87.9 2.0 %collective-permute-start.27 = (f32[3,128,128]{2,1,0:T(8,128)S(1)}, f32[3,128,128]{2,1,0:T(8,128)S(1)}, u32[]{:S(2)}, u32[]{:S(2)}) collective-permute-start(f32[3,128,128]{2,1,0:T(8,128)S(1)} %get-tuple-element.73), channel_id=1, source_target_pairs={{0,16},{1,17},{2,18},{3,19},{4,20},{5,21},{6,22},{7,23},{8,24},{9,... | collective-permute-start | bytes 589832 | tf_op jit(solution)/shard_map/ppermute | solution.py:80
  88.2 6.4 %collective-permute-start.29 = (f32[3,128,128]{2,1,0:T(8,128)S(1)}, f32[3,128,128]{2,1,0:T(8,128)S(1)}, u32[]{:S(2)}, u32[]{:S(2)}) collective-permute-start(f32[3,128,128]{2,1,0:T(8,128)S(1)} %get-tuple-element.74), channel_id=1, source_target_pairs={{0,192},{1,193},{2,194},{3,195},{4,196},{5,197},{6,198},{7,199},{8... | collective-permute-start | bytes 589832 | tf_op jit(solution)/shard_map/ppermute | solution.py:80
  (12 other events, 42.4 us)
